TPU v7x, 32 devices: a whole 2x2x4 slice. The times are simulated.
32 devices in a mesh: dp: 8 (over z, x), expert: 4 (over y, core).
Axes of the slice: x: 2, y: 2, z: 4, core: 2. Of those that a mesh axis runs over, the one named last changes fastest.
Arguments:
- tokens: bfloat16 [4096, 2048], P(('dp', 'expert')), may hold values from -6 to 6
- expert_ids: int32 [4096, 2], P(('dp', 'expert')), may hold values from 0 to 3, all different within a row; in each aligned block of 128 rows (0 to 127, 128 to 255, ...) at most 72 rows name the same one
- gate_probs: float32 [4096, 2], P(('dp', 'expert')), may hold values from 0.2 to 1
- w_gate: bfloat16 [4, 2048, 768], P('expert', 'dp'), may hold values from -0.125 to 0.125
- w_up: bfloat16 [4, 2048, 768], P('expert', 'dp'), may hold values from -0.125 to 0.125
- w_down: bfloat16 [4, 768, 2048], P('expert', 'dp'), may hold values from -0.21875 to 0.21875
- d_out: bfloat16 [4096, 2048], P(('dp', 'expert')), may hold values from -6 to 6
Outputs:
- mixed: bfloat16 [4096, 2048], P(('dp', 'expert'))
- d_tokens: bfloat16 [4096, 2048], P(('dp', 'expert'))
- d_probs: float32 [4096, 2], P(('dp', 'expert'))
- d_w_gate: float32 [4, 2048, 768], P('expert', 'dp')
- d_w_up: float32 [4, 2048, 768], P('expert', 'dp')
- d_w_down: float32 [4, 768, 2048], P('expert', 'dp')
Inputs may be any that keep to these rules, and one draw needn't show every extreme that they name: `expert_ids`: in the rows of one device no expert is named more than 72 times, a bound that some block reaches; the 2 ids of a token differ.
All inputs are finite; a program needn't handle non-finite values.
Results may differ from a plain program's by a relative error of at most 0.017.
Values may be sent and summed in bfloat16 or wider, within the bound.
No kernel may reach another device: no remote copies, remote signals or barrier semaphores. Data moves between devices by JAX's collectives and lax.ppermute only.
A program may use at most 128 MiB of HBM per device.

v0:
```python
import jax
import jax.numpy as jnp
from jax import lax
from jax.sharding import PartitionSpec as P


def destinations(ids, experts, cap):
    flat = ids.reshape(-1)
    onehot = (flat[:, None] == jnp.arange(experts, dtype=jnp.int32)[None, :]).astype(jnp.int32)
    before = jnp.cumsum(onehot, axis=0) - onehot
    return flat * cap + jnp.sum(before * onehot, axis=1)


def local(tokens, expert_ids, gate_probs, w_gate, w_up, w_down, d_out):
    experts = lax.axis_size("expert")
    tok_rows, topk = expert_ids.shape
    width = tokens.shape[1]
    hidden_width = w_gate.shape[2]
    cap = tok_rows * topk * 9 // (8 * experts)
    slots = experts * cap
    dest = destinations(expert_ids, experts, cap)
    slot_ids = jnp.arange(slots, dtype=jnp.int32)
    match = dest.reshape(tok_rows, topk)[None, :, :] == slot_ids[:, None, None]
    placing = jnp.any(match, axis=2).astype(jnp.bfloat16)
    slot_probs = jnp.sum(jnp.where(match, gate_probs[None, :, :], 0.0), axis=(1, 2))
    sent = jnp.dot(placing, tokens, preferred_element_type=jnp.float32).astype(jnp.bfloat16)
    gathered = (
        lax.all_gather(w_gate, "dp", axis=1, tiled=True),
        lax.all_gather(w_up, "dp", axis=1, tiled=True),
        lax.all_gather(w_down, "dp", axis=1, tiled=True),
    )
    gate_full, up_full, down_full = (gathered[0][0], gathered[1][0], gathered[2][0])
    arrived = lax.all_to_all(
        sent.reshape(experts, cap, width), "expert", split_axis=0, concat_axis=0, tiled=True
    ).reshape(slots, width)
    gate_pre = jnp.dot(arrived, gate_full, preferred_element_type=jnp.float32)
    up_pre = jnp.dot(arrived, up_full, preferred_element_type=jnp.float32)
    sig = jax.nn.sigmoid(gate_pre)
    act = gate_pre * sig
    hidden = (act * up_pre).astype(jnp.bfloat16)
    produced = jnp.dot(hidden, down_full, preferred_element_type=jnp.float32).astype(jnp.bfloat16)
    returned = lax.all_to_all(
        produced.reshape(experts, cap, width), "expert", split_axis=0, concat_axis=0, tiled=True
    ).reshape(slots, width)
    picked = returned[dest].reshape(tok_rows, topk, width).astype(jnp.float32)
    mixed = jnp.sum(gate_probs[:, :, None] * picked, axis=1).astype(jnp.bfloat16)
    d_probs = jnp.sum(d_out.astype(jnp.float32)[:, None, :] * picked, axis=2)
    grads_sent = jnp.dot(placing, d_out, preferred_element_type=jnp.float32).astype(jnp.bfloat16)
    got_rows, got_probs = (
        lax.all_to_all(
            grads_sent.reshape(experts, cap, width),
            "expert",
            split_axis=0,
            concat_axis=0,
            tiled=True,
        ),
        lax.all_to_all(
            slot_probs.reshape(experts, cap).astype(jnp.bfloat16),
            "expert",
            split_axis=0,
            concat_axis=0,
            tiled=True,
        ).astype(jnp.float32),
    )
    d_produced = (
        got_probs.reshape(slots, 1) * got_rows.reshape(slots, width).astype(jnp.float32)
    ).astype(jnp.bfloat16)
    again = (
        lax.all_gather(w_gate, "dp", axis=1, tiled=True),
        lax.all_gather(w_up, "dp", axis=1, tiled=True),
        lax.all_gather(w_down, "dp", axis=1, tiled=True),
    )
    gate_back, up_back, down_back = (again[0][0], again[1][0], again[2][0])
    gate_again = jnp.dot(arrived, gate_back, preferred_element_type=jnp.float32)
    up_again = jnp.dot(arrived, up_back, preferred_element_type=jnp.float32)
    sig_again = jax.nn.sigmoid(gate_again)
    act_again = gate_again * sig_again
    hidden_again = (act_again * up_again).astype(jnp.bfloat16)
    d_hidden = lax.dot_general(
        d_produced, down_back, (((1,), (1,)), ((), ())), preferred_element_type=jnp.float32
    )
    d_gate = (d_hidden * up_again * sig_again * (1.0 + gate_again * (1.0 - sig_again))).astype(
        jnp.bfloat16
    )
    d_up = (d_hidden * act_again).astype(jnp.bfloat16)
    d_arrived = (
        lax.dot_general(
            d_gate, gate_back, (((1,), (1,)), ((), ())), preferred_element_type=jnp.float32
        )
        + lax.dot_general(
            d_up, up_back, (((1,), (1,)), ((), ())), preferred_element_type=jnp.float32
        )
    ).astype(jnp.bfloat16)
    back_rows = lax.all_to_all(
        d_arrived.reshape(experts, cap, width), "expert", split_axis=0, concat_axis=0, tiled=True
    ).reshape(slots, width)
    d_tokens = jnp.sum(
        back_rows[dest].reshape(tok_rows, topk, width).astype(jnp.float32), axis=1
    ).astype(jnp.bfloat16)
    both_grads = jnp.concatenate([d_gate, d_up], axis=1)
    contract = (((0,), (0,)), ((), ()))
    columns = arrived
    gate_up_local = lax.psum_scatter(
        lax.dot_general(columns, both_grads, contract, preferred_element_type=jnp.float32).astype(
            jnp.bfloat16
        ),
        "dp",
        scatter_dimension=0,
        tiled=True,
    ).astype(jnp.float32)
    columns = hidden_again
    down_local = lax.psum_scatter(
        lax.dot_general(columns, d_produced, contract, preferred_element_type=jnp.float32).astype(
            jnp.bfloat16
        ),
        "dp",
        scatter_dimension=0,
        tiled=True,
    ).astype(jnp.float32)
    d_w_gate = gate_up_local[:, :hidden_width][None]
    d_w_up = gate_up_local[:, hidden_width:][None]
    d_w_down = down_local[None]
    return (mixed, d_tokens, d_probs, d_w_gate, d_w_up, d_w_down)


def solution(mesh):
    placed = (
        P(("dp", "expert"), None),
        P(("dp", "expert"), None),
        P(("dp", "expert"), None),
        P("expert", "dp", None),
        P("expert", "dp", None),
        P("expert", "dp", None),
        P(("dp", "expert"), None),
    )
    return jax.shard_map(
        local,
        mesh=mesh,
        in_specs=placed,
        out_specs=(
            P(("dp", "expert"), None),
            P(("dp", "expert"), None),
            P(("dp", "expert"), None),
            P("expert", "dp", None),
            P("expert", "dp", None),
            P("expert", "dp", None),
        ),
        check_vma=False,
    )
```

profile of v0, /device:TPU:9, one launch (start us, length us, event | category | flops | bytes accessed | tf_op | source)
XLA Modules:
  0.0 405.5 jit_solution(2620030230412113873)
XLA Ops:
  13.9 3.9 all-to-all-start.2
  17.8 1.5 convolution_convert_fusion.2
  19.3 1.4 all-to-all-done.2
  20.7 4.2 %all-to-all-start.3 = ((bf16[4,72,2048]{2,1,0:T(8,128)(2,1)}), bf16[4,72,2048]{2,1,0:T(8,128)(2,1)S(1)}, u32[]{:S(2)}, u32[]{:S(2)}) async-start(bf16[4,72,2048]{2,1,0:T(8,128)(2,1)} %bitcast.12), calls=%async_computation.3 | async-start | bytes 2359296 | tf_op jit(solution)/shard_map/all_to_all | solution.py:50
  24.9 1.5 convolution_convert_fusion.3
  26.5 13.4 %all-to-all-done.3 = bf16[4,72,2048]{2,1,0:T(8,128)(2,1)S(1)} async-done(((bf16[4,72,2048]{2,1,0:T(8,128)(2,1)}), bf16[4,72,2048]{2,1,0:T(8,128)(2,1)S(1)}, u32[]{:S(2)}, u32[]{:S(2)}) %all-to-all-start.3) | async-done | bytes 1179680 | tf_op jit(solution)/shard_map/all_to_all | solution.py:50
  39.9 4.4 %all-to-all-start = ((bf16[4,72,2048]{2,1,0:T(8,128)(2,1)}), bf16[4,72,2048]{2,1,0:T(8,128)(2,1)S(1)}, u32[]{:S(2)}, u32[]{:S(2)}) async-start(bf16[4,72,2048]{2,1,0:T(8,128)(2,1)} %bitcast.2), calls=%async_computation | async-start | bytes 2359296 | tf_op jit(solution)/shard_map/all_to_all | solution.py:33
  46.9 23.7 %all-gather.8.cloned.1.call-done = bf16[1,768,2048]{2,1,0:T(8,128)(2,1)} async-done(((bf16[1,96,2048]{2,1,0:T(8,128)(2,1)}), bf16[1,768,2048]{2,1,0:T(8,128)(2,1)}) %all-gather.8.cloned.1.call-update) | async-done | bytes 3145744 | tf_op jit(solution)/shard_map/all_gather | solution.py:30
  70.6 4.3 %fusion = f32[288,768]{1,0:T(8,128)} fusion(bf16[288,2048]{1,0:T(8,128)(2,1)} %bitcast.83, bf16[1,768,2048]{2,1,0:T(8,128)(2,1)} %all-gather.8.cloned.1.call-done), kind=kOutput, calls=%fused_computation.4 | convolution fusion | flops 905969664 | bytes 5210112 | tf_op jit(solution)/shard_map/dot_general | solution.py:79
  74.9 57.0 %all-gather.6.cloned.1.call-done = bf16[1,2048,768]{2,1,0:T(8,128)(2,1)} async-done(((bf16[1,256,768]{2,1,0:T(8,128)(2,1)}), bf16[1,2048,768]{2,1,0:T(8,128)(2,1)}) %all-gather.6.cloned.1.call-update) | async-done | bytes 3145744 | tf_op jit(solution)/shard_map/all_gather | solution.py:29
  131.9 3.9 fusion.6
  135.8 57.4 %all-gather.4.cloned.1.call-done = bf16[1,2048,768]{2,1,0:T(8,128)(2,1)} async-done(((bf16[1,256,768]{2,1,0:T(8,128)(2,1)}), bf16[1,2048,768]{2,1,0:T(8,128)(2,1)}) %all-gather.4.cloned.1.call-update) | async-done | bytes 3145744 | tf_op jit(solution)/shard_map/all_gather | solution.py:28
  193.2 4.6 %multiply_convert_fusion.2 = (bf16[288,768]{1,0:T(8,128)(2,1)}, bf16[288,768]{1,0:T(8,128)(2,1)}, bf16[288,768]{1,0:T(8,128)(2,1)S(1)}) fusion(f32[288,768]{1,0:T(8,128)} %fusion, f32[288,768]{1,0:T(8,128)} %fusion.6, bf16[288,2048]{1,0:T(8,128)(2,1)S(1)} %bitcast.80, bf16[1,2048,768]{2,1,0:T(8,128)(2,1)} %all-gather.4.cloned.1.call-done), kind=kOutput, calls=%fused_computation.30 | convolution fusion | flops 909287424 | bytes 7421952 | tf_op jit(solution)/shard_map/dot_general | solution.py:36
  198.6 3.6 convolution_convert_fusion.1
  203.3 5.5 %convolution_convert_fusion = bf16[2048,1536]{1,0:T(8,128)(2,1)} fusion(bf16[288,2048]{1,0:T(8,128)(2,1)S(1)} %bitcast.81, bf16[288,768]{1,0:T(8,128)(2,1)S(1)} %copy-done.6, bf16[288,768]{1,0:T(8,128)(2,1)S(1)} %copy-done.8), kind=kOutput, calls=%fused_computation.2 | convolution fusion | flops 1816854528 | bytes 8355840 | tf_op jit(solution)/shard_map/dot_general | solution.py:104
  209.8 4.0 fusion.18
  213.8 5.5 %all-to-all-start.1 = ((bf16[4,72,2048]{2,1,0:T(8,128)(2,1)}), bf16[4,72,2048]{2,1,0:T(8,128)(2,1)S(1)}, u32[]{:S(2)}, u32[]{:S(2)}) async-start(bf16[4,72,2048]{2,1,0:T(8,128)(2,1)} %bitcast.7), calls=%async_computation.1 | async-start | bytes 2359296 | tf_op jit(solution)/shard_map/all_to_all | solution.py:42
  219.3 3.2 fusion.4
  222.6 2.2 fusion.15
  224.7 9.7 %all-to-all-done.1 = bf16[4,72,2048]{2,1,0:T(8,128)(2,1)S(1)} async-done(((bf16[4,72,2048]{2,1,0:T(8,128)(2,1)}), bf16[4,72,2048]{2,1,0:T(8,128)(2,1)S(1)}, u32[]{:S(2)}, u32[]{:S(2)}) %all-to-all-start.1) | async-done | bytes 1179680 | tf_op jit(solution)/shard_map/all_to_all | solution.py:42
  234.4 4.3 %all-to-all-start.4 = ((bf16[4,72,2048]{2,1,0:T(8,128)(2,1)}), bf16[4,72,2048]{2,1,0:T(8,128)(2,1)S(1)}, u32[]{:S(2)}, u32[]{:S(2)}) async-start(bf16[4,72,2048]{2,1,0:T(8,128)(2,1)} %bitcast.82), calls=%async_computation.4 | async-start | bytes 2359296 | tf_op jit(solution)/shard_map/all_to_all | solution.py:94
  240.1 2.3 gather_fusion
  242.5 3.3 reshape.147
  245.8 7.9 %all-to-all-done.4 = bf16[4,72,2048]{2,1,0:T(8,128)(2,1)S(1)} async-done(((bf16[4,72,2048]{2,1,0:T(8,128)(2,1)}), bf16[4,72,2048]{2,1,0:T(8,128)(2,1)S(1)}, u32[]{:S(2)}, u32[]{:S(2)}) %all-to-all-start.4) | async-done | bytes 1179680 | tf_op jit(solution)/shard_map/all_to_all | solution.py:94
  253.7 2.3 gather_fusion.1
  256.0 2.7 reshape.146
  258.7 6.0 %multiply_reduce_fusion = (f32[128,2]{1,0:T(8,128)S(1)}, bf16[128,2048]{1,0:T(8,128)(2,1)}) fusion(f32[128,2,2048]{2,1,0:T(2,128)S(1)} %copy-done.1, f32[128,2048]{1,0:T(8,128)} %convert_element_type.123, f32[128,2]{1,0:T(8,128)S(1)} %copy.42), kind=kLoop, calls=%fused_computation.24 | loop fusion | flops 1834752 | bytes 3672064 | tf_op jit(solution)/shard_map/reduce_sum | solution.py:47
  265.3 4.6 %reduce_sum.57 = bf16[128,2048]{1,0:T(8,128)(2,1)} reduce(bf16[128,2,2048]{2,1,0:T(2,128)(2,1)} %reshape.146, bf16[]{:T(256)} %constant.18.clone.1), dimensions={1}, to_apply=%region_6.7 | reduce | flops 262144 | bytes 1572866 | tf_op jit(solution)/shard_map/reduce_sum | solution.py:97
  269.9 6.0 %reduce-scatter.5.cloned.1.call-done = bf16[96,2048]{1,0:T(8,128)(2,1)} async-done(((bf16[768,2048]{1,0:T(8,128)(2,1)}), bf16[96,2048]{1,0:T(8,128)(2,1)}) %reduce-scatter.5.cloned.1.call-update) | async-done | bytes 393232 | tf_op jit(solution)/shard_map/reduce_scatter | solution.py:112
  275.8 1.9 bitcast_convert_fusion
  277.8 118.6 %reduce-scatter.3.cloned.1.call-done = bf16[256,1536]{1,0:T(8,128)(2,1)} async-done(((bf16[2048,1536]{1,0:T(8,128)(2,1)}), bf16[256,1536]{1,0:T(8,128)(2,1)}) %reduce-scatter.3.cloned.1.call-update) | async-done | bytes 786448 | tf_op jit(solution)/shard_map/reduce_scatter | solution.py:103
  396.4 1.3 convert_element_type.125
  (65 shorter events, 15.6 us)
Async XLA Ops:
  7.2 17.8 %copy-start = (bf16[128,2048]{1,0:T(8,128)(2,1)S(1)}, bf16[128,2048]{1,0:T(8,128)(2,1)}, u32[]{:S(2)}) copy-start(bf16[128,2048]{1,0:T(8,128)(2,1)} %param.7) | copy-start | bytes 1572868
  7.2 10.6 %copy-start.2 = (bf16[128,2048]{1,0:T(8,128)(2,1)S(1)}, bf16[128,2048]{1,0:T(8,128)(2,1)}, u32[]{:S(2)}) copy-start(bf16[128,2048]{1,0:T(8,128)(2,1)} %param.13) | copy-start | bytes 1572868
  7.2 63.4 %all-gather.8.cloned.1.call-start = ((), (), s32[]{:S(2)}) async-start(), calls=%async_computation.9 | async-start | bytes 3538944 | tf_op jit(solution)/shard_map/all_gather | solution.py:30
  7.9 124.0 %all-gather.6.cloned.1.call-start = ((), (), s32[]{:S(2)}) async-start(), calls=%async_computation.8 | async-start | bytes 3538944 | tf_op jit(solution)/shard_map/all_gather | solution.py:29
  8.7 184.5 %all-gather.4.cloned.1.call-start = ((), (), s32[]{:S(2)}) async-start(), calls=%async_computation.7 | async-start | bytes 3538944 | tf_op jit(solution)/shard_map/all_gather | solution.py:28
  13.9 6.9 %all-to-all-start.2 = ((bf16[4,1,72]{2,1,0:T(2,128)(2,1)}), bf16[4,1,72]{2,1,0:T(2,128)(2,1)S(1)}, u32[]{:S(2)}, u32[]{:S(2)}) async-start(bf16[4,1,72]{2,1,0:T(2,128)(2,1)} %convert_element_type.136), calls=%async_computation.2 | async-start | bytes 4096 | tf_op jit(solution)/shard_map/all_to_all | solution.py:57
  20.7 19.2 %all-to-all-start.3 = ((bf16[4,72,2048]{2,1,0:T(8,128)(2,1)}), bf16[4,72,2048]{2,1,0:T(8,128)(2,1)S(1)}, u32[]{:S(2)}, u32[]{:S(2)}) async-start(bf16[4,72,2048]{2,1,0:T(8,128)(2,1)} %bitcast.12), calls=%async_computation.3 | async-start | bytes 2359296 | tf_op jit(solution)/shard_map/all_to_all | solution.py:50
  39.9 35.0 %all-to-all-start = ((bf16[4,72,2048]{2,1,0:T(8,128)(2,1)}), bf16[4,72,2048]{2,1,0:T(8,128)(2,1)S(1)}, u32[]{:S(2)}, u32[]{:S(2)}) async-start(bf16[4,72,2048]{2,1,0:T(8,128)(2,1)} %bitcast.2), calls=%async_computation | async-start | bytes 2359296 | tf_op jit(solution)/shard_map/all_to_all | solution.py:33
  44.3 231.6 %reduce-scatter.5.cloned.1.call-start = ((), (), s32[]{:S(2)}) async-start(), calls=%async_computation.11 | async-start | bytes 3538944 | tf_op jit(solution)/shard_map/reduce_scatter | solution.py:112
  135.8 62.7 %copy-start.3 = (bf16[288,2048]{1,0:T(8,128)(2,1)S(1)}, bf16[288,2048]{1,0:T(8,128)(2,1)}, u32[]{:S(2)}) copy-start(bf16[288,2048]{1,0:T(8,128)(2,1)} %fusion.21) | copy-start | bytes 3538948
  197.8 0.8 copy-start.10
  202.1 1.0 copy-start.6
  202.1 1.1 copy-start.8
  202.2 194.2 %reduce-scatter.3.cloned.1.call-start = ((), (), s32[]{:S(2)}) async-start(), calls=%async_computation.10 | async-start | bytes 7077888 | tf_op jit(solution)/shard_map/reduce_scatter | solution.py:103
  208.8 1.0 copy-start.11
  213.8 5.5 %copy-start.7 = (bf16[288,768]{1,0:T(8,128)(2,1)S(1)}, bf16[288,768]{1,0:T(8,128)(2,1)}, u32[]{:S(2)}) copy-start(bf16[288,768]{1,0:T(8,128)(2,1)} %get-tuple-element.27) | copy-start | bytes 1327108
  213.8 20.6 %all-to-all-start.1 = ((bf16[4,72,2048]{2,1,0:T(8,128)(2,1)}), bf16[4,72,2048]{2,1,0:T(8,128)(2,1)S(1)}, u32[]{:S(2)}, u32[]{:S(2)}) async-start(bf16[4,72,2048]{2,1,0:T(8,128)(2,1)} %bitcast.7), calls=%async_computation.1 | async-start | bytes 2359296 | tf_op jit(solution)/shard_map/all_to_all | solution.py:42
  219.3 3.2 copy-start.5
  219.3 3.2 copy-start.9
  224.7 15.1 %copy-start.4 = (f32[128,2]{0,1:T(2,128)S(1)}, f32[128,2]{0,1:T(2,128)}, u32[]{:S(2)}) copy-start(f32[128,2]{0,1:T(2,128)} %param.9) | copy-start | bytes 3076
  234.4 19.3 %all-to-all-start.4 = ((bf16[4,72,2048]{2,1,0:T(8,128)(2,1)}), bf16[4,72,2048]{2,1,0:T(8,128)(2,1)S(1)}, u32[]{:S(2)}, u32[]{:S(2)}) async-start(bf16[4,72,2048]{2,1,0:T(8,128)(2,1)} %bitcast.82), calls=%async_computation.4 | async-start | bytes 2359296 | tf_op jit(solution)/shard_map/all_to_all | solution.py:94
  256.0 2.7 copy-start.1
Sparse Core Ops, SparseCore 0:
  10.2 60.3 all-gather.7
  72.8 59.0 all-gather.5
  134.1 59.0 all-gather.3
  202.3 73.5 reduce-scatter.4
  279.3 117.0 reduce-scatter.2
where the time goes:
time: 409 us; the launch traced here: 406 us
  waiting for transfers between devices  297 us (73%)
  matrix products  34.3 us (8%)
  starting transfers between devices  22.4 us (5%)
  other arithmetic  19.8 us (5%)
  local copies, waits for them, and re-layouts  18 us (4%)
  between operations  13.9 us (3%)
    reduce_scatter x1, waiting for transfers between devices, local(): lax.psum_scatter(lax.dot_general(columns, both_grads, contract, preferred...  119 us
    all_gather x1, waiting for transfers between devices, local(): lax.all_gather(w_gate, 'dp', axis=1, tiled=True)  57.4 us
    all_gather x1, waiting for transfers between devices, local(): lax.all_gather(w_up, 'dp', axis=1, tiled=True)  57 us
    all_gather x1, waiting for transfers between devices, local(): lax.all_gather(w_down, 'dp', axis=1, tiled=True)  23.7 us
    all_to_all x1, waiting for transfers between devices, local(): lax.all_to_all(grads_sent.reshape(experts, cap, width), 'expert', split_a...  13.4 us
    all_to_all x1, waiting for transfers between devices, local(): lax.all_to_all(produced.reshape(experts, cap, width), 'expert', split_axi...  9.7 us
  transfers between devices with their start and end apart: 10, of which 9 were waited for; matrix products, arithmetic and copies ran while one was open for 14% of the time, Pallas kernels for 0%

commit v1 on v0

v1 whole, which is shorter than its diff:
```python
import jax
import jax.numpy as jnp
from jax import lax
from jax.sharding import PartitionSpec as P

BF = jnp.bfloat16
F32 = jnp.float32
BOTH = ("dp", "expert")


def dot(a, b, dims=((1,), (0,))):
    return lax.dot_general(a, b, (dims, ((), ())), preferred_element_type=F32)


class Grid:
    def __init__(self):
        self.dps, self.experts = lax.axis_size("dp"), lax.axis_size("expert")
        self.zs, self.qs = self.dps // 2, self.experts // 2
        dp, ex = lax.axis_index("dp"), lax.axis_index("expert")
        self.z, self.x, self.q, self.c = dp // 2, dp % 2, ex // 2, ex % 2
        self.z_groups = [[z * 2 + x for z in range(self.zs)] for x in range(2)]

    def send(self, value, move):
        pairs = []
        for z in range(self.zs):
            for x in range(2):
                for q in range(self.qs):
                    for c in range(2):
                        to = move(z, x, q, c)
                        if 0 <= to[0] < self.zs:
                            pairs.append((self.flat(z, x, q, c), self.flat(*to)))
        return lax.ppermute(value, BOTH, pairs)

    def flat(self, z, x, q, c):
        return (z * 2 + x) * self.experts + q * 2 + c


def local(tokens, expert_ids, gate_probs, w_gate, w_up, w_down, d_out):
    g = Grid()
    rows, topk = expert_ids.shape
    width = tokens.shape[1]
    hidden_width = w_gate.shape[2]
    half = hidden_width // 2
    experts = g.experts
    cap = rows * topk * 9 // (8 * experts)
    slots = experts * cap
    first = g.c == 0

    block = hidden_width // g.dps
    part = block // 2
    place = jnp.arange(hidden_width, dtype=jnp.int32)
    in_half = place % half
    source_col = (in_half // part) * block + ((place // half) ^ g.x) * part + in_half % part
    shuffle = (jnp.arange(hidden_width, dtype=jnp.int32)[:, None] == source_col[None, :]).astype(BF)

    def out_a(z, x, q, c):
        return z, c, q, x

    def out_b(z, x, q, c):
        return z, c, q, 1 - x

    def back_a(z, x, q, c):
        return z, c, q, x

    def back_b(z, x, q, c):
        return z, 1 - c, q, x

    def spread(part_a, part_b):
        got_a, got_b = g.send(part_a, out_a), g.send(part_b, out_b)
        return jnp.concatenate([jnp.where(first, got_a, got_b), jnp.where(first, got_b, got_a)], axis=0)

    def unspread(both):
        n = both.shape[0] // 2
        low, high = both[:n], both[n:]
        return g.send(jnp.where(first, low, high), back_a), g.send(jnp.where(first, high, low), back_b)

    gate_cols = dot(w_gate[0], shuffle).astype(BF)
    up_cols = dot(w_up[0], shuffle).astype(BF)
    gate_up_shard = spread(
        jnp.concatenate([gate_cols[:, :half], up_cols[:, :half]], axis=1),
        jnp.concatenate([gate_cols[:, half:], up_cols[:, half:]], axis=1),
    )
    down_low, down_high = w_down[0, :part], w_down[0, part:]
    even = g.x == 0
    down_shard = spread(jnp.where(even, down_low, down_high), jnp.where(even, down_high, down_low))
    gate_up = lax.all_gather(gate_up_shard, "dp", axis=0, tiled=True, axis_index_groups=g.z_groups)
    down = lax.all_gather(down_shard, "dp", axis=0, tiled=True, axis_index_groups=g.z_groups)

    expert_iota = jnp.arange(experts, dtype=jnp.int32)
    chosen = expert_ids[:, :, None] == expert_iota
    named = jnp.any(chosen, axis=1).astype(BF)
    token_iota = jnp.arange(rows, dtype=jnp.int32)
    earlier = (token_iota[:, None] > token_iota[None, :]).astype(BF)
    before = dot(earlier, named)
    slot = jnp.sum(jnp.where(chosen, before[:, None, :], 0.0), axis=2).astype(jnp.int32)
    relative = ((expert_ids // 2 - g.q + g.qs) % g.qs) * 2 + ((expert_ids % 2) ^ g.x)
    dest = relative * cap + slot
    slot_iota = jnp.arange(slots, dtype=jnp.int32)
    pair = dest[:, :, None] == slot_iota
    placing = jnp.any(pair, axis=1).astype(BF)
    weighted = jnp.sum(jnp.where(pair, gate_probs[:, :, None], 0.0), axis=1)
    slot_probs = jnp.sum(weighted, axis=0)

    def member(r, sign):
        def move(z, x, q, c):
            return z, x ^ (r % 2), (q + sign * (r // 2)) % g.qs, c

        return move

    def other_core(z, x, q, c):
        return z, x, q, 1 - c

    def dispatch(sent):
        got = [sent[:cap]] + [g.send(sent[r * cap:(r + 1) * cap], member(r, 1)) for r in range(1, experts)]
        mine = jnp.concatenate(got, axis=0)
        return jnp.concatenate([mine, g.send(mine, other_core)], axis=0)

    def give_back(partial):
        other = g.send(partial[slots:].astype(BF), other_core)
        mine = (partial[:slots] + other.astype(F32)).astype(BF)
        got = [mine[:cap]] + [g.send(mine[r * cap:(r + 1) * cap], member(r, -1)) for r in range(1, experts)]
        return jnp.concatenate(got, axis=0)

    arrived = dispatch(dot(placing, tokens, ((0,), (0,))).astype(BF))
    d_produced = dispatch((slot_probs[:, None] * dot(placing, d_out, ((0,), (0,)))).astype(BF))

    pre = dot(arrived, gate_up)
    gate_pre, up_pre = pre[:, :half], pre[:, half:]
    sig = jax.nn.sigmoid(gate_pre)
    act = gate_pre * sig
    hidden = (act * up_pre).astype(BF)

    def scatter(partial):
        return lax.psum_scatter(
            partial.astype(BF), "dp", scatter_dimension=0, tiled=True, axis_index_groups=g.z_groups
        ).astype(BF)

    down_grad = scatter(dot(hidden, d_produced, ((0,), (0,))))
    returned = give_back(dot(hidden, down))

    d_hidden = dot(d_produced, down, ((1,), (1,)))
    d_gate = (d_hidden * up_pre * sig * (1.0 + gate_pre * (1.0 - sig))).astype(BF)
    d_up = (d_hidden * act).astype(BF)
    d_both = jnp.concatenate([d_gate, d_up], axis=1)
    gate_up_grad = scatter(dot(arrived, d_both, ((0,), (0,))))
    back_rows = give_back(dot(d_both, gate_up, ((1,), (1,))))

    high = lax.reduce_precision(weighted, 8, 7)
    mixed = (dot(high.astype(BF), returned) + dot((weighted - high).astype(BF), returned)).astype(BF)
    products = dot(d_out, returned, ((1,), (1,)))
    d_probs = jnp.sum(jnp.where(pair, products[:, None, :], 0.0), axis=2)
    d_tokens = dot(placing, back_rows).astype(BF)

    down_a, down_b = unspread(down_grad)
    d_w_down = jnp.where(
        even, jnp.concatenate([down_a, down_b], axis=0), jnp.concatenate([down_b, down_a], axis=0)
    ).astype(F32)[None]
    both_a, both_b = unspread(gate_up_grad)
    d_w_gate = dot(jnp.concatenate([both_a[:, :half], both_b[:, :half]], axis=1), shuffle, ((1,), (1,)))[None]
    d_w_up = dot(jnp.concatenate([both_a[:, half:], both_b[:, half:]], axis=1), shuffle, ((1,), (1,)))[None]
    return (mixed, d_tokens, d_probs, d_w_gate, d_w_up, d_w_down)


def solution(mesh):
    rows = P(("dp", "expert"), None)
    weight = P("expert", "dp", None)
    return jax.shard_map(
        local,
        mesh=mesh,
        in_specs=(rows, rows, rows, weight, weight, weight, rows),
        out_specs=(rows, rows, rows, weight, weight, weight),
        check_vma=False,
    )
```

time: 409 us -> 292 us (0.71)
  waiting for transfers between devices: 297 us -> 194 us
  other arithmetic: 19.8 us -> 7.63 us
  local copies, waits for them, and re-layouts: 18 us -> 9.11 us
  starting transfers between devices: 22.4 us -> 30 us
    all_gather x3 -> x2, waiting for transfers between devices: 138 us -> 67 us  [the longest x1 34 us: local(): lax.all_gather(gate_up_shard, 'dp', axis=0, tiled=True, axis_index_groups...]
    ppermute x0 -> x24, waiting for transfers between devices: none -> 59.4 us  [send(): return lax.ppermute(value, BOTH, pairs)]
    reduce_scatter x2, waiting for transfers between devices: 125 us -> 67.8 us  [scatter(): lax.psum_scatter(partial.astype(BF), 'dp', scatter_dimension=0, tiled=Tru...]
    all_to_all x5 -> x0, waiting for transfers between devices: 32.4 us -> none  [the longest x1 13.4 us: local(): lax.all_to_all(grads_sent.reshape(experts, cap, width), 'expert', split_a...]
    ppermute x0 -> x24, starting transfers between devices: none -> 29.7 us  [send(): return lax.ppermute(value, BOTH, pairs)]
    all_to_all x5 -> x0, starting transfers between devices: 22.2 us -> none  [the longest x1 5.49 us: local(): lax.all_to_all(produced.reshape(experts, cap, width), 'expert', split_axi...]
    reduce_sum x4 -> x2, other arithmetic: 11.4 us -> 0.65 us  [the longest x1 0.62 us: local(): slot_probs = jnp.sum(weighted, axis=0)]
    gather x2 -> x0, local copies, waits for them, and re-layouts: 4.64 us -> none  [the longest x1 2.32 us: local(): picked = returned[dest].reshape(tok_rows, topk, width).astype(jnp.float32)]
  transfers between devices with their start and end apart: 10 -> 28, of which waited for: 9 -> 20; matrix products, arithmetic and copies ran while one was open for 14% -> 11% of each run, Pallas kernels for 0% -> 0%
where the time goes in v1:
time: 292 us; the launch traced here: 290 us
  waiting for transfers between devices  194 us (66%)
  matrix products  35.1 us (12%)
  starting transfers between devices  30 us (10%)
  between operations  14.3 us (5%)
  local copies, waits for them, and re-layouts  9.11 us (3%)
  other arithmetic  7.63 us (3%)
    reduce_scatter x2, waiting for transfers between devices, scatter(): lax.psum_scatter(partial.astype(BF), 'dp', scatter_dimension=0, tiled=Tru...  67.8 us
    ppermute x24, waiting for transfers between devices, send(): return lax.ppermute(value, BOTH, pairs)  59.4 us
    dot_general x17, matrix products, dot(): return lax.dot_general(a, b, (dims, ((), ())), preferred_element_type=F32)  35.1 us
    all_gather x1, waiting for transfers between devices, local(): lax.all_gather(gate_up_shard, 'dp', axis=0, tiled=True, axis_index_groups...  34 us
    all_gather x1, waiting for transfers between devices, local(): lax.all_gather(down_shard, 'dp', axis=0, tiled=True, axis_index_groups=g....  33 us
    ppermute x24, starting transfers between devices, send(): return lax.ppermute(value, BOTH, pairs)  29.7 us
    unnamed x38, local copies, waits for them, and re-layouts  6.15 us
  transfers between devices with their start and end apart: 28, of which 20 were waited for; matrix products, arithmetic and copies ran while one was open for 11% of the time, Pallas kernels for 0%

profile of v1, /device:TPU:9, one launch (start us, length us, event | category | flops | bytes accessed | tf_op | source)
XLA Modules:
  0.0 290.3 jit_solution(17639002228202620563)
XLA Ops:
  7.3 1.6 fusion.19
  11.7 3.1 %collective-permute-start.4 = (bf16[256,768]{0,1:T(8,128)(2,1)S(1)}, bf16[256,768]{0,1:T(8,128)(2,1)S(1)}, u32[]{:S(2)}, u32[]{:S(2)}) collective-permute-start(bf16[256,768]{0,1:T(8,128)(2,1)S(1)} %pad_maximum_fusion.7), channel_id=1, source_target_pairs={{0,0},{1,4},{2,2},{3,6},{4,1},{5,5},{6,3},{7,7},{8,8},{9,12},{10,1... | collective-permute-start | bytes 1179656 | tf_op jit(solution)/shard_map/ppermute | solution.py:32
  16.4 6.0 %collective-permute-done.4 = bf16[256,768]{0,1:T(8,128)(2,1)S(1)} collective-permute-done((bf16[256,768]{0,1:T(8,128)(2,1)S(1)}, bf16[256,768]{0,1:T(8,128)(2,1)S(1)}, u32[]{:S(2)}, u32[]{:S(2)}) %collective-permute-start.4) | collective-permute-done | bytes 393248 | tf_op jit(solution)/shard_map/ppermute | solution.py:32
  24.3 2.5 collective-permute-start.6
  28.5 2.1 collective-permute-start.2
  32.6 5.9 %collective-permute-done.2 = bf16[72,2048]{1,0:T(8,128)(2,1)S(1)} collective-permute-done((bf16[72,2048]{1,0:T(8,128)(2,1)S(1)}, bf16[72,2048]{1,0:T(8,128)(2,1)S(1)}, u32[]{:S(2)}, u32[]{:S(2)}) %collective-permute-start.2) | collective-permute-done | bytes 294944 | tf_op jit(solution)/shard_map/ppermute | solution.py:32
  38.5 6.6 %collective-permute-done.1 = bf16[72,2048]{1,0:T(8,128)(2,1)S(1)} collective-permute-done((bf16[72,2048]{1,0:T(8,128)(2,1)S(1)}, bf16[72,2048]{1,0:T(8,128)(2,1)S(1)}, u32[]{:S(2)}, u32[]{:S(2)}) %collective-permute-start.1) | collective-permute-done | bytes 294944 | tf_op jit(solution)/shard_map/ppermute | solution.py:32
  45.2 1.8 collective-permute-start.3
  50.8 34.0 %all-gather.3.cloned.1.call-done = bf16[2048,768]{0,1:T(8,128)(2,1)} async-done(((bf16[512,768]{0,1:T(8,128)(2,1)}), bf16[2048,768]{0,1:T(8,128)(2,1)}) %all-gather.3.cloned.1.call-update) | async-done | bytes 3145744 | tf_op jit(solution)/shard_map/all_gather | solution.py:86
  84.7 4.6 %fusion.85 = f32[576,768]{1,0:T(8,128)S(1)} fusion(bf16[576,2048]{1,0:T(8,128)(2,1)} %constant_dynamic-update-slice_fusion, bf16[2048,768]{0,1:T(8,128)(2,1)} %all-gather.3.cloned.1.call-done), kind=kOutput, calls=%fused_computation.145 | convolution fusion | flops 1811939328 | bytes 7274496 | tf_op jit(solution)/shard_map/dot_general | solution.py:12
  90.9 33.0 %all-gather.5.cloned.1.call-done = bf16[384,2048]{1,0:T(8,128)(2,1)} async-done(((bf16[96,2048]{1,0:T(8,128)(2,1)}), bf16[384,2048]{1,0:T(8,128)(2,1)}) %all-gather.5.cloned.1.call-update) | async-done | bytes 1572880 | tf_op jit(solution)/shard_map/all_gather | solution.py:87
  123.9 2.8 fusion.86
  127.8 2.5 collective-permute-done.8
  130.7 2.2 collective-permute-start.11
  133.4 6.5 %collective-permute-done.11 = bf16[72,2048]{1,0:T(8,128)(2,1)S(1)} collective-permute-done((bf16[72,2048]{1,0:T(8,128)(2,1)S(1)}, bf16[72,2048]{1,0:T(8,128)(2,1)S(1)}, u32[]{:S(2)}, u32[]{:S(2)}) %collective-permute-start.11) | collective-permute-done | bytes 294944 | tf_op jit(solution)/shard_map/ppermute | solution.py:32
  139.9 7.0 %collective-permute-done.10 = bf16[72,2048]{1,0:T(8,128)(2,1)S(1)} collective-permute-done((bf16[72,2048]{1,0:T(8,128)(2,1)S(1)}, bf16[72,2048]{1,0:T(8,128)(2,1)S(1)}, u32[]{:S(2)}, u32[]{:S(2)}) %collective-permute-start.10) | collective-permute-done | bytes 294944 | tf_op jit(solution)/shard_map/ppermute | solution.py:32
  149.9 1.6 collective-permute-start.13
  151.7 6.4 %collective-permute-done.14 = bf16[72,2048]{1,0:T(8,128)(2,1)S(1)} collective-permute-done((bf16[72,2048]{1,0:T(8,128)(2,1)S(1)}, bf16[72,2048]{1,0:T(8,128)(2,1)S(1)}, u32[]{:S(2)}, u32[]{:S(2)}) %collective-permute-start.14) | collective-permute-done | bytes 294944 | tf_op jit(solution)/shard_map/ppermute | solution.py:32
  158.1 7.1 %collective-permute-done.13 = bf16[72,2048]{1,0:T(8,128)(2,1)S(1)} collective-permute-done((bf16[72,2048]{1,0:T(8,128)(2,1)S(1)}, bf16[72,2048]{1,0:T(8,128)(2,1)S(1)}, u32[]{:S(2)}, u32[]{:S(2)}) %collective-permute-start.13) | collective-permute-done | bytes 294944 | tf_op jit(solution)/shard_map/ppermute | solution.py:32
  166.0 2.4 collective-permute-done.15
  168.5 2.5 convolution_convert_fusion.1
  171.3 3.5 %multiply_convert_fusion.1 = (bf16[576,384]{1,0:T(8,128)(2,1)S(1)}, bf16[576,384]{1,0:T(8,128)(2,1)S(1)}) fusion(f32[576,768]{1,0:T(8,128)} %copy-done.1, bf16[576,2048]{1,0:T(8,128)(2,1)S(1)} %constant_dynamic-update-slice_fusion.5, bf16[384,2048]{1,0:T(8,128)(2,1)} %all-gather.5.cloned.1.call-done), kind=kOutput, calls=%fused_computation.43 | convolution fusion | flops 908845056 | bytes 6586368 | tf_op jit(solution)/shard_map/dot_general | solution.py:12
  175.6 6.1 %convolution_convert_fusion = bf16[2048,768]{0,1:T(8,128)(2,1)} fusion(bf16[576,2048]{1,0:T(8,128)(2,1)} %constant_dynamic-update-slice_fusion, bf16[576,384]{1,0:T(8,128)(2,1)S(1)} %get-tuple-element.10, bf16[576,384]{1,0:T(8,128)(2,1)S(1)} %get-tuple-element.9), kind=kOutput, calls=%fused_computation | convolution fusion | flops 1815281664 | bytes 6389760 | tf_op jit(solution)/shard_map/dot_general | solution.py:12
  182.7 3.9 %fusion.37 = f32[576,2048]{1,0:T(8,128)S(1)} fusion(bf16[2048,768]{0,1:T(8,128)(2,1)} %all-gather.3.cloned.1.call-done, bf16[576,384]{1,0:T(8,128)(2,1)S(1)} %copy-done.15, bf16[576,384]{1,0:T(8,128)(2,1)S(1)} %get-tuple-element.9), kind=kOutput, calls=%fused_computation.48 | convolution fusion | flops 1813708800 | bytes 8749056 | tf_op jit(solution)/shard_map/dot_general | solution.py:12
  192.9 10.4 %reduce-scatter.5.cloned.1.call-done = bf16[96,2048]{1,0:T(8,128)(2,1)} async-done(((bf16[384,2048]{1,0:T(8,128)(2,1)}), bf16[96,2048]{1,0:T(8,128)(2,1)}) %reduce-scatter.5.cloned.1.call-update) | async-done | bytes 393232 | tf_op jit(solution)/shard_map/reduce_scatter | solution.py:134
  204.4 4.4 %collective-permute-start.22 = (bf16[48,2048]{1,0:T(8,128)(2,1)S(1)}, bf16[48,2048]{1,0:T(8,128)(2,1)S(1)}, u32[]{:S(2)}, u32[]{:S(2)}) collective-permute-start(bf16[48,2048]{1,0:T(8,128)(2,1)S(1)} %get-tuple-element.33), channel_id=1, source_target_pairs={{0,0},{1,4},{2,2},{3,6},{4,1},{5,5},{6,3},{7,7},{8,8},{9,12},{10,1... | collective-permute-start | bytes 589832 | tf_op jit(solution)/shard_map/ppermute | solution.py:32
  208.9 57.3 %reduce-scatter.3.cloned.1.call-done = bf16[512,768]{0,1:T(8,128)(2,1)} async-done(((bf16[2048,768]{0,1:T(8,128)(2,1)}), bf16[512,768]{0,1:T(8,128)(2,1)}) %reduce-scatter.3.cloned.1.call-update) | async-done | bytes 786448 | tf_op jit(solution)/shard_map/reduce_scatter | solution.py:134
  267.4 3.6 %collective-permute-start.20 = (bf16[256,768]{0,1:T(8,128)(2,1)S(1)}, bf16[256,768]{0,1:T(8,128)(2,1)S(1)}, u32[]{:S(2)}, u32[]{:S(2)}) collective-permute-start(bf16[256,768]{0,1:T(8,128)(2,1)S(1)} %get-tuple-element.29), channel_id=1, source_target_pairs={{0,0},{1,4},{2,2},{3,6},{4,1},{5,5},{6,3},{7,7},{8,8},{9,12},{10,1... | collective-permute-start | bytes 1179656 | tf_op jit(solution)/shard_map/ppermute | solution.py:32
  271.0 2.2 convolution_convert_fusion.3
  274.2 3.0 %collective-permute-done.20 = bf16[256,768]{0,1:T(8,128)(2,1)S(1)} collective-permute-done((bf16[256,768]{0,1:T(8,128)(2,1)S(1)}, bf16[256,768]{0,1:T(8,128)(2,1)S(1)}, u32[]{:S(2)}, u32[]{:S(2)}) %collective-permute-start.20) | collective-permute-done | bytes 393248 | tf_op jit(solution)/shard_map/ppermute | solution.py:32
  277.2 3.4 %collective-permute-done.21 = bf16[256,768]{0,1:T(8,128)(2,1)S(1)} collective-permute-done((bf16[256,768]{0,1:T(8,128)(2,1)S(1)}, bf16[256,768]{0,1:T(8,128)(2,1)S(1)}, u32[]{:S(2)}, u32[]{:S(2)}) %collective-permute-start.21) | collective-permute-done | bytes 393248 | tf_op jit(solution)/shard_map/ppermute | solution.py:32
  282.3 1.6 fusion.12
  (115 shorter events, 34.3 us)
Async XLA Ops:
  7.2 139.8 %copy-start = (bf16[128,2048]{1,0:T(8,128)(2,1)S(1)}, bf16[128,2048]{1,0:T(8,128)(2,1)}, u32[]{:S(2)}) copy-start(bf16[128,2048]{1,0:T(8,128)(2,1)} %param.13) | copy-start | bytes 1572868
  7.2 77.5 %all-gather.3.cloned.1.call-start = ((), (), s32[]{:S(2)}) async-start(), calls=%async_computation.2 | async-start | bytes 3932160 | tf_op jit(solution)/shard_map/all_gather | solution.py:86
  10.5 5.9 %collective-permute-start.5 = (bf16[256,768]{0,1:T(8,128)(2,1)S(1)}, bf16[256,768]{0,1:T(8,128)(2,1)S(1)}, u32[]{:S(2)}, u32[]{:S(2)}) collective-permute-start(bf16[256,768]{0,1:T(8,128)(2,1)S(1)} %pad_maximum_fusion.8), channel_id=1, source_target_pairs={{0,1},{1,5},{2,3},{3,7},{4,0},{5,4},{6,2},{7,6},{8,9},{9,13},{10,1... | collective-permute-start | bytes 1179656 | tf_op jit(solution)/shard_map/ppermute | solution.py:32
  11.7 10.7 %collective-permute-start.4 = (bf16[256,768]{0,1:T(8,128)(2,1)S(1)}, bf16[256,768]{0,1:T(8,128)(2,1)S(1)}, u32[]{:S(2)}, u32[]{:S(2)}) collective-permute-start(bf16[256,768]{0,1:T(8,128)(2,1)S(1)} %pad_maximum_fusion.7), channel_id=1, source_target_pairs={{0,0},{1,4},{2,2},{3,6},{4,1},{5,5},{6,3},{7,7},{8,8},{9,12},{10,1... | collective-permute-start | bytes 1179656 | tf_op jit(solution)/shard_map/ppermute | solution.py:32
  14.9 12.0 %copy-start.6 = (s32[128,2]{0,1:T(2,128)S(1)}, s32[128,2]{0,1:T(2,128)}, u32[]{:S(2)}) copy-start(s32[128,2]{0,1:T(2,128)} %param.8) | copy-start | bytes 3076
  14.9 12.2 %copy-start.2 = (bf16[128,2048]{1,0:T(8,128)(2,1)S(1)}, bf16[128,2048]{1,0:T(8,128)(2,1)}, u32[]{:S(2)}) copy-start(bf16[128,2048]{1,0:T(8,128)(2,1)} %param.7) | copy-start | bytes 1572868
  23.5 100.4 %all-gather.5.cloned.1.call-start = ((), (), s32[]{:S(2)}) async-start(), calls=%async_computation.3 | async-start | bytes 1966080 | tf_op jit(solution)/shard_map/all_gather | solution.py:87
  24.3 7.2 %collective-permute-start.6 = (bf16[48,2048]{1,0:T(8,128)(2,1)}, bf16[48,2048]{1,0:T(8,128)(2,1)S(1)}, u32[]{:S(2)}, u32[]{:S(2)}) collective-permute-start(bf16[48,2048]{1,0:T(8,128)(2,1)} %get-tuple-element.41), channel_id=1, source_target_pairs={{0,0},{1,4},{2,2},{3,6},{4,1},{5,5},{6,3},{7,7},{8,8},{9,12},{10,1... | collective-permute-start | bytes 589832 | tf_op jit(solution)/shard_map/ppermute | solution.py:32
  26.8 4.9 %collective-permute-start.7 = (bf16[48,2048]{1,0:T(8,128)(2,1)S(1)}, bf16[48,2048]{1,0:T(8,128)(2,1)S(1)}, u32[]{:S(2)}, u32[]{:S(2)}) collective-permute-start(bf16[48,2048]{1,0:T(8,128)(2,1)S(1)} %get-tuple-element.42), channel_id=1, source_target_pairs={{0,1},{1,5},{2,3},{3,7},{4,0},{5,4},{6,2},{7,6},{8,9},{9,13},{10,1... | collective-permute-start | bytes 589832 | tf_op jit(solution)/shard_map/ppermute | solution.py:32
  28.5 10.0 %collective-permute-start.2 = (bf16[72,2048]{1,0:T(8,128)(2,1)S(1)}, bf16[72,2048]{1,0:T(8,128)(2,1)S(1)}, u32[]{:S(2)}, u32[]{:S(2)}) collective-permute-start(bf16[72,2048]{1,0:T(8,128)(2,1)S(1)} %get-tuple-element.26), channel_id=1, source_target_pairs={{0,6},{1,7},{2,4},{3,5},{4,2},{5,3},{6,0},{7,1},{8,14},{9,15},{10,... | collective-permute-start | bytes 884744 | tf_op jit(solution)/shard_map/ppermute | solution.py:32
  30.6 14.5 %collective-permute-start.1 = (bf16[72,2048]{1,0:T(8,128)(2,1)S(1)}, bf16[72,2048]{1,0:T(8,128)(2,1)S(1)}, u32[]{:S(2)}, u32[]{:S(2)}) collective-permute-start(bf16[72,2048]{1,0:T(8,128)(2,1)S(1)} %get-tuple-element.27), channel_id=1, source_target_pairs={{0,2},{1,3},{2,0},{3,1},{4,6},{5,7},{6,4},{7,5},{8,10},{9,11},{10,... | collective-permute-start | bytes 884744 | tf_op jit(solution)/shard_map/ppermute | solution.py:32
  30.9 14.3 %collective-permute-start = (bf16[72,2048]{1,0:T(8,128)(2,1)S(1)}, bf16[72,2048]{1,0:T(8,128)(2,1)S(1)}, u32[]{:S(2)}, u32[]{:S(2)}) collective-permute-start(bf16[72,2048]{1,0:T(8,128)(2,1)S(1)} %get-tuple-element.28), channel_id=1, source_target_pairs={{0,4},{1,5},{2,6},{3,7},{4,0},{5,1},{6,2},{7,3},{8,12},{9,13},{10,... | collective-permute-start | bytes 884744 | tf_op jit(solution)/shard_map/ppermute | solution.py:32
  32.6 170.8 %reduce-scatter.5.cloned.1.call-start = ((), (), s32[]{:S(2)}) async-start(), calls=%async_computation.5 | async-start | bytes 1966080 | tf_op jit(solution)/shard_map/reduce_scatter | solution.py:134
  45.2 4.3 %collective-permute-start.3 = (bf16[288,2048]{1,0:T(8,128)(2,1)S(1)}, bf16[288,2048]{1,0:T(8,128)(2,1)S(1)}, u32[]{:S(2)}, u32[]{:S(2)}) collective-permute-start(bf16[288,2048]{1,0:T(8,128)(2,1)S(1)} %pad_maximum_fusion), channel_id=1, source_target_pairs={{0,1},{1,0},{2,3},{3,2},{4,5},{5,4},{6,7},{7,6},{8,9},{9,8},{10,11... | collective-permute-start | bytes 3538952 | tf_op jit(solution)/shard_map/ppermute | solution.py:32
  126.8 3.4 %collective-permute-start.8 = (bf16[288,2048]{1,0:T(8,128)(2,1)S(1)}, bf16[288,2048]{1,0:T(8,128)(2,1)S(1)}, u32[]{:S(2)}, u32[]{:S(2)}) collective-permute-start(bf16[288,2048]{1,0:T(8,128)(2,1)S(1)} %slice.211), channel_id=1, source_target_pairs={{0,1},{1,0},{2,3},{3,2},{4,5},{5,4},{6,7},{7,6},{8,9},{9,8},{10,11... | collective-permute-start | bytes 3538952 | tf_op jit(solution)/shard_map/ppermute | solution.py:32
  130.7 16.7 %copy-start.4 = (bf16[72,2048]{1,0:T(8,128)(2,1)}, bf16[72,2048]{1,0:T(8,128)(2,1)S(1)}, u32[]{:S(2)}) copy-start(bf16[72,2048]{1,0:T(8,128)(2,1)S(1)} %get-tuple-element.20) | copy-start | bytes 884740
  130.7 9.2 %collective-permute-start.11 = (bf16[72,2048]{1,0:T(8,128)(2,1)S(1)}, bf16[72,2048]{1,0:T(8,128)(2,1)S(1)}, u32[]{:S(2)}, u32[]{:S(2)}) collective-permute-start(bf16[72,2048]{1,0:T(8,128)(2,1)S(1)} %get-tuple-element.21), channel_id=1, source_target_pairs={{0,6},{1,7},{2,4},{3,5},{4,2},{5,3},{6,0},{7,1},{8,14},{9,15},{10,... | collective-permute-start | bytes 884744 | tf_op jit(solution)/shard_map/ppermute | solution.py:32
  132.9 14.1 %collective-permute-start.10 = (bf16[72,2048]{1,0:T(8,128)(2,1)S(1)}, bf16[72,2048]{1,0:T(8,128)(2,1)S(1)}, u32[]{:S(2)}, u32[]{:S(2)}) collective-permute-start(bf16[72,2048]{1,0:T(8,128)(2,1)S(1)} %get-tuple-element.22), channel_id=1, source_target_pairs={{0,2},{1,3},{2,0},{3,1},{4,6},{5,7},{6,4},{7,5},{8,10},{9,11},{10,... | collective-permute-start | bytes 884744 | tf_op jit(solution)/shard_map/ppermute | solution.py:32
  133.1 13.8 %collective-permute-start.9 = (bf16[72,2048]{1,0:T(8,128)(2,1)S(1)}, bf16[72,2048]{1,0:T(8,128)(2,1)S(1)}, u32[]{:S(2)}, u32[]{:S(2)}) collective-permute-start(bf16[72,2048]{1,0:T(8,128)(2,1)S(1)} %get-tuple-element.23), channel_id=1, source_target_pairs={{0,4},{1,5},{2,6},{3,7},{4,0},{5,1},{6,2},{7,3},{8,12},{9,13},{10,... | collective-permute-start | bytes 884744 | tf_op jit(solution)/shard_map/ppermute | solution.py:32
  149.0 9.1 %collective-permute-start.14 = (bf16[72,2048]{1,0:T(8,128)(2,1)S(1)}, bf16[72,2048]{1,0:T(8,128)(2,1)S(1)}, u32[]{:S(2)}, u32[]{:S(2)}) collective-permute-start(bf16[72,2048]{1,0:T(8,128)(2,1)S(1)} %get-tuple-element.17), channel_id=1, source_target_pairs={{0,6},{1,7},{2,4},{3,5},{4,2},{5,3},{6,0},{7,1},{8,14},{9,15},{10,... | collective-permute-start | bytes 884744 | tf_op jit(solution)/shard_map/ppermute | solution.py:32
  149.9 15.3 %collective-permute-start.13 = (bf16[72,2048]{1,0:T(8,128)(2,1)S(1)}, bf16[72,2048]{1,0:T(8,128)(2,1)S(1)}, u32[]{:S(2)}, u32[]{:S(2)}) collective-permute-start(bf16[72,2048]{1,0:T(8,128)(2,1)S(1)} %get-tuple-element.18), channel_id=1, source_target_pairs={{0,2},{1,3},{2,0},{3,1},{4,6},{5,7},{6,4},{7,5},{8,10},{9,11},{10,... | collective-permute-start | bytes 884744 | tf_op jit(solution)/shard_map/ppermute | solution.py:32
  151.4 13.8 %collective-permute-start.12 = (bf16[72,2048]{1,0:T(8,128)(2,1)S(1)}, bf16[72,2048]{1,0:T(8,128)(2,1)S(1)}, u32[]{:S(2)}, u32[]{:S(2)}) collective-permute-start(bf16[72,2048]{1,0:T(8,128)(2,1)S(1)} %get-tuple-element.19), channel_id=1, source_target_pairs={{0,4},{1,5},{2,6},{3,7},{4,0},{5,1},{6,2},{7,3},{8,12},{9,13},{10,... | collective-permute-start | bytes 884744 | tf_op jit(solution)/shard_map/ppermute | solution.py:32
  165.3 3.1 %collective-permute-start.15 = (bf16[288,2048]{1,0:T(8,128)(2,1)S(1)}, bf16[288,2048]{1,0:T(8,128)(2,1)S(1)}, u32[]{:S(2)}, u32[]{:S(2)}) collective-permute-start(bf16[288,2048]{1,0:T(8,128)(2,1)S(1)} %pad_maximum_fusion.2), channel_id=1, source_target_pairs={{0,1},{1,0},{2,3},{3,2},{4,5},{5,4},{6,7},{7,6},{8,9},{9,8},{10,11... | collective-permute-start | bytes 3538952 | tf_op jit(solution)/shard_map/ppermute | solution.py:32
  171.1 95.1 %reduce-scatter.3.cloned.1.call-start = ((), (), s32[]{:S(2)}) async-start(), calls=%async_computation.4 | async-start | bytes 3932160 | tf_op jit(solution)/shard_map/reduce_scatter | solution.py:134
  186.8 2.9 %collective-permute-start.16 = (bf16[288,2048]{1,0:T(8,128)(2,1)S(1)}, bf16[288,2048]{1,0:T(8,128)(2,1)S(1)}, u32[]{:S(2)}, u32[]{:S(2)}) collective-permute-start(bf16[288,2048]{1,0:T(8,128)(2,1)S(1)} %slice.210), channel_id=1, source_target_pairs={{0,1},{1,0},{2,3},{3,2},{4,5},{5,4},{6,7},{7,6},{8,9},{9,8},{10,11... | collective-permute-start | bytes 3538952 | tf_op jit(solution)/shard_map/ppermute | solution.py:32
  190.2 77.2 %collective-permute-start.19 = (bf16[72,2048]{1,0:T(8,128)(2,1)S(1)}, bf16[72,2048]{1,0:T(8,128)(2,1)S(1)}, u32[]{:S(2)}, u32[]{:S(2)}) collective-permute-start(bf16[72,2048]{1,0:T(8,128)(2,1)S(1)} %get-tuple-element.12), channel_id=1, source_target_pairs={{0,6},{1,7},{2,4},{3,5},{4,2},{5,3},{6,0},{7,1},{8,14},{9,15},{10,... | collective-permute-start | bytes 884744 | tf_op jit(solution)/shard_map/ppermute | solution.py:32
  191.2 79.8 %collective-permute-start.18 = (bf16[72,2048]{1,0:T(8,128)(2,1)S(1)}, bf16[72,2048]{1,0:T(8,128)(2,1)S(1)}, u32[]{:S(2)}, u32[]{:S(2)}) collective-permute-start(bf16[72,2048]{1,0:T(8,128)(2,1)S(1)} %get-tuple-element.13), channel_id=1, source_target_pairs={{0,2},{1,3},{2,0},{3,1},{4,6},{5,7},{6,4},{7,5},{8,10},{9,11},{10,... | collective-permute-start | bytes 884744 | tf_op jit(solution)/shard_map/ppermute | solution.py:32
  192.6 78.5 %collective-permute-start.17 = (bf16[72,2048]{1,0:T(8,128)(2,1)S(1)}, bf16[72,2048]{1,0:T(8,128)(2,1)}, u32[]{:S(2)}, u32[]{:S(2)}) collective-permute-start(bf16[72,2048]{1,0:T(8,128)(2,1)S(1)} %get-tuple-element.14), channel_id=1, source_target_pairs={{0,4},{1,5},{2,6},{3,7},{4,0},{5,1},{6,2},{7,3},{8,12},{9,13},{10,... | collective-permute-start | bytes 884744 | tf_op jit(solution)/shard_map/ppermute | solution.py:32
  204.4 68.9 %collective-permute-start.22 = (bf16[48,2048]{1,0:T(8,128)(2,1)S(1)}, bf16[48,2048]{1,0:T(8,128)(2,1)S(1)}, u32[]{:S(2)}, u32[]{:S(2)}) collective-permute-start(bf16[48,2048]{1,0:T(8,128)(2,1)S(1)} %get-tuple-element.33), channel_id=1, source_target_pairs={{0,0},{1,4},{2,2},{3,6},{4,1},{5,5},{6,3},{7,7},{8,8},{9,12},{10,1... | collective-permute-start | bytes 589832 | tf_op jit(solution)/shard_map/ppermute | solution.py:32
  208.8 64.4 %collective-permute-start.23 = (bf16[48,2048]{1,0:T(8,128)(2,1)S(1)}, bf16[48,2048]{1,0:T(8,128)(2,1)S(1)}, u32[]{:S(2)}, u32[]{:S(2)}) collective-permute-start(bf16[48,2048]{1,0:T(8,128)(2,1)S(1)} %get-tuple-element.34), channel_id=1, source_target_pairs={{0,4},{1,0},{2,6},{3,2},{4,5},{5,1},{6,7},{7,3},{8,12},{9,8},{10,1... | collective-permute-start | bytes 589832 | tf_op jit(solution)/shard_map/ppermute | solution.py:32
  267.4 9.8 %collective-permute-start.20 = (bf16[256,768]{0,1:T(8,128)(2,1)S(1)}, bf16[256,768]{0,1:T(8,128)(2,1)S(1)}, u32[]{:S(2)}, u32[]{:S(2)}) collective-permute-start(bf16[256,768]{0,1:T(8,128)(2,1)S(1)} %get-tuple-element.29), channel_id=1, source_target_pairs={{0,0},{1,4},{2,2},{3,6},{4,1},{5,5},{6,3},{7,7},{8,8},{9,12},{10,1... | collective-permute-start | bytes 1179656 | tf_op jit(solution)/shard_map/ppermute | solution.py:32
  273.3 7.4 %collective-permute-start.21 = (bf16[256,768]{0,1:T(8,128)(2,1)S(1)}, bf16[256,768]{0,1:T(8,128)(2,1)S(1)}, u32[]{:S(2)}, u32[]{:S(2)}) collective-permute-start(bf16[256,768]{0,1:T(8,128)(2,1)S(1)} %get-tuple-element.30), channel_id=1, source_target_pairs={{0,4},{1,0},{2,6},{3,2},{4,5},{5,1},{6,7},{7,3},{8,12},{9,8},{10,1... | collective-permute-start | bytes 1179656 | tf_op jit(solution)/shard_map/ppermute | solution.py:32
  (12 other events, 29.0 us)
Sparse Core Ops, SparseCore 0:
  23.6 61.0 all-gather.2
  86.9 36.9 all-gather.4
  171.2 32.0 reduce-scatter.4
  205.5 60.6 reduce-scatter.2

commit v2 on v1

--- a/solution.py
+++ b/solution.py
@@ -10,6 +10,10 @@
 
 def dot(a, b, dims=((1,), (0,))):
     return lax.dot_general(a, b, (dims, ((), ())), preferred_element_type=F32)
+
+
+def added(*terms):
+    return sum(t.astype(F32) for t in terms).astype(BF)
 
 
 class Grid:
@@ -18,7 +22,6 @@
         self.zs, self.qs = self.dps // 2, self.experts // 2
         dp, ex = lax.axis_index("dp"), lax.axis_index("expert")
         self.z, self.x, self.q, self.c = dp // 2, dp % 2, ex // 2, ex % 2
-        self.z_groups = [[z * 2 + x for z in range(self.zs)] for x in range(2)]
 
     def send(self, value, move):
         pairs = []
@@ -27,12 +30,51 @@
                 for q in range(self.qs):
                     for c in range(2):
                         to = move(z, x, q, c)
-                        if 0 <= to[0] < self.zs:
+                        if to is not None:
                             pairs.append((self.flat(z, x, q, c), self.flat(*to)))
         return lax.ppermute(value, BOTH, pairs)
 
     def flat(self, z, x, q, c):
         return (z * 2 + x) * self.experts + q * 2 + c
+
+    def step(self, value, by, senders):
+        return self.send(value, lambda z, x, q, c: (z + by, x, q, c) if z in senders else None)
+
+    def gather(self, shard):
+        up, down = [shard], [shard]
+        for s in range(1, self.zs):
+            up.append(self.step(up[-1], 1, range(s - 1, self.zs - 1)))
+            down.append(self.step(down[-1], -1, range(1, self.zs - s + 1)))
+        return up, down
+
+    def rotated(self, shard):
+        up, down = self.gather(shard)
+        blocks = [shard]
+        for s in range(1, self.zs):
+            blocks.append(jnp.where(self.z + s < self.zs, down[s], up[self.zs - s]))
+        return blocks
+
+    def straight(self, shard):
+        up, down = self.gather(shard)
+        blocks = []
+        for j in range(self.zs):
+            block = shard
+            for s in range(1, self.zs):
+                if j + s < self.zs:
+                    block = jnp.where(self.z == j + s, up[s], block)
+                if j - s >= 0:
+                    block = jnp.where(self.z == j - s, down[s], block)
+            blocks.append(block)
+        return blocks
+
+    def scatter(self, block):
+        n = self.zs
+        up = self.step(block(n - 1), 1, range(0, 1))
+        down = self.step(block(1 - n), -1, range(n - 1, n))
+        for r in range(2, n):
+            up = self.step(added(block(n - r), up), 1, range(0, r))
+            down = self.step(added(block(r - n), down), -1, range(n - r, n))
+        return added(block(0), up, down)
 
 
 def local(tokens, expert_ids, gate_probs, w_gate, w_up, w_down, d_out):
@@ -83,8 +125,8 @@
     down_low, down_high = w_down[0, :part], w_down[0, part:]
     even = g.x == 0
     down_shard = spread(jnp.where(even, down_low, down_high), jnp.where(even, down_high, down_low))
-    gate_up = lax.all_gather(gate_up_shard, "dp", axis=0, tiled=True, axis_index_groups=g.z_groups)
-    down = lax.all_gather(down_shard, "dp", axis=0, tiled=True, axis_index_groups=g.z_groups)
+    gate_up = jnp.concatenate(g.rotated(gate_up_shard), axis=0)
+    down = jnp.concatenate(g.straight(down_shard), axis=0)
 
     expert_iota = jnp.arange(experts, dtype=jnp.int32)
     chosen = expert_ids[:, :, None] == expert_iota
@@ -121,7 +163,9 @@
         got = [mine[:cap]] + [g.send(mine[r * cap:(r + 1) * cap], member(r, -1)) for r in range(1, experts)]
         return jnp.concatenate(got, axis=0)
 
-    arrived = dispatch(dot(placing, tokens, ((0,), (0,))).astype(BF))
+    line_width = width // g.zs
+    turned = lax.dynamic_slice(jnp.concatenate([tokens, tokens], axis=1), (0, g.z * line_width), (rows, width))
+    arrived = dispatch(dot(placing, turned, ((0,), (0,))).astype(BF))
     d_produced = dispatch((slot_probs[:, None] * dot(placing, d_out, ((0,), (0,)))).astype(BF))
 
     pre = dot(arrived, gate_up)
@@ -130,26 +174,27 @@
     act = gate_pre * sig
     hidden = (act * up_pre).astype(BF)
 
-    def scatter(partial):
-        return lax.psum_scatter(
-            partial.astype(BF), "dp", scatter_dimension=0, tiled=True, axis_index_groups=g.z_groups
-        ).astype(BF)
-
-    down_grad = scatter(dot(hidden, d_produced, ((0,), (0,))))
+    down_part = dot(hidden, d_produced, ((0,), (0,))).astype(BF)
+    down_rows = 2 * part
+    down_grad = g.scatter(lambda k: lax.dynamic_slice_in_dim(down_part, (g.z + k) * down_rows, down_rows))
     returned = give_back(dot(hidden, down))
 
     d_hidden = dot(d_produced, down, ((1,), (1,)))
     d_gate = (d_hidden * up_pre * sig * (1.0 + gate_pre * (1.0 - sig))).astype(BF)
     d_up = (d_hidden * act).astype(BF)
     d_both = jnp.concatenate([d_gate, d_up], axis=1)
-    gate_up_grad = scatter(dot(arrived, d_both, ((0,), (0,))))
+    both_part = dot(arrived, d_both, ((0,), (0,))).astype(BF)
+    gate_up_grad = g.scatter(lambda k: both_part[(k % g.zs) * line_width:(k % g.zs + 1) * line_width])
     back_rows = give_back(dot(d_both, gate_up, ((1,), (1,))))
 
     high = lax.reduce_precision(weighted, 8, 7)
     mixed = (dot(high.astype(BF), returned) + dot((weighted - high).astype(BF), returned)).astype(BF)
     products = dot(d_out, returned, ((1,), (1,)))
     d_probs = jnp.sum(jnp.where(pair, products[:, None, :], 0.0), axis=2)
-    d_tokens = dot(placing, back_rows).astype(BF)
+    d_turned = dot(placing, back_rows).astype(BF)
+    d_tokens = lax.dynamic_slice(
+        jnp.concatenate([d_turned, d_turned], axis=1), (0, (g.zs - g.z) * line_width), (rows, width)
+    )
 
     down_a, down_b = unspread(down_grad)
     d_w_down = jnp.where(

time: 292 us -> 288 us (0.986)
  starting transfers between devices: 30 us -> 99.9 us
  waiting for transfers between devices: 194 us -> 139 us
  matrix products: 35.1 us -> 21.8 us
  between operations: 14.3 us -> 1.89 us
  other arithmetic: 7.63 us -> 17.2 us
  local copies, waits for them, and re-layouts: 9.11 us -> 5.11 us
    ppermute x24 -> x48, waiting for transfers between devices: 59.4 us -> 139 us  [send(): return lax.ppermute(value, BOTH, pairs)]
    ppermute x24 -> x48, starting transfers between devices: 29.7 us -> 99.9 us  [send(): return lax.ppermute(value, BOTH, pairs)]
    reduce_scatter x2 -> x0, waiting for transfers between devices: 67.8 us -> none  [scatter(): lax.psum_scatter(partial.astype(BF), 'dp', scatter_dimension=0, tiled=Tru...]
    all_gather x2 -> x0, waiting for transfers between devices: 67 us -> none  [the longest x1 34 us: local(): lax.all_gather(gate_up_shard, 'dp', axis=0, tiled=True, axis_index_groups...]
    dot_general x17, matrix products: 35.1 us -> 21.8 us  [dot(): return lax.dot_general(a, b, (dims, ((), ())), preferred_element_type=F32)]
    unnamed x38 -> x72, local copies, waits for them, and re-layouts: 6.15 us -> 1.57 us
    unnamed x0 -> x4, other arithmetic: none -> 3.93 us
  transfers between devices with their start and end apart: 28 -> 48, of which waited for: 20 -> 20; matrix products, arithmetic and copies ran while one was open for 11% -> 7% of each run, Pallas kernels for 0% -> 0%
where the time goes in v2:
time: 288 us; the launch traced here: 285 us
  waiting for transfers between devices  139 us (48%)
  starting transfers between devices  99.9 us (35%)
  matrix products  21.8 us (8%)
  other arithmetic  17.2 us (6%)
  local copies, waits for them, and re-layouts  5.11 us (2%)
    ppermute x48, waiting for transfers between devices, send(): return lax.ppermute(value, BOTH, pairs)  139 us
    ppermute x48, starting transfers between devices, send(): return lax.ppermute(value, BOTH, pairs)  99.9 us
    dot_general x17, matrix products, dot(): return lax.dot_general(a, b, (dims, ((), ())), preferred_element_type=F32)  21.8 us
  transfers between devices with their start and end apart: 48, of which 20 were waited for; matrix products, arithmetic and copies ran while one was open for 7% of the time, Pallas kernels for 0%

profile of v2, /device:TPU:9, one launch (start us, length us, event | category | flops | bytes accessed | tf_op | source)
XLA Modules:
  0.0 285.1 jit_solution(7163724958903122120)
XLA Ops:
  9.3 3.3 %collective-permute-start.4 = (bf16[256,768]{0,1:T(8,128)(2,1)S(1)}, bf16[256,768]{0,1:T(8,128)(2,1)S(1)}, u32[]{:S(2)}, u32[]{:S(2)}) collective-permute-start(bf16[256,768]{0,1:T(8,128)(2,1)S(1)} %pad_maximum_fusion.8), channel_id=1, source_target_pairs={{0,0},{1,4},{2,2},{3,6},{4,1},{5,5},{6,3},{7,7},{8,8},{9,12},{10,1... | collective-permute-start | bytes 1179656 | tf_op jit(solution)/shard_map/ppermute | solution.py:35
  15.8 3.0 %collective-permute-done.4 = bf16[256,768]{0,1:T(8,128)(2,1)S(1)} collective-permute-done((bf16[256,768]{0,1:T(8,128)(2,1)S(1)}, bf16[256,768]{0,1:T(8,128)(2,1)S(1)}, u32[]{:S(2)}, u32[]{:S(2)}) %collective-permute-start.4) | collective-permute-done | bytes 393248 | tf_op jit(solution)/shard_map/ppermute | solution.py:35
  18.8 3.5 %collective-permute-done.5 = bf16[256,768]{0,1:T(8,128)(2,1)S(1)} collective-permute-done((bf16[256,768]{0,1:T(8,128)(2,1)S(1)}, bf16[256,768]{0,1:T(8,128)(2,1)S(1)}, u32[]{:S(2)}, u32[]{:S(2)}) %collective-permute-start.5) | collective-permute-done | bytes 393248 | tf_op jit(solution)/shard_map/ppermute | solution.py:35
  25.0 3.2 %collective-permute-start.7 = (bf16[512,768]{0,1:T(8,128)(2,1)}, bf16[512,768]{0,1:T(8,128)(2,1)S(1)}, u32[]{:S(2)}, u32[]{:S(2)}) collective-permute-start(bf16[512,768]{0,1:T(8,128)(2,1)} %pad_maximum_fusion.5), channel_id=1, source_target_pairs={{0,8},{1,9},{2,10},{3,11},{4,12},{5,13},{6,14},{7,15},{8,16},{9,17... | collective-permute-start | bytes 2359304 | tf_op jit(solution)/shard_map/ppermute | solution.py:35
  28.3 3.2 %collective-permute-start.14 = (bf16[96,2048]{1,0:T(8,128)(2,1)S(1)}, bf16[96,2048]{1,0:T(8,128)(2,1)}, u32[]{:S(2)}, u32[]{:S(2)}) collective-permute-start(bf16[96,2048]{1,0:T(8,128)(2,1)S(1)} %pad_maximum_fusion.10), channel_id=1, source_target_pairs={{0,8},{1,9},{2,10},{3,11},{4,12},{5,13},{6,14},{7,15},{8,16},{9,17... | collective-permute-start | bytes 1179656 | tf_op jit(solution)/shard_map/ppermute | solution.py:35
  31.6 2.8 collective-permute-start.17
  36.3 2.9 %collective-permute-start.2 = (bf16[72,2048]{1,0:T(8,128)(2,1)}, bf16[72,2048]{1,0:T(8,128)(2,1)S(1)}, u32[]{:S(2)}, u32[]{:S(2)}) collective-permute-start(bf16[72,2048]{1,0:T(8,128)(2,1)} %get-tuple-element.44), channel_id=1, source_target_pairs={{0,6},{1,7},{2,4},{3,5},{4,2},{5,3},{6,0},{7,1},{8,14},{9,15},{10,... | collective-permute-start | bytes 884744 | tf_op jit(solution)/shard_map/ppermute | solution.py:35
  39.2 14.0 %collective-permute-done.14 = bf16[96,2048]{1,0:T(8,128)(2,1)} collective-permute-done((bf16[96,2048]{1,0:T(8,128)(2,1)S(1)}, bf16[96,2048]{1,0:T(8,128)(2,1)}, u32[]{:S(2)}, u32[]{:S(2)}) %collective-permute-start.14) | collective-permute-done | bytes 393248 | tf_op jit(solution)/shard_map/ppermute | solution.py:35
  53.3 3.2 %collective-permute-start.15 = (bf16[96,2048]{1,0:T(8,128)(2,1)}, bf16[96,2048]{1,0:T(8,128)(2,1)S(1)}, u32[]{:S(2)}, u32[]{:S(2)}) collective-permute-start(bf16[96,2048]{1,0:T(8,128)(2,1)} %collective-permute-done.14), channel_id=1, source_target_pairs={{8,16},{9,17},{10,18},{11,19},{12,20},{13,21},{14,22},{15,23},{16,... | collective-permute-start | bytes 1179656 | tf_op jit(solution)/shard_map/ppermute | solution.py:35
  58.5 3.4 %collective-permute-start.8 = (bf16[512,768]{0,1:T(8,128)(2,1)S(1)}, bf16[512,768]{0,1:T(8,128)(2,1)S(1)}, u32[]{:S(2)}, u32[]{:S(2)}) collective-permute-start(bf16[512,768]{0,1:T(8,128)(2,1)S(1)} %collective-permute-done.7), channel_id=1, source_target_pairs={{8,16},{9,17},{10,18},{11,19},{12,20},{13,21},{14,22},{15,23},{16,... | collective-permute-start | bytes 2359304 | tf_op jit(solution)/shard_map/ppermute | solution.py:35
  62.0 3.2 %collective-permute-start.3 = (bf16[288,2048]{1,0:T(8,128)(2,1)S(1)}, bf16[288,2048]{1,0:T(8,128)(2,1)S(1)}, u32[]{:S(2)}, u32[]{:S(2)}) collective-permute-start(bf16[288,2048]{1,0:T(8,128)(2,1)S(1)} %pad_maximum_fusion.1), channel_id=1, source_target_pairs={{0,1},{1,0},{2,3},{3,2},{4,5},{5,4},{6,7},{7,6},{8,9},{9,8},{10,11... | collective-permute-start | bytes 3538952 | tf_op jit(solution)/shard_map/ppermute | solution.py:35
  66.9 3.9 %collective-permute-start.19 = (bf16[96,2048]{1,0:T(8,128)(2,1)S(1)}, bf16[96,2048]{1,0:T(8,128)(2,1)S(1)}, u32[]{:S(2)}, u32[]{:S(2)}) collective-permute-start(bf16[96,2048]{1,0:T(8,128)(2,1)S(1)} %collective-permute-done.18), channel_id=1, source_target_pairs={{8,0},{9,1},{10,2},{11,3},{12,4},{13,5},{14,6},{15,7}} | collective-permute-start | bytes 1179656 | tf_op jit(solution)/shard_map/ppermute | solution.py:35
  72.8 6.8 %collective-permute-done.8 = bf16[512,768]{0,1:T(8,128)(2,1)S(1)} collective-permute-done((bf16[512,768]{0,1:T(8,128)(2,1)S(1)}, bf16[512,768]{0,1:T(8,128)(2,1)S(1)}, u32[]{:S(2)}, u32[]{:S(2)}) %collective-permute-start.8) | collective-permute-done | bytes 786464 | tf_op jit(solution)/shard_map/ppermute | solution.py:35
  82.1 11.8 %collective-permute-done.10 = bf16[512,768]{0,1:T(8,128)(2,1)S(1)} collective-permute-done((bf16[512,768]{0,1:T(8,128)(2,1)}, bf16[512,768]{0,1:T(8,128)(2,1)S(1)}, u32[]{:S(2)}, u32[]{:S(2)}) %collective-permute-start.10) | collective-permute-done | bytes 786464 | tf_op jit(solution)/shard_map/ppermute | solution.py:35
  93.9 4.2 %collective-permute-start.11 = (bf16[512,768]{0,1:T(8,128)(2,1)S(1)}, bf16[512,768]{0,1:T(8,128)(2,1)S(1)}, u32[]{:S(2)}, u32[]{:S(2)}) collective-permute-start(bf16[512,768]{0,1:T(8,128)(2,1)S(1)} %collective-permute-done.10), channel_id=1, source_target_pairs={{8,0},{9,1},{10,2},{11,3},{12,4},{13,5},{14,6},{15,7}} | collective-permute-start | bytes 2359304 | tf_op jit(solution)/shard_map/ppermute | solution.py:35
  100.5 11.0 %collective-permute-done.11 = bf16[512,768]{0,1:T(8,128)(2,1)S(1)} collective-permute-done((bf16[512,768]{0,1:T(8,128)(2,1)S(1)}, bf16[512,768]{0,1:T(8,128)(2,1)S(1)}, u32[]{:S(2)}, u32[]{:S(2)}) %collective-permute-start.11) | collective-permute-done | bytes 786464 | tf_op jit(solution)/shard_map/ppermute | solution.py:35
  115.7 4.2 %collective-permute-start.20 = (bf16[288,2048]{1,0:T(8,128)(2,1)S(1)}, bf16[288,2048]{1,0:T(8,128)(2,1)S(1)}, u32[]{:S(2)}, u32[]{:S(2)}) collective-permute-start(bf16[288,2048]{1,0:T(8,128)(2,1)S(1)} %slice.239), channel_id=1, source_target_pairs={{0,1},{1,0},{2,3},{3,2},{4,5},{5,4},{6,7},{7,6},{8,9},{9,8},{10,11... | collective-permute-start | bytes 3538952 | tf_op jit(solution)/shard_map/ppermute | solution.py:35
  122.9 6.7 %collective-permute-start.23 = (bf16[72,2048]{1,0:T(8,128)(2,1)S(1)}, bf16[72,2048]{1,0:T(8,128)(2,1)S(1)}, u32[]{:S(2)}, u32[]{:S(2)}) collective-permute-start(bf16[72,2048]{1,0:T(8,128)(2,1)S(1)} %get-tuple-element.35), channel_id=1, source_target_pairs={{0,6},{1,7},{2,4},{3,5},{4,2},{5,3},{6,0},{7,1},{8,14},{9,15},{10,... | collective-permute-start | bytes 884744 | tf_op jit(solution)/shard_map/ppermute | solution.py:35
  129.9 6.8 %collective-permute-done.23 = bf16[72,2048]{1,0:T(8,128)(2,1)S(1)} collective-permute-done((bf16[72,2048]{1,0:T(8,128)(2,1)S(1)}, bf16[72,2048]{1,0:T(8,128)(2,1)S(1)}, u32[]{:S(2)}, u32[]{:S(2)}) %collective-permute-start.23) | collective-permute-done | bytes 294944 | tf_op jit(solution)/shard_map/ppermute | solution.py:35
  136.7 6.7 %collective-permute-done.22 = bf16[72,2048]{1,0:T(8,128)(2,1)S(1)} collective-permute-done((bf16[72,2048]{1,0:T(8,128)(2,1)S(1)}, bf16[72,2048]{1,0:T(8,128)(2,1)S(1)}, u32[]{:S(2)}, u32[]{:S(2)}) %collective-permute-start.22) | collective-permute-done | bytes 294944 | tf_op jit(solution)/shard_map/ppermute | solution.py:35
  148.2 5.4 %collective-permute-done.24 = bf16[72,2048]{1,0:T(8,128)(2,1)S(1)} collective-permute-done((bf16[72,2048]{1,0:T(8,128)(2,1)S(1)}, bf16[72,2048]{1,0:T(8,128)(2,1)S(1)}, u32[]{:S(2)}, u32[]{:S(2)}) %collective-permute-start.24) | collective-permute-done | bytes 294944 | tf_op jit(solution)/shard_map/ppermute | solution.py:35
  153.7 6.3 %collective-permute-done.26 = bf16[72,2048]{1,0:T(8,128)(2,1)S(1)} collective-permute-done((bf16[72,2048]{1,0:T(8,128)(2,1)S(1)}, bf16[72,2048]{1,0:T(8,128)(2,1)S(1)}, u32[]{:S(2)}, u32[]{:S(2)}) %collective-permute-start.26) | collective-permute-done | bytes 294944 | tf_op jit(solution)/shard_map/ppermute | solution.py:35
  171.5 3.0 %convolution_convert_fusion = bf16[2048,768]{0,1:T(8,128)(2,1)S(1)} fusion(bf16[576,2048]{1,0:T(8,128)(2,1)S(1)} %copy-done.23, bf16[576,384]{1,0:T(8,128)(2,1)S(1)} %get-tuple-element.20, bf16[576,384]{1,0:T(8,128)(2,1)S(1)} %get-tuple-element.19), kind=kOutput, calls=%fused_computation | convolution fusion | flops 1815281664 | bytes 6389760 | tf_op jit(solution)/shard_map/dot_general | solution.py:12
  181.8 22.4 %collective-permute-done.40 = bf16[96,2048]{1,0:T(8,128)(2,1)S(1)} collective-permute-done((bf16[96,2048]{1,0:T(8,128)(2,1)S(1)}, bf16[96,2048]{1,0:T(8,128)(2,1)S(1)}, u32[]{:S(2)}, u32[]{:S(2)}) %collective-permute-start.40) | collective-permute-done | bytes 393248 | tf_op jit(solution)/shard_map/ppermute | solution.py:35
  211.2 4.5 %collective-permute-done.41 = bf16[96,2048]{1,0:T(8,128)(2,1)S(1)} collective-permute-done((bf16[96,2048]{1,0:T(8,128)(2,1)S(1)}, bf16[96,2048]{1,0:T(8,128)(2,1)S(1)}, u32[]{:S(2)}, u32[]{:S(2)}) %collective-permute-start.41) | collective-permute-done | bytes 393248 | tf_op jit(solution)/shard_map/ppermute | solution.py:35
  219.9 18.4 %collective-permute-done.44 = bf16[96,2048]{1,0:T(8,128)(2,1)S(1)} collective-permute-done((bf16[96,2048]{1,0:T(8,128)(2,1)S(1)}, bf16[96,2048]{1,0:T(8,128)(2,1)S(1)}, u32[]{:S(2)}, u32[]{:S(2)}) %collective-permute-start.44) | collective-permute-done | bytes 393248 | tf_op jit(solution)/shard_map/ppermute | solution.py:35
  241.1 3.4 %collective-permute-start.45 = (bf16[96,2048]{1,0:T(8,128)(2,1)S(1)}, bf16[96,2048]{1,0:T(8,128)(2,1)S(1)}, u32[]{:S(2)}, u32[]{:S(2)}) collective-permute-start(bf16[96,2048]{1,0:T(8,128)(2,1)S(1)} %add_convert_fusion.4), channel_id=1, source_target_pairs={{8,0},{9,1},{10,2},{11,3},{12,4},{13,5},{14,6},{15,7},{16,8},{17,9... | collective-permute-start | bytes 1179656 | tf_op jit(solution)/shard_map/ppermute | solution.py:35
  247.9 3.4 %collective-permute-start.34 = (bf16[512,768]{0,1:T(8,128)(2,1)S(1)}, bf16[512,768]{0,1:T(8,128)(2,1)S(1)}, u32[]{:S(2)}, u32[]{:S(2)}) collective-permute-start(bf16[512,768]{0,1:T(8,128)(2,1)S(1)} %get-tuple-element.13), channel_id=1, source_target_pairs={{0,8},{1,9},{2,10},{3,11},{4,12},{5,13},{6,14},{7,15},{8,16},{9,17... | collective-permute-start | bytes 2359304 | tf_op jit(solution)/shard_map/ppermute | solution.py:35
  251.6 5.9 %collective-permute-start.47 = (bf16[48,2048]{1,0:T(8,128)(2,1)S(1)}, bf16[48,2048]{1,0:T(8,128)(2,1)S(1)}, u32[]{:S(2)}, u32[]{:S(2)}) collective-permute-start(bf16[48,2048]{1,0:T(8,128)(2,1)S(1)} %get-tuple-element.50), channel_id=1, source_target_pairs={{0,4},{1,0},{2,6},{3,2},{4,5},{5,1},{6,7},{7,3},{8,12},{9,8},{10,1... | collective-permute-start | bytes 589832 | tf_op jit(solution)/shard_map/ppermute | solution.py:35
  260.0 8.2 %collective-permute-done.37 = bf16[512,768]{0,1:T(8,128)(2,1)S(1)} collective-permute-done((bf16[512,768]{0,1:T(8,128)(2,1)S(1)}, bf16[512,768]{0,1:T(8,128)(2,1)S(1)}, u32[]{:S(2)}, u32[]{:S(2)}) %collective-permute-start.37) | collective-permute-done | bytes 786464 | tf_op jit(solution)/shard_map/ppermute | solution.py:35
  268.7 3.2 %collective-permute-start.39 = (bf16[256,768]{0,1:T(8,128)(2,1)S(1)}, bf16[256,768]{0,1:T(8,128)(2,1)S(1)}, u32[]{:S(2)}, u32[]{:S(2)}) collective-permute-start(bf16[256,768]{0,1:T(8,128)(2,1)S(1)} %get-tuple-element.48), channel_id=1, source_target_pairs={{0,4},{1,0},{2,6},{3,2},{4,5},{5,1},{6,7},{7,3},{8,12},{9,8},{10,1... | collective-permute-start | bytes 1179656 | tf_op jit(solution)/shard_map/ppermute | solution.py:35
  276.4 5.6 %collective-permute-done.38 = bf16[256,768]{0,1:T(8,128)(2,1)S(1)} collective-permute-done((bf16[256,768]{0,1:T(8,128)(2,1)S(1)}, bf16[256,768]{0,1:T(8,128)(2,1)S(1)}, u32[]{:S(2)}, u32[]{:S(2)}) %collective-permute-start.38) | collective-permute-done | bytes 393248 | tf_op jit(solution)/shard_map/ppermute | solution.py:35
  (200 shorter events, 85.7 us)
Async XLA Ops:
  5.7 28.7 %collective-permute-start = (bf16[72,2048]{1,0:T(8,128)(2,1)}, bf16[72,2048]{1,0:T(8,128)(2,1)S(1)}, u32[]{:S(2)}, u32[]{:S(2)}) collective-permute-start(bf16[72,2048]{1,0:T(8,128)(2,1)} %get-tuple-element.46), channel_id=1, source_target_pairs={{0,4},{1,5},{2,6},{3,7},{4,0},{5,1},{6,2},{7,3},{8,12},{9,13},{10,... | collective-permute-start | bytes 884744 | tf_op jit(solution)/shard_map/ppermute | solution.py:35
  6.9 29.4 %collective-permute-start.1 = (bf16[72,2048]{1,0:T(8,128)(2,1)}, bf16[72,2048]{1,0:T(8,128)(2,1)S(1)}, u32[]{:S(2)}, u32[]{:S(2)}) collective-permute-start(bf16[72,2048]{1,0:T(8,128)(2,1)} %get-tuple-element.45), channel_id=1, source_target_pairs={{0,2},{1,3},{2,0},{3,1},{4,6},{5,7},{6,4},{7,5},{8,10},{9,11},{10,... | collective-permute-start | bytes 884744 | tf_op jit(solution)/shard_map/ppermute | solution.py:35
  13.5 14.7 %collective-permute-start.12 = (bf16[48,2048]{1,0:T(8,128)(2,1)}, bf16[48,2048]{1,0:T(8,128)(2,1)S(1)}, u32[]{:S(2)}, u32[]{:S(2)}) collective-permute-start(bf16[48,2048]{1,0:T(8,128)(2,1)} %get-tuple-element.57), channel_id=1, source_target_pairs={{0,0},{1,4},{2,2},{3,6},{4,1},{5,5},{6,3},{7,7},{8,8},{9,12},{10,1... | collective-permute-start | bytes 589832 | tf_op jit(solution)/shard_map/ppermute | solution.py:35
  25.0 33.4 %collective-permute-start.7 = (bf16[512,768]{0,1:T(8,128)(2,1)}, bf16[512,768]{0,1:T(8,128)(2,1)S(1)}, u32[]{:S(2)}, u32[]{:S(2)}) collective-permute-start(bf16[512,768]{0,1:T(8,128)(2,1)} %pad_maximum_fusion.5), channel_id=1, source_target_pairs={{0,8},{1,9},{2,10},{3,11},{4,12},{5,13},{6,14},{7,15},{8,16},{9,17... | collective-permute-start | bytes 2359304 | tf_op jit(solution)/shard_map/ppermute | solution.py:35
  28.3 25.0 %collective-permute-start.14 = (bf16[96,2048]{1,0:T(8,128)(2,1)S(1)}, bf16[96,2048]{1,0:T(8,128)(2,1)}, u32[]{:S(2)}, u32[]{:S(2)}) collective-permute-start(bf16[96,2048]{1,0:T(8,128)(2,1)S(1)} %pad_maximum_fusion.10), channel_id=1, source_target_pairs={{0,8},{1,9},{2,10},{3,11},{4,12},{5,13},{6,14},{7,15},{8,16},{9,17... | collective-permute-start | bytes 1179656 | tf_op jit(solution)/shard_map/ppermute | solution.py:35
  31.6 24.9 %collective-permute-start.17 = (bf16[96,2048]{1,0:T(8,128)(2,1)S(1)}, bf16[96,2048]{1,0:T(8,128)(2,1)}, u32[]{:S(2)}, u32[]{:S(2)}) collective-permute-start(bf16[96,2048]{1,0:T(8,128)(2,1)S(1)} %pad_maximum_fusion.10), channel_id=1, source_target_pairs={{8,0},{9,1},{10,2},{11,3},{12,4},{13,5},{14,6},{15,7},{16,8},{17,9... | collective-permute-start | bytes 1179656 | tf_op jit(solution)/shard_map/ppermute | solution.py:35
  34.4 36.5 %collective-permute-start.6 = (bf16[512,768]{0,1:T(8,128)(2,1)}, bf16[512,768]{0,1:T(8,128)(2,1)}, u32[]{:S(2)}, u32[]{:S(2)}) collective-permute-start(bf16[512,768]{0,1:T(8,128)(2,1)} %pad_maximum_fusion.5), channel_id=1, source_target_pairs={{8,0},{9,1},{10,2},{11,3},{12,4},{13,5},{14,6},{15,7},{16,8},{17,9... | collective-permute-start | bytes 2359304 | tf_op jit(solution)/shard_map/ppermute | solution.py:35
  36.3 25.6 %collective-permute-start.2 = (bf16[72,2048]{1,0:T(8,128)(2,1)}, bf16[72,2048]{1,0:T(8,128)(2,1)S(1)}, u32[]{:S(2)}, u32[]{:S(2)}) collective-permute-start(bf16[72,2048]{1,0:T(8,128)(2,1)} %get-tuple-element.44), channel_id=1, source_target_pairs={{0,6},{1,7},{2,4},{3,5},{4,2},{5,3},{6,0},{7,1},{8,14},{9,15},{10,... | collective-permute-start | bytes 884744 | tf_op jit(solution)/shard_map/ppermute | solution.py:35
  58.5 21.2 %collective-permute-start.8 = (bf16[512,768]{0,1:T(8,128)(2,1)S(1)}, bf16[512,768]{0,1:T(8,128)(2,1)S(1)}, u32[]{:S(2)}, u32[]{:S(2)}) collective-permute-start(bf16[512,768]{0,1:T(8,128)(2,1)S(1)} %collective-permute-done.7), channel_id=1, source_target_pairs={{8,16},{9,17},{10,18},{11,19},{12,20},{13,21},{14,22},{15,23},{16,... | collective-permute-start | bytes 2359304 | tf_op jit(solution)/shard_map/ppermute | solution.py:35
  62.0 36.1 %collective-permute-start.3 = (bf16[288,2048]{1,0:T(8,128)(2,1)S(1)}, bf16[288,2048]{1,0:T(8,128)(2,1)S(1)}, u32[]{:S(2)}, u32[]{:S(2)}) collective-permute-start(bf16[288,2048]{1,0:T(8,128)(2,1)S(1)} %pad_maximum_fusion.1), channel_id=1, source_target_pairs={{0,1},{1,0},{2,3},{3,2},{4,5},{5,4},{6,7},{7,6},{8,9},{9,8},{10,11... | collective-permute-start | bytes 3538952 | tf_op jit(solution)/shard_map/ppermute | solution.py:35
  65.3 15.1 %collective-permute-start.16 = (bf16[96,2048]{1,0:T(8,128)(2,1)S(1)}, bf16[96,2048]{1,0:T(8,128)(2,1)S(1)}, u32[]{:S(2)}, u32[]{:S(2)}) collective-permute-start(bf16[96,2048]{1,0:T(8,128)(2,1)S(1)} %collective-permute-done.15), channel_id=1, source_target_pairs={{16,24},{17,25},{18,26},{19,27},{20,28},{21,29},{22,30},{23,31}} | collective-permute-start | bytes 1179656 | tf_op jit(solution)/shard_map/ppermute | solution.py:35
  66.9 13.5 %collective-permute-start.19 = (bf16[96,2048]{1,0:T(8,128)(2,1)S(1)}, bf16[96,2048]{1,0:T(8,128)(2,1)S(1)}, u32[]{:S(2)}, u32[]{:S(2)}) collective-permute-start(bf16[96,2048]{1,0:T(8,128)(2,1)S(1)} %collective-permute-done.18), channel_id=1, source_target_pairs={{8,0},{9,1},{10,2},{11,3},{12,4},{13,5},{14,6},{15,7}} | collective-permute-start | bytes 1179656 | tf_op jit(solution)/shard_map/ppermute | solution.py:35
  70.8 23.1 %collective-permute-start.10 = (bf16[512,768]{0,1:T(8,128)(2,1)}, bf16[512,768]{0,1:T(8,128)(2,1)S(1)}, u32[]{:S(2)}, u32[]{:S(2)}) collective-permute-start(bf16[512,768]{0,1:T(8,128)(2,1)} %collective-permute-done.6), channel_id=1, source_target_pairs={{8,0},{9,1},{10,2},{11,3},{12,4},{13,5},{14,6},{15,7},{16,8},{17,9... | collective-permute-start | bytes 2359304 | tf_op jit(solution)/shard_map/ppermute | solution.py:35
  79.6 18.6 %collective-permute-start.9 = (bf16[512,768]{0,1:T(8,128)(2,1)S(1)}, bf16[512,768]{0,1:T(8,128)(2,1)S(1)}, u32[]{:S(2)}, u32[]{:S(2)}) collective-permute-start(bf16[512,768]{0,1:T(8,128)(2,1)S(1)} %collective-permute-done.8), channel_id=1, source_target_pairs={{16,24},{17,25},{18,26},{19,27},{20,28},{21,29},{22,30},{23,31}} | collective-permute-start | bytes 2359304 | tf_op jit(solution)/shard_map/ppermute | solution.py:35
  93.9 17.6 %collective-permute-start.11 = (bf16[512,768]{0,1:T(8,128)(2,1)S(1)}, bf16[512,768]{0,1:T(8,128)(2,1)S(1)}, u32[]{:S(2)}, u32[]{:S(2)}) collective-permute-start(bf16[512,768]{0,1:T(8,128)(2,1)S(1)} %collective-permute-done.10), channel_id=1, source_target_pairs={{8,0},{9,1},{10,2},{11,3},{12,4},{13,5},{14,6},{15,7}} | collective-permute-start | bytes 2359304 | tf_op jit(solution)/shard_map/ppermute | solution.py:35
  122.9 13.8 %collective-permute-start.23 = (bf16[72,2048]{1,0:T(8,128)(2,1)S(1)}, bf16[72,2048]{1,0:T(8,128)(2,1)S(1)}, u32[]{:S(2)}, u32[]{:S(2)}) collective-permute-start(bf16[72,2048]{1,0:T(8,128)(2,1)S(1)} %get-tuple-element.35), channel_id=1, source_target_pairs={{0,6},{1,7},{2,4},{3,5},{4,2},{5,3},{6,0},{7,1},{8,14},{9,15},{10,... | collective-permute-start | bytes 884744 | tf_op jit(solution)/shard_map/ppermute | solution.py:35
  129.5 13.8 %collective-permute-start.22 = (bf16[72,2048]{1,0:T(8,128)(2,1)S(1)}, bf16[72,2048]{1,0:T(8,128)(2,1)S(1)}, u32[]{:S(2)}, u32[]{:S(2)}) collective-permute-start(bf16[72,2048]{1,0:T(8,128)(2,1)S(1)} %get-tuple-element.36), channel_id=1, source_target_pairs={{0,2},{1,3},{2,0},{3,1},{4,6},{5,7},{6,4},{7,5},{8,10},{9,11},{10,... | collective-permute-start | bytes 884744 | tf_op jit(solution)/shard_map/ppermute | solution.py:35
  129.8 13.6 %collective-permute-start.21 = (bf16[72,2048]{1,0:T(8,128)(2,1)S(1)}, bf16[72,2048]{1,0:T(8,128)(2,1)S(1)}, u32[]{:S(2)}, u32[]{:S(2)}) collective-permute-start(bf16[72,2048]{1,0:T(8,128)(2,1)S(1)} %get-tuple-element.37), channel_id=1, source_target_pairs={{0,4},{1,5},{2,6},{3,7},{4,0},{5,1},{6,2},{7,3},{8,12},{9,13},{10,... | collective-permute-start | bytes 884744 | tf_op jit(solution)/shard_map/ppermute | solution.py:35
  174.7 32.9 %collective-permute-start.32 = (bf16[512,768]{0,1:T(8,128)(2,1)S(1)}, bf16[512,768]{0,1:T(8,128)(2,1)S(1)}, u32[]{:S(2)}, u32[]{:S(2)}) collective-permute-start(bf16[512,768]{0,1:T(8,128)(2,1)S(1)} %get-tuple-element.17), channel_id=1, source_target_pairs={{0,8},{1,9},{2,10},{3,11},{4,12},{5,13},{6,14},{7,15}} | collective-permute-start | bytes 2359304 | tf_op jit(solution)/shard_map/ppermute | solution.py:35
  176.1 31.4 %collective-permute-start.35 = (bf16[512,768]{0,1:T(8,128)(2,1)S(1)}, bf16[512,768]{0,1:T(8,128)(2,1)S(1)}, u32[]{:S(2)}, u32[]{:S(2)}) collective-permute-start(bf16[512,768]{0,1:T(8,128)(2,1)S(1)} %get-tuple-element.18), channel_id=1, source_target_pairs={{24,16},{25,17},{26,18},{27,19},{28,20},{29,21},{30,22},{31,23}} | collective-permute-start | bytes 2359304 | tf_op jit(solution)/shard_map/ppermute | solution.py:35
  176.9 27.3 %collective-permute-start.40 = (bf16[96,2048]{1,0:T(8,128)(2,1)S(1)}, bf16[96,2048]{1,0:T(8,128)(2,1)S(1)}, u32[]{:S(2)}, u32[]{:S(2)}) collective-permute-start(bf16[96,2048]{1,0:T(8,128)(2,1)S(1)} %get-tuple-element.23), channel_id=1, source_target_pairs={{0,8},{1,9},{2,10},{3,11},{4,12},{5,13},{6,14},{7,15}} | collective-permute-start | bytes 1179656 | tf_op jit(solution)/shard_map/ppermute | solution.py:35
  180.7 36.7 %collective-permute-start.28 = (bf16[288,2048]{1,0:T(8,128)(2,1)S(1)}, bf16[288,2048]{1,0:T(8,128)(2,1)S(1)}, u32[]{:S(2)}, u32[]{:S(2)}) collective-permute-start(bf16[288,2048]{1,0:T(8,128)(2,1)S(1)} %slice.238), channel_id=1, source_target_pairs={{0,1},{1,0},{2,3},{3,2},{4,5},{5,4},{6,7},{7,6},{8,9},{9,8},{10,11... | collective-permute-start | bytes 3538952 | tf_op jit(solution)/shard_map/ppermute | solution.py:35
  181.1 30.1 %collective-permute-start.43 = (bf16[96,2048]{1,0:T(8,128)(2,1)S(1)}, bf16[96,2048]{1,0:T(8,128)(2,1)S(1)}, u32[]{:S(2)}, u32[]{:S(2)}) collective-permute-start(bf16[96,2048]{1,0:T(8,128)(2,1)S(1)} %get-tuple-element.24), channel_id=1, source_target_pairs={{24,16},{25,17},{26,18},{27,19},{28,20},{29,21},{30,22},{31,23}} | collective-permute-start | bytes 1179656 | tf_op jit(solution)/shard_map/ppermute | solution.py:35
  208.0 37.3 %collective-permute-start.33 = (bf16[512,768]{0,1:T(8,128)(2,1)S(1)}, bf16[512,768]{0,1:T(8,128)(2,1)S(1)}, u32[]{:S(2)}, u32[]{:S(2)}) collective-permute-start(bf16[512,768]{0,1:T(8,128)(2,1)S(1)} %get-tuple-element.15), channel_id=1, source_target_pairs={{0,8},{1,9},{2,10},{3,11},{4,12},{5,13},{6,14},{7,15},{8,16},{9,17... | collective-permute-start | bytes 2359304 | tf_op jit(solution)/shard_map/ppermute | solution.py:35
  209.9 35.4 %collective-permute-start.36 = (bf16[512,768]{0,1:T(8,128)(2,1)S(1)}, bf16[512,768]{0,1:T(8,128)(2,1)S(1)}, u32[]{:S(2)}, u32[]{:S(2)}) collective-permute-start(bf16[512,768]{0,1:T(8,128)(2,1)S(1)} %get-tuple-element.16), channel_id=1, source_target_pairs={{16,8},{17,9},{18,10},{19,11},{20,12},{21,13},{22,14},{23,15},{24,... | collective-permute-start | bytes 2359304 | tf_op jit(solution)/shard_map/ppermute | solution.py:35
  216.0 22.2 %collective-permute-start.44 = (bf16[96,2048]{1,0:T(8,128)(2,1)S(1)}, bf16[96,2048]{1,0:T(8,128)(2,1)S(1)}, u32[]{:S(2)}, u32[]{:S(2)}) collective-permute-start(bf16[96,2048]{1,0:T(8,128)(2,1)S(1)} %get-tuple-element.22), channel_id=1, source_target_pairs={{16,8},{17,9},{18,10},{19,11},{20,12},{21,13},{22,14},{23,15},{24,... | collective-permute-start | bytes 1179656 | tf_op jit(solution)/shard_map/ppermute | solution.py:35
  217.8 21.3 %collective-permute-start.31 = (bf16[72,2048]{1,0:T(8,128)(2,1)S(1)}, bf16[72,2048]{1,0:T(8,128)(2,1)S(1)}, u32[]{:S(2)}, u32[]{:S(2)}) collective-permute-start(bf16[72,2048]{1,0:T(8,128)(2,1)S(1)} %get-tuple-element.26), channel_id=1, source_target_pairs={{0,6},{1,7},{2,4},{3,5},{4,2},{5,3},{6,0},{7,1},{8,14},{9,15},{10,... | collective-permute-start | bytes 884744 | tf_op jit(solution)/shard_map/ppermute | solution.py:35
  218.8 22.3 %collective-permute-start.30 = (bf16[72,2048]{1,0:T(8,128)(2,1)S(1)}, bf16[72,2048]{1,0:T(8,128)(2,1)S(1)}, u32[]{:S(2)}, u32[]{:S(2)}) collective-permute-start(bf16[72,2048]{1,0:T(8,128)(2,1)S(1)} %get-tuple-element.27), channel_id=1, source_target_pairs={{0,2},{1,3},{2,0},{3,1},{4,6},{5,7},{6,4},{7,5},{8,10},{9,11},{10,... | collective-permute-start | bytes 884744 | tf_op jit(solution)/shard_map/ppermute | solution.py:35
  245.9 22.3 %collective-permute-start.37 = (bf16[512,768]{0,1:T(8,128)(2,1)S(1)}, bf16[512,768]{0,1:T(8,128)(2,1)S(1)}, u32[]{:S(2)}, u32[]{:S(2)}) collective-permute-start(bf16[512,768]{0,1:T(8,128)(2,1)S(1)} %get-tuple-element.14), channel_id=1, source_target_pairs={{8,0},{9,1},{10,2},{11,3},{12,4},{13,5},{14,6},{15,7},{16,8},{17,9... | collective-permute-start | bytes 2359304 | tf_op jit(solution)/shard_map/ppermute | solution.py:35
  247.9 20.3 %collective-permute-start.34 = (bf16[512,768]{0,1:T(8,128)(2,1)S(1)}, bf16[512,768]{0,1:T(8,128)(2,1)S(1)}, u32[]{:S(2)}, u32[]{:S(2)}) collective-permute-start(bf16[512,768]{0,1:T(8,128)(2,1)S(1)} %get-tuple-element.13), channel_id=1, source_target_pairs={{0,8},{1,9},{2,10},{3,11},{4,12},{5,13},{6,14},{7,15},{8,16},{9,17... | collective-permute-start | bytes 2359304 | tf_op jit(solution)/shard_map/ppermute | solution.py:35
  251.6 23.9 %collective-permute-start.47 = (bf16[48,2048]{1,0:T(8,128)(2,1)S(1)}, bf16[48,2048]{1,0:T(8,128)(2,1)S(1)}, u32[]{:S(2)}, u32[]{:S(2)}) collective-permute-start(bf16[48,2048]{1,0:T(8,128)(2,1)S(1)} %get-tuple-element.50), channel_id=1, source_target_pairs={{0,4},{1,0},{2,6},{3,2},{4,5},{5,1},{6,7},{7,3},{8,12},{9,8},{10,1... | collective-permute-start | bytes 589832 | tf_op jit(solution)/shard_map/ppermute | solution.py:35
  257.5 18.0 %collective-permute-start.46 = (bf16[48,2048]{1,0:T(8,128)(2,1)S(1)}, bf16[48,2048]{1,0:T(8,128)(2,1)S(1)}, u32[]{:S(2)}, u32[]{:S(2)}) collective-permute-start(bf16[48,2048]{1,0:T(8,128)(2,1)S(1)} %get-tuple-element.49), channel_id=1, source_target_pairs={{0,0},{1,4},{2,2},{3,6},{4,1},{5,5},{6,3},{7,7},{8,8},{9,12},{10,1... | collective-permute-start | bytes 589832 | tf_op jit(solution)/shard_map/ppermute | solution.py:35
  (49 other events, 694.6 us)

commit v3 on v2

--- a/solution.py
+++ b/solution.py
@@ -10,6 +10,10 @@
 
 def dot(a, b, dims=((1,), (0,))):
     return lax.dot_general(a, b, (dims, ((), ())), preferred_element_type=F32)
+
+
+def tie(value, *others):
+    return lax.optimization_barrier((value,) + others)[0]
 
 
 def added(*terms):
@@ -47,15 +51,13 @@
             down.append(self.step(down[-1], -1, range(1, self.zs - s + 1)))
         return up, down
 
-    def rotated(self, shard):
-        up, down = self.gather(shard)
+    def rotated(self, shard, up, down):
         blocks = [shard]
         for s in range(1, self.zs):
             blocks.append(jnp.where(self.z + s < self.zs, down[s], up[self.zs - s]))
         return blocks
 
-    def straight(self, shard):
-        up, down = self.gather(shard)
+    def straight(self, shard, up, down):
         blocks = []
         for j in range(self.zs):
             block = shard
@@ -72,9 +74,11 @@
         up = self.step(block(n - 1), 1, range(0, 1))
         down = self.step(block(1 - n), -1, range(n - 1, n))
         for r in range(2, n):
+            if r == 2:
+                early = up, down
             up = self.step(added(block(n - r), up), 1, range(0, r))
             down = self.step(added(block(r - n), down), -1, range(n - r, n))
-        return added(block(0), up, down)
+        return added(block(0), up, down), early
 
 
 def local(tokens, expert_ids, gate_probs, w_gate, w_up, w_down, d_out):
@@ -118,15 +122,18 @@
 
     gate_cols = dot(w_gate[0], shuffle).astype(BF)
     up_cols = dot(w_up[0], shuffle).astype(BF)
-    gate_up_shard = spread(
-        jnp.concatenate([gate_cols[:, :half], up_cols[:, :half]], axis=1),
-        jnp.concatenate([gate_cols[:, half:], up_cols[:, half:]], axis=1),
-    )
-    down_low, down_high = w_down[0, :part], w_down[0, part:]
+    part_a = jnp.concatenate([gate_cols[:, :half], up_cols[:, :half]], axis=1)
+    part_b = jnp.concatenate([gate_cols[:, half:], up_cols[:, half:]], axis=1)
+    gate_up_shard = spread(part_a, part_b)
+    tokens, d_out = tie(tokens, part_a, part_b), tie(d_out, part_a, part_b)
+    w_down_late = tie(w_down[0], gate_up_shard)
+    down_low, down_high = w_down_late[:part], w_down_late[part:]
     even = g.x == 0
     down_shard = spread(jnp.where(even, down_low, down_high), jnp.where(even, down_high, down_low))
-    gate_up = jnp.concatenate(g.rotated(gate_up_shard), axis=0)
-    down = jnp.concatenate(g.straight(down_shard), axis=0)
+    up, dn = g.gather(gate_up_shard)
+    gate_up = jnp.concatenate(g.rotated(gate_up_shard, up, dn), axis=0)
+    down_shard = tie(down_shard, up[-2], dn[-2])
+    down = jnp.concatenate(g.straight(down_shard, *g.gather(down_shard)), axis=0)
 
     expert_iota = jnp.arange(experts, dtype=jnp.int32)
     chosen = expert_ids[:, :, None] == expert_iota
@@ -176,16 +183,17 @@
 
     down_part = dot(hidden, d_produced, ((0,), (0,))).astype(BF)
     down_rows = 2 * part
-    down_grad = g.scatter(lambda k: lax.dynamic_slice_in_dim(down_part, (g.z + k) * down_rows, down_rows))
-    returned = give_back(dot(hidden, down))
-
-    d_hidden = dot(d_produced, down, ((1,), (1,)))
+    down_grad, first_sums = g.scatter(lambda k: lax.dynamic_slice_in_dim(down_part, (g.z + k) * down_rows, down_rows))
+
+    d_hidden = dot(tie(d_produced, *first_sums), down, ((1,), (1,)))
     d_gate = (d_hidden * up_pre * sig * (1.0 + gate_pre * (1.0 - sig))).astype(BF)
     d_up = (d_hidden * act).astype(BF)
     d_both = jnp.concatenate([d_gate, d_up], axis=1)
     both_part = dot(arrived, d_both, ((0,), (0,))).astype(BF)
-    gate_up_grad = g.scatter(lambda k: both_part[(k % g.zs) * line_width:(k % g.zs + 1) * line_width])
-    back_rows = give_back(dot(d_both, gate_up, ((1,), (1,))))
+    gate_up_grad, early = g.scatter(lambda k: both_part[(k % g.zs) * line_width:(k % g.zs + 1) * line_width])
+    returned = give_back(dot(tie(hidden, both_part), down))
+    back_rows = give_back(dot(tie(d_both, both_part), gate_up, ((1,), (1,))))
+    returned, back_rows = tie(returned, *early), tie(back_rows, *early)
 
     high = lax.reduce_precision(weighted, 8, 7)
     mixed = (dot(high.astype(BF), returned) + dot((weighted - high).astype(BF), returned)).astype(BF)

time: 288 us -> 279 us (0.969)
  waiting for transfers between devices: 139 us -> 112 us
  starting transfers between devices: 99.9 us -> 115 us
  local copies, waits for them, and re-layouts: 5.11 us -> 9.66 us
    ppermute x48, waiting for transfers between devices: 139 us -> 112 us  [send(): return lax.ppermute(value, BOTH, pairs)]
    ppermute x48, starting transfers between devices: 99.9 us -> 115 us  [send(): return lax.ppermute(value, BOTH, pairs)]
    unnamed x72 -> x40, local copies, waits for them, and re-layouts: 1.57 us -> 5.49 us
    unnamed x4, other arithmetic: 3.93 us -> 0.69 us
  transfers between devices with their start and end apart: 48 -> 48, of which waited for: 20 -> 26; matrix products, arithmetic and copies ran while one was open for 7% -> 10% of each run, Pallas kernels for 0% -> 0%
where the time goes in v3:
time: 279 us; the launch traced here: 277 us
  starting transfers between devices  115 us (41%)
  waiting for transfers between devices  112 us (40%)
  matrix products  21.5 us (8%)
  other arithmetic  17.2 us (6%)
  local copies, waits for them, and re-layouts  9.66 us (3%)
    ppermute x48, starting transfers between devices, send(): return lax.ppermute(value, BOTH, pairs)  115 us
    ppermute x48, waiting for transfers between devices, send(): return lax.ppermute(value, BOTH, pairs)  112 us
    dot_general x17, matrix products, dot(): return lax.dot_general(a, b, (dims, ((), ())), preferred_element_type=F32)  21.5 us
  transfers between devices with their start and end apart: 48, of which 26 were waited for; matrix products, arithmetic and copies ran while one was open for 10% of the time, Pallas kernels for 0%

profile of v3, /device:TPU:9, one launch (start us, length us, event | category | flops | bytes accessed | tf_op | source)
XLA Modules:
  0.0 276.7 jit_solution(2767485248050025744)
XLA Ops:
  19.5 7.1 %collective-permute-done.1 = bf16[72,2048]{1,0:T(8,128)(2,1)} collective-permute-done((bf16[72,2048]{1,0:T(8,128)(2,1)}, bf16[72,2048]{1,0:T(8,128)(2,1)}, u32[]{:S(2)}, u32[]{:S(2)}) %collective-permute-start.1) | collective-permute-done | bytes 294944 | tf_op jit(solution)/shard_map/ppermute | solution.py:39
  26.6 3.7 %collective-permute-start.4 = (bf16[256,768]{0,1:T(8,128)(2,1)}, bf16[256,768]{0,1:T(8,128)(2,1)S(1)}, u32[]{:S(2)}, u32[]{:S(2)}) collective-permute-start(bf16[256,768]{0,1:T(8,128)(2,1)} %pad_maximum_fusion.7), channel_id=1, source_target_pairs={{0,0},{1,4},{2,2},{3,6},{4,1},{5,5},{6,3},{7,7},{8,8},{9,12},{10,1... | collective-permute-start | bytes 1179656 | tf_op jit(solution)/shard_map/ppermute | solution.py:39
  33.6 4.7 %collective-permute-done.13 = bf16[72,2048]{1,0:T(8,128)(2,1)} collective-permute-done((bf16[72,2048]{1,0:T(8,128)(2,1)}, bf16[72,2048]{1,0:T(8,128)(2,1)}, u32[]{:S(2)}, u32[]{:S(2)}) %collective-permute-start.13) | collective-permute-done | bytes 294944 | tf_op jit(solution)/shard_map/ppermute | solution.py:39
  42.3 3.6 %collective-permute-done.5 = bf16[256,768]{0,1:T(8,128)(2,1)S(1)} collective-permute-done((bf16[256,768]{0,1:T(8,128)(2,1)}, bf16[256,768]{0,1:T(8,128)(2,1)S(1)}, u32[]{:S(2)}, u32[]{:S(2)}) %collective-permute-start.5) | collective-permute-done | bytes 393248 | tf_op jit(solution)/shard_map/ppermute | solution.py:39
  46.3 3.3 %collective-permute-start.7 = (bf16[512,768]{0,1:T(8,128)(2,1)S(1)}, bf16[512,768]{0,1:T(8,128)(2,1)S(1)}, u32[]{:S(2)}, u32[]{:S(2)}) collective-permute-start(bf16[512,768]{0,1:T(8,128)(2,1)S(1)} %pad_maximum_fusion.6), channel_id=1, source_target_pairs={{0,8},{1,9},{2,10},{3,11},{4,12},{5,13},{6,14},{7,15},{8,16},{9,17... | collective-permute-start | bytes 2359304 | tf_op jit(solution)/shard_map/ppermute | solution.py:39
  55.7 10.4 %collective-permute-done.7 = bf16[512,768]{0,1:T(8,128)(2,1)S(1)} collective-permute-done((bf16[512,768]{0,1:T(8,128)(2,1)S(1)}, bf16[512,768]{0,1:T(8,128)(2,1)S(1)}, u32[]{:S(2)}, u32[]{:S(2)}) %collective-permute-start.7) | collective-permute-done | bytes 786464 | tf_op jit(solution)/shard_map/ppermute | solution.py:39
  66.1 3.2 %collective-permute-start.8 = (bf16[512,768]{0,1:T(8,128)(2,1)S(1)}, bf16[512,768]{0,1:T(8,128)(2,1)S(1)}, u32[]{:S(2)}, u32[]{:S(2)}) collective-permute-start(bf16[512,768]{0,1:T(8,128)(2,1)S(1)} %collective-permute-done.7), channel_id=1, source_target_pairs={{8,16},{9,17},{10,18},{11,19},{12,20},{13,21},{14,22},{15,23},{16,... | collective-permute-start | bytes 2359304 | tf_op jit(solution)/shard_map/ppermute | solution.py:39
  69.3 4.7 %collective-permute-start.18 = (bf16[48,2048]{1,0:T(8,128)(2,1)S(1)}, bf16[48,2048]{1,0:T(8,128)(2,1)S(1)}, u32[]{:S(2)}, u32[]{:S(2)}) collective-permute-start(bf16[48,2048]{1,0:T(8,128)(2,1)S(1)} %get-tuple-element.74), channel_id=1, source_target_pairs={{0,0},{1,4},{2,2},{3,6},{4,1},{5,5},{6,3},{7,7},{8,8},{9,12},{10,1... | collective-permute-start | bytes 589832 | tf_op jit(solution)/shard_map/ppermute | solution.py:39
  79.4 4.5 %collective-permute-done.8 = bf16[512,768]{0,1:T(8,128)(2,1)S(1)} collective-permute-done((bf16[512,768]{0,1:T(8,128)(2,1)S(1)}, bf16[512,768]{0,1:T(8,128)(2,1)S(1)}, u32[]{:S(2)}, u32[]{:S(2)}) %collective-permute-start.8) | collective-permute-done | bytes 786464 | tf_op jit(solution)/shard_map/ppermute | solution.py:39
  84.6 13.3 %collective-permute-done.10 = bf16[512,768]{0,1:T(8,128)(2,1)S(1)} collective-permute-done((bf16[512,768]{0,1:T(8,128)(2,1)S(1)}, bf16[512,768]{0,1:T(8,128)(2,1)S(1)}, u32[]{:S(2)}, u32[]{:S(2)}) %collective-permute-start.10) | collective-permute-done | bytes 786464 | tf_op jit(solution)/shard_map/ppermute | solution.py:39
  100.2 3.0 %collective-permute-start.20 = (bf16[96,2048]{1,0:T(8,128)(2,1)S(1)}, bf16[96,2048]{1,0:T(8,128)(2,1)S(1)}, u32[]{:S(2)}, u32[]{:S(2)}) collective-permute-start(bf16[96,2048]{1,0:T(8,128)(2,1)S(1)} %pad_maximum_fusion.9), channel_id=1, source_target_pairs={{0,8},{1,9},{2,10},{3,11},{4,12},{5,13},{6,14},{7,15},{8,16},{9,17... | collective-permute-start | bytes 1179656 | tf_op jit(solution)/shard_map/ppermute | solution.py:39
  105.8 3.3 %collective-permute-done.23 = bf16[96,2048]{1,0:T(8,128)(2,1)S(1)} collective-permute-done((bf16[96,2048]{1,0:T(8,128)(2,1)S(1)}, bf16[96,2048]{1,0:T(8,128)(2,1)S(1)}, u32[]{:S(2)}, u32[]{:S(2)}) %collective-permute-start.23) | collective-permute-done | bytes 393248 | tf_op jit(solution)/shard_map/ppermute | solution.py:39
  111.6 4.2 %collective-permute-start.21 = (bf16[96,2048]{1,0:T(8,128)(2,1)S(1)}, bf16[96,2048]{1,0:T(8,128)(2,1)}, u32[]{:S(2)}, u32[]{:S(2)}) collective-permute-start(bf16[96,2048]{1,0:T(8,128)(2,1)S(1)} %collective-permute-done.20), channel_id=1, source_target_pairs={{8,16},{9,17},{10,18},{11,19},{12,20},{13,21},{14,22},{15,23},{16,... | collective-permute-start | bytes 1179656 | tf_op jit(solution)/shard_map/ppermute | solution.py:39
  116.3 8.0 %collective-permute-done.11 = bf16[512,768]{0,1:T(8,128)(2,1)S(1)} collective-permute-done((bf16[512,768]{0,1:T(8,128)(2,1)S(1)}, bf16[512,768]{0,1:T(8,128)(2,1)S(1)}, u32[]{:S(2)}, u32[]{:S(2)}) %collective-permute-start.11) | collective-permute-done | bytes 786464 | tf_op jit(solution)/shard_map/ppermute | solution.py:39
  132.8 5.4 %collective-permute-start.25 = (bf16[96,2048]{1,0:T(8,128)(2,1)}, bf16[96,2048]{1,0:T(8,128)(2,1)}, u32[]{:S(2)}, u32[]{:S(2)}) collective-permute-start(bf16[96,2048]{1,0:T(8,128)(2,1)} %collective-permute-done.24), channel_id=1, source_target_pairs={{8,0},{9,1},{10,2},{11,3},{12,4},{13,5},{14,6},{15,7}} | collective-permute-start | bytes 1179656 | tf_op jit(solution)/shard_map/ppermute | solution.py:39
  145.7 3.0 %convolution_convert_fusion = bf16[2048,768]{0,1:T(8,128)(2,1)S(1)} fusion(bf16[576,2048]{1,0:T(8,128)(2,1)S(1)} %copy-done.15, bf16[576,384]{1,0:T(8,128)(2,1)S(1)} %get-tuple-element.37, bf16[576,384]{1,0:T(8,128)(2,1)S(1)} %get-tuple-element.36), kind=kOutput, calls=%fused_computation | convolution fusion | flops 1815281664 | bytes 6389760 | tf_op jit(solution)/shard_map/dot_general | solution.py:12
  154.0 4.7 %collective-permute-start.32 = (bf16[288,2048]{1,0:T(8,128)(2,1)S(1)}, bf16[288,2048]{1,0:T(8,128)(2,1)S(1)}, u32[]{:S(2)}, u32[]{:S(2)}) collective-permute-start(bf16[288,2048]{1,0:T(8,128)(2,1)S(1)} %slice.238), channel_id=1, source_target_pairs={{0,1},{1,0},{2,3},{3,2},{4,5},{5,4},{6,7},{7,6},{8,9},{9,8},{10,11... | collective-permute-start | bytes 3538952 | tf_op jit(solution)/shard_map/ppermute | solution.py:39
  165.0 5.6 %collective-permute-start.26 = (bf16[288,2048]{1,0:T(8,128)(2,1)S(1)}, bf16[288,2048]{1,0:T(8,128)(2,1)S(1)}, u32[]{:S(2)}, u32[]{:S(2)}) collective-permute-start(bf16[288,2048]{1,0:T(8,128)(2,1)S(1)} %slice.239), channel_id=1, source_target_pairs={{0,1},{1,0},{2,3},{3,2},{4,5},{5,4},{6,7},{7,6},{8,9},{9,8},{10,11... | collective-permute-start | bytes 3538952 | tf_op jit(solution)/shard_map/ppermute | solution.py:39
  170.6 4.3 %collective-permute-start.43 = (bf16[96,2048]{1,0:T(8,128)(2,1)S(1)}, bf16[96,2048]{1,0:T(8,128)(2,1)S(1)}, u32[]{:S(2)}, u32[]{:S(2)}) collective-permute-start(bf16[96,2048]{1,0:T(8,128)(2,1)S(1)} %get-tuple-element.38), channel_id=1, source_target_pairs={{0,8},{1,9},{2,10},{3,11},{4,12},{5,13},{6,14},{7,15},{8,16},{9,17... | collective-permute-start | bytes 1179656 | tf_op jit(solution)/shard_map/ppermute | solution.py:39
  178.0 9.8 %collective-permute-start.36 = (bf16[512,768]{0,1:T(8,128)(2,1)S(1)}, bf16[512,768]{0,1:T(8,128)(2,1)S(1)}, u32[]{:S(2)}, u32[]{:S(2)}) collective-permute-start(bf16[512,768]{0,1:T(8,128)(2,1)S(1)} %get-tuple-element.32), channel_id=1, source_target_pairs={{0,8},{1,9},{2,10},{3,11},{4,12},{5,13},{6,14},{7,15},{8,16},{9,17... | collective-permute-start | bytes 2359304 | tf_op jit(solution)/shard_map/ppermute | solution.py:39
  189.7 5.8 %collective-permute-start.35 = (bf16[72,2048]{1,0:T(8,128)(2,1)S(1)}, bf16[72,2048]{1,0:T(8,128)(2,1)S(1)}, u32[]{:S(2)}, u32[]{:S(2)}) collective-permute-start(bf16[72,2048]{1,0:T(8,128)(2,1)S(1)} %get-tuple-element.43), channel_id=1, source_target_pairs={{0,6},{1,7},{2,4},{3,5},{4,2},{5,3},{6,0},{7,1},{8,14},{9,15},{10,... | collective-permute-start | bytes 884744 | tf_op jit(solution)/shard_map/ppermute | solution.py:39
  195.7 12.7 %collective-permute-start.46 = (bf16[48,2048]{1,0:T(8,128)(2,1)S(1)}, bf16[48,2048]{1,0:T(8,128)(2,1)S(1)}, u32[]{:S(2)}, u32[]{:S(2)}) collective-permute-start(bf16[48,2048]{1,0:T(8,128)(2,1)S(1)} %get-tuple-element.66), channel_id=1, source_target_pairs={{0,0},{1,4},{2,2},{3,6},{4,1},{5,5},{6,3},{7,7},{8,8},{9,12},{10,1... | collective-permute-start | bytes 589832 | tf_op jit(solution)/shard_map/ppermute | solution.py:39
  208.8 4.1 %collective-permute-done.46 = bf16[48,2048]{1,0:T(8,128)(2,1)S(1)} collective-permute-done((bf16[48,2048]{1,0:T(8,128)(2,1)S(1)}, bf16[48,2048]{1,0:T(8,128)(2,1)S(1)}, u32[]{:S(2)}, u32[]{:S(2)}) %collective-permute-start.46) | collective-permute-done | bytes 196640 | tf_op jit(solution)/shard_map/ppermute | solution.py:39
  215.8 3.0 %collective-permute-done.34 = bf16[72,2048]{1,0:T(8,128)(2,1)S(1)} collective-permute-done((bf16[72,2048]{1,0:T(8,128)(2,1)S(1)}, bf16[72,2048]{1,0:T(8,128)(2,1)S(1)}, u32[]{:S(2)}, u32[]{:S(2)}) %collective-permute-start.34) | collective-permute-done | bytes 294944 | tf_op jit(solution)/shard_map/ppermute | solution.py:39
  219.0 3.9 %collective-permute-done.33 = bf16[72,2048]{1,0:T(8,128)(2,1)S(1)} collective-permute-done((bf16[72,2048]{1,0:T(8,128)(2,1)S(1)}, bf16[72,2048]{1,0:T(8,128)(2,1)S(1)}, u32[]{:S(2)}, u32[]{:S(2)}) %collective-permute-start.33) | collective-permute-done | bytes 294944 | tf_op jit(solution)/shard_map/ppermute | solution.py:39
  224.0 4.3 %collective-permute-done.29 = bf16[72,2048]{1,0:T(8,128)(2,1)S(1)} collective-permute-done((bf16[72,2048]{1,0:T(8,128)(2,1)S(1)}, bf16[72,2048]{1,0:T(8,128)(2,1)S(1)}, u32[]{:S(2)}, u32[]{:S(2)}) %collective-permute-start.29) | collective-permute-done | bytes 294944 | tf_op jit(solution)/shard_map/ppermute | solution.py:39
  228.3 4.6 %collective-permute-done.28 = bf16[72,2048]{1,0:T(8,128)(2,1)S(1)} collective-permute-done((bf16[72,2048]{1,0:T(8,128)(2,1)S(1)}, bf16[72,2048]{1,0:T(8,128)(2,1)S(1)}, u32[]{:S(2)}, u32[]{:S(2)}) %collective-permute-start.28) | collective-permute-done | bytes 294944 | tf_op jit(solution)/shard_map/ppermute | solution.py:39
  236.1 4.0 %collective-permute-start.37 = (bf16[512,768]{0,1:T(8,128)(2,1)S(1)}, bf16[512,768]{0,1:T(8,128)(2,1)S(1)}, u32[]{:S(2)}, u32[]{:S(2)}) collective-permute-start(bf16[512,768]{0,1:T(8,128)(2,1)S(1)} %get-tuple-element.30), channel_id=1, source_target_pairs={{0,8},{1,9},{2,10},{3,11},{4,12},{5,13},{6,14},{7,15},{8,16},{9,17... | collective-permute-start | bytes 2359304 | tf_op jit(solution)/shard_map/ppermute | solution.py:39
  244.5 11.5 %collective-permute-done.37 = bf16[512,768]{0,1:T(8,128)(2,1)S(1)} collective-permute-done((bf16[512,768]{0,1:T(8,128)(2,1)S(1)}, bf16[512,768]{0,1:T(8,128)(2,1)S(1)}, u32[]{:S(2)}, u32[]{:S(2)}) %collective-permute-start.37) | collective-permute-done | bytes 786464 | tf_op jit(solution)/shard_map/ppermute | solution.py:39
  256.0 3.7 %collective-permute-done.39 = bf16[512,768]{0,1:T(8,128)(2,1)S(1)} collective-permute-done((bf16[512,768]{0,1:T(8,128)(2,1)S(1)}, bf16[512,768]{0,1:T(8,128)(2,1)S(1)}, u32[]{:S(2)}, u32[]{:S(2)}) %collective-permute-start.39) | collective-permute-done | bytes 786464 | tf_op jit(solution)/shard_map/ppermute | solution.py:39
  260.2 3.3 %collective-permute-start.40 = (bf16[256,768]{0,1:T(8,128)(2,1)S(1)}, bf16[256,768]{0,1:T(8,128)(2,1)S(1)}, u32[]{:S(2)}, u32[]{:S(2)}) collective-permute-start(bf16[256,768]{0,1:T(8,128)(2,1)S(1)} %get-tuple-element.64), channel_id=1, source_target_pairs={{0,0},{1,4},{2,2},{3,6},{4,1},{5,5},{6,3},{7,7},{8,8},{9,12},{10,1... | collective-permute-start | bytes 1179656 | tf_op jit(solution)/shard_map/ppermute | solution.py:39
  265.7 6.4 %collective-permute-done.40 = bf16[256,768]{0,1:T(8,128)(2,1)S(1)} collective-permute-done((bf16[256,768]{0,1:T(8,128)(2,1)S(1)}, bf16[256,768]{0,1:T(8,128)(2,1)S(1)}, u32[]{:S(2)}, u32[]{:S(2)}) %collective-permute-start.40) | collective-permute-done | bytes 393248 | tf_op jit(solution)/shard_map/ppermute | solution.py:39
  (172 shorter events, 97.8 us)
Async XLA Ops:
  11.5 15.1 %collective-permute-start.1 = (bf16[72,2048]{1,0:T(8,128)(2,1)}, bf16[72,2048]{1,0:T(8,128)(2,1)}, u32[]{:S(2)}, u32[]{:S(2)}) collective-permute-start(bf16[72,2048]{1,0:T(8,128)(2,1)} %get-tuple-element.62), channel_id=1, source_target_pairs={{0,2},{1,3},{2,0},{3,1},{4,6},{5,7},{6,4},{7,5},{8,10},{9,11},{10,... | collective-permute-start | bytes 884744 | tf_op jit(solution)/shard_map/ppermute | solution.py:39
  11.8 18.6 %collective-permute-start = (bf16[72,2048]{1,0:T(8,128)(2,1)}, bf16[72,2048]{1,0:T(8,128)(2,1)}, u32[]{:S(2)}, u32[]{:S(2)}) collective-permute-start(bf16[72,2048]{1,0:T(8,128)(2,1)} %get-tuple-element.63), channel_id=1, source_target_pairs={{0,4},{1,5},{2,6},{3,7},{4,0},{5,1},{6,2},{7,3},{8,12},{9,13},{10,... | collective-permute-start | bytes 884744 | tf_op jit(solution)/shard_map/ppermute | solution.py:39
  13.8 17.9 %collective-permute-start.14 = (bf16[72,2048]{1,0:T(8,128)(2,1)}, bf16[72,2048]{1,0:T(8,128)(2,1)S(1)}, u32[]{:S(2)}, u32[]{:S(2)}) collective-permute-start(bf16[72,2048]{1,0:T(8,128)(2,1)} %get-tuple-element.56), channel_id=1, source_target_pairs={{0,6},{1,7},{2,4},{3,5},{4,2},{5,3},{6,0},{7,1},{8,14},{9,15},{10,... | collective-permute-start | bytes 884744 | tf_op jit(solution)/shard_map/ppermute | solution.py:39
  16.0 22.3 %collective-permute-start.13 = (bf16[72,2048]{1,0:T(8,128)(2,1)}, bf16[72,2048]{1,0:T(8,128)(2,1)}, u32[]{:S(2)}, u32[]{:S(2)}) collective-permute-start(bf16[72,2048]{1,0:T(8,128)(2,1)} %get-tuple-element.57), channel_id=1, source_target_pairs={{0,2},{1,3},{2,0},{3,1},{4,6},{5,7},{6,4},{7,5},{8,10},{9,11},{10,... | collective-permute-start | bytes 884744 | tf_op jit(solution)/shard_map/ppermute | solution.py:39
  18.3 20.0 %collective-permute-start.12 = (bf16[72,2048]{1,0:T(8,128)(2,1)}, bf16[72,2048]{1,0:T(8,128)(2,1)}, u32[]{:S(2)}, u32[]{:S(2)}) collective-permute-start(bf16[72,2048]{1,0:T(8,128)(2,1)} %get-tuple-element.58), channel_id=1, source_target_pairs={{0,4},{1,5},{2,6},{3,7},{4,0},{5,1},{6,2},{7,3},{8,12},{9,13},{10,... | collective-permute-start | bytes 884744 | tf_op jit(solution)/shard_map/ppermute | solution.py:39
  26.6 15.7 %collective-permute-start.4 = (bf16[256,768]{0,1:T(8,128)(2,1)}, bf16[256,768]{0,1:T(8,128)(2,1)S(1)}, u32[]{:S(2)}, u32[]{:S(2)}) collective-permute-start(bf16[256,768]{0,1:T(8,128)(2,1)} %pad_maximum_fusion.7), channel_id=1, source_target_pairs={{0,0},{1,4},{2,2},{3,6},{4,1},{5,5},{6,3},{7,7},{8,8},{9,12},{10,1... | collective-permute-start | bytes 1179656 | tf_op jit(solution)/shard_map/ppermute | solution.py:39
  30.4 15.6 %collective-permute-start.5 = (bf16[256,768]{0,1:T(8,128)(2,1)}, bf16[256,768]{0,1:T(8,128)(2,1)S(1)}, u32[]{:S(2)}, u32[]{:S(2)}) collective-permute-start(bf16[256,768]{0,1:T(8,128)(2,1)} %pad_maximum_fusion.8), channel_id=1, source_target_pairs={{0,1},{1,5},{2,3},{3,7},{4,0},{5,4},{6,2},{7,6},{8,9},{9,13},{10,1... | collective-permute-start | bytes 1179656 | tf_op jit(solution)/shard_map/ppermute | solution.py:39
  31.7 71.5 %collective-permute-start.3 = (bf16[288,2048]{1,0:T(8,128)(2,1)S(1)}, bf16[288,2048]{1,0:T(8,128)(2,1)S(1)}, u32[]{:S(2)}, u32[]{:S(2)}) collective-permute-start(bf16[288,2048]{1,0:T(8,128)(2,1)S(1)} %pad_maximum_fusion.1), channel_id=1, source_target_pairs={{0,1},{1,0},{2,3},{3,2},{4,5},{5,4},{6,7},{7,6},{8,9},{9,8},{10,11... | collective-permute-start | bytes 3538952 | tf_op jit(solution)/shard_map/ppermute | solution.py:39
  39.5 66.2 %collective-permute-start.15 = (bf16[288,2048]{1,0:T(8,128)(2,1)S(1)}, bf16[288,2048]{1,0:T(8,128)(2,1)S(1)}, u32[]{:S(2)}, u32[]{:S(2)}) collective-permute-start(bf16[288,2048]{1,0:T(8,128)(2,1)S(1)} %pad_maximum_fusion.2), channel_id=1, source_target_pairs={{0,1},{1,0},{2,3},{3,2},{4,5},{5,4},{6,7},{7,6},{8,9},{9,8},{10,11... | collective-permute-start | bytes 3538952 | tf_op jit(solution)/shard_map/ppermute | solution.py:39
  46.3 19.8 %collective-permute-start.7 = (bf16[512,768]{0,1:T(8,128)(2,1)S(1)}, bf16[512,768]{0,1:T(8,128)(2,1)S(1)}, u32[]{:S(2)}, u32[]{:S(2)}) collective-permute-start(bf16[512,768]{0,1:T(8,128)(2,1)S(1)} %pad_maximum_fusion.6), channel_id=1, source_target_pairs={{0,8},{1,9},{2,10},{3,11},{4,12},{5,13},{6,14},{7,15},{8,16},{9,17... | collective-permute-start | bytes 2359304 | tf_op jit(solution)/shard_map/ppermute | solution.py:39
  52.6 24.9 %collective-permute-start.6 = (bf16[512,768]{0,1:T(8,128)(2,1)S(1)}, bf16[512,768]{0,1:T(8,128)(2,1)S(1)}, u32[]{:S(2)}, u32[]{:S(2)}) collective-permute-start(bf16[512,768]{0,1:T(8,128)(2,1)S(1)} %pad_maximum_fusion.6), channel_id=1, source_target_pairs={{8,0},{9,1},{10,2},{11,3},{12,4},{13,5},{14,6},{15,7},{16,8},{17,9... | collective-permute-start | bytes 2359304 | tf_op jit(solution)/shard_map/ppermute | solution.py:39
  66.1 17.8 %collective-permute-start.8 = (bf16[512,768]{0,1:T(8,128)(2,1)S(1)}, bf16[512,768]{0,1:T(8,128)(2,1)S(1)}, u32[]{:S(2)}, u32[]{:S(2)}) collective-permute-start(bf16[512,768]{0,1:T(8,128)(2,1)S(1)} %collective-permute-done.7), channel_id=1, source_target_pairs={{8,16},{9,17},{10,18},{11,19},{12,20},{13,21},{14,22},{15,23},{16,... | collective-permute-start | bytes 2359304 | tf_op jit(solution)/shard_map/ppermute | solution.py:39
  77.4 20.5 %collective-permute-start.10 = (bf16[512,768]{0,1:T(8,128)(2,1)S(1)}, bf16[512,768]{0,1:T(8,128)(2,1)S(1)}, u32[]{:S(2)}, u32[]{:S(2)}) collective-permute-start(bf16[512,768]{0,1:T(8,128)(2,1)S(1)} %collective-permute-done.6), channel_id=1, source_target_pairs={{8,0},{9,1},{10,2},{11,3},{12,4},{13,5},{14,6},{15,7},{16,8},{17,9... | collective-permute-start | bytes 2359304 | tf_op jit(solution)/shard_map/ppermute | solution.py:39
  83.9 32.0 %collective-permute-start.9 = (bf16[512,768]{0,1:T(8,128)(2,1)S(1)}, bf16[512,768]{0,1:T(8,128)(2,1)S(1)}, u32[]{:S(2)}, u32[]{:S(2)}) collective-permute-start(bf16[512,768]{0,1:T(8,128)(2,1)S(1)} %collective-permute-done.8), channel_id=1, source_target_pairs={{16,24},{17,25},{18,26},{19,27},{20,28},{21,29},{22,30},{23,31}} | collective-permute-start | bytes 2359304 | tf_op jit(solution)/shard_map/ppermute | solution.py:39
  103.3 21.0 %collective-permute-start.11 = (bf16[512,768]{0,1:T(8,128)(2,1)S(1)}, bf16[512,768]{0,1:T(8,128)(2,1)S(1)}, u32[]{:S(2)}, u32[]{:S(2)}) collective-permute-start(bf16[512,768]{0,1:T(8,128)(2,1)S(1)} %collective-permute-done.10), channel_id=1, source_target_pairs={{8,0},{9,1},{10,2},{11,3},{12,4},{13,5},{14,6},{15,7}} | collective-permute-start | bytes 2359304 | tf_op jit(solution)/shard_map/ppermute | solution.py:39
  109.0 23.7 %collective-permute-start.24 = (bf16[96,2048]{1,0:T(8,128)(2,1)S(1)}, bf16[96,2048]{1,0:T(8,128)(2,1)}, u32[]{:S(2)}, u32[]{:S(2)}) collective-permute-start(bf16[96,2048]{1,0:T(8,128)(2,1)S(1)} %collective-permute-done.23), channel_id=1, source_target_pairs={{8,0},{9,1},{10,2},{11,3},{12,4},{13,5},{14,6},{15,7},{16,8},{17,9... | collective-permute-start | bytes 1179656 | tf_op jit(solution)/shard_map/ppermute | solution.py:39
  111.6 26.5 %collective-permute-start.21 = (bf16[96,2048]{1,0:T(8,128)(2,1)S(1)}, bf16[96,2048]{1,0:T(8,128)(2,1)}, u32[]{:S(2)}, u32[]{:S(2)}) collective-permute-start(bf16[96,2048]{1,0:T(8,128)(2,1)S(1)} %collective-permute-done.20), channel_id=1, source_target_pairs={{8,16},{9,17},{10,18},{11,19},{12,20},{13,21},{14,22},{15,23},{16,... | collective-permute-start | bytes 1179656 | tf_op jit(solution)/shard_map/ppermute | solution.py:39
  154.0 33.9 %collective-permute-start.32 = (bf16[288,2048]{1,0:T(8,128)(2,1)S(1)}, bf16[288,2048]{1,0:T(8,128)(2,1)S(1)}, u32[]{:S(2)}, u32[]{:S(2)}) collective-permute-start(bf16[288,2048]{1,0:T(8,128)(2,1)S(1)} %slice.238), channel_id=1, source_target_pairs={{0,1},{1,0},{2,3},{3,2},{4,5},{5,4},{6,7},{7,6},{8,9},{9,8},{10,11... | collective-permute-start | bytes 3538952 | tf_op jit(solution)/shard_map/ppermute | solution.py:39
  161.4 13.5 %collective-permute-start.31 = (bf16[512,768]{0,1:T(8,128)(2,1)S(1)}, bf16[512,768]{0,1:T(8,128)(2,1)S(1)}, u32[]{:S(2)}, u32[]{:S(2)}) collective-permute-start(bf16[512,768]{0,1:T(8,128)(2,1)S(1)} %get-tuple-element.34), channel_id=1, source_target_pairs={{24,16},{25,17},{26,18},{27,19},{28,20},{29,21},{30,22},{31,23}} | collective-permute-start | bytes 2359304 | tf_op jit(solution)/shard_map/ppermute | solution.py:39
  162.1 15.4 %collective-permute-start.30 = (bf16[512,768]{0,1:T(8,128)(2,1)S(1)}, bf16[512,768]{0,1:T(8,128)(2,1)S(1)}, u32[]{:S(2)}, u32[]{:S(2)}) collective-permute-start(bf16[512,768]{0,1:T(8,128)(2,1)S(1)} %get-tuple-element.35), channel_id=1, source_target_pairs={{0,8},{1,9},{2,10},{3,11},{4,12},{5,13},{6,14},{7,15}} | collective-permute-start | bytes 2359304 | tf_op jit(solution)/shard_map/ppermute | solution.py:39
  165.0 43.4 %collective-permute-start.26 = (bf16[288,2048]{1,0:T(8,128)(2,1)S(1)}, bf16[288,2048]{1,0:T(8,128)(2,1)S(1)}, u32[]{:S(2)}, u32[]{:S(2)}) collective-permute-start(bf16[288,2048]{1,0:T(8,128)(2,1)S(1)} %slice.239), channel_id=1, source_target_pairs={{0,1},{1,0},{2,3},{3,2},{4,5},{5,4},{6,7},{7,6},{8,9},{9,8},{10,11... | collective-permute-start | bytes 3538952 | tf_op jit(solution)/shard_map/ppermute | solution.py:39
  170.6 19.1 %collective-permute-start.43 = (bf16[96,2048]{1,0:T(8,128)(2,1)S(1)}, bf16[96,2048]{1,0:T(8,128)(2,1)S(1)}, u32[]{:S(2)}, u32[]{:S(2)}) collective-permute-start(bf16[96,2048]{1,0:T(8,128)(2,1)S(1)} %get-tuple-element.38), channel_id=1, source_target_pairs={{0,8},{1,9},{2,10},{3,11},{4,12},{5,13},{6,14},{7,15},{8,16},{9,17... | collective-permute-start | bytes 1179656 | tf_op jit(solution)/shard_map/ppermute | solution.py:39
  175.0 20.6 %collective-permute-start.45 = (bf16[96,2048]{1,0:T(8,128)(2,1)S(1)}, bf16[96,2048]{1,0:T(8,128)(2,1)S(1)}, u32[]{:S(2)}, u32[]{:S(2)}) collective-permute-start(bf16[96,2048]{1,0:T(8,128)(2,1)S(1)} %add_convert_fusion.4), channel_id=1, source_target_pairs={{8,0},{9,1},{10,2},{11,3},{12,4},{13,5},{14,6},{15,7},{16,8},{17,9... | collective-permute-start | bytes 1179656 | tf_op jit(solution)/shard_map/ppermute | solution.py:39
  178.0 57.3 %collective-permute-start.36 = (bf16[512,768]{0,1:T(8,128)(2,1)S(1)}, bf16[512,768]{0,1:T(8,128)(2,1)S(1)}, u32[]{:S(2)}, u32[]{:S(2)}) collective-permute-start(bf16[512,768]{0,1:T(8,128)(2,1)S(1)} %get-tuple-element.32), channel_id=1, source_target_pairs={{0,8},{1,9},{2,10},{3,11},{4,12},{5,13},{6,14},{7,15},{8,16},{9,17... | collective-permute-start | bytes 2359304 | tf_op jit(solution)/shard_map/ppermute | solution.py:39
  187.9 47.5 %collective-permute-start.38 = (bf16[512,768]{0,1:T(8,128)(2,1)S(1)}, bf16[512,768]{0,1:T(8,128)(2,1)S(1)}, u32[]{:S(2)}, u32[]{:S(2)}) collective-permute-start(bf16[512,768]{0,1:T(8,128)(2,1)S(1)} %get-tuple-element.33), channel_id=1, source_target_pairs={{16,8},{17,9},{18,10},{19,11},{20,12},{21,13},{22,14},{23,15},{24,... | collective-permute-start | bytes 2359304 | tf_op jit(solution)/shard_map/ppermute | solution.py:39
  189.7 24.6 %collective-permute-start.35 = (bf16[72,2048]{1,0:T(8,128)(2,1)S(1)}, bf16[72,2048]{1,0:T(8,128)(2,1)S(1)}, u32[]{:S(2)}, u32[]{:S(2)}) collective-permute-start(bf16[72,2048]{1,0:T(8,128)(2,1)S(1)} %get-tuple-element.43), channel_id=1, source_target_pairs={{0,6},{1,7},{2,4},{3,5},{4,2},{5,3},{6,0},{7,1},{8,14},{9,15},{10,... | collective-permute-start | bytes 884744 | tf_op jit(solution)/shard_map/ppermute | solution.py:39
  195.7 17.2 %collective-permute-start.46 = (bf16[48,2048]{1,0:T(8,128)(2,1)S(1)}, bf16[48,2048]{1,0:T(8,128)(2,1)S(1)}, u32[]{:S(2)}, u32[]{:S(2)}) collective-permute-start(bf16[48,2048]{1,0:T(8,128)(2,1)S(1)} %get-tuple-element.66), channel_id=1, source_target_pairs={{0,0},{1,4},{2,2},{3,6},{4,1},{5,5},{6,3},{7,7},{8,8},{9,12},{10,1... | collective-permute-start | bytes 589832 | tf_op jit(solution)/shard_map/ppermute | solution.py:39
  214.3 14.0 %collective-permute-start.29 = (bf16[72,2048]{1,0:T(8,128)(2,1)S(1)}, bf16[72,2048]{1,0:T(8,128)(2,1)S(1)}, u32[]{:S(2)}, u32[]{:S(2)}) collective-permute-start(bf16[72,2048]{1,0:T(8,128)(2,1)S(1)} %get-tuple-element.47), channel_id=1, source_target_pairs={{0,6},{1,7},{2,4},{3,5},{4,2},{5,3},{6,0},{7,1},{8,14},{9,15},{10,... | collective-permute-start | bytes 884744 | tf_op jit(solution)/shard_map/ppermute | solution.py:39
  218.8 14.1 %collective-permute-start.28 = (bf16[72,2048]{1,0:T(8,128)(2,1)S(1)}, bf16[72,2048]{1,0:T(8,128)(2,1)S(1)}, u32[]{:S(2)}, u32[]{:S(2)}) collective-permute-start(bf16[72,2048]{1,0:T(8,128)(2,1)S(1)} %get-tuple-element.48), channel_id=1, source_target_pairs={{0,2},{1,3},{2,0},{3,1},{4,6},{5,7},{6,4},{7,5},{8,10},{9,11},{10,... | collective-permute-start | bytes 884744 | tf_op jit(solution)/shard_map/ppermute | solution.py:39
  222.9 12.3 %collective-permute-start.27 = (bf16[72,2048]{1,0:T(8,128)(2,1)S(1)}, bf16[72,2048]{1,0:T(8,128)(2,1)S(1)}, u32[]{:S(2)}, u32[]{:S(2)}) collective-permute-start(bf16[72,2048]{1,0:T(8,128)(2,1)S(1)} %get-tuple-element.49), channel_id=1, source_target_pairs={{0,4},{1,5},{2,6},{3,7},{4,0},{5,1},{6,2},{7,3},{8,12},{9,13},{10,... | collective-permute-start | bytes 884744 | tf_op jit(solution)/shard_map/ppermute | solution.py:39
  236.1 19.9 %collective-permute-start.37 = (bf16[512,768]{0,1:T(8,128)(2,1)S(1)}, bf16[512,768]{0,1:T(8,128)(2,1)S(1)}, u32[]{:S(2)}, u32[]{:S(2)}) collective-permute-start(bf16[512,768]{0,1:T(8,128)(2,1)S(1)} %get-tuple-element.30), channel_id=1, source_target_pairs={{0,8},{1,9},{2,10},{3,11},{4,12},{5,13},{6,14},{7,15},{8,16},{9,17... | collective-permute-start | bytes 2359304 | tf_op jit(solution)/shard_map/ppermute | solution.py:39
  240.1 19.6 %collective-permute-start.39 = (bf16[512,768]{0,1:T(8,128)(2,1)S(1)}, bf16[512,768]{0,1:T(8,128)(2,1)S(1)}, u32[]{:S(2)}, u32[]{:S(2)}) collective-permute-start(bf16[512,768]{0,1:T(8,128)(2,1)S(1)} %get-tuple-element.31), channel_id=1, source_target_pairs={{8,0},{9,1},{10,2},{11,3},{12,4},{13,5},{14,6},{15,7},{16,8},{17,9... | collective-permute-start | bytes 2359304 | tf_op jit(solution)/shard_map/ppermute | solution.py:39
  (33 other events, 279.7 us)

commit v4 on v1

--- a/solution.py
+++ b/solution.py
@@ -10,6 +10,14 @@
 
 def dot(a, b, dims=((1,), (0,))):
     return lax.dot_general(a, b, (dims, ((), ())), preferred_element_type=F32)
+
+
+def tie(value, *others):
+    return lax.optimization_barrier((value,) + others)[0]
+
+
+def added(*terms):
+    return sum(t.astype(F32) for t in terms).astype(BF)
 
 
 class Grid:
@@ -18,7 +26,6 @@
         self.zs, self.qs = self.dps // 2, self.experts // 2
         dp, ex = lax.axis_index("dp"), lax.axis_index("expert")
         self.z, self.x, self.q, self.c = dp // 2, dp % 2, ex // 2, ex % 2
-        self.z_groups = [[z * 2 + x for z in range(self.zs)] for x in range(2)]
 
     def send(self, value, move):
         pairs = []
@@ -27,12 +34,73 @@
                 for q in range(self.qs):
                     for c in range(2):
                         to = move(z, x, q, c)
-                        if 0 <= to[0] < self.zs:
+                        if to is not None:
                             pairs.append((self.flat(z, x, q, c), self.flat(*to)))
         return lax.ppermute(value, BOTH, pairs)
 
     def flat(self, z, x, q, c):
         return (z * 2 + x) * self.experts + q * 2 + c
+
+    def hop(self, value, where):
+        return self.send(value, lambda z, x, q, c: (where[z], x, q, c) if z in where else None)
+
+    def gather(self, shard, *ahead):
+        n, z = self.zs, self.z
+        if n == 4:
+            up = self.hop(shard, {0: 1, 1: 2, 2: 3})
+            down = self.hop(shard, {1: 0, 2: 1, 3: 2})
+            if ahead:
+                up, down = tie(up, *ahead), tie(down, *ahead)
+            passed = jnp.where(z == 1, up, down)
+            far = self.hop(passed, {1: 3, 2: 0})
+            up_2 = self.hop(up, {1: 2, 2: 3})
+            down_2 = self.hop(down, {1: 0, 2: 1})
+            blocks = [
+                shard,
+                jnp.where(z == 3, far, down),
+                jnp.where(z < 2, down_2, up_2),
+                jnp.where(z == 0, far, up),
+            ]
+            return blocks, (up, down, passed)
+        ups, downs = [shard], [shard]
+        for s in range(1, n):
+            ups.append(self.hop(ups[-1], {i: i + 1 for i in range(s - 1, n - 1)}))
+            downs.append(self.hop(downs[-1], {i: i - 1 for i in range(1, n - s + 1)}))
+        blocks = [shard] + [jnp.where(z + s < n, downs[s], ups[n - s]) for s in range(1, n)]
+        return blocks, (ups[1], downs[1])
+
+    def straight(self, blocks):
+        n = self.zs
+        rows = []
+        for j in range(n):
+            row = blocks[j]
+            for z in range(1, n):
+                row = jnp.where(self.z == z, blocks[(j - z) % n], row)
+            rows.append(row)
+        return rows
+
+    def scatter(self, block, *ahead):
+        n, z = self.zs, self.z
+        if n == 4:
+            far = self.hop(jnp.where(z == 0, block(3), block(1)), {0: 2, 3: 1})
+            middle = block(2)
+            up = self.hop(middle, {0: 1, 1: 2})
+            down = self.hop(middle, {3: 2, 2: 1})
+            near = self.hop(jnp.where(z == 0, block(1), block(3)), {0: 1, 3: 2})
+            is_low = z == 1
+            to_end = added(jnp.where(is_low, block(3), block(1)), jnp.where(is_low, down, up), far)
+            to_mid = added(jnp.where(is_low, block(1), block(3)), jnp.where(is_low, up, down))
+            to_end, to_mid = tie(to_end, *ahead), tie(to_mid, *ahead)
+            end = self.hop(to_end, {1: 0, 2: 3})
+            mid = self.hop(to_mid, {1: 2, 2: 1})
+            return added(block(0), near, mid, end), (to_end, to_mid)
+        up = self.hop(block(n - 1), {0: 1})
+        down = self.hop(block(1), {n - 1: n - 2})
+        early = up, down
+        for r in range(2, n):
+            up = self.hop(added(block(n - r), up), {i: i + 1 for i in range(r)})
+            down = self.hop(added(block(r), down), {i: i - 1 for i in range(n - r, n)})
+        return added(block(0), up, down), early
 
 
 def local(tokens, expert_ids, gate_probs, w_gate, w_up, w_down, d_out):
@@ -45,6 +113,7 @@
     cap = rows * topk * 9 // (8 * experts)
     slots = experts * cap
     first = g.c == 0
+    even = g.x == 0
 
     block = hidden_width // g.dps
     part = block // 2
@@ -80,12 +149,6 @@
         jnp.concatenate([gate_cols[:, :half], up_cols[:, :half]], axis=1),
         jnp.concatenate([gate_cols[:, half:], up_cols[:, half:]], axis=1),
     )
-    down_low, down_high = w_down[0, :part], w_down[0, part:]
-    even = g.x == 0
-    down_shard = spread(jnp.where(even, down_low, down_high), jnp.where(even, down_high, down_low))
-    gate_up = lax.all_gather(gate_up_shard, "dp", axis=0, tiled=True, axis_index_groups=g.z_groups)
-    down = lax.all_gather(down_shard, "dp", axis=0, tiled=True, axis_index_groups=g.z_groups)
-
     expert_iota = jnp.arange(experts, dtype=jnp.int32)
     chosen = expert_ids[:, :, None] == expert_iota
     named = jnp.any(chosen, axis=1).astype(BF)
@@ -110,46 +173,68 @@
     def other_core(z, x, q, c):
         return z, x, q, 1 - c
 
-    def dispatch(sent):
-        got = [sent[:cap]] + [g.send(sent[r * cap:(r + 1) * cap], member(r, 1)) for r in range(1, experts)]
-        mine = jnp.concatenate(got, axis=0)
-        return jnp.concatenate([mine, g.send(mine, other_core)], axis=0)
-
-    def give_back(partial):
-        other = g.send(partial[slots:].astype(BF), other_core)
-        mine = (partial[:slots] + other.astype(F32)).astype(BF)
-        got = [mine[:cap]] + [g.send(mine[r * cap:(r + 1) * cap], member(r, -1)) for r in range(1, experts)]
+    def exchange(value, sign):
+        got = [value[:cap]] + [g.send(value[r * cap:(r + 1) * cap], member(r, sign)) for r in range(1, experts)]
         return jnp.concatenate(got, axis=0)
 
-    arrived = dispatch(dot(placing, tokens, ((0,), (0,))).astype(BF))
-    d_produced = dispatch((slot_probs[:, None] * dot(placing, d_out, ((0,), (0,)))).astype(BF))
+    line_width = width // g.zs
+    turned = lax.dynamic_slice(jnp.concatenate([tokens, tokens], axis=1), (0, g.z * line_width), (rows, width))
+    sent = jnp.concatenate(
+        [
+            dot(placing, turned, ((0,), (0,))).astype(BF),
+            (slot_probs[:, None] * dot(placing, d_out, ((0,), (0,)))).astype(BF),
+        ],
+        axis=1,
+    )
+    gate_up_blocks, gate_up_passed = g.gather(gate_up_shard)
+    gate_up = jnp.concatenate(gate_up_blocks, axis=0)
+    mine = tie(exchange(tie(sent, gate_up_shard), 1), *gate_up_passed)
+    inputs = jnp.concatenate([mine, g.send(mine, other_core)], axis=0)
+    arrived, d_produced = inputs[:, :width], inputs[:, width:]
+
+    w_down_late = tie(w_down[0], *gate_up_passed)
+    down_low, down_high = w_down_late[:part], w_down_late[part:]
+    down_shard = spread(jnp.where(even, down_low, down_high), jnp.where(even, down_high, down_low))
 
     pre = dot(arrived, gate_up)
     gate_pre, up_pre = pre[:, :half], pre[:, half:]
     sig = jax.nn.sigmoid(gate_pre)
     act = gate_pre * sig
     hidden = (act * up_pre).astype(BF)
-
-    def scatter(partial):
-        return lax.psum_scatter(
-            partial.astype(BF), "dp", scatter_dimension=0, tiled=True, axis_index_groups=g.z_groups
-        ).astype(BF)
-
-    down_grad = scatter(dot(hidden, d_produced, ((0,), (0,))))
-    returned = give_back(dot(hidden, down))
-
-    d_hidden = dot(d_produced, down, ((1,), (1,)))
+    down_part = dot(hidden, d_produced, ((0,), (0,))).astype(BF)
+    down_rows = 2 * part
+    down_blocks, _ = g.gather(down_shard, down_part)
+    down = jnp.concatenate(g.straight(down_blocks), axis=0)
+
+    d_hidden = dot(tie(d_produced, down_part), down, ((1,), (1,)))
     d_gate = (d_hidden * up_pre * sig * (1.0 + gate_pre * (1.0 - sig))).astype(BF)
     d_up = (d_hidden * act).astype(BF)
     d_both = jnp.concatenate([d_gate, d_up], axis=1)
-    gate_up_grad = scatter(dot(arrived, d_both, ((0,), (0,))))
-    back_rows = give_back(dot(d_both, gate_up, ((1,), (1,))))
+    both_part = dot(arrived, d_both, ((0,), (0,))).astype(BF)
+
+    produced = dot(tie(hidden, both_part), down)
+    d_arrived = dot(tie(d_both, both_part), gate_up, ((1,), (1,)))
+    theirs = jnp.concatenate([produced[slots:].astype(BF), d_arrived[slots:].astype(BF)], axis=1)
+    other = g.send(theirs, other_core).astype(F32)
+    sums = jnp.concatenate(
+        [(produced[:slots] + other[:, :width]).astype(BF), (d_arrived[:slots] + other[:, width:]).astype(BF)], axis=1
+    )
+    down_grad, _ = g.scatter(
+        lambda k: lax.dynamic_slice_in_dim(down_part, ((g.z + k) % g.zs) * down_rows, down_rows), sums
+    )
+    gate_up_grad, second = g.scatter(lambda k: both_part[k * line_width:(k + 1) * line_width], sums)
+    got = tie(exchange(sums, -1), *second)
+    returned, back_rows = got[:, :width], got[:, width:]
+    gate_up_grad, down_grad = tie(gate_up_grad, got), tie(down_grad, *second)
 
     high = lax.reduce_precision(weighted, 8, 7)
     mixed = (dot(high.astype(BF), returned) + dot((weighted - high).astype(BF), returned)).astype(BF)
     products = dot(d_out, returned, ((1,), (1,)))
     d_probs = jnp.sum(jnp.where(pair, products[:, None, :], 0.0), axis=2)
-    d_tokens = dot(placing, back_rows).astype(BF)
+    d_turned = dot(placing, back_rows).astype(BF)
+    d_tokens = lax.dynamic_slice(
+        jnp.concatenate([d_turned, d_turned], axis=1), (0, (g.zs - g.z) * line_width), (rows, width)
+    )
 
     down_a, down_b = unspread(down_grad)
     d_w_down = jnp.where(

time: 292 us -> 263 us (0.901)
  waiting for transfers between devices: 194 us -> 127 us
  starting transfers between devices: 30 us -> 76 us
  other arithmetic: 7.63 us -> 27.3 us
  between operations: 14.3 us -> 1.68 us
  matrix products: 35.1 us -> 22.7 us
    reduce_scatter x2 -> x0, waiting for transfers between devices: 67.8 us -> none  [scatter(): lax.psum_scatter(partial.astype(BF), 'dp', scatter_dimension=0, tiled=Tru...]
    ppermute x24 -> x38, waiting for transfers between devices: 59.4 us -> 127 us  [send(): return lax.ppermute(value, BOTH, pairs)]
    all_gather x2 -> x0, waiting for transfers between devices: 67 us -> none  [the longest x1 34 us: local(): lax.all_gather(gate_up_shard, 'dp', axis=0, tiled=True, axis_index_groups...]
    ppermute x24 -> x38, starting transfers between devices: 29.7 us -> 76 us  [send(): return lax.ppermute(value, BOTH, pairs)]
    dot_general x17, matrix products: 35.1 us -> 22.7 us  [dot(): return lax.dot_general(a, b, (dims, ((), ())), preferred_element_type=F32)]
    convert_element_type x2 -> x6, other arithmetic: 0.69 us -> 9.75 us  [the longest x4 6.39 us: added(): return sum((t.astype(F32) for t in terms)).astype(BF)]
    select_n x0 -> x6, other arithmetic: none -> 6.63 us  [the longest x2 3.83 us: scatter(): near = self.hop(jnp.where(z == 0, block(1), block(3)), {0: 1, 3: 2})]
    concatenate x2 -> x8, other arithmetic: 0.19 us -> 5.39 us  [the longest x2 1.85 us: exchange(): return jnp.concatenate(got, axis=0)]
  transfers between devices with their start and end apart: 28 -> 38, of which waited for: 20 -> 20; matrix products, arithmetic and copies ran while one was open for 11% -> 11% of each run, Pallas kernels for 0% -> 0%
where the time goes in v4:
time: 263 us; the launch traced here: 262 us
  waiting for transfers between devices  127 us (48%)
  starting transfers between devices  76 us (29%)
  other arithmetic  27.3 us (10%)
  matrix products  22.7 us (9%)
  local copies, waits for them, and re-layouts  7.54 us (3%)
    ppermute x38, waiting for transfers between devices, send(): return lax.ppermute(value, BOTH, pairs)  127 us
    ppermute x38, starting transfers between devices, send(): return lax.ppermute(value, BOTH, pairs)  76 us
    dot_general x17, matrix products, dot(): return lax.dot_general(a, b, (dims, ((), ())), preferred_element_type=F32)  22.7 us
    convert_element_type x4, other arithmetic, added(): return sum((t.astype(F32) for t in terms)).astype(BF)  6.39 us
  transfers between devices with their start and end apart: 38, of which 20 were waited for; matrix products, arithmetic and copies ran while one was open for 11% of the time, Pallas kernels for 0%

profile of v4, /device:TPU:9, one launch (start us, length us, event | category | flops | bytes accessed | tf_op | source)
XLA Modules:
  0.0 261.8 jit_solution(18186120210537703261)
XLA Ops:
  3.9 3.8 %collective-permute-start = (bf16[256,768]{0,1:T(8,128)(2,1)S(1)}, bf16[256,768]{0,1:T(8,128)(2,1)S(1)}, u32[]{:S(2)}, u32[]{:S(2)}) collective-permute-start(bf16[256,768]{0,1:T(8,128)(2,1)S(1)} %pad_maximum_fusion.8), channel_id=1, source_target_pairs={{0,0},{1,4},{2,2},{3,6},{4,1},{5,5},{6,3},{7,7},{8,8},{9,12},{10,1... | collective-permute-start | bytes 1179656 | tf_op jit(solution)/shard_map/ppermute | solution.py:39
  9.6 3.6 %collective-permute-done = bf16[256,768]{0,1:T(8,128)(2,1)S(1)} collective-permute-done((bf16[256,768]{0,1:T(8,128)(2,1)S(1)}, bf16[256,768]{0,1:T(8,128)(2,1)S(1)}, u32[]{:S(2)}, u32[]{:S(2)}) %collective-permute-start) | collective-permute-done | bytes 393248 | tf_op jit(solution)/shard_map/ppermute | solution.py:39
  13.2 3.5 %collective-permute-done.1 = bf16[256,768]{0,1:T(8,128)(2,1)S(1)} collective-permute-done((bf16[256,768]{0,1:T(8,128)(2,1)S(1)}, bf16[256,768]{0,1:T(8,128)(2,1)S(1)}, u32[]{:S(2)}, u32[]{:S(2)}) %collective-permute-start.1) | collective-permute-done | bytes 393248 | tf_op jit(solution)/shard_map/ppermute | solution.py:39
  20.6 2.9 %collective-permute-start.4 = (bf16[72,4096]{1,0:T(8,128)(2,1)}, bf16[72,4096]{1,0:T(8,128)(2,1)}, u32[]{:S(2)}, u32[]{:S(2)}) collective-permute-start(bf16[72,4096]{1,0:T(8,128)(2,1)} %get-tuple-element.62), channel_id=1, source_target_pairs={{0,6},{1,7},{2,4},{3,5},{4,2},{5,3},{6,0},{7,1},{8,14},{9,15},{10,... | collective-permute-start | bytes 1769480 | tf_op jit(solution)/shard_map/ppermute | solution.py:39
  23.7 3.2 %collective-permute-start.5 = (bf16[512,768]{0,1:T(8,128)(2,1)}, bf16[512,768]{0,1:T(8,128)(2,1)S(1)}, u32[]{:S(2)}, u32[]{:S(2)}) collective-permute-start(bf16[512,768]{0,1:T(8,128)(2,1)} %pad_maximum_fusion.7), channel_id=1, source_target_pairs={{0,8},{1,9},{2,10},{3,11},{4,12},{5,13},{6,14},{7,15},{8,16},{9,17... | collective-permute-start | bytes 2359304 | tf_op jit(solution)/shard_map/ppermute | solution.py:39
  29.1 7.8 %collective-permute-done.4 = bf16[72,4096]{1,0:T(8,128)(2,1)} collective-permute-done((bf16[72,4096]{1,0:T(8,128)(2,1)}, bf16[72,4096]{1,0:T(8,128)(2,1)}, u32[]{:S(2)}, u32[]{:S(2)}) %collective-permute-start.4) | collective-permute-done | bytes 589856 | tf_op jit(solution)/shard_map/ppermute | solution.py:39
  36.9 13.3 %collective-permute-done.3 = bf16[72,4096]{1,0:T(8,128)(2,1)} collective-permute-done((bf16[72,4096]{1,0:T(8,128)(2,1)}, bf16[72,4096]{1,0:T(8,128)(2,1)}, u32[]{:S(2)}, u32[]{:S(2)}) %collective-permute-start.3) | collective-permute-done | bytes 589856 | tf_op jit(solution)/shard_map/ppermute | solution.py:39
  52.0 4.3 %collective-permute-start.8 = (bf16[512,768]{0,1:T(8,128)(2,1)S(1)}, bf16[512,768]{0,1:T(8,128)(2,1)S(1)}, u32[]{:S(2)}, u32[]{:S(2)}) collective-permute-start(bf16[512,768]{0,1:T(8,128)(2,1)S(1)} %broadcast_select_fusion.2), channel_id=1, source_target_pairs={{8,24},{9,25},{10,26},{11,27},{12,28},{13,29},{14,30},{15,31},{16,... | collective-permute-start | bytes 2359304 | tf_op jit(solution)/shard_map/ppermute | solution.py:39
  57.1 2.9 %collective-permute-start.11 = (bf16[48,2048]{1,0:T(8,128)(2,1)S(1)}, bf16[48,2048]{1,0:T(8,128)(2,1)S(1)}, u32[]{:S(2)}, u32[]{:S(2)}) collective-permute-start(bf16[48,2048]{1,0:T(8,128)(2,1)S(1)} %get-tuple-element.81), channel_id=1, source_target_pairs={{0,0},{1,4},{2,2},{3,6},{4,1},{5,5},{6,3},{7,7},{8,8},{9,12},{10,1... | collective-permute-start | bytes 589832 | tf_op jit(solution)/shard_map/ppermute | solution.py:39
  67.7 5.1 %collective-permute-done.8 = bf16[512,768]{0,1:T(8,128)(2,1)S(1)} collective-permute-done((bf16[512,768]{0,1:T(8,128)(2,1)S(1)}, bf16[512,768]{0,1:T(8,128)(2,1)S(1)}, u32[]{:S(2)}, u32[]{:S(2)}) %collective-permute-start.8) | collective-permute-done | bytes 786464 | tf_op jit(solution)/shard_map/ppermute | solution.py:39
  72.8 2.9 %collective-permute-start.14 = (bf16[96,2048]{1,0:T(8,128)(2,1)S(1)}, bf16[96,2048]{1,0:T(8,128)(2,1)S(1)}, u32[]{:S(2)}, u32[]{:S(2)}) collective-permute-start(bf16[96,2048]{1,0:T(8,128)(2,1)S(1)} %pad_maximum_fusion.10), channel_id=1, source_target_pairs={{8,0},{9,1},{10,2},{11,3},{12,4},{13,5},{14,6},{15,7},{16,8},{17,9... | collective-permute-start | bytes 1179656 | tf_op jit(solution)/shard_map/ppermute | solution.py:39
  75.9 13.5 %collective-permute-done.9 = bf16[512,768]{0,1:T(8,128)(2,1)S(1)} collective-permute-done((bf16[512,768]{0,1:T(8,128)(2,1)S(1)}, bf16[512,768]{0,1:T(8,128)(2,1)S(1)}, u32[]{:S(2)}, u32[]{:S(2)}) %collective-permute-start.9) | collective-permute-done | bytes 786464 | tf_op jit(solution)/shard_map/ppermute | solution.py:39
  94.7 3.4 %collective-permute-done.13 = bf16[96,2048]{1,0:T(8,128)(2,1)S(1)} collective-permute-done((bf16[96,2048]{1,0:T(8,128)(2,1)S(1)}, bf16[96,2048]{1,0:T(8,128)(2,1)S(1)}, u32[]{:S(2)}, u32[]{:S(2)}) %collective-permute-start.13) | collective-permute-done | bytes 393248 | tf_op jit(solution)/shard_map/ppermute | solution.py:39
  98.9 6.5 %collective-permute-start.15 = (bf16[96,2048]{1,0:T(8,128)(2,1)}, bf16[96,2048]{1,0:T(8,128)(2,1)}, u32[]{:S(2)}, u32[]{:S(2)}) collective-permute-start(bf16[96,2048]{1,0:T(8,128)(2,1)} %broadcast_select_fusion.7), channel_id=1, source_target_pairs={{8,24},{9,25},{10,26},{11,27},{12,28},{13,29},{14,30},{15,31},{16,... | collective-permute-start | bytes 1179656 | tf_op jit(solution)/shard_map/ppermute | solution.py:39
  107.3 4.9 %collective-permute-start.17 = (bf16[96,2048]{1,0:T(8,128)(2,1)S(1)}, bf16[96,2048]{1,0:T(8,128)(2,1)}, u32[]{:S(2)}, u32[]{:S(2)}) collective-permute-start(bf16[96,2048]{1,0:T(8,128)(2,1)S(1)} %collective-permute-done.13), channel_id=1, source_target_pairs={{8,16},{9,17},{10,18},{11,19},{12,20},{13,21},{14,22},{15,23},{16,... | collective-permute-start | bytes 1179656 | tf_op jit(solution)/shard_map/ppermute | solution.py:39
  114.0 7.2 %collective-permute-done.16 = bf16[96,2048]{1,0:T(8,128)(2,1)} collective-permute-done((bf16[96,2048]{1,0:T(8,128)(2,1)S(1)}, bf16[96,2048]{1,0:T(8,128)(2,1)}, u32[]{:S(2)}, u32[]{:S(2)}) %collective-permute-start.16) | collective-permute-done | bytes 393248 | tf_op jit(solution)/shard_map/ppermute | solution.py:39
  126.0 4.1 %convolution_convert_fusion = bf16[2048,768]{0,1:T(8,128)(2,1)} fusion(bf16[576,4096]{1,0:T(8,128)(2,1)S(1)} %bitcast.32, bf16[576,384]{1,0:T(8,128)(2,1)S(1)} %get-tuple-element.54, bf16[576,384]{1,0:T(8,128)(2,1)S(1)} %get-tuple-element.53), kind=kOutput, calls=%fused_computation.9 | convolution fusion | flops 1815281664 | bytes 6389760 | tf_op jit(solution)/shard_map/dot_general | solution.py:12
  140.0 4.2 %collective-permute-start.31 = (bf16[96,2048]{1,0:T(8,128)(2,1)S(1)}, bf16[96,2048]{1,0:T(8,128)(2,1)}, u32[]{:S(2)}, u32[]{:S(2)}) collective-permute-start(bf16[96,2048]{1,0:T(8,128)(2,1)S(1)} %get-tuple-element.66), channel_id=1, source_target_pairs={{0,8},{1,9},{2,10},{3,11},{4,12},{5,13},{6,14},{7,15},{8,16},{9,17... | collective-permute-start | bytes 1179656 | tf_op jit(solution)/shard_map/ppermute | solution.py:39
  146.8 2.9 %broadcast_select_fusion = (bf16[512,768]{0,1:T(8,128)(2,1)S(1)}, bf16[512,768]{0,1:T(8,128)(2,1)}, bf16[512,768]{0,1:T(8,128)(2,1)}) fusion(pred[]{:T(512)S(6)} %eq.108, bf16[2048,768]{0,1:T(8,128)(2,1)} %convolution_convert_fusion), kind=kLoop, calls=%fused_computation.73 | loop fusion | flops 786432 | bytes 4718593 | tf_op jit(solution)/shard_map/jit(_where)/select_n | solution.py:89
  149.8 4.0 %collective-permute-start.23 = (bf16[512,768]{0,1:T(8,128)(2,1)}, bf16[512,768]{0,1:T(8,128)(2,1)}, u32[]{:S(2)}, u32[]{:S(2)}) collective-permute-start(bf16[512,768]{0,1:T(8,128)(2,1)} %get-tuple-element.51), channel_id=1, source_target_pairs={{0,8},{1,9},{2,10},{3,11},{4,12},{5,13},{6,14},{7,15},{8,16},{9,17... | collective-permute-start | bytes 2359304 | tf_op jit(solution)/shard_map/ppermute | solution.py:39
  153.7 7.3 %collective-permute-done.31 = bf16[96,2048]{1,0:T(8,128)(2,1)} collective-permute-done((bf16[96,2048]{1,0:T(8,128)(2,1)S(1)}, bf16[96,2048]{1,0:T(8,128)(2,1)}, u32[]{:S(2)}, u32[]{:S(2)}) %collective-permute-start.31) | collective-permute-done | bytes 393248 | tf_op jit(solution)/shard_map/ppermute | solution.py:39
  162.3 2.8 %collective-permute-done.32 = bf16[96,2048]{1,0:T(8,128)(2,1)} collective-permute-done((bf16[96,2048]{1,0:T(8,128)(2,1)S(1)}, bf16[96,2048]{1,0:T(8,128)(2,1)}, u32[]{:S(2)}, u32[]{:S(2)}) %collective-permute-start.32) | collective-permute-done | bytes 393248 | tf_op jit(solution)/shard_map/ppermute | solution.py:39
  169.6 25.2 %collective-permute-done.23 = bf16[512,768]{0,1:T(8,128)(2,1)} collective-permute-done((bf16[512,768]{0,1:T(8,128)(2,1)}, bf16[512,768]{0,1:T(8,128)(2,1)}, u32[]{:S(2)}, u32[]{:S(2)}) %collective-permute-start.23) | collective-permute-done | bytes 786464 | tf_op jit(solution)/shard_map/ppermute | solution.py:39
  196.2 3.9 %collective-permute-done.24 = bf16[512,768]{0,1:T(8,128)(2,1)} collective-permute-done((bf16[512,768]{0,1:T(8,128)(2,1)}, bf16[512,768]{0,1:T(8,128)(2,1)}, u32[]{:S(2)}, u32[]{:S(2)}) %collective-permute-start.24) | collective-permute-done | bytes 786464 | tf_op jit(solution)/shard_map/ppermute | solution.py:39
  200.1 2.8 %add_convert_fusion.1 = (bf16[512,768]{0,1:T(8,128)(2,1)S(1)}, bf16[512,768]{0,1:T(8,128)(2,1)S(1)}) fusion(bf16[512,768]{0,1:T(8,128)(2,1)} %collective-permute-done.23, bf16[512,768]{0,1:T(8,128)(2,1)} %collective-permute-done.22, pred[]{:T(512)S(6)} %eq.106, bf16[2048,768]{0,1:T(8,128)(2,1)} %convolution_convert_fusion, ...), kind=kLoop, calls=%fused_computation.38 | loop fusion | flops 5505024 | bytes 5505025 | tf_op jit(solution)/shard_map/convert_element_type | solution.py:20
  207.7 3.2 %collective-permute-start.33 = (bf16[96,2048]{1,0:T(8,128)(2,1)S(1)}, bf16[96,2048]{1,0:T(8,128)(2,1)S(1)}, u32[]{:S(2)}, u32[]{:S(2)}) collective-permute-start(bf16[96,2048]{1,0:T(8,128)(2,1)S(1)} %get-tuple-element.33), channel_id=1, source_target_pairs={{8,16},{9,17},{10,18},{11,19},{12,20},{13,21},{14,22},{15,23},{16,... | collective-permute-start | bytes 1179656 | tf_op jit(solution)/shard_map/ppermute | solution.py:39
  213.7 2.8 %collective-permute-done.33 = bf16[96,2048]{1,0:T(8,128)(2,1)S(1)} collective-permute-done((bf16[96,2048]{1,0:T(8,128)(2,1)S(1)}, bf16[96,2048]{1,0:T(8,128)(2,1)S(1)}, u32[]{:S(2)}, u32[]{:S(2)}) %collective-permute-start.33) | collective-permute-done | bytes 393248 | tf_op jit(solution)/shard_map/ppermute | solution.py:39
  218.1 5.5 %collective-permute-done.21 = bf16[72,4096]{1,0:T(8,128)(2,1)S(1)} collective-permute-done((bf16[72,4096]{1,0:T(8,128)(2,1)S(1)}, bf16[72,4096]{1,0:T(8,128)(2,1)S(1)}, u32[]{:S(2)}, u32[]{:S(2)}) %collective-permute-start.21) | collective-permute-done | bytes 589856 | tf_op jit(solution)/shard_map/ppermute | solution.py:39
  225.6 14.3 %collective-permute-done.20 = bf16[72,4096]{1,0:T(8,128)(2,1)S(1)} collective-permute-done((bf16[72,4096]{1,0:T(8,128)(2,1)S(1)}, bf16[72,4096]{1,0:T(8,128)(2,1)S(1)}, u32[]{:S(2)}, u32[]{:S(2)}) %collective-permute-start.20) | collective-permute-done | bytes 589856 | tf_op jit(solution)/shard_map/ppermute | solution.py:39
  240.4 2.8 %collective-permute-start.36 = (bf16[48,2048]{1,0:T(8,128)(2,1)S(1)}, bf16[48,2048]{1,0:T(8,128)(2,1)S(1)}, u32[]{:S(2)}, u32[]{:S(2)}) collective-permute-start(bf16[48,2048]{1,0:T(8,128)(2,1)S(1)} %get-tuple-element.73), channel_id=1, source_target_pairs={{0,0},{1,4},{2,2},{3,6},{4,1},{5,5},{6,3},{7,7},{8,8},{9,12},{10,1... | collective-permute-start | bytes 589832 | tf_op jit(solution)/shard_map/ppermute | solution.py:39
  248.8 2.9 %collective-permute-start.28 = (bf16[256,768]{0,1:T(8,128)(2,1)S(1)}, bf16[256,768]{0,1:T(8,128)(2,1)S(1)}, u32[]{:S(2)}, u32[]{:S(2)}) collective-permute-start(bf16[256,768]{0,1:T(8,128)(2,1)S(1)} %get-tuple-element.71), channel_id=1, source_target_pairs={{0,0},{1,4},{2,2},{3,6},{4,1},{5,5},{6,3},{7,7},{8,8},{9,12},{10,1... | collective-permute-start | bytes 1179656 | tf_op jit(solution)/shard_map/ppermute | solution.py:39
  255.2 3.5 %collective-permute-done.28 = bf16[256,768]{0,1:T(8,128)(2,1)S(1)} collective-permute-done((bf16[256,768]{0,1:T(8,128)(2,1)S(1)}, bf16[256,768]{0,1:T(8,128)(2,1)S(1)}, u32[]{:S(2)}, u32[]{:S(2)}) %collective-permute-start.28) | collective-permute-done | bytes 393248 | tf_op jit(solution)/shard_map/ppermute | solution.py:39
  (156 shorter events, 79.3 us)
Async XLA Ops:
  3.9 9.3 %collective-permute-start = (bf16[256,768]{0,1:T(8,128)(2,1)S(1)}, bf16[256,768]{0,1:T(8,128)(2,1)S(1)}, u32[]{:S(2)}, u32[]{:S(2)}) collective-permute-start(bf16[256,768]{0,1:T(8,128)(2,1)S(1)} %pad_maximum_fusion.8), channel_id=1, source_target_pairs={{0,0},{1,4},{2,2},{3,6},{4,1},{5,5},{6,3},{7,7},{8,8},{9,12},{10,1... | collective-permute-start | bytes 1179656 | tf_op jit(solution)/shard_map/ppermute | solution.py:39
  7.8 8.9 %collective-permute-start.1 = (bf16[256,768]{0,1:T(8,128)(2,1)S(1)}, bf16[256,768]{0,1:T(8,128)(2,1)S(1)}, u32[]{:S(2)}, u32[]{:S(2)}) collective-permute-start(bf16[256,768]{0,1:T(8,128)(2,1)S(1)} %pad_maximum_fusion.9), channel_id=1, source_target_pairs={{0,1},{1,5},{2,3},{3,7},{4,0},{5,4},{6,2},{7,6},{8,9},{9,13},{10,1... | collective-permute-start | bytes 1179656 | tf_op jit(solution)/shard_map/ppermute | solution.py:39
  20.6 16.3 %collective-permute-start.4 = (bf16[72,4096]{1,0:T(8,128)(2,1)}, bf16[72,4096]{1,0:T(8,128)(2,1)}, u32[]{:S(2)}, u32[]{:S(2)}) collective-permute-start(bf16[72,4096]{1,0:T(8,128)(2,1)} %get-tuple-element.62), channel_id=1, source_target_pairs={{0,6},{1,7},{2,4},{3,5},{4,2},{5,3},{6,0},{7,1},{8,14},{9,15},{10,... | collective-permute-start | bytes 1769480 | tf_op jit(solution)/shard_map/ppermute | solution.py:39
  23.4 26.8 %collective-permute-start.3 = (bf16[72,4096]{1,0:T(8,128)(2,1)}, bf16[72,4096]{1,0:T(8,128)(2,1)}, u32[]{:S(2)}, u32[]{:S(2)}) collective-permute-start(bf16[72,4096]{1,0:T(8,128)(2,1)} %get-tuple-element.63), channel_id=1, source_target_pairs={{0,2},{1,3},{2,0},{3,1},{4,6},{5,7},{6,4},{7,5},{8,10},{9,11},{10,... | collective-permute-start | bytes 1769480 | tf_op jit(solution)/shard_map/ppermute | solution.py:39
  23.7 26.6 %collective-permute-start.2 = (bf16[72,4096]{1,0:T(8,128)(2,1)S(1)}, bf16[72,4096]{1,0:T(8,128)(2,1)}, u32[]{:S(2)}, u32[]{:S(2)}) collective-permute-start(bf16[72,4096]{1,0:T(8,128)(2,1)S(1)} %get-tuple-element.64), channel_id=1, source_target_pairs={{0,4},{1,5},{2,6},{3,7},{4,0},{5,1},{6,2},{7,3},{8,12},{9,13},{10,... | collective-permute-start | bytes 1769480 | tf_op jit(solution)/shard_map/ppermute | solution.py:39
  23.7 28.2 %collective-permute-start.5 = (bf16[512,768]{0,1:T(8,128)(2,1)}, bf16[512,768]{0,1:T(8,128)(2,1)S(1)}, u32[]{:S(2)}, u32[]{:S(2)}) collective-permute-start(bf16[512,768]{0,1:T(8,128)(2,1)} %pad_maximum_fusion.7), channel_id=1, source_target_pairs={{0,8},{1,9},{2,10},{3,11},{4,12},{5,13},{6,14},{7,15},{8,16},{9,17... | collective-permute-start | bytes 2359304 | tf_op jit(solution)/shard_map/ppermute | solution.py:39
  26.9 25.0 %collective-permute-start.6 = (bf16[512,768]{0,1:T(8,128)(2,1)}, bf16[512,768]{0,1:T(8,128)(2,1)S(1)}, u32[]{:S(2)}, u32[]{:S(2)}) collective-permute-start(bf16[512,768]{0,1:T(8,128)(2,1)} %pad_maximum_fusion.7), channel_id=1, source_target_pairs={{8,0},{9,1},{10,2},{11,3},{12,4},{13,5},{14,6},{15,7},{16,8},{17,9... | collective-permute-start | bytes 2359304 | tf_op jit(solution)/shard_map/ppermute | solution.py:39
  52.0 20.8 %collective-permute-start.8 = (bf16[512,768]{0,1:T(8,128)(2,1)S(1)}, bf16[512,768]{0,1:T(8,128)(2,1)S(1)}, u32[]{:S(2)}, u32[]{:S(2)}) collective-permute-start(bf16[512,768]{0,1:T(8,128)(2,1)S(1)} %broadcast_select_fusion.2), channel_id=1, source_target_pairs={{8,24},{9,25},{10,26},{11,27},{12,28},{13,29},{14,30},{15,31},{16,... | collective-permute-start | bytes 2359304 | tf_op jit(solution)/shard_map/ppermute | solution.py:39
  56.3 33.8 %collective-permute-start.7 = (bf16[288,4096]{1,0:T(8,128)(2,1)S(1)}, bf16[288,4096]{1,0:T(8,128)(2,1)S(1)}, u32[]{:S(2)}, u32[]{:S(2)}) collective-permute-start(bf16[288,4096]{1,0:T(8,128)(2,1)S(1)} %pad_maximum_fusion.2), channel_id=1, source_target_pairs={{0,1},{1,0},{2,3},{3,2},{4,5},{5,4},{6,7},{7,6},{8,9},{9,8},{10,11... | collective-permute-start | bytes 7077896 | tf_op jit(solution)/shard_map/ppermute | solution.py:39
  60.2 29.3 %collective-permute-start.9 = (bf16[512,768]{0,1:T(8,128)(2,1)S(1)}, bf16[512,768]{0,1:T(8,128)(2,1)S(1)}, u32[]{:S(2)}, u32[]{:S(2)}) collective-permute-start(bf16[512,768]{0,1:T(8,128)(2,1)S(1)} %collective-permute-done.6), channel_id=1, source_target_pairs={{8,0},{9,1},{10,2},{11,3},{12,4},{13,5},{14,6},{15,7},{16,8},{17,9... | collective-permute-start | bytes 2359304 | tf_op jit(solution)/shard_map/ppermute | solution.py:39
  64.1 25.6 %collective-permute-start.10 = (bf16[512,768]{0,1:T(8,128)(2,1)S(1)}, bf16[512,768]{0,1:T(8,128)(2,1)S(1)}, u32[]{:S(2)}, u32[]{:S(2)}) collective-permute-start(bf16[512,768]{0,1:T(8,128)(2,1)S(1)} %collective-permute-done.5), channel_id=1, source_target_pairs={{8,16},{9,17},{10,18},{11,19},{12,20},{13,21},{14,22},{15,23},{16,... | collective-permute-start | bytes 2359304 | tf_op jit(solution)/shard_map/ppermute | solution.py:39
  65.8 32.3 %collective-permute-start.13 = (bf16[96,2048]{1,0:T(8,128)(2,1)S(1)}, bf16[96,2048]{1,0:T(8,128)(2,1)S(1)}, u32[]{:S(2)}, u32[]{:S(2)}) collective-permute-start(bf16[96,2048]{1,0:T(8,128)(2,1)S(1)} %pad_maximum_fusion.10), channel_id=1, source_target_pairs={{0,8},{1,9},{2,10},{3,11},{4,12},{5,13},{6,14},{7,15},{8,16},{9,17... | collective-permute-start | bytes 1179656 | tf_op jit(solution)/shard_map/ppermute | solution.py:39
  72.8 25.3 %collective-permute-start.14 = (bf16[96,2048]{1,0:T(8,128)(2,1)S(1)}, bf16[96,2048]{1,0:T(8,128)(2,1)S(1)}, u32[]{:S(2)}, u32[]{:S(2)}) collective-permute-start(bf16[96,2048]{1,0:T(8,128)(2,1)S(1)} %pad_maximum_fusion.10), channel_id=1, source_target_pairs={{8,0},{9,1},{10,2},{11,3},{12,4},{13,5},{14,6},{15,7},{16,8},{17,9... | collective-permute-start | bytes 1179656 | tf_op jit(solution)/shard_map/ppermute | solution.py:39
  98.9 15.1 %collective-permute-start.15 = (bf16[96,2048]{1,0:T(8,128)(2,1)}, bf16[96,2048]{1,0:T(8,128)(2,1)}, u32[]{:S(2)}, u32[]{:S(2)}) collective-permute-start(bf16[96,2048]{1,0:T(8,128)(2,1)} %broadcast_select_fusion.7), channel_id=1, source_target_pairs={{8,24},{9,25},{10,26},{11,27},{12,28},{13,29},{14,30},{15,31},{16,... | collective-permute-start | bytes 1179656 | tf_op jit(solution)/shard_map/ppermute | solution.py:39
  105.4 15.8 %collective-permute-start.16 = (bf16[96,2048]{1,0:T(8,128)(2,1)S(1)}, bf16[96,2048]{1,0:T(8,128)(2,1)}, u32[]{:S(2)}, u32[]{:S(2)}) collective-permute-start(bf16[96,2048]{1,0:T(8,128)(2,1)S(1)} %collective-permute-done.14), channel_id=1, source_target_pairs={{8,0},{9,1},{10,2},{11,3},{12,4},{13,5},{14,6},{15,7},{16,8},{17,9... | collective-permute-start | bytes 1179656 | tf_op jit(solution)/shard_map/ppermute | solution.py:39
  107.3 14.0 %collective-permute-start.17 = (bf16[96,2048]{1,0:T(8,128)(2,1)S(1)}, bf16[96,2048]{1,0:T(8,128)(2,1)}, u32[]{:S(2)}, u32[]{:S(2)}) collective-permute-start(bf16[96,2048]{1,0:T(8,128)(2,1)S(1)} %collective-permute-done.13), channel_id=1, source_target_pairs={{8,16},{9,17},{10,18},{11,19},{12,20},{13,21},{14,22},{15,23},{16,... | collective-permute-start | bytes 1179656 | tf_op jit(solution)/shard_map/ppermute | solution.py:39
  137.8 65.1 %collective-permute-start.18 = (bf16[288,4096]{1,0:T(8,128)(2,1)}, bf16[288,4096]{1,0:T(8,128)(2,1)}, u32[]{:S(2)}, u32[]{:S(2)}) collective-permute-start(bf16[288,4096]{1,0:T(8,128)(2,1)} %pad_maximum_fusion.3), channel_id=1, source_target_pairs={{0,1},{1,0},{2,3},{3,2},{4,5},{5,4},{6,7},{7,6},{8,9},{9,8},{10,11... | collective-permute-start | bytes 7077896 | tf_op jit(solution)/shard_map/ppermute | solution.py:39
  140.0 21.0 %collective-permute-start.31 = (bf16[96,2048]{1,0:T(8,128)(2,1)S(1)}, bf16[96,2048]{1,0:T(8,128)(2,1)}, u32[]{:S(2)}, u32[]{:S(2)}) collective-permute-start(bf16[96,2048]{1,0:T(8,128)(2,1)S(1)} %get-tuple-element.66), channel_id=1, source_target_pairs={{0,8},{1,9},{2,10},{3,11},{4,12},{5,13},{6,14},{7,15},{8,16},{9,17... | collective-permute-start | bytes 1179656 | tf_op jit(solution)/shard_map/ppermute | solution.py:39
  144.2 20.9 %collective-permute-start.32 = (bf16[96,2048]{1,0:T(8,128)(2,1)S(1)}, bf16[96,2048]{1,0:T(8,128)(2,1)}, u32[]{:S(2)}, u32[]{:S(2)}) collective-permute-start(bf16[96,2048]{1,0:T(8,128)(2,1)S(1)} %get-tuple-element.66), channel_id=1, source_target_pairs={{16,8},{17,9},{18,10},{19,11},{20,12},{21,13},{22,14},{23,15},{24,... | collective-permute-start | bytes 1179656 | tf_op jit(solution)/shard_map/ppermute | solution.py:39
  145.5 20.9 %collective-permute-start.34 = (bf16[96,2048]{1,0:T(8,128)(2,1)}, bf16[96,2048]{1,0:T(8,128)(2,1)}, u32[]{:S(2)}, u32[]{:S(2)}) collective-permute-start(bf16[96,2048]{1,0:T(8,128)(2,1)} %get-tuple-element.67), channel_id=1, source_target_pairs={{0,16},{1,17},{2,18},{3,19},{4,20},{5,21},{6,22},{7,23},{24,8},{25... | collective-permute-start | bytes 1179656 | tf_op jit(solution)/shard_map/ppermute | solution.py:39
  149.8 45.0 %collective-permute-start.23 = (bf16[512,768]{0,1:T(8,128)(2,1)}, bf16[512,768]{0,1:T(8,128)(2,1)}, u32[]{:S(2)}, u32[]{:S(2)}) collective-permute-start(bf16[512,768]{0,1:T(8,128)(2,1)} %get-tuple-element.51), channel_id=1, source_target_pairs={{0,8},{1,9},{2,10},{3,11},{4,12},{5,13},{6,14},{7,15},{8,16},{9,17... | collective-permute-start | bytes 2359304 | tf_op jit(solution)/shard_map/ppermute | solution.py:39
  161.0 35.2 %collective-permute-start.22 = (bf16[512,768]{0,1:T(8,128)(2,1)}, bf16[512,768]{0,1:T(8,128)(2,1)}, u32[]{:S(2)}, u32[]{:S(2)}) collective-permute-start(bf16[512,768]{0,1:T(8,128)(2,1)} %get-tuple-element.51), channel_id=1, source_target_pairs={{16,8},{17,9},{18,10},{19,11},{20,12},{21,13},{22,14},{23,15},{24,... | collective-permute-start | bytes 2359304 | tf_op jit(solution)/shard_map/ppermute | solution.py:39
  165.1 35.0 %collective-permute-start.24 = (bf16[512,768]{0,1:T(8,128)(2,1)}, bf16[512,768]{0,1:T(8,128)(2,1)}, u32[]{:S(2)}, u32[]{:S(2)}) collective-permute-start(bf16[512,768]{0,1:T(8,128)(2,1)} %get-tuple-element.52), channel_id=1, source_target_pairs={{0,16},{1,17},{2,18},{3,19},{4,20},{5,21},{6,22},{7,23},{24,8},{25... | collective-permute-start | bytes 2359304 | tf_op jit(solution)/shard_map/ppermute | solution.py:39
  166.4 45.9 %collective-permute-start.30 = (bf16[96,2048]{1,0:T(8,128)(2,1)S(1)}, bf16[96,2048]{1,0:T(8,128)(2,1)S(1)}, u32[]{:S(2)}, u32[]{:S(2)}) collective-permute-start(bf16[96,2048]{1,0:T(8,128)(2,1)S(1)} %get-tuple-element.65), channel_id=1, source_target_pairs={{0,8},{1,9},{2,10},{3,11},{4,12},{5,13},{6,14},{7,15},{24,16},{25,... | collective-permute-start | bytes 1179656 | tf_op jit(solution)/shard_map/ppermute | solution.py:39
  194.8 51.4 %collective-permute-start.25 = (bf16[512,768]{0,1:T(8,128)(2,1)S(1)}, bf16[512,768]{0,1:T(8,128)(2,1)S(1)}, u32[]{:S(2)}, u32[]{:S(2)}) collective-permute-start(bf16[512,768]{0,1:T(8,128)(2,1)S(1)} %get-tuple-element.50), channel_id=1, source_target_pairs={{0,8},{1,9},{2,10},{3,11},{4,12},{5,13},{6,14},{7,15},{24,16},{25,... | collective-permute-start | bytes 2359304 | tf_op jit(solution)/shard_map/ppermute | solution.py:39
  207.7 8.8 %collective-permute-start.33 = (bf16[96,2048]{1,0:T(8,128)(2,1)S(1)}, bf16[96,2048]{1,0:T(8,128)(2,1)S(1)}, u32[]{:S(2)}, u32[]{:S(2)}) collective-permute-start(bf16[96,2048]{1,0:T(8,128)(2,1)S(1)} %get-tuple-element.33), channel_id=1, source_target_pairs={{8,16},{9,17},{10,18},{11,19},{12,20},{13,21},{14,22},{15,23},{16,... | collective-permute-start | bytes 1179656 | tf_op jit(solution)/shard_map/ppermute | solution.py:39
  211.0 12.6 %collective-permute-start.21 = (bf16[72,4096]{1,0:T(8,128)(2,1)S(1)}, bf16[72,4096]{1,0:T(8,128)(2,1)S(1)}, u32[]{:S(2)}, u32[]{:S(2)}) collective-permute-start(bf16[72,4096]{1,0:T(8,128)(2,1)S(1)} %get-tuple-element.60), channel_id=1, source_target_pairs={{0,6},{1,7},{2,4},{3,5},{4,2},{5,3},{6,0},{7,1},{8,14},{9,15},{10,... | collective-permute-start | bytes 1769480 | tf_op jit(solution)/shard_map/ppermute | solution.py:39
  212.4 27.5 %collective-permute-start.20 = (bf16[72,4096]{1,0:T(8,128)(2,1)S(1)}, bf16[72,4096]{1,0:T(8,128)(2,1)S(1)}, u32[]{:S(2)}, u32[]{:S(2)}) collective-permute-start(bf16[72,4096]{1,0:T(8,128)(2,1)S(1)} %get-tuple-element.59), channel_id=1, source_target_pairs={{0,2},{1,3},{2,0},{3,1},{4,6},{5,7},{6,4},{7,5},{8,10},{9,11},{10,... | collective-permute-start | bytes 1769480 | tf_op jit(solution)/shard_map/ppermute | solution.py:39
  213.1 27.3 %collective-permute-start.19 = (bf16[72,4096]{1,0:T(8,128)(2,1)S(1)}, bf16[72,4096]{1,0:T(8,128)(2,1)S(1)}, u32[]{:S(2)}, u32[]{:S(2)}) collective-permute-start(bf16[72,4096]{1,0:T(8,128)(2,1)S(1)} %get-tuple-element.58), channel_id=1, source_target_pairs={{0,4},{1,5},{2,6},{3,7},{4,0},{5,1},{6,2},{7,3},{8,12},{9,13},{10,... | collective-permute-start | bytes 1769480 | tf_op jit(solution)/shard_map/ppermute | solution.py:39
  216.5 29.7 %collective-permute-start.27 = (bf16[512,768]{0,1:T(8,128)(2,1)S(1)}, bf16[512,768]{0,1:T(8,128)(2,1)S(1)}, u32[]{:S(2)}, u32[]{:S(2)}) collective-permute-start(bf16[512,768]{0,1:T(8,128)(2,1)S(1)} %get-tuple-element.29), channel_id=1, source_target_pairs={{8,0},{9,1},{10,2},{11,3},{12,4},{13,5},{14,6},{15,7},{16,24},{17,... | collective-permute-start | bytes 2359304 | tf_op jit(solution)/shard_map/ppermute | solution.py:39
  223.6 22.5 %collective-permute-start.26 = (bf16[512,768]{0,1:T(8,128)(2,1)S(1)}, bf16[512,768]{0,1:T(8,128)(2,1)S(1)}, u32[]{:S(2)}, u32[]{:S(2)}) collective-permute-start(bf16[512,768]{0,1:T(8,128)(2,1)S(1)} %get-tuple-element.30), channel_id=1, source_target_pairs={{8,16},{9,17},{10,18},{11,19},{12,20},{13,21},{14,22},{15,23},{16,... | collective-permute-start | bytes 2359304 | tf_op jit(solution)/shard_map/ppermute | solution.py:39
  248.8 9.8 %collective-permute-start.28 = (bf16[256,768]{0,1:T(8,128)(2,1)S(1)}, bf16[256,768]{0,1:T(8,128)(2,1)S(1)}, u32[]{:S(2)}, u32[]{:S(2)}) collective-permute-start(bf16[256,768]{0,1:T(8,128)(2,1)S(1)} %get-tuple-element.71), channel_id=1, source_target_pairs={{0,0},{1,4},{2,2},{3,6},{4,1},{5,5},{6,3},{7,7},{8,8},{9,12},{10,1... | collective-permute-start | bytes 1179656 | tf_op jit(solution)/shard_map/ppermute | solution.py:39
  (27 other events, 209.2 us)

commit v5 on v4

--- a/solution.py
+++ b/solution.py
@@ -26,6 +26,7 @@
         self.zs, self.qs = self.dps // 2, self.experts // 2
         dp, ex = lax.axis_index("dp"), lax.axis_index("expert")
         self.z, self.x, self.q, self.c = dp // 2, dp % 2, ex // 2, ex % 2
+        self.lines = [[z * 2 + x for z in range(self.zs)] for x in range(2)]
 
     def send(self, value, move):
         pairs = []
@@ -44,13 +45,11 @@
     def hop(self, value, where):
         return self.send(value, lambda z, x, q, c: (where[z], x, q, c) if z in where else None)
 
-    def gather(self, shard, *ahead):
+    def gather(self, shard):
         n, z = self.zs, self.z
         if n == 4:
             up = self.hop(shard, {0: 1, 1: 2, 2: 3})
             down = self.hop(shard, {1: 0, 2: 1, 3: 2})
-            if ahead:
-                up, down = tie(up, *ahead), tie(down, *ahead)
             passed = jnp.where(z == 1, up, down)
             far = self.hop(passed, {1: 3, 2: 0})
             up_2 = self.hop(up, {1: 2, 2: 3})
@@ -61,25 +60,15 @@
                 jnp.where(z < 2, down_2, up_2),
                 jnp.where(z == 0, far, up),
             ]
-            return blocks, (up, down, passed)
+            return blocks, (up, down, passed), (far, up_2, down_2)
         ups, downs = [shard], [shard]
         for s in range(1, n):
             ups.append(self.hop(ups[-1], {i: i + 1 for i in range(s - 1, n - 1)}))
             downs.append(self.hop(downs[-1], {i: i - 1 for i in range(1, n - s + 1)}))
         blocks = [shard] + [jnp.where(z + s < n, downs[s], ups[n - s]) for s in range(1, n)]
-        return blocks, (ups[1], downs[1])
-
-    def straight(self, blocks):
-        n = self.zs
-        rows = []
-        for j in range(n):
-            row = blocks[j]
-            for z in range(1, n):
-                row = jnp.where(self.z == z, blocks[(j - z) % n], row)
-            rows.append(row)
-        return rows
-
-    def scatter(self, block, *ahead):
+        return blocks, (ups[-2], downs[-2]), (ups[-1], downs[-1])
+
+    def scatter(self, block):
         n, z = self.zs, self.z
         if n == 4:
             far = self.hop(jnp.where(z == 0, block(3), block(1)), {0: 2, 3: 1})
@@ -90,7 +79,6 @@
             is_low = z == 1
             to_end = added(jnp.where(is_low, block(3), block(1)), jnp.where(is_low, down, up), far)
             to_mid = added(jnp.where(is_low, block(1), block(3)), jnp.where(is_low, up, down))
-            to_end, to_mid = tie(to_end, *ahead), tie(to_mid, *ahead)
             end = self.hop(to_end, {1: 0, 2: 3})
             mid = self.hop(to_mid, {1: 2, 2: 1})
             return added(block(0), near, mid, end), (to_end, to_mid)
@@ -179,22 +167,19 @@
 
     line_width = width // g.zs
     turned = lax.dynamic_slice(jnp.concatenate([tokens, tokens], axis=1), (0, g.z * line_width), (rows, width))
-    sent = jnp.concatenate(
-        [
-            dot(placing, turned, ((0,), (0,))).astype(BF),
-            (slot_probs[:, None] * dot(placing, d_out, ((0,), (0,)))).astype(BF),
-        ],
-        axis=1,
-    )
-    gate_up_blocks, gate_up_passed = g.gather(gate_up_shard)
+    gate_up_blocks, gate_up_passed, gate_up_last = g.gather(gate_up_shard)
     gate_up = jnp.concatenate(gate_up_blocks, axis=0)
-    mine = tie(exchange(tie(sent, gate_up_shard), 1), *gate_up_passed)
-    inputs = jnp.concatenate([mine, g.send(mine, other_core)], axis=0)
-    arrived, d_produced = inputs[:, :width], inputs[:, width:]
-
-    w_down_late = tie(w_down[0], *gate_up_passed)
+    sent_rows = dot(placing, turned, ((0,), (0,))).astype(BF)
+    sent_grads = (slot_probs[:, None] * dot(placing, d_out, ((0,), (0,)))).astype(BF)
+    mine = exchange(tie(sent_rows, gate_up_shard), 1)
+    arrived = jnp.concatenate([mine, g.send(mine, other_core)], axis=0)
+    mine = tie(exchange(tie(sent_grads, *gate_up_passed), 1), *gate_up_last)
+    d_produced = jnp.concatenate([mine, g.send(mine, other_core)], axis=0)
+
+    w_down_late = tie(w_down[0], gate_up_shard)
     down_low, down_high = w_down_late[:part], w_down_late[part:]
     down_shard = spread(jnp.where(even, down_low, down_high), jnp.where(even, down_high, down_low))
+    down = lax.all_gather(down_shard, "dp", axis=0, tiled=True, axis_index_groups=g.lines)
 
     pre = dot(arrived, gate_up)
     gate_pre, up_pre = pre[:, :half], pre[:, half:]
@@ -202,9 +187,7 @@
     act = gate_pre * sig
     hidden = (act * up_pre).astype(BF)
     down_part = dot(hidden, d_produced, ((0,), (0,))).astype(BF)
-    down_rows = 2 * part
-    down_blocks, _ = g.gather(down_shard, down_part)
-    down = jnp.concatenate(g.straight(down_blocks), axis=0)
+    down_grad = lax.psum_scatter(down_part, "dp", scatter_dimension=0, tiled=True, axis_index_groups=g.lines)
 
     d_hidden = dot(tie(d_produced, down_part), down, ((1,), (1,)))
     d_gate = (d_hidden * up_pre * sig * (1.0 + gate_pre * (1.0 - sig))).astype(BF)
@@ -215,15 +198,12 @@
     produced = dot(tie(hidden, both_part), down)
     d_arrived = dot(tie(d_both, both_part), gate_up, ((1,), (1,)))
     theirs = jnp.concatenate([produced[slots:].astype(BF), d_arrived[slots:].astype(BF)], axis=1)
-    other = g.send(theirs, other_core).astype(F32)
+    gate_up_grad, second = g.scatter(lambda k: both_part[k * line_width:(k + 1) * line_width])
+    other = tie(g.send(theirs, other_core), *second).astype(F32)
     sums = jnp.concatenate(
         [(produced[:slots] + other[:, :width]).astype(BF), (d_arrived[:slots] + other[:, width:]).astype(BF)], axis=1
     )
-    down_grad, _ = g.scatter(
-        lambda k: lax.dynamic_slice_in_dim(down_part, ((g.z + k) % g.zs) * down_rows, down_rows), sums
-    )
-    gate_up_grad, second = g.scatter(lambda k: both_part[k * line_width:(k + 1) * line_width], sums)
-    got = tie(exchange(sums, -1), *second)
+    got = exchange(sums, -1)
     returned, back_rows = got[:, :width], got[:, width:]
     gate_up_grad, down_grad = tie(gate_up_grad, got), tie(down_grad, *second)
 

time: 263 us -> 288 us (1.095)
  waiting for transfers between devices: 127 us -> 152 us
  starting transfers between devices: 76 us -> 53 us
  between operations: 1.68 us -> 14.8 us
  local copies, waits for them, and re-layouts: 7.54 us -> 15 us
    ppermute x38 -> x31, waiting for transfers between devices: 127 us -> 152 us  [send(): return lax.ppermute(value, BOTH, pairs)]
    ppermute x38 -> x31, starting transfers between devices: 76 us -> 52.9 us  [send(): return lax.ppermute(value, BOTH, pairs)]
    unnamed x43 -> x54, local copies, waits for them, and re-layouts: 3.88 us -> 10.2 us
    concatenate x2 -> x3, other arithmetic: 1.85 us -> 4.79 us  [exchange(): return jnp.concatenate(got, axis=0)]
    convert_element_type x4 -> x2, other arithmetic: 6.39 us -> 6.21 us  [added(): return sum((t.astype(F32) for t in terms)).astype(BF)]
  transfers between devices with their start and end apart: 38 -> 33, of which waited for: 20 -> 19; matrix products, arithmetic and copies ran while one was open for 11% -> 14% of each run, Pallas kernels for 0% -> 0%
where the time goes in v5:
time: 288 us; the launch traced here: 287 us
  waiting for transfers between devices  152 us (53%)
  starting transfers between devices  53 us (18%)
  other arithmetic  28.2 us (10%)
  matrix products  24.7 us (9%)
  local copies, waits for them, and re-layouts  15 us (5%)
  between operations  14.8 us (5%)
    ppermute x31, waiting for transfers between devices, send(): return lax.ppermute(value, BOTH, pairs)  152 us
    ppermute x31, starting transfers between devices, send(): return lax.ppermute(value, BOTH, pairs)  52.9 us
    dot_general x17, matrix products, dot(): return lax.dot_general(a, b, (dims, ((), ())), preferred_element_type=F32)  24.7 us
    unnamed x54, local copies, waits for them, and re-layouts  10.2 us
    convert_element_type x2, other arithmetic, added(): return sum((t.astype(F32) for t in terms)).astype(BF)  6.21 us
  transfers between devices with their start and end apart: 33, of which 19 were waited for; matrix products, arithmetic and copies ran while one was open for 14% of the time, Pallas kernels for 0%

profile of v5, /device:TPU:9, one launch (start us, length us, event | category | flops | bytes accessed | tf_op | source)
XLA Modules:
  0.0 287.4 jit_solution(2744344689502755065)
XLA Ops:
  11.3 3.7 %collective-permute-start = (bf16[256,768]{0,1:T(8,128)(2,1)}, bf16[256,768]{0,1:T(8,128)(2,1)S(1)}, u32[]{:S(2)}, u32[]{:S(2)}) collective-permute-start(bf16[256,768]{0,1:T(8,128)(2,1)} %pad_maximum_fusion.7), channel_id=1, source_target_pairs={{0,0},{1,4},{2,2},{3,6},{4,1},{5,5},{6,3},{7,7},{8,8},{9,12},{10,1... | collective-permute-start | bytes 1179656 | tf_op jit(solution)/shard_map/ppermute | solution.py:40
  17.3 3.4 %collective-permute-done = bf16[256,768]{0,1:T(8,128)(2,1)S(1)} collective-permute-done((bf16[256,768]{0,1:T(8,128)(2,1)}, bf16[256,768]{0,1:T(8,128)(2,1)S(1)}, u32[]{:S(2)}, u32[]{:S(2)}) %collective-permute-start) | collective-permute-done | bytes 393248 | tf_op jit(solution)/shard_map/ppermute | solution.py:40
  20.7 3.6 %collective-permute-done.1 = bf16[256,768]{0,1:T(8,128)(2,1)S(1)} collective-permute-done((bf16[256,768]{0,1:T(8,128)(2,1)}, bf16[256,768]{0,1:T(8,128)(2,1)S(1)}, u32[]{:S(2)}, u32[]{:S(2)}) %collective-permute-start.1) | collective-permute-done | bytes 393248 | tf_op jit(solution)/shard_map/ppermute | solution.py:40
  26.0 2.1 collective-permute-start.7
  28.1 3.2 %collective-permute-start.6 = (bf16[512,768]{0,1:T(8,128)(2,1)S(1)}, bf16[512,768]{0,1:T(8,128)(2,1)S(1)}, u32[]{:S(2)}, u32[]{:S(2)}) collective-permute-start(bf16[512,768]{0,1:T(8,128)(2,1)S(1)} %pad_maximum_fusion.5), channel_id=1, source_target_pairs={{0,8},{1,9},{2,10},{3,11},{4,12},{5,13},{6,14},{7,15},{8,16},{9,17... | collective-permute-start | bytes 2359304 | tf_op jit(solution)/shard_map/ppermute | solution.py:40
  31.4 3.1 %collective-permute-start.15 = (bf16[48,2048]{1,0:T(8,128)(2,1)S(1)}, bf16[48,2048]{1,0:T(8,128)(2,1)S(1)}, u32[]{:S(2)}, u32[]{:S(2)}) collective-permute-start(bf16[48,2048]{1,0:T(8,128)(2,1)S(1)} %get-tuple-element.64), channel_id=1, source_target_pairs={{0,0},{1,4},{2,2},{3,6},{4,1},{5,5},{6,3},{7,7},{8,8},{9,12},{10,1... | collective-permute-start | bytes 589832 | tf_op jit(solution)/shard_map/ppermute | solution.py:40
  41.9 4.1 %collective-permute-done.4 = bf16[72,2048]{1,0:T(8,128)(2,1)S(1)} collective-permute-done((bf16[72,2048]{1,0:T(8,128)(2,1)S(1)}, bf16[72,2048]{1,0:T(8,128)(2,1)S(1)}, u32[]{:S(2)}, u32[]{:S(2)}) %collective-permute-start.4) | collective-permute-done | bytes 294944 | tf_op jit(solution)/shard_map/ppermute | solution.py:40
  46.1 6.5 %collective-permute-done.3 = bf16[72,2048]{1,0:T(8,128)(2,1)S(1)} collective-permute-done((bf16[72,2048]{1,0:T(8,128)(2,1)S(1)}, bf16[72,2048]{1,0:T(8,128)(2,1)S(1)}, u32[]{:S(2)}, u32[]{:S(2)}) %collective-permute-start.3) | collective-permute-done | bytes 294944 | tf_op jit(solution)/shard_map/ppermute | solution.py:40
  59.8 2.4 collective-permute-start.8
  63.7 3.2 %collective-permute-done.13 = bf16[72,2048]{1,0:T(8,128)(2,1)} collective-permute-done((bf16[72,2048]{1,0:T(8,128)(2,1)}, bf16[72,2048]{1,0:T(8,128)(2,1)}, u32[]{:S(2)}, u32[]{:S(2)}) %collective-permute-start.13) | collective-permute-done | bytes 294944 | tf_op jit(solution)/shard_map/ppermute | solution.py:40
  66.9 2.1 collective-permute-start.9
  69.0 4.4 %collective-permute-done.12 = bf16[72,2048]{1,0:T(8,128)(2,1)} collective-permute-done((bf16[72,2048]{1,0:T(8,128)(2,1)}, bf16[72,2048]{1,0:T(8,128)(2,1)}, u32[]{:S(2)}, u32[]{:S(2)}) %collective-permute-start.12) | collective-permute-done | bytes 294944 | tf_op jit(solution)/shard_map/ppermute | solution.py:40
  73.3 3.5 %collective-permute-start.10 = (bf16[512,768]{0,1:T(8,128)(2,1)S(1)}, bf16[512,768]{0,1:T(8,128)(2,1)S(1)}, u32[]{:S(2)}, u32[]{:S(2)}) collective-permute-start(bf16[512,768]{0,1:T(8,128)(2,1)S(1)} %collective-permute-done.6), channel_id=1, source_target_pairs={{8,16},{9,17},{10,18},{11,19},{12,20},{13,21},{14,22},{15,23},{16,... | collective-permute-start | bytes 2359304 | tf_op jit(solution)/shard_map/ppermute | solution.py:40
  79.6 2.4 constant_dynamic-update-slice_fusion
  82.1 40.1 %collective-permute-done.9 = bf16[512,768]{0,1:T(8,128)(2,1)S(1)} collective-permute-done((bf16[512,768]{0,1:T(8,128)(2,1)S(1)}, bf16[512,768]{0,1:T(8,128)(2,1)S(1)}, u32[]{:S(2)}, u32[]{:S(2)}) %collective-permute-start.9) | collective-permute-done | bytes 786464 | tf_op jit(solution)/shard_map/ppermute | solution.py:40
  129.5 2.6 convolution_convert_fusion.1
  132.1 3.7 %multiply_convert_fusion.1 = (bf16[576,384]{1,0:T(8,128)(2,1)S(1)}, bf16[576,384]{1,0:T(8,128)(2,1)S(1)}) fusion(f32[576,768]{1,0:T(8,128)} %copy-done.6, bf16[576,2048]{1,0:T(8,128)(2,1)S(1)} %constant_dynamic-update-slice_fusion.7, bf16[384,2048]{1,0:T(8,128)(2,1)} %all-gather.2.cloned.1.call-done), kind=kOutput, calls=%fused_computation.55 | convolution fusion | flops 908845056 | bytes 6586368 | tf_op jit(solution)/shard_map/dot_general | solution.py:12
  135.8 3.0 %convolution_convert_fusion = bf16[2048,768]{0,1:T(8,128)(2,1)S(1)} fusion(bf16[576,2048]{1,0:T(8,128)(2,1)S(1)} %copy-done.16, bf16[576,384]{1,0:T(8,128)(2,1)S(1)} %get-tuple-element.40, bf16[576,384]{1,0:T(8,128)(2,1)S(1)} %get-tuple-element.39), kind=kOutput, calls=%fused_computation | convolution fusion | flops 1815281664 | bytes 6389760 | tf_op jit(solution)/shard_map/dot_general | solution.py:12
  140.9 2.2 copy-done.5
  145.9 2.2 copy-done.1
  152.5 2.3 collective-permute-start.19
  157.7 19.5 %collective-permute-done.20 = bf16[512,768]{0,1:T(8,128)(2,1)} collective-permute-done((bf16[512,768]{0,1:T(8,128)(2,1)}, bf16[512,768]{0,1:T(8,128)(2,1)}, u32[]{:S(2)}, u32[]{:S(2)}) %collective-permute-start.20) | collective-permute-done | bytes 786464 | tf_op jit(solution)/shard_map/ppermute | solution.py:40
  177.2 35.8 %collective-permute-done.19 = bf16[512,768]{0,1:T(8,128)(2,1)} collective-permute-done((bf16[512,768]{0,1:T(8,128)(2,1)}, bf16[512,768]{0,1:T(8,128)(2,1)}, u32[]{:S(2)}, u32[]{:S(2)}) %collective-permute-start.19) | collective-permute-done | bytes 786464 | tf_op jit(solution)/shard_map/ppermute | solution.py:40
  214.9 4.0 %add_convert_fusion.1 = (bf16[512,768]{0,1:T(8,128)(2,1)}, bf16[512,768]{0,1:T(8,128)(2,1)}) fusion(bf16[512,768]{0,1:T(8,128)(2,1)} %collective-permute-done.19, bf16[512,768]{0,1:T(8,128)(2,1)} %collective-permute-done.18, pred[]{:T(512)S(6)} %eq.77, bf16[2048,768]{0,1:T(8,128)(2,1)} %copy-done.2, bf16[512,768]{0,1:T(8,128)(2,1)} %collective-permute-done.20), kind=kLoop, calls=%fused_computation.29 | loop fusion | flops 5505024 | bytes 5505025 | tf_op jit(solution)/shard_map/convert_element_type | solution.py:20
  218.9 2.3 collective-permute-start.25
  221.1 2.2 collective-permute-start.26
  223.9 2.4 fusion.3
  232.5 6.9 %collective-permute-done.25 = bf16[512,768]{0,1:T(8,128)(2,1)} collective-permute-done((bf16[512,768]{0,1:T(8,128)(2,1)}, bf16[512,768]{0,1:T(8,128)(2,1)}, u32[]{:S(2)}, u32[]{:S(2)}) %collective-permute-start.25) | collective-permute-done | bytes 786464 | tf_op jit(solution)/shard_map/ppermute | solution.py:40
  239.4 2.3 add_convert_fusion
  241.9 13.5 %collective-permute-done.23 = bf16[72,4096]{1,0:T(8,128)(2,1)} collective-permute-done((bf16[72,4096]{1,0:T(8,128)(2,1)S(1)}, bf16[72,4096]{1,0:T(8,128)(2,1)}, u32[]{:S(2)}, u32[]{:S(2)}) %collective-permute-start.23) | collective-permute-done | bytes 589856 | tf_op jit(solution)/shard_map/ppermute | solution.py:40
  257.4 2.4 pad_maximum_fusion.1
  259.8 5.6 %collective-permute-start.27 = (bf16[256,768]{0,1:T(8,128)(2,1)S(1)}, bf16[256,768]{0,1:T(8,128)(2,1)S(1)}, u32[]{:S(2)}, u32[]{:S(2)}) collective-permute-start(bf16[256,768]{0,1:T(8,128)(2,1)S(1)} %get-tuple-element.54), channel_id=1, source_target_pairs={{0,0},{1,4},{2,2},{3,6},{4,1},{5,5},{6,3},{7,7},{8,8},{9,12},{10,1... | collective-permute-start | bytes 1179656 | tf_op jit(solution)/shard_map/ppermute | solution.py:40
  (152 shorter events, 72.2 us)
Async XLA Ops:
  7.2 124.9 %all-gather.2.cloned.1.call-start = ((), (), s32[]{:S(2)}) async-start(), calls=%async_computation.1 | async-start | bytes 1966080 | tf_op jit(solution)/shard_map/all_gather | solution.py:182
  11.3 9.3 %collective-permute-start = (bf16[256,768]{0,1:T(8,128)(2,1)}, bf16[256,768]{0,1:T(8,128)(2,1)S(1)}, u32[]{:S(2)}, u32[]{:S(2)}) collective-permute-start(bf16[256,768]{0,1:T(8,128)(2,1)} %pad_maximum_fusion.7), channel_id=1, source_target_pairs={{0,0},{1,4},{2,2},{3,6},{4,1},{5,5},{6,3},{7,7},{8,8},{9,12},{10,1... | collective-permute-start | bytes 1179656 | tf_op jit(solution)/shard_map/ppermute | solution.py:40
  15.8 8.5 %collective-permute-start.1 = (bf16[256,768]{0,1:T(8,128)(2,1)}, bf16[256,768]{0,1:T(8,128)(2,1)S(1)}, u32[]{:S(2)}, u32[]{:S(2)}) collective-permute-start(bf16[256,768]{0,1:T(8,128)(2,1)} %pad_maximum_fusion.8), channel_id=1, source_target_pairs={{0,1},{1,5},{2,3},{3,7},{4,0},{5,4},{6,2},{7,6},{8,9},{9,13},{10,1... | collective-permute-start | bytes 1179656 | tf_op jit(solution)/shard_map/ppermute | solution.py:40
  26.0 29.0 %collective-permute-start.7 = (bf16[512,768]{0,1:T(8,128)(2,1)S(1)}, bf16[512,768]{0,1:T(8,128)(2,1)S(1)}, u32[]{:S(2)}, u32[]{:S(2)}) collective-permute-start(bf16[512,768]{0,1:T(8,128)(2,1)S(1)} %pad_maximum_fusion.5), channel_id=1, source_target_pairs={{8,0},{9,1},{10,2},{11,3},{12,4},{13,5},{14,6},{15,7},{16,8},{17,9... | collective-permute-start | bytes 2359304 | tf_op jit(solution)/shard_map/ppermute | solution.py:40
  28.1 26.9 %collective-permute-start.6 = (bf16[512,768]{0,1:T(8,128)(2,1)S(1)}, bf16[512,768]{0,1:T(8,128)(2,1)S(1)}, u32[]{:S(2)}, u32[]{:S(2)}) collective-permute-start(bf16[512,768]{0,1:T(8,128)(2,1)S(1)} %pad_maximum_fusion.5), channel_id=1, source_target_pairs={{0,8},{1,9},{2,10},{3,11},{4,12},{5,13},{6,14},{7,15},{8,16},{9,17... | collective-permute-start | bytes 2359304 | tf_op jit(solution)/shard_map/ppermute | solution.py:40
  31.4 7.3 %collective-permute-start.15 = (bf16[48,2048]{1,0:T(8,128)(2,1)S(1)}, bf16[48,2048]{1,0:T(8,128)(2,1)S(1)}, u32[]{:S(2)}, u32[]{:S(2)}) collective-permute-start(bf16[48,2048]{1,0:T(8,128)(2,1)S(1)} %get-tuple-element.64), channel_id=1, source_target_pairs={{0,0},{1,4},{2,2},{3,6},{4,1},{5,5},{6,3},{7,7},{8,8},{9,12},{10,1... | collective-permute-start | bytes 589832 | tf_op jit(solution)/shard_map/ppermute | solution.py:40
  35.3 10.8 %collective-permute-start.4 = (bf16[72,2048]{1,0:T(8,128)(2,1)S(1)}, bf16[72,2048]{1,0:T(8,128)(2,1)S(1)}, u32[]{:S(2)}, u32[]{:S(2)}) collective-permute-start(bf16[72,2048]{1,0:T(8,128)(2,1)S(1)} %get-tuple-element.47), channel_id=1, source_target_pairs={{0,6},{1,7},{2,4},{3,5},{4,2},{5,3},{6,0},{7,1},{8,14},{9,15},{10,... | collective-permute-start | bytes 884744 | tf_op jit(solution)/shard_map/ppermute | solution.py:40
  38.7 14.0 %collective-permute-start.3 = (bf16[72,2048]{1,0:T(8,128)(2,1)S(1)}, bf16[72,2048]{1,0:T(8,128)(2,1)S(1)}, u32[]{:S(2)}, u32[]{:S(2)}) collective-permute-start(bf16[72,2048]{1,0:T(8,128)(2,1)S(1)} %get-tuple-element.48), channel_id=1, source_target_pairs={{0,2},{1,3},{2,0},{3,1},{4,6},{5,7},{6,4},{7,5},{8,10},{9,11},{10,... | collective-permute-start | bytes 884744 | tf_op jit(solution)/shard_map/ppermute | solution.py:40
  40.5 12.1 %collective-permute-start.2 = (bf16[72,2048]{1,0:T(8,128)(2,1)S(1)}, bf16[72,2048]{1,0:T(8,128)(2,1)S(1)}, u32[]{:S(2)}, u32[]{:S(2)}) collective-permute-start(bf16[72,2048]{1,0:T(8,128)(2,1)S(1)} %get-tuple-element.49), channel_id=1, source_target_pairs={{0,4},{1,5},{2,6},{3,7},{4,0},{5,1},{6,2},{7,3},{8,12},{9,13},{10,... | collective-permute-start | bytes 884744 | tf_op jit(solution)/shard_map/ppermute | solution.py:40
  53.8 25.9 %collective-permute-start.5 = (bf16[288,2048]{1,0:T(8,128)(2,1)}, bf16[288,2048]{1,0:T(8,128)(2,1)}, u32[]{:S(2)}, u32[]{:S(2)}) collective-permute-start(bf16[288,2048]{1,0:T(8,128)(2,1)} %pad_maximum_fusion.2), channel_id=1, source_target_pairs={{0,1},{1,0},{2,3},{3,2},{4,5},{5,4},{6,7},{7,6},{8,9},{9,8},{10,11... | collective-permute-start | bytes 3538952 | tf_op jit(solution)/shard_map/ppermute | solution.py:40
  57.0 9.9 %collective-permute-start.13 = (bf16[72,2048]{1,0:T(8,128)(2,1)}, bf16[72,2048]{1,0:T(8,128)(2,1)}, u32[]{:S(2)}, u32[]{:S(2)}) collective-permute-start(bf16[72,2048]{1,0:T(8,128)(2,1)} %get-tuple-element.51), channel_id=1, source_target_pairs={{0,6},{1,7},{2,4},{3,5},{4,2},{5,3},{6,0},{7,1},{8,14},{9,15},{10,... | collective-permute-start | bytes 884744 | tf_op jit(solution)/shard_map/ppermute | solution.py:40
  57.8 15.5 %collective-permute-start.12 = (bf16[72,2048]{1,0:T(8,128)(2,1)}, bf16[72,2048]{1,0:T(8,128)(2,1)}, u32[]{:S(2)}, u32[]{:S(2)}) collective-permute-start(bf16[72,2048]{1,0:T(8,128)(2,1)} %get-tuple-element.52), channel_id=1, source_target_pairs={{0,2},{1,3},{2,0},{3,1},{4,6},{5,7},{6,4},{7,5},{8,10},{9,11},{10,... | collective-permute-start | bytes 884744 | tf_op jit(solution)/shard_map/ppermute | solution.py:40
  59.0 211.0 %reduce-scatter.2.cloned.1.call-start = ((), (), s32[]{:S(2)}) async-start(), calls=%async_computation.2 | async-start | bytes 1966080 | tf_op jit(solution)/shard_map/reduce_scatter | solution.py:190
  59.8 62.4 %collective-permute-start.8 = (bf16[512,768]{0,1:T(8,128)(2,1)}, bf16[512,768]{0,1:T(8,128)(2,1)S(1)}, u32[]{:S(2)}, u32[]{:S(2)}) collective-permute-start(bf16[512,768]{0,1:T(8,128)(2,1)} %broadcast_select_fusion.2), channel_id=1, source_target_pairs={{8,24},{9,25},{10,26},{11,27},{12,28},{13,29},{14,30},{15,31},{16,... | collective-permute-start | bytes 2359304 | tf_op jit(solution)/shard_map/ppermute | solution.py:40
  62.1 16.2 %collective-permute-start.11 = (bf16[72,2048]{1,0:T(8,128)(2,1)}, bf16[72,2048]{1,0:T(8,128)(2,1)S(1)}, u32[]{:S(2)}, u32[]{:S(2)}) collective-permute-start(bf16[72,2048]{1,0:T(8,128)(2,1)} %get-tuple-element.53), channel_id=1, source_target_pairs={{0,4},{1,5},{2,6},{3,7},{4,0},{5,1},{6,2},{7,3},{8,12},{9,13},{10,... | collective-permute-start | bytes 884744 | tf_op jit(solution)/shard_map/ppermute | solution.py:40
  66.9 55.3 %collective-permute-start.9 = (bf16[512,768]{0,1:T(8,128)(2,1)S(1)}, bf16[512,768]{0,1:T(8,128)(2,1)S(1)}, u32[]{:S(2)}, u32[]{:S(2)}) collective-permute-start(bf16[512,768]{0,1:T(8,128)(2,1)S(1)} %collective-permute-done.7), channel_id=1, source_target_pairs={{8,0},{9,1},{10,2},{11,3},{12,4},{13,5},{14,6},{15,7},{16,8},{17,9... | collective-permute-start | bytes 2359304 | tf_op jit(solution)/shard_map/ppermute | solution.py:40
  73.3 48.9 %collective-permute-start.10 = (bf16[512,768]{0,1:T(8,128)(2,1)S(1)}, bf16[512,768]{0,1:T(8,128)(2,1)S(1)}, u32[]{:S(2)}, u32[]{:S(2)}) collective-permute-start(bf16[512,768]{0,1:T(8,128)(2,1)S(1)} %collective-permute-done.6), channel_id=1, source_target_pairs={{8,16},{9,17},{10,18},{11,19},{12,20},{13,21},{14,22},{15,23},{16,... | collective-permute-start | bytes 2359304 | tf_op jit(solution)/shard_map/ppermute | solution.py:40
  122.2 6.4 %collective-permute-start.14 = (bf16[288,2048]{1,0:T(8,128)(2,1)S(1)}, bf16[288,2048]{1,0:T(8,128)(2,1)S(1)}, u32[]{:S(2)}, u32[]{:S(2)}) collective-permute-start(bf16[288,2048]{1,0:T(8,128)(2,1)S(1)} %pad_maximum_fusion.3), channel_id=1, source_target_pairs={{0,1},{1,0},{2,3},{3,2},{4,5},{5,4},{6,7},{7,6},{8,9},{9,8},{10,11... | collective-permute-start | bytes 3538952 | tf_op jit(solution)/shard_map/ppermute | solution.py:40
  149.8 73.6 %collective-permute-start.17 = (bf16[288,4096]{1,0:T(8,128)(2,1)}, bf16[288,4096]{1,0:T(8,128)(2,1)S(1)}, u32[]{:S(2)}, u32[]{:S(2)}) collective-permute-start(bf16[288,4096]{1,0:T(8,128)(2,1)} %pad_maximum_fusion), channel_id=1, source_target_pairs={{0,1},{1,0},{2,3},{3,2},{4,5},{5,4},{6,7},{7,6},{8,9},{9,8},{10,11... | collective-permute-start | bytes 7077896 | tf_op jit(solution)/shard_map/ppermute | solution.py:40
  151.3 26.0 %collective-permute-start.20 = (bf16[512,768]{0,1:T(8,128)(2,1)}, bf16[512,768]{0,1:T(8,128)(2,1)}, u32[]{:S(2)}, u32[]{:S(2)}) collective-permute-start(bf16[512,768]{0,1:T(8,128)(2,1)} %get-tuple-element.38), channel_id=1, source_target_pairs={{0,16},{1,17},{2,18},{3,19},{4,20},{5,21},{6,22},{7,23},{24,8},{25... | collective-permute-start | bytes 2359304 | tf_op jit(solution)/shard_map/ppermute | solution.py:40
  152.5 60.5 %collective-permute-start.19 = (bf16[512,768]{0,1:T(8,128)(2,1)}, bf16[512,768]{0,1:T(8,128)(2,1)}, u32[]{:S(2)}, u32[]{:S(2)}) collective-permute-start(bf16[512,768]{0,1:T(8,128)(2,1)} %get-tuple-element.37), channel_id=1, source_target_pairs={{0,8},{1,9},{2,10},{3,11},{4,12},{5,13},{6,14},{7,15},{8,16},{9,17... | collective-permute-start | bytes 2359304 | tf_op jit(solution)/shard_map/ppermute | solution.py:40
  154.8 60.1 %collective-permute-start.18 = (bf16[512,768]{0,1:T(8,128)(2,1)}, bf16[512,768]{0,1:T(8,128)(2,1)}, u32[]{:S(2)}, u32[]{:S(2)}) collective-permute-start(bf16[512,768]{0,1:T(8,128)(2,1)} %get-tuple-element.37), channel_id=1, source_target_pairs={{16,8},{17,9},{18,10},{19,11},{20,12},{21,13},{22,14},{23,15},{24,... | collective-permute-start | bytes 2359304 | tf_op jit(solution)/shard_map/ppermute | solution.py:40
  156.2 75.0 %collective-permute-start.24 = (bf16[512,768]{0,1:T(8,128)(2,1)}, bf16[512,768]{0,1:T(8,128)(2,1)}, u32[]{:S(2)}, u32[]{:S(2)}) collective-permute-start(bf16[512,768]{0,1:T(8,128)(2,1)} %get-tuple-element.36), channel_id=1, source_target_pairs={{0,8},{1,9},{2,10},{3,11},{4,12},{5,13},{6,14},{7,15},{24,16},{25,... | collective-permute-start | bytes 2359304 | tf_op jit(solution)/shard_map/ppermute | solution.py:40
  218.9 20.5 %collective-permute-start.25 = (bf16[512,768]{0,1:T(8,128)(2,1)}, bf16[512,768]{0,1:T(8,128)(2,1)}, u32[]{:S(2)}, u32[]{:S(2)}) collective-permute-start(bf16[512,768]{0,1:T(8,128)(2,1)} %get-tuple-element.34), channel_id=1, source_target_pairs={{8,16},{9,17},{10,18},{11,19},{12,20},{13,21},{14,22},{15,23},{16,... | collective-permute-start | bytes 2359304 | tf_op jit(solution)/shard_map/ppermute | solution.py:40
  221.1 18.3 %collective-permute-start.26 = (bf16[512,768]{0,1:T(8,128)(2,1)}, bf16[512,768]{0,1:T(8,128)(2,1)}, u32[]{:S(2)}, u32[]{:S(2)}) collective-permute-start(bf16[512,768]{0,1:T(8,128)(2,1)} %get-tuple-element.35), channel_id=1, source_target_pairs={{8,0},{9,1},{10,2},{11,3},{12,4},{13,5},{14,6},{15,7},{16,24},{17,... | collective-permute-start | bytes 2359304 | tf_op jit(solution)/shard_map/ppermute | solution.py:40
  227.3 14.6 %collective-permute-start.21 = (bf16[72,4096]{1,0:T(8,128)(2,1)}, bf16[72,4096]{1,0:T(8,128)(2,1)S(1)}, u32[]{:S(2)}, u32[]{:S(2)}) collective-permute-start(bf16[72,4096]{1,0:T(8,128)(2,1)} %get-tuple-element.42), channel_id=1, source_target_pairs={{0,4},{1,5},{2,6},{3,7},{4,0},{5,1},{6,2},{7,3},{8,12},{9,13},{10,... | collective-permute-start | bytes 1769480 | tf_op jit(solution)/shard_map/ppermute | solution.py:40
  228.9 26.5 %collective-permute-start.23 = (bf16[72,4096]{1,0:T(8,128)(2,1)S(1)}, bf16[72,4096]{1,0:T(8,128)(2,1)}, u32[]{:S(2)}, u32[]{:S(2)}) collective-permute-start(bf16[72,4096]{1,0:T(8,128)(2,1)S(1)} %get-tuple-element.43), channel_id=1, source_target_pairs={{0,6},{1,7},{2,4},{3,5},{4,2},{5,3},{6,0},{7,1},{8,14},{9,15},{10,... | collective-permute-start | bytes 1769480 | tf_op jit(solution)/shard_map/ppermute | solution.py:40
  231.2 26.2 %collective-permute-start.22 = (bf16[72,4096]{1,0:T(8,128)(2,1)S(1)}, bf16[72,4096]{1,0:T(8,128)(2,1)}, u32[]{:S(2)}, u32[]{:S(2)}) collective-permute-start(bf16[72,4096]{1,0:T(8,128)(2,1)S(1)} %get-tuple-element.44), channel_id=1, source_target_pairs={{0,2},{1,3},{2,0},{3,1},{4,6},{5,7},{6,4},{7,5},{8,10},{9,11},{10,... | collective-permute-start | bytes 1769480 | tf_op jit(solution)/shard_map/ppermute | solution.py:40
  259.8 14.1 %collective-permute-start.27 = (bf16[256,768]{0,1:T(8,128)(2,1)S(1)}, bf16[256,768]{0,1:T(8,128)(2,1)S(1)}, u32[]{:S(2)}, u32[]{:S(2)}) collective-permute-start(bf16[256,768]{0,1:T(8,128)(2,1)S(1)} %get-tuple-element.54), channel_id=1, source_target_pairs={{0,0},{1,4},{2,2},{3,6},{4,1},{5,5},{6,3},{7,7},{8,8},{9,12},{10,1... | collective-permute-start | bytes 1179656 | tf_op jit(solution)/shard_map/ppermute | solution.py:40
  265.5 9.7 %collective-permute-start.28 = (bf16[256,768]{0,1:T(8,128)(2,1)S(1)}, bf16[256,768]{0,1:T(8,128)(2,1)S(1)}, u32[]{:S(2)}, u32[]{:S(2)}) collective-permute-start(bf16[256,768]{0,1:T(8,128)(2,1)S(1)} %get-tuple-element.55), channel_id=1, source_target_pairs={{0,4},{1,0},{2,6},{3,2},{4,5},{5,1},{6,7},{7,3},{8,12},{9,8},{10,1... | collective-permute-start | bytes 1179656 | tf_op jit(solution)/shard_map/ppermute | solution.py:40
  271.0 8.6 %collective-permute-start.29 = (bf16[48,2048]{1,0:T(8,128)(2,1)S(1)}, bf16[48,2048]{1,0:T(8,128)(2,1)S(1)}, u32[]{:S(2)}, u32[]{:S(2)}) collective-permute-start(bf16[48,2048]{1,0:T(8,128)(2,1)S(1)} %get-tuple-element.56), channel_id=1, source_target_pairs={{0,0},{1,4},{2,2},{3,6},{4,1},{5,5},{6,3},{7,7},{8,8},{9,12},{10,1... | collective-permute-start | bytes 589832 | tf_op jit(solution)/shard_map/ppermute | solution.py:40
  272.9 6.6 %collective-permute-start.30 = (bf16[48,2048]{1,0:T(8,128)(2,1)S(1)}, bf16[48,2048]{1,0:T(8,128)(2,1)S(1)}, u32[]{:S(2)}, u32[]{:S(2)}) collective-permute-start(bf16[48,2048]{1,0:T(8,128)(2,1)S(1)} %get-tuple-element.57), channel_id=1, source_target_pairs={{0,4},{1,0},{2,6},{3,2},{4,5},{5,1},{6,7},{7,3},{8,12},{9,8},{10,1... | collective-permute-start | bytes 589832 | tf_op jit(solution)/shard_map/ppermute | solution.py:40
  (26 other events, 325.0 us)
Sparse Core Ops, SparseCore 0:
  59.1 58.8 all-gather.1
  156.3 59.7 reduce-scatter.1

commit v6 on v1

v6 whole, which is shorter than its diff:
```python
import jax
import jax.numpy as jnp
from jax import lax
from jax.experimental import pallas as pl
from jax.experimental.pallas import tpu as pltpu
from jax.sharding import PartitionSpec as P

BF = jnp.bfloat16
F32 = jnp.float32
BOTH = ("dp", "expert")


def dot(a, b, dims=((1,), (0,))):
    return lax.dot_general(a, b, (dims, ((), ())), preferred_element_type=F32)


def added(*terms):
    return sum(t.astype(F32) for t in terms).astype(BF)


class Grid:
    def __init__(self):
        self.dps, self.experts = lax.axis_size("dp"), lax.axis_size("expert")
        self.zs, self.qs = self.dps // 2, self.experts // 2
        dp, ex = lax.axis_index("dp"), lax.axis_index("expert")
        self.z, self.x, self.q, self.c = dp // 2, dp % 2, ex // 2, ex % 2

    def send(self, value, move):
        pairs = []
        for z in range(self.zs):
            for x in range(2):
                for q in range(self.qs):
                    for c in range(2):
                        to = move(z, x, q, c)
                        if to is not None:
                            pairs.append((self.flat(z, x, q, c), self.flat(*to)))
        return lax.ppermute(value, BOTH, pairs)

    def flat(self, z, x, q, c):
        return (z * 2 + x) * self.experts + q * 2 + c

    def hop(self, value, where):
        return self.send(value, lambda z, x, q, c: (where[z], x, q, c) if z in where else None)

    def line(self, shard):
        n = self.zs
        ups, downs = [shard], [shard]
        for s in range(1, n):
            ups.append(self.hop(ups[-1], {i: i + 1 for i in range(s - 1, n - 1)}))
            downs.append(self.hop(downs[-1], {i: i - 1 for i in range(1, n - s + 1)}))
        return [shard] + [jnp.where(self.z + s < n, downs[s], ups[n - s]) for s in range(1, n)]

    def straight(self, blocks):
        n = self.zs
        rows = []
        for j in range(n):
            row = blocks[j]
            for z in range(1, n):
                row = jnp.where(self.z == z, blocks[(j - z) % n], row)
            rows.append(row)
        return rows

    def line_sum(self, block):
        n = self.zs
        up, down = self.hop(block(n - 1), {0: 1}), self.hop(block(1), {n - 1: n - 2})
        for r in range(2, n):
            up = self.hop(added(block(n - r), up), {i: i + 1 for i in range(r)})
            down = self.hop(added(block(r), down), {i: i - 1 for i in range(n - r, n)})
        return added(block(0), up, down)


LANES = 256
VMEM_BYTES = 48 * 2**20


def pack_kernel(x_ref, gate_ref, up_ref, down_ref, shuffle_ref, a_ref, b_ref):
    rows, hidden_width = gate_ref.shape
    half, part = hidden_width // 2, down_ref.shape[0] // 2
    shuffle = shuffle_ref[...]
    gate, up = dot(gate_ref[...], shuffle).astype(BF), dot(up_ref[...], shuffle).astype(BF)
    x = x_ref[0]
    for ref, at, start in ((a_ref, 0, x), (b_ref, half, 1 - x)):
        both = jnp.concatenate([gate[:, at:at + half], up[:, at:at + half]], axis=1)
        count = hidden_width // LANES
        for i in range(count):
            ref[i * rows:(i + 1) * rows, :] = both[:, i * LANES:(i + 1) * LANES]
        source = pl.ds(pl.multiple_of(start * part, 16), part)
        for j in range(down_ref.shape[1] // LANES):
            to = count * rows + j * part
            ref[to:to + part, :] = down_ref[source, j * LANES:(j + 1) * LANES]


def unpack_kernel(x_ref, a_ref, b_ref, shuffle_ref, gate_ref, up_ref, down_ref):
    rows, hidden_width = gate_ref.shape
    half, part = hidden_width // 2, down_ref.shape[0] // 2
    count = hidden_width // LANES
    x = x_ref[0]
    a, b = (
        jnp.concatenate([ref[i * rows:(i + 1) * rows, :] for i in range(count)], axis=1) for ref in (a_ref, b_ref)
    )
    shuffle = shuffle_ref[...]
    gate_ref[...] = dot(jnp.concatenate([a[:, :half], b[:, :half]], axis=1), shuffle, ((1,), (1,)))
    up_ref[...] = dot(jnp.concatenate([a[:, half:], b[:, half:]], axis=1), shuffle, ((1,), (1,)))
    for ref, start in ((a_ref, x), (b_ref, 1 - x)):
        to = pl.ds(pl.multiple_of(start * part, 16), part)
        for j in range(down_ref.shape[1] // LANES):
            at = count * rows + j * part
            down_ref[to, j * LANES:(j + 1) * LANES] = ref[at:at + part, :].astype(F32)


def expert_kernel(
    z_ref, own, up, down, far, up_2, down_2, mine, theirs,
    keep_out, give_out, outer_out, inner_out, middle_out, own_out,
    packed, x, grads, gate_up, w_down, pre, d_hidden, hidden, d_both, d_down, keep, give, terms, load, store,
):
    places, size, _ = packed.shape
    rows, width = x.shape
    slots = rows // 2
    line = width // places
    part_rows = line // 2
    hidden_width = gate_up.shape[1]
    half = hidden_width // 2
    part = half // places // 2
    count, columns = hidden_width // LANES, width // LANES
    size_half = size // 2
    z = z_ref[0]

    for number, (source, target) in enumerate(
        (
            (mine.at[:, :width], x.at[:slots]),
            (theirs.at[:, :width], x.at[slots:]),
            (mine.at[:, width:], grads.at[:slots]),
            (theirs.at[:, width:], grads.at[slots:]),
        )
    ):
        pltpu.make_async_copy(source, target, load.at[number]).start()
    pltpu.make_async_copy(own, packed.at[0], load.at[4]).start()
    for s, is_one, one, other in (
        (1, z == places - 1, far, down),
        (2, z < 2, down_2, up_2),
        (3, z == 0, far, up),
    ):
        @pl.when(is_one)
        def _():
            pltpu.make_async_copy(one, packed.at[s], load.at[4 + s]).start()

        @pl.when(jnp.logical_not(is_one))
        def _():
            pltpu.make_async_copy(other, packed.at[s], load.at[4 + s]).start()

    def down_rows(k, h):
        return pl.ds(pl.multiple_of(lax.rem(z + k, places) * (2 * part) + h * part, 16), part)

    pltpu.make_async_copy(mine.at[:, :width], x.at[:slots], load.at[0]).wait()
    pltpu.make_async_copy(theirs.at[:, :width], x.at[slots:], load.at[1]).wait()
    for s in range(places):
        pltpu.make_async_copy(own, packed.at[s], load.at[4 + s]).wait()
        for h in range(2):
            for i in range(count):
                at = h * size_half + i * part_rows
                to = s * line + h * part_rows
                gate_up[to:to + part_rows, i * LANES:(i + 1) * LANES] = packed[s, at:at + part_rows, :]
            for j in range(columns):
                at = h * size_half + count * part_rows + j * part
                w_down[down_rows(s, h), j * LANES:(j + 1) * LANES] = packed[s, at:at + part, :]
        block = slice(s * line, (s + 1) * line)
        for i in range(count):
            cols = slice(i * LANES, (i + 1) * LANES)
            product = dot(x[:, block], gate_up[block, cols])
            pre[:, cols] = product if s == 0 else pre[:, cols] + product

    step = 64 if rows % 64 == 0 else 16

    def activate(r, _):
        at = pl.ds(pl.multiple_of(r * step, 16), step)
        gate_pre, up_pre = pre[at, :half], pre[at, half:]
        sig = 1.0 / (1.0 + jnp.exp(-gate_pre))
        act = gate_pre * sig
        hidden[at, :] = (act * up_pre).astype(BF)
        pre[at, :half] = up_pre * sig * (1.0 + gate_pre * (1.0 - sig))
        pre[at, half:] = act
        return 0

    lax.fori_loop(0, rows // step, activate, 0)

    pltpu.make_async_copy(mine.at[:, width:], grads.at[:slots], load.at[2]).wait()
    pltpu.make_async_copy(theirs.at[:, width:], grads.at[slots:], load.at[3]).wait()
    d_hidden[...] = dot(grads[...], w_down[...], ((1,), (1,)))

    def differentiate(r, _):
        at = pl.ds(pl.multiple_of(r * step, 16), step)
        d_h = d_hidden[at, :]
        d_both[at, :half] = (d_h * pre[at, :half]).astype(BF)
        d_both[at, half:] = (d_h * pre[at, half:]).astype(BF)
        return 0

    lax.fori_loop(0, rows // step, differentiate, 0)

    def to_tokens(n, _):
        at = pl.multiple_of(n * LANES, LANES)
        cols, beyond = pl.ds(at, LANES), pl.ds(at + width, LANES)
        produced = dot(hidden[...], w_down[:, cols]).astype(BF)
        keep[:, cols], give[:, cols] = produced[:slots], produced[slots:]
        d_arrived = dot(d_both[...], gate_up[cols, :], ((1,), (1,))).astype(BF)
        keep[:, beyond], give[:, beyond] = d_arrived[:slots], d_arrived[slots:]
        d_down[:, cols] = dot(hidden[...], grads[:, cols], ((0,), (0,))).astype(BF)
        return 0

    lax.fori_loop(0, columns, to_tokens, 0)
    pltpu.make_async_copy(keep, keep_out, store.at[4]).start()
    pltpu.make_async_copy(give, give_out, store.at[5]).start()

    outer_k = jnp.where(z < places // 2, places - 1, 1)
    roles = ((0, outer_k, outer_out), (1, 2, middle_out), (2, places - outer_k, inner_out), (3, 0, own_out))
    for r, k, out in roles:
        for h in range(2):
            from_cols = pl.ds(pl.multiple_of(k * line + h * part_rows, LANES), part_rows)
            weights = dot(x[:, from_cols], d_both[...], ((0,), (0,))).astype(BF)
            for i in range(count):
                to = h * size_half + i * part_rows
                terms[r, to:to + part_rows, :] = weights[:, i * LANES:(i + 1) * LANES]
            for j in range(columns):
                to = h * size_half + count * part_rows + j * part
                terms[r, to:to + part, :] = d_down[down_rows(k, h), j * LANES:(j + 1) * LANES]
        pltpu.make_async_copy(terms.at[r], out, store.at[r]).start()
    for r, k, out in roles:
        pltpu.make_async_copy(terms.at[r], out, store.at[r]).wait()
    pltpu.make_async_copy(keep, keep_out, store.at[4]).wait()
    pltpu.make_async_copy(give, give_out, store.at[5]).wait()


def in_vmem(count):
    return [pl.BlockSpec(memory_space=pltpu.VMEM)] * count


IN_SMEM = pl.BlockSpec(memory_space=pltpu.SMEM)


def pack(x, gate, up, down, shuffle):
    rows, hidden_width = gate.shape
    size = (rows * hidden_width + down.size // 2) // LANES
    return pl.pallas_call(
        pack_kernel,
        out_shape=[jax.ShapeDtypeStruct((size, LANES), BF)] * 2,
        in_specs=[IN_SMEM] + in_vmem(4),
        out_specs=in_vmem(2),
        compiler_params=pltpu.CompilerParams(vmem_limit_bytes=VMEM_BYTES // 2),
    )(x, gate, up, down, shuffle)


def unpack(x, a, b, shuffle, gate_shape, down_shape):
    return pl.pallas_call(
        unpack_kernel,
        out_shape=[jax.ShapeDtypeStruct(shape, F32) for shape in (gate_shape, gate_shape, down_shape)],
        in_specs=[IN_SMEM] + in_vmem(3),
        out_specs=in_vmem(3),
        compiler_params=pltpu.CompilerParams(vmem_limit_bytes=VMEM_BYTES // 2),
    )(x, a, b, shuffle)


def expert(z, places, half, weights, mine, theirs):
    size = weights[0].shape[0]
    slots, width = mine.shape[0], mine.shape[1] // 2
    rows = 2 * slots
    row_shape, term_shape = jax.ShapeDtypeStruct(mine.shape, BF), jax.ShapeDtypeStruct((size, LANES), BF)
    return pl.pallas_call(
        expert_kernel,
        out_shape=[row_shape] * 2 + [term_shape] * 4,
        in_specs=[IN_SMEM] + [pl.BlockSpec(memory_space=pl.ANY)] * 8,
        out_specs=[pl.BlockSpec(memory_space=pl.ANY)] * 6,
        scratch_shapes=[
            pltpu.VMEM((places, size, LANES), BF),
            pltpu.VMEM((rows, width), BF),
            pltpu.VMEM((rows, width), BF),
            pltpu.VMEM((width, 2 * half), BF),
            pltpu.VMEM((half, width), BF),
            pltpu.VMEM((rows, 2 * half), F32),
            pltpu.VMEM((rows, half), F32),
            pltpu.VMEM((rows, half), BF),
            pltpu.VMEM((rows, 2 * half), BF),
            pltpu.VMEM((half, width), BF),
            pltpu.VMEM((slots, 2 * width), BF),
            pltpu.VMEM((slots, 2 * width), BF),
            pltpu.VMEM((places, size, LANES), BF),
            pltpu.SemaphoreType.DMA((4 + places,)),
            pltpu.SemaphoreType.DMA((6,)),
        ],
        compiler_params=pltpu.CompilerParams(vmem_limit_bytes=VMEM_BYTES),
        cost_estimate=pl.CostEstimate(
            flops=18 * rows * width * half, bytes_accessed=20 * 2**20, transcendentals=rows * half
        ),
    )(z, *weights, mine, theirs)


def local(tokens, expert_ids, gate_probs, w_gate, w_up, w_down, d_out):
    g = Grid()
    rows, topk = expert_ids.shape
    width = tokens.shape[1]
    hidden_width = w_gate.shape[2]
    half = hidden_width // 2
    experts = g.experts
    cap = rows * topk * 9 // (8 * experts)
    slots = experts * cap
    first = g.c == 0
    even = g.x == 0

    block = hidden_width // g.dps
    part = block // 2
    place = jnp.arange(hidden_width, dtype=jnp.int32)
    in_half = place % half
    source_col = (in_half // part) * block + ((place // half) ^ g.x) * part + in_half % part
    shuffle = (jnp.arange(hidden_width, dtype=jnp.int32)[:, None] == source_col[None, :]).astype(BF)

    def out_a(z, x, q, c):
        return z, c, q, x

    def out_b(z, x, q, c):
        return z, c, q, 1 - x

    def back_a(z, x, q, c):
        return z, c, q, x

    def back_b(z, x, q, c):
        return z, 1 - c, q, x

    def spread(part_a, part_b):
        got_a, got_b = g.send(part_a, out_a), g.send(part_b, out_b)
        return jnp.concatenate([jnp.where(first, got_a, got_b), jnp.where(first, got_b, got_a)], axis=0)

    def unspread(both):
        n = both.shape[0] // 2
        low, high = both[:n], both[n:]
        return g.send(jnp.where(first, low, high), back_a), g.send(jnp.where(first, high, low), back_b)

    expert_iota = jnp.arange(experts, dtype=jnp.int32)
    chosen = expert_ids[:, :, None] == expert_iota
    named = jnp.any(chosen, axis=1).astype(BF)
    token_iota = jnp.arange(rows, dtype=jnp.int32)
    earlier = (token_iota[:, None] > token_iota[None, :]).astype(BF)
    before = dot(earlier, named)
    slot = jnp.sum(jnp.where(chosen, before[:, None, :], 0.0), axis=2).astype(jnp.int32)
    relative = ((expert_ids // 2 - g.q + g.qs) % g.qs) * 2 + ((expert_ids % 2) ^ g.x)
    dest = relative * cap + slot
    slot_iota = jnp.arange(slots, dtype=jnp.int32)
    pair = dest[:, :, None] == slot_iota
    placing = jnp.any(pair, axis=1).astype(BF)
    weighted = jnp.sum(jnp.where(pair, gate_probs[:, :, None], 0.0), axis=1)
    slot_probs = jnp.sum(weighted, axis=0)

    def member(r, sign):
        def move(z, x, q, c):
            return z, x ^ (r % 2), (q + sign * (r // 2)) % g.qs, c

        return move

    def other_core(z, x, q, c):
        return z, x, q, 1 - c

    def exchange(value, sign):
        got = [value[:cap]] + [g.send(value[r * cap:(r + 1) * cap], member(r, sign)) for r in range(1, experts)]
        return jnp.concatenate(got, axis=0)

    line_width = width // g.zs
    turned = lax.dynamic_slice(jnp.concatenate([tokens, tokens], axis=1), (0, g.z * line_width), (rows, width))
    sent = jnp.concatenate(
        [
            dot(placing, turned, ((0,), (0,))).astype(BF),
            (slot_probs[:, None] * dot(placing, d_out, ((0,), (0,)))).astype(BF),
        ],
        axis=1,
    )
    shapes = w_gate.shape[1:], w_down.shape[1:]
    if g.zs == 4 and cap % 8 == 0 and slots % 16 == 0 and part % 16 == 0:
        place_x, place_z = g.x.reshape(1).astype(jnp.int32), g.z.reshape(1).astype(jnp.int32)
        shard = spread(*pack(place_x, w_gate[0], w_up[0], w_down[0], shuffle))
        shard, sent = lax.optimization_barrier((shard, sent))
        up, down = g.hop(shard, {0: 1, 1: 2, 2: 3}), g.hop(shard, {1: 0, 2: 1, 3: 2})
        up, down, mine = lax.optimization_barrier((up, down, exchange(sent, 1)))
        passed, mine = lax.optimization_barrier((jnp.where(g.z == 1, up, down), mine))
        far = g.hop(passed, {1: 3, 2: 0})
        up_2, down_2 = g.hop(up, {1: 2, 2: 3}), g.hop(down, {1: 0, 2: 1})
        theirs = g.send(mine, other_core)
        keep, give, outer, inner, middle, own = expert(
            place_z, g.zs, half, (shard, up, down, far, up_2, down_2), mine, theirs
        )
        far = g.hop(outer, {0: 2, 3: 1})
        up, down = g.hop(middle, {0: 1, 1: 2}), g.hop(middle, {3: 2, 2: 1})
        near = g.hop(inner, {0: 1, 3: 2})
        far, up, down, near, given = lax.optimization_barrier((far, up, down, near, g.send(give, other_core)))
        is_low = g.z == 1
        to_end = added(outer, jnp.where(is_low, down, up), far)
        to_mid = added(inner, jnp.where(is_low, up, down))
        to_end, to_mid, sums = lax.optimization_barrier((to_end, to_mid, added(keep, given)))
        end, mid = g.hop(to_end, {1: 0, 2: 3}), g.hop(to_mid, {1: 2, 2: 1})
        end, mid, got = lax.optimization_barrier((end, mid, exchange(sums, -1)))
        grad = added(own, near, end, mid)
        d_w_gate, d_w_up, d_w_down = unpack(place_x, *unspread(grad), shuffle, *shapes)
    else:
        gate_cols, up_cols = dot(w_gate[0], shuffle).astype(BF), dot(w_up[0], shuffle).astype(BF)
        gate_up_shard = spread(
            jnp.concatenate([gate_cols[:, :half], up_cols[:, :half]], axis=1),
            jnp.concatenate([gate_cols[:, half:], up_cols[:, half:]], axis=1),
        )
        down_low, down_high = w_down[0, :part], w_down[0, part:]
        down_shard = spread(jnp.where(even, down_low, down_high), jnp.where(even, down_high, down_low))
        gate_up = jnp.concatenate(g.line(gate_up_shard), axis=0)
        down = jnp.concatenate(g.straight(g.line(down_shard)), axis=0)
        mine = exchange(sent, 1)
        inputs = jnp.concatenate([mine, g.send(mine, other_core)], axis=0)
        arrived, d_produced = inputs[:, :width], inputs[:, width:]
        pre = dot(arrived, gate_up)
        gate_pre, up_pre = pre[:, :half], pre[:, half:]
        sig = jax.nn.sigmoid(gate_pre)
        act = gate_pre * sig
        hidden = (act * up_pre).astype(BF)
        d_hidden = dot(d_produced, down, ((1,), (1,)))
        d_gate = (d_hidden * up_pre * sig * (1.0 + gate_pre * (1.0 - sig))).astype(BF)
        d_up = (d_hidden * act).astype(BF)
        d_both = jnp.concatenate([d_gate, d_up], axis=1)
        down_part = dot(hidden, d_produced, ((0,), (0,))).astype(BF)
        both_part = dot(arrived, d_both, ((0,), (0,))).astype(BF)
        partial = jnp.concatenate([dot(hidden, down), dot(d_both, gate_up, ((1,), (1,)))], axis=1).astype(BF)
        got = exchange(added(partial[:slots], g.send(partial[slots:], other_core)), -1)
        down_a, down_b = unspread(
            g.line_sum(
                lambda k: lax.dynamic_slice_in_dim(down_part, ((g.z + k) % g.zs) * (2 * part), 2 * part)
            )
        )
        d_w_down = jnp.where(
            even, jnp.concatenate([down_a, down_b], axis=0), jnp.concatenate([down_b, down_a], axis=0)
        ).astype(F32)
        both_a, both_b = unspread(g.line_sum(lambda k: both_part[k * line_width:(k + 1) * line_width]))
        d_w_gate, d_w_up = (
            dot(jnp.concatenate([both_a[:, cols], both_b[:, cols]], axis=1), shuffle, ((1,), (1,)))
            for cols in (slice(0, half), slice(half, None))
        )
    returned, back_rows = got[:, :width], got[:, width:]

    high = lax.reduce_precision(weighted, 8, 7)
    mixed = (dot(high.astype(BF), returned) + dot((weighted - high).astype(BF), returned)).astype(BF)
    products = dot(d_out, returned, ((1,), (1,)))
    d_probs = jnp.sum(jnp.where(pair, products[:, None, :], 0.0), axis=2)
    d_turned = dot(placing, back_rows).astype(BF)
    d_tokens = lax.dynamic_slice(
        jnp.concatenate([d_turned, d_turned], axis=1), (0, (g.zs - g.z) * line_width), (rows, width)
    )

    return (mixed, d_tokens, d_probs, d_w_gate[None], d_w_up[None], d_w_down[None])


def solution(mesh):
    rows = P(("dp", "expert"), None)
    weight = P("expert", "dp", None)
    return jax.shard_map(
        local,
        mesh=mesh,
        in_specs=(rows, rows, rows, weight, weight, weight, rows),
        out_specs=(rows, rows, rows, weight, weight, weight),
        check_vma=False,
    )
```

time: 292 us -> 287 us (0.983)
  matrix products: 35.1 us -> 6.9 us
  Pallas kernels: 0 us -> 19.9 us
  between operations: 14.3 us -> 1.04 us
  starting transfers between devices: 30 us -> 42.7 us
  other arithmetic: 7.63 us -> 18.7 us
  waiting for transfers between devices: 194 us -> 189 us
    ppermute x24 -> x23, waiting for transfers between devices: 59.4 us -> 189 us  [send(): return lax.ppermute(value, BOTH, pairs)]
    reduce_scatter x2 -> x0, waiting for transfers between devices: 67.8 us -> none  [scatter(): lax.psum_scatter(partial.astype(BF), 'dp', scatter_dimension=0, tiled=Tru...]
    all_gather x2 -> x0, waiting for transfers between devices: 67 us -> none  [the longest x1 34 us: local(): lax.all_gather(gate_up_shard, 'dp', axis=0, tiled=True, axis_index_groups...]
    dot_general x17 -> x7, matrix products: 35.1 us -> 6.9 us  [dot(): return lax.dot_general(a, b, (dims, ((), ())), preferred_element_type=F32)]
    pallas_call x0 -> x3, Pallas kernels: none -> 19.9 us  [the longest x1 17.1 us: expert(): pl.pallas_call(expert_kernel, out_shape=[row_shape] * 2 + [term_shape] *...]
    ppermute x24 -> x23, starting transfers between devices: 29.7 us -> 42.7 us  [send(): return lax.ppermute(value, BOTH, pairs)]
    concatenate x4, other arithmetic: 0.25 us -> 6.18 us  [the longest x2 3.32 us: exchange(): return jnp.concatenate(got, axis=0)]
    convert_element_type x4, other arithmetic: 1.91 us -> 7.54 us  [the longest x3 7.13 us: added(): return sum((t.astype(F32) for t in terms)).astype(BF)]
  transfers between devices with their start and end apart: 28 -> 23, of which waited for: 20 -> 14; matrix products, arithmetic and copies ran while one was open for 11% -> 6% of each run, Pallas kernels for 0% -> 0%
where the time goes in v6:
time: 287 us; the launch traced here: 286 us
  waiting for transfers between devices  189 us (66%)
  starting transfers between devices  42.7 us (15%)
  Pallas kernels  19.9 us (7%)
  other arithmetic  18.7 us (7%)
  local copies, waits for them, and re-layouts  8.31 us (3%)
  matrix products  6.9 us (2%)
    ppermute x23, waiting for transfers between devices, send(): return lax.ppermute(value, BOTH, pairs)  189 us
    ppermute x23, starting transfers between devices, send(): return lax.ppermute(value, BOTH, pairs)  42.7 us
    pallas_call x1, Pallas kernels, expert(): pl.pallas_call(expert_kernel, out_shape=[row_shape] * 2 + [term_shape] *...  17.1 us
    convert_element_type x3, other arithmetic, added(): return sum((t.astype(F32) for t in terms)).astype(BF)  7.13 us
    dot_general x7, matrix products, dot(): return lax.dot_general(a, b, (dims, ((), ())), preferred_element_type=F32)  6.9 us
    unnamed x28, local copies, waits for them, and re-layouts  5.82 us
  transfers between devices with their start and end apart: 23, of which 14 were waited for; matrix products, arithmetic and copies ran while one was open for 6% of the time, Pallas kernels for 0%

profile of v6, /device:TPU:9, one launch (start us, length us, event | category | flops | bytes accessed | tf_op | source)
XLA Modules:
  0.0 286.2 jit_solution(1563014453866752950)
XLA Ops:
  4.9 3.7 %collective-permute-start = (bf16[1152,256]{1,0:T(8,128)(2,1)S(1)}, bf16[1152,256]{1,0:T(8,128)(2,1)S(1)}, u32[]{:S(2)}, u32[]{:S(2)}) collective-permute-start(bf16[1152,256]{1,0:T(8,128)(2,1)S(1)} %get-tuple-element.35), channel_id=1, source_target_pairs={{0,0},{1,4},{2,2},{3,6},{4,1},{5,5},{6,3},{7,7},{8,8},{9,12},{10,1... | collective-permute-start | bytes 1769480 | tf_op jit(solution)/shard_map/ppermute | solution.py:37
  11.1 2.6 convolution_convert_fusion
  13.7 1.8 pad_maximum_fusion
  16.1 5.6 %collective-permute-done.1 = bf16[1152,256]{1,0:T(8,128)(2,1)} collective-permute-done((bf16[1152,256]{1,0:T(8,128)(2,1)S(1)}, bf16[1152,256]{1,0:T(8,128)(2,1)}, u32[]{:S(2)}, u32[]{:S(2)}) %collective-permute-start.1) | collective-permute-done | bytes 589856 | tf_op jit(solution)/shard_map/ppermute | solution.py:37
  22.9 3.2 %collective-permute-start.2 = (bf16[2304,256]{1,0:T(8,128)(2,1)S(1)}, bf16[2304,256]{1,0:T(8,128)(2,1)}, u32[]{:S(2)}, u32[]{:S(2)}) collective-permute-start(bf16[2304,256]{1,0:T(8,128)(2,1)S(1)} %pad_maximum_fusion.3.own), channel_id=1, source_target_pairs={{0,8},{1,9},{2,10},{3,11},{4,12},{5,13},{6,14},{7,15},{8,16},{9,17... | collective-permute-start | bytes 3538952 | tf_op jit(solution)/shard_map/ppermute | solution.py:37
  26.2 3.1 %collective-permute-start.3 = (bf16[2304,256]{1,0:T(8,128)(2,1)S(1)}, bf16[2304,256]{1,0:T(8,128)(2,1)}, u32[]{:S(2)}, u32[]{:S(2)}) collective-permute-start(bf16[2304,256]{1,0:T(8,128)(2,1)S(1)} %pad_maximum_fusion.3.own), channel_id=1, source_target_pairs={{8,0},{9,1},{10,2},{11,3},{12,4},{13,5},{14,6},{15,7},{16,8},{17,9... | collective-permute-start | bytes 3538952 | tf_op jit(solution)/shard_map/ppermute | solution.py:37
  30.5 2.0 collective-permute-start.4
  33.8 11.9 %collective-permute-done.4 = bf16[72,4096]{1,0:T(8,128)(2,1)} collective-permute-done((bf16[72,4096]{1,0:T(8,128)(2,1)}, bf16[72,4096]{1,0:T(8,128)(2,1)}, u32[]{:S(2)}, u32[]{:S(2)}) %collective-permute-start.4) | collective-permute-done | bytes 589856 | tf_op jit(solution)/shard_map/ppermute | solution.py:37
  45.7 13.7 %collective-permute-done.5 = bf16[72,4096]{1,0:T(8,128)(2,1)} collective-permute-done((bf16[72,4096]{1,0:T(8,128)(2,1)}, bf16[72,4096]{1,0:T(8,128)(2,1)}, u32[]{:S(2)}, u32[]{:S(2)}) %collective-permute-start.5) | collective-permute-done | bytes 589856 | tf_op jit(solution)/shard_map/ppermute | solution.py:37
  59.4 1.7 pad_maximum_fusion.1.mine
  61.1 2.2 broadcast_select_fusion
  63.4 1.9 collective-permute-start.10
  65.3 4.3 %collective-permute-start.7 = (bf16[2304,256]{1,0:T(8,128)(2,1)S(1)}, bf16[2304,256]{1,0:T(8,128)(2,1)S(1)}, u32[]{:S(2)}, u32[]{:S(2)}) collective-permute-start(bf16[2304,256]{1,0:T(8,128)(2,1)S(1)} %broadcast_select_fusion), channel_id=1, source_target_pairs={{8,24},{9,25},{10,26},{11,27},{12,28},{13,29},{14,30},{15,31},{16,... | collective-permute-start | bytes 3538952 | tf_op jit(solution)/shard_map/ppermute | solution.py:37
  70.9 1.9 collective-permute-start.9
  72.8 22.0 %collective-permute-done.7.far = bf16[2304,256]{1,0:T(8,128)(2,1)S(1)} collective-permute-done((bf16[2304,256]{1,0:T(8,128)(2,1)S(1)}, bf16[2304,256]{1,0:T(8,128)(2,1)S(1)}, u32[]{:S(2)}, u32[]{:S(2)}) %collective-permute-start.7) | collective-permute-done | bytes 1179680 | tf_op jit(solution)/shard_map/ppermute | solution.py:37
  94.9 25.4 %collective-permute-done.8.up_2 = bf16[2304,256]{1,0:T(8,128)(2,1)S(1)} collective-permute-done((bf16[2304,256]{1,0:T(8,128)(2,1)}, bf16[2304,256]{1,0:T(8,128)(2,1)S(1)}, u32[]{:S(2)}, u32[]{:S(2)}) %collective-permute-start.8) | collective-permute-done | bytes 1179680 | tf_op jit(solution)/shard_map/ppermute | solution.py:37
  122.8 17.1 %shard_map.119 = (bf16[288,4096]{1,0:T(8,128)(2,1)}, bf16[288,4096]{1,0:T(8,128)(2,1)}, bf16[2304,256]{1,0:T(8,128)(2,1)S(1)}, bf16[2304,256]{1,0:T(8,128)(2,1)S...) custom-call(s32[1]{0:T(128)} %bitcast.z_ref, bf16[2304,256]{1,0:T(8,128)(2,1)S(1)} %pad_maximum_fusion.3.own, ...), custom_call_target="tpu_custom_call" | custom-call | flops 8153726976 | bytes 20971520 | tf_op jit(solution)/shard_map/pallas_call | solution.py:266
  142.1 4.0 %collective-permute-start.12 = (bf16[2304,256]{1,0:T(8,128)(2,1)S(1)}, bf16[2304,256]{1,0:T(8,128)(2,1)S(1)}, u32[]{:S(2)}, u32[]{:S(2)}) collective-permute-start(bf16[2304,256]{1,0:T(8,128)(2,1)S(1)} %get-tuple-element.45), channel_id=1, source_target_pairs={{0,8},{1,9},{2,10},{3,11},{4,12},{5,13},{6,14},{7,15},{8,16},{9,17... | collective-permute-start | bytes 3538952 | tf_op jit(solution)/shard_map/ppermute | solution.py:37
  148.9 22.3 %collective-permute-done.11 = bf16[2304,256]{1,0:T(8,128)(2,1)S(1)} collective-permute-done((bf16[2304,256]{1,0:T(8,128)(2,1)S(1)}, bf16[2304,256]{1,0:T(8,128)(2,1)S(1)}, u32[]{:S(2)}, u32[]{:S(2)}) %collective-permute-start.11) | collective-permute-done | bytes 1179680 | tf_op jit(solution)/shard_map/ppermute | solution.py:37
  171.2 26.2 %collective-permute-done.12 = bf16[2304,256]{1,0:T(8,128)(2,1)S(1)} collective-permute-done((bf16[2304,256]{1,0:T(8,128)(2,1)S(1)}, bf16[2304,256]{1,0:T(8,128)(2,1)S(1)}, u32[]{:S(2)}, u32[]{:S(2)}) %collective-permute-start.12) | collective-permute-done | bytes 1179680 | tf_op jit(solution)/shard_map/ppermute | solution.py:37
  197.4 25.3 %collective-permute-done.14 = bf16[2304,256]{1,0:T(8,128)(2,1)S(1)} collective-permute-done((bf16[2304,256]{1,0:T(8,128)(2,1)S(1)}, bf16[2304,256]{1,0:T(8,128)(2,1)S(1)}, u32[]{:S(2)}, u32[]{:S(2)}) %collective-permute-start.14) | collective-permute-done | bytes 1179680 | tf_op jit(solution)/shard_map/ppermute | solution.py:37
  222.7 2.6 add_convert_fusion
  225.3 2.3 add_convert_fusion.2
  227.5 2.3 collective-permute-start.16
  229.9 1.9 collective-permute-start.17
  235.7 11.5 %collective-permute-done.18 = bf16[72,4096]{1,0:T(8,128)(2,1)} collective-permute-done((bf16[72,4096]{1,0:T(8,128)(2,1)}, bf16[72,4096]{1,0:T(8,128)(2,1)}, u32[]{:S(2)}, u32[]{:S(2)}) %collective-permute-start.18) | collective-permute-done | bytes 589856 | tf_op jit(solution)/shard_map/ppermute | solution.py:37
  247.9 12.9 %collective-permute-done.20 = bf16[72,4096]{1,0:T(8,128)(2,1)} collective-permute-done((bf16[72,4096]{1,0:T(8,128)(2,1)}, bf16[72,4096]{1,0:T(8,128)(2,1)}, u32[]{:S(2)}, u32[]{:S(2)}) %collective-permute-start.20) | collective-permute-done | bytes 589856 | tf_op jit(solution)/shard_map/ppermute | solution.py:37
  260.8 1.7 pad_maximum_fusion.2
  263.7 2.3 add_convert_fusion.1
  266.1 4.2 %collective-permute-start.21 = (bf16[1152,256]{1,0:T(8,128)(2,1)S(1)}, bf16[1152,256]{1,0:T(8,128)(2,1)S(1)}, u32[]{:S(2)}, u32[]{:S(2)}) collective-permute-start(bf16[1152,256]{1,0:T(8,128)(2,1)S(1)} %get-tuple-element.77), channel_id=1, source_target_pairs={{0,0},{1,4},{2,2},{3,6},{4,1},{5,5},{6,3},{7,7},{8,8},{9,12},{10,1... | collective-permute-start | bytes 1769480 | tf_op jit(solution)/shard_map/ppermute | solution.py:37
  273.8 9.2 %collective-permute-done.21.a_ref = bf16[1152,256]{1,0:T(8,128)(2,1)S(1)} collective-permute-done((bf16[1152,256]{1,0:T(8,128)(2,1)S(1)}, bf16[1152,256]{1,0:T(8,128)(2,1)S(1)}, u32[]{:S(2)}, u32[]{:S(2)}) %collective-permute-start.21) | collective-permute-done | bytes 589856 | tf_op jit(solution)/shard_map/ppermute | solution.py:37
  284.2 2.0 shard_map.120
  (73 shorter events, 30.5 us)
Async XLA Ops:
  0.6 9.0 %copy-start = (bf16[128,2048]{1,0:T(8,128)(2,1)S(1)}, bf16[128,2048]{1,0:T(8,128)(2,1)}, u32[]{:S(2)}) copy-start(bf16[128,2048]{1,0:T(8,128)(2,1)} %param.13) | copy-start | bytes 1572868
  0.6 8.0 %copy-start.8 = (s32[128,2]{0,1:T(2,128)S(1)}, s32[128,2]{0,1:T(2,128)}, u32[]{:S(2)}) copy-start(s32[128,2]{0,1:T(2,128)} %param.8) | copy-start | bytes 3076
  0.7 8.3 %copy-start.9 = (f32[128,2]{0,1:T(2,128)S(1)}, f32[128,2]{0,1:T(2,128)}, u32[]{:S(2)}) copy-start(f32[128,2]{0,1:T(2,128)} %param.9) | copy-start | bytes 3076
  4.9 11.2 %collective-permute-start = (bf16[1152,256]{1,0:T(8,128)(2,1)S(1)}, bf16[1152,256]{1,0:T(8,128)(2,1)S(1)}, u32[]{:S(2)}, u32[]{:S(2)}) collective-permute-start(bf16[1152,256]{1,0:T(8,128)(2,1)S(1)} %get-tuple-element.35), channel_id=1, source_target_pairs={{0,0},{1,4},{2,2},{3,6},{4,1},{5,5},{6,3},{7,7},{8,8},{9,12},{10,1... | collective-permute-start | bytes 1769480 | tf_op jit(solution)/shard_map/ppermute | solution.py:37
  8.6 13.1 %collective-permute-start.1 = (bf16[1152,256]{1,0:T(8,128)(2,1)S(1)}, bf16[1152,256]{1,0:T(8,128)(2,1)}, u32[]{:S(2)}, u32[]{:S(2)}) collective-permute-start(bf16[1152,256]{1,0:T(8,128)(2,1)S(1)} %get-tuple-element.36), channel_id=1, source_target_pairs={{0,1},{1,5},{2,3},{3,7},{4,0},{5,4},{6,2},{7,6},{8,9},{9,13},{10,1... | collective-permute-start | bytes 1769480 | tf_op jit(solution)/shard_map/ppermute | solution.py:37
  22.9 38.1 %collective-permute-start.2 = (bf16[2304,256]{1,0:T(8,128)(2,1)S(1)}, bf16[2304,256]{1,0:T(8,128)(2,1)}, u32[]{:S(2)}, u32[]{:S(2)}) collective-permute-start(bf16[2304,256]{1,0:T(8,128)(2,1)S(1)} %pad_maximum_fusion.3.own), channel_id=1, source_target_pairs={{0,8},{1,9},{2,10},{3,11},{4,12},{5,13},{6,14},{7,15},{8,16},{9,17... | collective-permute-start | bytes 3538952 | tf_op jit(solution)/shard_map/ppermute | solution.py:37
  26.2 34.9 %collective-permute-start.3 = (bf16[2304,256]{1,0:T(8,128)(2,1)S(1)}, bf16[2304,256]{1,0:T(8,128)(2,1)}, u32[]{:S(2)}, u32[]{:S(2)}) collective-permute-start(bf16[2304,256]{1,0:T(8,128)(2,1)S(1)} %pad_maximum_fusion.3.own), channel_id=1, source_target_pairs={{8,0},{9,1},{10,2},{11,3},{12,4},{13,5},{14,6},{15,7},{16,8},{17,9... | collective-permute-start | bytes 3538952 | tf_op jit(solution)/shard_map/ppermute | solution.py:37
  30.5 15.2 %collective-permute-start.4 = (bf16[72,4096]{1,0:T(8,128)(2,1)}, bf16[72,4096]{1,0:T(8,128)(2,1)}, u32[]{:S(2)}, u32[]{:S(2)}) collective-permute-start(bf16[72,4096]{1,0:T(8,128)(2,1)} %get-tuple-element.75), channel_id=1, source_target_pairs={{0,4},{1,5},{2,6},{3,7},{4,0},{5,1},{6,2},{7,3},{8,12},{9,13},{10,... | collective-permute-start | bytes 1769480 | tf_op jit(solution)/shard_map/ppermute | solution.py:37
  32.5 26.9 %collective-permute-start.5 = (bf16[72,4096]{1,0:T(8,128)(2,1)}, bf16[72,4096]{1,0:T(8,128)(2,1)}, u32[]{:S(2)}, u32[]{:S(2)}) collective-permute-start(bf16[72,4096]{1,0:T(8,128)(2,1)} %get-tuple-element.74), channel_id=1, source_target_pairs={{0,2},{1,3},{2,0},{3,1},{4,6},{5,7},{6,4},{7,5},{8,10},{9,11},{10,... | collective-permute-start | bytes 1769480 | tf_op jit(solution)/shard_map/ppermute | solution.py:37
  33.8 25.6 %collective-permute-start.6 = (bf16[72,4096]{1,0:T(8,128)(2,1)}, bf16[72,4096]{1,0:T(8,128)(2,1)}, u32[]{:S(2)}, u32[]{:S(2)}) collective-permute-start(bf16[72,4096]{1,0:T(8,128)(2,1)} %get-tuple-element.73), channel_id=1, source_target_pairs={{0,6},{1,7},{2,4},{3,5},{4,2},{5,3},{6,0},{7,1},{8,14},{9,15},{10,... | collective-permute-start | bytes 1769480 | tf_op jit(solution)/shard_map/ppermute | solution.py:37
  61.1 60.2 %copy-start.6 = (bf16[288,4096]{1,0:T(8,128)(2,1)}, bf16[288,4096]{1,0:T(8,128)(2,1)S(1)}, u32[]{:S(2)}) copy-start(bf16[288,4096]{1,0:T(8,128)(2,1)S(1)} %pad_maximum_fusion.1.mine) | copy-start | bytes 7077892
  63.4 56.9 %collective-permute-start.10 = (bf16[288,4096]{1,0:T(8,128)(2,1)S(1)}, bf16[288,4096]{1,0:T(8,128)(2,1)S(1)}, u32[]{:S(2)}, u32[]{:S(2)}) collective-permute-start(bf16[288,4096]{1,0:T(8,128)(2,1)S(1)} %pad_maximum_fusion.1.mine), channel_id=1, source_target_pairs={{0,1},{1,0},{2,3},{3,2},{4,5},{5,4},{6,7},{7,6},{8,9},{9,8},{10,11... | collective-permute-start | bytes 7077896 | tf_op jit(solution)/shard_map/ppermute | solution.py:37
  65.3 29.6 %collective-permute-start.7 = (bf16[2304,256]{1,0:T(8,128)(2,1)S(1)}, bf16[2304,256]{1,0:T(8,128)(2,1)S(1)}, u32[]{:S(2)}, u32[]{:S(2)}) collective-permute-start(bf16[2304,256]{1,0:T(8,128)(2,1)S(1)} %broadcast_select_fusion), channel_id=1, source_target_pairs={{8,24},{9,25},{10,26},{11,27},{12,28},{13,29},{14,30},{15,31},{16,... | collective-permute-start | bytes 3538952 | tf_op jit(solution)/shard_map/ppermute | solution.py:37
  69.5 50.7 %collective-permute-start.8 = (bf16[2304,256]{1,0:T(8,128)(2,1)}, bf16[2304,256]{1,0:T(8,128)(2,1)S(1)}, u32[]{:S(2)}, u32[]{:S(2)}) collective-permute-start(bf16[2304,256]{1,0:T(8,128)(2,1)} %collective-permute-done.2.up), channel_id=1, source_target_pairs={{8,16},{9,17},{10,18},{11,19},{12,20},{13,21},{14,22},{15,23},{16,... | collective-permute-start | bytes 3538952 | tf_op jit(solution)/shard_map/ppermute | solution.py:37
  70.9 49.3 %collective-permute-start.9 = (bf16[2304,256]{1,0:T(8,128)(2,1)}, bf16[2304,256]{1,0:T(8,128)(2,1)S(1)}, u32[]{:S(2)}, u32[]{:S(2)}) collective-permute-start(bf16[2304,256]{1,0:T(8,128)(2,1)} %collective-permute-done.3.down), channel_id=1, source_target_pairs={{8,0},{9,1},{10,2},{11,3},{12,4},{13,5},{14,6},{15,7},{16,8},{17,9... | collective-permute-start | bytes 3538952 | tf_op jit(solution)/shard_map/ppermute | solution.py:37
  94.9 26.5 %copy-start.11 = (bf16[2304,256]{1,0:T(8,128)(2,1)}, bf16[2304,256]{1,0:T(8,128)(2,1)S(1)}, u32[]{:S(2)}) copy-start(bf16[2304,256]{1,0:T(8,128)(2,1)S(1)} %collective-permute-done.7.far) | copy-start | bytes 3538948
  120.2 1.4 copy-start.12
  121.3 1.5 copy-start.10
  139.9 85.3 %copy-start.1 = (bf16[2304,256]{1,0:T(8,128)(2,1)}, bf16[2304,256]{1,0:T(8,128)(2,1)S(1)}, u32[]{:S(2)}) copy-start(bf16[2304,256]{1,0:T(8,128)(2,1)S(1)} %get-tuple-element.57) | copy-start | bytes 3538948
  139.9 82.8 %collective-permute-start.15 = (bf16[288,4096]{1,0:T(8,128)(2,1)}, bf16[288,4096]{1,0:T(8,128)(2,1)S(1)}, u32[]{:S(2)}, u32[]{:S(2)}) collective-permute-start(bf16[288,4096]{1,0:T(8,128)(2,1)} %get-tuple-element.47), channel_id=1, source_target_pairs={{0,1},{1,0},{2,3},{3,2},{4,5},{5,4},{6,7},{7,6},{8,9},{9,8},{10,11... | collective-permute-start | bytes 7077896 | tf_op jit(solution)/shard_map/ppermute | solution.py:37
  140.8 30.4 %collective-permute-start.11 = (bf16[2304,256]{1,0:T(8,128)(2,1)S(1)}, bf16[2304,256]{1,0:T(8,128)(2,1)S(1)}, u32[]{:S(2)}, u32[]{:S(2)}) collective-permute-start(bf16[2304,256]{1,0:T(8,128)(2,1)S(1)} %get-tuple-element.44), channel_id=1, source_target_pairs={{0,16},{1,17},{2,18},{3,19},{4,20},{5,21},{6,22},{7,23},{24,8},{25... | collective-permute-start | bytes 3538952 | tf_op jit(solution)/shard_map/ppermute | solution.py:37
  142.1 55.3 %collective-permute-start.12 = (bf16[2304,256]{1,0:T(8,128)(2,1)S(1)}, bf16[2304,256]{1,0:T(8,128)(2,1)S(1)}, u32[]{:S(2)}, u32[]{:S(2)}) collective-permute-start(bf16[2304,256]{1,0:T(8,128)(2,1)S(1)} %get-tuple-element.45), channel_id=1, source_target_pairs={{0,8},{1,9},{2,10},{3,11},{4,12},{5,13},{6,14},{7,15},{8,16},{9,17... | collective-permute-start | bytes 3538952 | tf_op jit(solution)/shard_map/ppermute | solution.py:37
  146.1 51.3 %collective-permute-start.13 = (bf16[2304,256]{1,0:T(8,128)(2,1)S(1)}, bf16[2304,256]{1,0:T(8,128)(2,1)S(1)}, u32[]{:S(2)}, u32[]{:S(2)}) collective-permute-start(bf16[2304,256]{1,0:T(8,128)(2,1)S(1)} %get-tuple-element.45), channel_id=1, source_target_pairs={{16,8},{17,9},{18,10},{19,11},{20,12},{21,13},{22,14},{23,15},{24,... | collective-permute-start | bytes 3538952 | tf_op jit(solution)/shard_map/ppermute | solution.py:37
  147.4 75.3 %collective-permute-start.14 = (bf16[2304,256]{1,0:T(8,128)(2,1)S(1)}, bf16[2304,256]{1,0:T(8,128)(2,1)S(1)}, u32[]{:S(2)}, u32[]{:S(2)}) collective-permute-start(bf16[2304,256]{1,0:T(8,128)(2,1)S(1)} %get-tuple-element.46), channel_id=1, source_target_pairs={{0,8},{1,9},{2,10},{3,11},{4,12},{5,13},{6,14},{7,15},{24,16},{25,... | collective-permute-start | bytes 3538952 | tf_op jit(solution)/shard_map/ppermute | solution.py:37
  227.5 34.9 %collective-permute-start.16 = (bf16[2304,256]{1,0:T(8,128)(2,1)}, bf16[2304,256]{1,0:T(8,128)(2,1)}, u32[]{:S(2)}, u32[]{:S(2)}) collective-permute-start(bf16[2304,256]{1,0:T(8,128)(2,1)} %get-tuple-element.53), channel_id=1, source_target_pairs={{8,0},{9,1},{10,2},{11,3},{12,4},{13,5},{14,6},{15,7},{16,24},{17,... | collective-permute-start | bytes 3538952 | tf_op jit(solution)/shard_map/ppermute | solution.py:37
  229.9 32.6 %collective-permute-start.17 = (bf16[2304,256]{1,0:T(8,128)(2,1)}, bf16[2304,256]{1,0:T(8,128)(2,1)}, u32[]{:S(2)}, u32[]{:S(2)}) collective-permute-start(bf16[2304,256]{1,0:T(8,128)(2,1)} %get-tuple-element.54), channel_id=1, source_target_pairs={{8,16},{9,17},{10,18},{11,19},{12,20},{13,21},{14,22},{15,23},{16,... | collective-permute-start | bytes 3538952 | tf_op jit(solution)/shard_map/ppermute | solution.py:37
  233.0 14.2 %collective-permute-start.18 = (bf16[72,4096]{1,0:T(8,128)(2,1)}, bf16[72,4096]{1,0:T(8,128)(2,1)}, u32[]{:S(2)}, u32[]{:S(2)}) collective-permute-start(bf16[72,4096]{1,0:T(8,128)(2,1)} %get-tuple-element.69), channel_id=1, source_target_pairs={{0,4},{1,5},{2,6},{3,7},{4,0},{5,1},{6,2},{7,3},{8,12},{9,13},{10,... | collective-permute-start | bytes 1769480 | tf_op jit(solution)/shard_map/ppermute | solution.py:37
  234.0 13.9 %collective-permute-start.19 = (bf16[72,4096]{1,0:T(8,128)(2,1)}, bf16[72,4096]{1,0:T(8,128)(2,1)}, u32[]{:S(2)}, u32[]{:S(2)}) collective-permute-start(bf16[72,4096]{1,0:T(8,128)(2,1)} %get-tuple-element.68), channel_id=1, source_target_pairs={{0,2},{1,3},{2,0},{3,1},{4,6},{5,7},{6,4},{7,5},{8,10},{9,11},{10,... | collective-permute-start | bytes 1769480 | tf_op jit(solution)/shard_map/ppermute | solution.py:37
  234.3 26.5 %collective-permute-start.20 = (bf16[72,4096]{1,0:T(8,128)(2,1)}, bf16[72,4096]{1,0:T(8,128)(2,1)}, u32[]{:S(2)}, u32[]{:S(2)}) collective-permute-start(bf16[72,4096]{1,0:T(8,128)(2,1)} %get-tuple-element.67), channel_id=1, source_target_pairs={{0,6},{1,7},{2,4},{3,5},{4,2},{5,3},{6,0},{7,1},{8,14},{9,15},{10,... | collective-permute-start | bytes 1769480 | tf_op jit(solution)/shard_map/ppermute | solution.py:37
  266.0 6.0 %copy-start.7 = (f32[128,288]{0,1:T(8,128)S(1)}, f32[128,288]{0,1:T(8,128)}, u32[]{:S(2)}) copy-start(f32[128,288]{0,1:T(8,128)} %get-tuple-element.64) | copy-start | bytes 442372
  266.1 16.8 %collective-permute-start.21 = (bf16[1152,256]{1,0:T(8,128)(2,1)S(1)}, bf16[1152,256]{1,0:T(8,128)(2,1)S(1)}, u32[]{:S(2)}, u32[]{:S(2)}) collective-permute-start(bf16[1152,256]{1,0:T(8,128)(2,1)S(1)} %get-tuple-element.77), channel_id=1, source_target_pairs={{0,0},{1,4},{2,2},{3,6},{4,1},{5,5},{6,3},{7,7},{8,8},{9,12},{10,1... | collective-permute-start | bytes 1769480 | tf_op jit(solution)/shard_map/ppermute | solution.py:37
  270.3 13.9 %collective-permute-start.22 = (bf16[1152,256]{1,0:T(8,128)(2,1)S(1)}, bf16[1152,256]{1,0:T(8,128)(2,1)S(1)}, u32[]{:S(2)}, u32[]{:S(2)}) collective-permute-start(bf16[1152,256]{1,0:T(8,128)(2,1)S(1)} %get-tuple-element.76), channel_id=1, source_target_pairs={{0,4},{1,0},{2,6},{3,2},{4,5},{5,1},{6,7},{7,3},{8,12},{9,8},{10,1... | collective-permute-start | bytes 1769480 | tf_op jit(solution)/shard_map/ppermute | solution.py:37
  (5 other events, 5.3 us)

commit v7 on v6

v7 whole, which is shorter than its diff:
```python
import functools

import jax
import jax.numpy as jnp
from jax import lax
from jax.experimental import pallas as pl
from jax.experimental.pallas import tpu as pltpu
from jax.sharding import PartitionSpec as P

BF = jnp.bfloat16
F32 = jnp.float32
BOTH = ("dp", "expert")


def dot(a, b, dims=((1,), (0,))):
    return lax.dot_general(a, b, (dims, ((), ())), preferred_element_type=F32)


def added(*terms):
    return sum(t.astype(F32) for t in terms).astype(BF)


class Grid:
    def __init__(self):
        self.dps, self.experts = lax.axis_size("dp"), lax.axis_size("expert")
        self.zs, self.qs = self.dps // 2, self.experts // 2
        dp, ex = lax.axis_index("dp"), lax.axis_index("expert")
        self.z, self.x, self.q, self.c = dp // 2, dp % 2, ex // 2, ex % 2

    def send(self, value, move):
        pairs = []
        for z in range(self.zs):
            for x in range(2):
                for q in range(self.qs):
                    for c in range(2):
                        to = move(z, x, q, c)
                        if to is not None:
                            pairs.append((self.flat(z, x, q, c), self.flat(*to)))
        return lax.ppermute(value, BOTH, pairs)

    def flat(self, z, x, q, c):
        return (z * 2 + x) * self.experts + q * 2 + c

    def hop(self, value, where):
        return self.send(value, lambda z, x, q, c: (where[z], x, q, c) if z in where else None)

    def line(self, shard):
        n = self.zs
        ups, downs = [shard], [shard]
        for s in range(1, n):
            ups.append(self.hop(ups[-1], {i: i + 1 for i in range(s - 1, n - 1)}))
            downs.append(self.hop(downs[-1], {i: i - 1 for i in range(1, n - s + 1)}))
        return [shard] + [jnp.where(self.z + s < n, downs[s], ups[n - s]) for s in range(1, n)]

    def straight(self, blocks):
        n = self.zs
        rows = []
        for j in range(n):
            row = blocks[j]
            for z in range(1, n):
                row = jnp.where(self.z == z, blocks[(j - z) % n], row)
            rows.append(row)
        return rows

    def line_sum(self, block):
        n = self.zs
        up, down = self.hop(block(n - 1), {0: 1}), self.hop(block(1), {n - 1: n - 2})
        for r in range(2, n):
            up = self.hop(added(block(n - r), up), {i: i + 1 for i in range(r)})
            down = self.hop(added(block(r), down), {i: i - 1 for i in range(n - r, n)})
        return added(block(0), up, down)


LANES = 256
VMEM_BYTES = 48 * 2**20


def shuffle_matrix(x, dps, hidden_width, pieces):
    block, half = hidden_width // dps, hidden_width // 2
    sources, start = [], 0
    for piece in pieces:
        unit = jnp.arange(piece * dps, dtype=jnp.int32)
        sources.append((unit // piece) * block + start + unit % piece)
        start += piece
    low = jnp.concatenate(sources)
    source = jnp.concatenate([low + x * (block // 2), low + (1 - x) * (block // 2)])
    return (jnp.arange(hidden_width, dtype=jnp.int32)[:, None] == source[None, :]).astype(BF)


def pack_kernel(pieces, x_ref, gate_ref, up_ref, down_ref, shuffle_ref, *outs):
    rows, hidden_width = gate_ref.shape
    half, block = hidden_width // 2, down_ref.shape[0]
    shuffle = shuffle_ref[...]
    gate, up = dot(gate_ref[...], shuffle).astype(BF), dot(up_ref[...], shuffle).astype(BF)
    x = x_ref[0]
    done = 0
    for number, piece in enumerate(pieces):
        units = piece * half // sum(pieces)
        count = 2 * units // LANES
        for side, start in ((0, x), (1, 1 - x)):
            ref = outs[2 * number + side]
            at = side * half + done * units // piece
            both = jnp.concatenate([gate[:, at:at + units], up[:, at:at + units]], axis=1)
            for i in range(count):
                ref[i * rows:(i + 1) * rows, :] = both[:, i * LANES:(i + 1) * LANES]
            source = pl.ds(pl.multiple_of(start * (block // 2) + done, 16), piece)
            for j in range(down_ref.shape[1] // LANES):
                to = count * rows + j * piece
                ref[to:to + piece, :] = down_ref[source, j * LANES:(j + 1) * LANES]
        done += piece


def unpack_kernel(pieces, x_ref, *refs):
    packed, (shuffle_ref, gate_ref, up_ref, down_ref) = refs[:-4], refs[-4:]
    rows, hidden_width = gate_ref.shape
    half, block = hidden_width // 2, down_ref.shape[0]
    x = x_ref[0]
    gates, ups = [[], []], [[], []]
    done = 0
    for number, piece in enumerate(pieces):
        units = piece * half // sum(pieces)
        count = 2 * units // LANES
        for side, start in ((0, x), (1, 1 - x)):
            ref = packed[2 * number + side]
            both = jnp.concatenate([ref[i * rows:(i + 1) * rows, :] for i in range(count)], axis=1)
            gates[side].append(both[:, :units])
            ups[side].append(both[:, units:])
            to = pl.ds(pl.multiple_of(start * (block // 2) + done, 16), piece)
            for j in range(down_ref.shape[1] // LANES):
                at = count * rows + j * piece
                down_ref[to, j * LANES:(j + 1) * LANES] = ref[at:at + piece, :].astype(F32)
        done += piece
    shuffle = shuffle_ref[...]
    gate_ref[...] = dot(jnp.concatenate(gates[0] + gates[1], axis=1), shuffle, ((1,), (1,)))
    up_ref[...] = dot(jnp.concatenate(ups[0] + ups[1], axis=1), shuffle, ((1,), (1,)))


def expert_kernel(
    adds, z_ref, own, up, down, up_2, down_2, last, mine, theirs, *refs
):
    earlier, refs = refs[:2 * adds], refs[2 * adds:]
    keep_out, give_out, outer_out, *refs = refs
    outs, refs = refs[:4], refs[4:]
    packed, x, grads, gate_up, w_down, pre, d_hidden, hidden, d_both, d_down, keep, give, terms, load, store = refs
    places, size, _ = packed.shape
    rows, width = x.shape
    slots = rows // 2
    line = width // places
    part_rows = line // 2
    units = w_down.shape[0]
    piece = units // places // 2
    count, columns = 2 * units // LANES, width // LANES
    size_half = size // 2
    z = z_ref[0]

    loads = [
        (mine.at[:, :width], x.at[:slots]),
        (theirs.at[:, :width], x.at[slots:]),
        (mine.at[:, width:], grads.at[:slots]),
        (theirs.at[:, width:], grads.at[slots:]),
    ]
    if adds:
        loads += [(earlier[0], keep), (earlier[1], give)]
    loads = [pltpu.make_async_copy(a, b, load.at[places + n]) for n, (a, b) in enumerate(loads)]
    for copy in loads[:2]:
        copy.start()
    pltpu.make_async_copy(own, packed.at[0], load.at[0]).start()
    for s, is_one, one, other in (
        (1, z == places - 1, last, down),
        (2, z < 2, down_2, up_2),
        (3, z == 0, last, up),
    ):
        @pl.when(is_one)
        def _():
            pltpu.make_async_copy(one, packed.at[s], load.at[s]).start()

        @pl.when(jnp.logical_not(is_one))
        def _():
            pltpu.make_async_copy(other, packed.at[s], load.at[s]).start()

    for copy in loads[2:]:
        copy.start()

    def down_rows(k, h):
        return pl.ds(pl.multiple_of(lax.rem(z + k, places) * (2 * piece) + h * piece, 16), piece)

    for copy in loads[:2]:
        copy.wait()
    for s in range(places):
        pltpu.make_async_copy(own, packed.at[s], load.at[s]).wait()
        for h in range(2):
            for i in range(count):
                at = h * size_half + i * part_rows
                to = s * line + h * part_rows
                gate_up[to:to + part_rows, i * LANES:(i + 1) * LANES] = packed[s, at:at + part_rows, :]
            for j in range(columns):
                at = h * size_half + count * part_rows + j * piece
                w_down[down_rows(s, h), j * LANES:(j + 1) * LANES] = packed[s, at:at + piece, :]
        block = slice(s * line, (s + 1) * line)
        for i in range(count):
            cols = slice(i * LANES, (i + 1) * LANES)
            product = dot(x[:, block], gate_up[block, cols])
            pre[:, cols] = product if s == 0 else pre[:, cols] + product

    step = 64 if rows % 64 == 0 else 16

    def activate(r, _):
        at = pl.ds(pl.multiple_of(r * step, 16), step)
        gate_pre, up_pre = pre[at, :units], pre[at, units:]
        sig = 1.0 / (1.0 + jnp.exp(-gate_pre))
        act = gate_pre * sig
        hidden[at, :] = (act * up_pre).astype(BF)
        pre[at, :units] = up_pre * sig * (1.0 + gate_pre * (1.0 - sig))
        pre[at, units:] = act
        return 0

    lax.fori_loop(0, rows // step, activate, 0)
    for copy in loads[2:]:
        copy.wait()
    d_hidden[...] = dot(grads[...], w_down[...], ((1,), (1,)))

    def differentiate(r, _):
        at = pl.ds(pl.multiple_of(r * step, 16), step)
        d_h = d_hidden[at, :]
        d_both[at, :units] = (d_h * pre[at, :units]).astype(BF)
        d_both[at, units:] = (d_h * pre[at, units:]).astype(BF)
        return 0

    lax.fori_loop(0, rows // step, differentiate, 0)

    def to_tokens(n, _):
        at = pl.multiple_of(n * LANES, LANES)
        cols, beyond = pl.ds(at, LANES), pl.ds(at + width, LANES)
        for to, value in (
            (cols, dot(hidden[...], w_down[:, cols])),
            (beyond, dot(d_both[...], gate_up[cols, :], ((1,), (1,)))),
        ):
            for ref, part in ((keep, value[:slots]), (give, value[slots:])):
                ref[:, to] = (part + ref[:, to].astype(F32) if adds else part).astype(BF)
        d_down[:, cols] = dot(hidden[...], grads[:, cols], ((0,), (0,))).astype(BF)
        return 0

    lax.fori_loop(0, columns, to_tokens, 0)
    stores = [pltpu.make_async_copy(keep, keep_out, store.at[0]), pltpu.make_async_copy(give, give_out, store.at[1])]
    for copy in stores:
        copy.start()

    def term(k, _):
        for h in range(2):
            from_cols = pl.ds(pl.multiple_of(k * line + h * part_rows, LANES), part_rows)
            weights = dot(x[:, from_cols], d_both[...], ((0,), (0,))).astype(BF)
            for i in range(count):
                to = h * size_half + i * part_rows
                terms[k, to:to + part_rows, :] = weights[:, i * LANES:(i + 1) * LANES]
            for j in range(columns):
                to = h * size_half + count * part_rows + j * piece
                terms[k, to:to + piece, :] = d_down[down_rows(k, h), j * LANES:(j + 1) * LANES]
        return 0

    lax.fori_loop(0, places, term, 0)
    outer_k = jnp.where(z == 0, places - 1, 1)
    stores.append(pltpu.make_async_copy(terms.at[outer_k], outer_out, store.at[2]))
    stores += [pltpu.make_async_copy(terms.at[k], out, store.at[3 + k]) for k, out in enumerate(outs)]
    for copy in stores[2:]:
        copy.start()
    for copy in stores:
        copy.wait()


def in_vmem(count):
    return [pl.BlockSpec(memory_space=pltpu.VMEM)] * count


IN_SMEM = pl.BlockSpec(memory_space=pltpu.SMEM)


def pack(pieces, x, gate, up, down, shuffle):
    rows, hidden_width = gate.shape
    sizes = [(rows * hidden_width + down.size // 2) * piece // sum(pieces) // LANES for piece in pieces]
    return pl.pallas_call(
        functools.partial(pack_kernel, pieces),
        out_shape=[jax.ShapeDtypeStruct((size, LANES), BF) for size in sizes for _ in range(2)],
        in_specs=[IN_SMEM] + in_vmem(4),
        out_specs=in_vmem(2 * len(pieces)),
        compiler_params=pltpu.CompilerParams(vmem_limit_bytes=VMEM_BYTES // 2),
    )(x, gate, up, down, shuffle)


def unpack(pieces, x, packed, shuffle, gate_shape, down_shape):
    return pl.pallas_call(
        functools.partial(unpack_kernel, pieces),
        out_shape=[jax.ShapeDtypeStruct(shape, F32) for shape in (gate_shape, gate_shape, down_shape)],
        in_specs=[IN_SMEM] + in_vmem(len(packed) + 1),
        out_specs=in_vmem(3),
        compiler_params=pltpu.CompilerParams(vmem_limit_bytes=VMEM_BYTES // 2),
    )(x, *packed, shuffle)


def expert(z, places, units, weights, mine, theirs, earlier=()):
    size = weights[0].shape[0]
    slots, width = mine.shape[0], mine.shape[1] // 2
    rows = 2 * slots
    row_shape, term_shape = jax.ShapeDtypeStruct(mine.shape, BF), jax.ShapeDtypeStruct((size, LANES), BF)
    return pl.pallas_call(
        functools.partial(expert_kernel, len(earlier) // 2),
        out_shape=[row_shape] * 2 + [term_shape] * 5,
        in_specs=[IN_SMEM] + [pl.BlockSpec(memory_space=pl.ANY)] * (8 + len(earlier)),
        out_specs=[pl.BlockSpec(memory_space=pl.ANY)] * 7,
        scratch_shapes=[
            pltpu.VMEM((places, size, LANES), BF),
            pltpu.VMEM((rows, width), BF),
            pltpu.VMEM((rows, width), BF),
            pltpu.VMEM((width, 2 * units), BF),
            pltpu.VMEM((units, width), BF),
            pltpu.VMEM((rows, 2 * units), F32),
            pltpu.VMEM((rows, units), F32),
            pltpu.VMEM((rows, units), BF),
            pltpu.VMEM((rows, 2 * units), BF),
            pltpu.VMEM((units, width), BF),
            pltpu.VMEM((slots, 2 * width), BF),
            pltpu.VMEM((slots, 2 * width), BF),
            pltpu.VMEM((places, size, LANES), BF),
            pltpu.SemaphoreType.DMA((places + 6,)),
            pltpu.SemaphoreType.DMA((7,)),
        ],
        compiler_params=pltpu.CompilerParams(vmem_limit_bytes=VMEM_BYTES),
        cost_estimate=pl.CostEstimate(
            flops=18 * rows * width * units, bytes_accessed=16 * 2**20, transcendentals=rows * units
        ),
    )(z, *weights, mine, theirs, *earlier)


def local(tokens, expert_ids, gate_probs, w_gate, w_up, w_down, d_out):
    g = Grid()
    rows, topk = expert_ids.shape
    width = tokens.shape[1]
    hidden_width = w_gate.shape[2]
    half = hidden_width // 2
    experts = g.experts
    cap = rows * topk * 9 // (8 * experts)
    slots = experts * cap
    first = g.c == 0
    even = g.x == 0

    block = hidden_width // g.dps
    part = block // 2
    pieces = (2 * part // 3, part // 3)
    in_kernels = g.zs == 4 and slots % 16 == 0 and part % 48 == 0 and all(2 * p * g.dps % LANES == 0 for p in pieces)
    if not in_kernels:
        pieces = (part,)
    shuffle = shuffle_matrix(g.x, g.dps, hidden_width, pieces)

    def out_a(z, x, q, c):
        return z, c, q, x

    def out_b(z, x, q, c):
        return z, c, q, 1 - x

    def back_a(z, x, q, c):
        return z, c, q, x

    def back_b(z, x, q, c):
        return z, 1 - c, q, x

    def spread(part_a, part_b):
        got_a, got_b = g.send(part_a, out_a), g.send(part_b, out_b)
        return jnp.concatenate([jnp.where(first, got_a, got_b), jnp.where(first, got_b, got_a)], axis=0)

    def unspread(both):
        n = both.shape[0] // 2
        low, high = both[:n], both[n:]
        return g.send(jnp.where(first, low, high), back_a), g.send(jnp.where(first, high, low), back_b)

    expert_iota = jnp.arange(experts, dtype=jnp.int32)
    chosen = expert_ids[:, :, None] == expert_iota
    named = jnp.any(chosen, axis=1).astype(BF)
    token_iota = jnp.arange(rows, dtype=jnp.int32)
    earlier = (token_iota[:, None] > token_iota[None, :]).astype(BF)
    before = dot(earlier, named)
    slot = jnp.sum(jnp.where(chosen, before[:, None, :], 0.0), axis=2).astype(jnp.int32)
    relative = ((expert_ids // 2 - g.q + g.qs) % g.qs) * 2 + ((expert_ids % 2) ^ g.x)
    dest = relative * cap + slot
    slot_iota = jnp.arange(slots, dtype=jnp.int32)
    pair = dest[:, :, None] == slot_iota
    placing = jnp.any(pair, axis=1).astype(BF)
    weighted = jnp.sum(jnp.where(pair, gate_probs[:, :, None], 0.0), axis=1)
    slot_probs = jnp.sum(weighted, axis=0)

    def member(r, sign):
        def move(z, x, q, c):
            return z, x ^ (r % 2), (q + sign * (r // 2)) % g.qs, c

        return move

    def other_core(z, x, q, c):
        return z, x, q, 1 - c

    def exchange(value, sign):
        got = [value[:cap]] + [g.send(value[r * cap:(r + 1) * cap], member(r, sign)) for r in range(1, experts)]
        return jnp.concatenate(got, axis=0)

    line_width = width // g.zs
    turned = lax.dynamic_slice(jnp.concatenate([tokens, tokens], axis=1), (0, g.z * line_width), (rows, width))
    sent = jnp.concatenate(
        [
            dot(placing, turned, ((0,), (0,))).astype(BF),
            (slot_probs[:, None] * dot(placing, d_out, ((0,), (0,)))).astype(BF),
        ],
        axis=1,
    )
    shapes = w_gate.shape[1:], w_down.shape[1:]
    together = lax.optimization_barrier
    if in_kernels:
        place_x, place_z = g.x.reshape(1).astype(jnp.int32), g.z.reshape(1).astype(jnp.int32)
        units = [piece * g.dps for piece in pieces]
        a, b, a2, b2 = pack(pieces, place_x, w_gate[0], w_up[0], w_down[0], shuffle)
        ups, downs, passing = {0: 1, 1: 2, 2: 3}, {1: 0, 2: 1, 3: 2}, {2: 3, 1: 0}
        outward, inward_up, inward_down = {0: 1, 3: 2}, {0: 1, 1: 2}, {3: 2, 2: 1}
        to_last = g.z == 2

        shard, a2, b2 = together((spread(a, b), a2, b2))
        up, down = g.hop(shard, ups), g.hop(shard, downs)
        shard2, sent = together((spread(a2, b2), sent))
        up, down, shard2 = together((up, down, shard2))
        up_2, down_2 = g.hop(up, {1: 2, 2: 3}), g.hop(down, {1: 0, 2: 1})
        up2, down2 = g.hop(shard2, ups), g.hop(shard2, downs)
        up_2, down_2, mine = together((up_2, down_2, exchange(sent, 1)))
        theirs = g.send(mine, other_core)
        last = g.hop(jnp.where(to_last, up_2, down_2), passing)
        up2, down2, up_2, down_2 = together((up2, down2, up_2, down_2))
        up2_2, down2_2 = g.hop(up2, {1: 2, 2: 3}), g.hop(down2, {1: 0, 2: 1})
        keep, give, outer, *terms = expert(
            place_z, g.zs, units[0], (shard, up, down, up_2, down_2, last), mine, theirs
        )
        up2_2, down2_2, outer, keep, give = together((up2_2, down2_2, outer, keep, give))
        last2 = g.hop(jnp.where(to_last, up2_2, down2_2), passing)
        begun = g.hop(outer, outward)
        keep, give, outer2, *terms2 = expert(
            place_z, g.zs, units[1], (shard2, up2, down2, up2_2, down2_2, last2), mine, theirs, (keep, give)
        )
        begun, give, outer2 = together((begun, give, outer2))
        middle = added(terms[2], begun)
        sum_up, sum_down = g.hop(middle, inward_up), g.hop(middle, inward_down)
        given = g.send(give, other_core)
        begun2 = g.hop(outer2, outward)
        sum_up, sum_down, keep = together((sum_up, sum_down, keep))
        sum_up, sum_down = g.hop(added(terms[1], sum_up), ups), g.hop(added(terms[3], sum_down), downs)
        begun2, given, keep = together((begun2, given, keep))
        middle2, sums = together((added(terms2[2], begun2), added(keep, given)))
        sum_up2, sum_down2 = g.hop(middle2, inward_up), g.hop(middle2, inward_down)
        sums = sums.reshape(g.qs, 2, cap, 2 * width)
        near = jnp.stack([sums[:, 0], g.send(sums[:, 1], lambda z, x, q, c: (z, 1 - x, q, c))], axis=1)
        sum_up, sum_down = together((sum_up, sum_down))
        grad = added(terms[0], sum_up, sum_down)
        sum_up2, sum_down2, near = together((sum_up2, sum_down2, near))
        sum_up2, sum_down2 = g.hop(added(terms2[1], sum_up2), ups), g.hop(added(terms2[3], sum_down2), downs)
        got = jnp.concatenate(
            [near[0]] + [g.send(near[d], lambda z, x, q, c, d=d: (z, x, (q - d) % g.qs, c)) for d in range(1, g.qs)]
        ).reshape(slots, 2 * width)
        grads = unspread(grad)
        sum_up2, sum_down2, got, grads = together((sum_up2, sum_down2, got, grads))
        grads += unspread(added(terms2[0], sum_up2, sum_down2))
        d_w_gate, d_w_up, d_w_down = unpack(pieces, place_x, grads, shuffle, *shapes)
    else:
        gate_cols, up_cols = dot(w_gate[0], shuffle).astype(BF), dot(w_up[0], shuffle).astype(BF)
        gate_up_shard = spread(
            jnp.concatenate([gate_cols[:, :half], up_cols[:, :half]], axis=1),
            jnp.concatenate([gate_cols[:, half:], up_cols[:, half:]], axis=1),
        )
        down_low, down_high = w_down[0, :part], w_down[0, part:]
        down_shard = spread(jnp.where(even, down_low, down_high), jnp.where(even, down_high, down_low))
        gate_up = jnp.concatenate(g.line(gate_up_shard), axis=0)
        down = jnp.concatenate(g.straight(g.line(down_shard)), axis=0)
        mine = exchange(sent, 1)
        inputs = jnp.concatenate([mine, g.send(mine, other_core)], axis=0)
        arrived, d_produced = inputs[:, :width], inputs[:, width:]
        pre = dot(arrived, gate_up)
        gate_pre, up_pre = pre[:, :half], pre[:, half:]
        sig = jax.nn.sigmoid(gate_pre)
        act = gate_pre * sig
        hidden = (act * up_pre).astype(BF)
        d_hidden = dot(d_produced, down, ((1,), (1,)))
        d_gate = (d_hidden * up_pre * sig * (1.0 + gate_pre * (1.0 - sig))).astype(BF)
        d_up = (d_hidden * act).astype(BF)
        d_both = jnp.concatenate([d_gate, d_up], axis=1)
        down_part = dot(hidden, d_produced, ((0,), (0,))).astype(BF)
        both_part = dot(arrived, d_both, ((0,), (0,))).astype(BF)
        partial = jnp.concatenate([dot(hidden, down), dot(d_both, gate_up, ((1,), (1,)))], axis=1).astype(BF)
        got = exchange(added(partial[:slots], g.send(partial[slots:], other_core)), -1)
        down_a, down_b = unspread(
            g.line_sum(
                lambda k: lax.dynamic_slice_in_dim(down_part, ((g.z + k) % g.zs) * (2 * part), 2 * part)
            )
        )
        d_w_down = jnp.where(
            even, jnp.concatenate([down_a, down_b], axis=0), jnp.concatenate([down_b, down_a], axis=0)
        ).astype(F32)
        both_a, both_b = unspread(g.line_sum(lambda k: both_part[k * line_width:(k + 1) * line_width]))
        d_w_gate, d_w_up = (
            dot(jnp.concatenate([both_a[:, cols], both_b[:, cols]], axis=1), shuffle, ((1,), (1,)))
            for cols in (slice(0, half), slice(half, None))
        )
    returned, back_rows = got[:, :width], got[:, width:]

    high = lax.reduce_precision(weighted, 8, 7)
    mixed = (dot(high.astype(BF), returned) + dot((weighted - high).astype(BF), returned)).astype(BF)
    products = dot(d_out, returned, ((1,), (1,)))
    d_probs = jnp.sum(jnp.where(pair, products[:, None, :], 0.0), axis=2)
    d_turned = dot(placing, back_rows).astype(BF)
    d_tokens = lax.dynamic_slice(
        jnp.concatenate([d_turned, d_turned], axis=1), (0, (g.zs - g.z) * line_width), (rows, width)
    )

    return (mixed, d_tokens, d_probs, d_w_gate[None], d_w_up[None], d_w_down[None])


def solution(mesh):
    rows = P(("dp", "expert"), None)
    weight = P("expert", "dp", None)
    return jax.shard_map(
        local,
        mesh=mesh,
        in_specs=(rows, rows, rows, weight, weight, weight, rows),
        out_specs=(rows, rows, rows, weight, weight, weight),
        check_vma=False,
    )
```

time: 287 us -> 262 us (0.913)
  waiting for transfers between devices: 189 us -> 127 us
  starting transfers between devices: 42.7 us -> 74.2 us
  Pallas kernels: 19.9 us -> 27.1 us
  other arithmetic: 18.7 us -> 15.7 us
    ppermute x23 -> x35, waiting for transfers between devices: 189 us -> 127 us  [send(): return lax.ppermute(value, BOTH, pairs)]
    ppermute x23 -> x35, starting transfers between devices: 42.7 us -> 74.2 us  [send(): return lax.ppermute(value, BOTH, pairs)]
    pallas_call x3 -> x4, Pallas kernels: 19.9 us -> 27.1 us  [the longest x2 24.3 us: expert(): pl.pallas_call(functools.partial(expert_kernel, len(earlier) // 2), out_s...]
    unnamed x28 -> x49, local copies, waits for them, and re-layouts: 5.82 us -> 8.26 us
    convert_element_type x3 -> x9, other arithmetic: 7.13 us -> 6.22 us  [added(): return sum((t.astype(F32) for t in terms)).astype(BF)]
  transfers between devices with their start and end apart: 23 -> 35, of which waited for: 14 -> 20; matrix products, arithmetic and copies ran while one was open for 6% -> 7% of each run, Pallas kernels for 0% -> 9%
where the time goes in v7:
time: 262 us; the launch traced here: 259 us
  waiting for transfers between devices  127 us (48%)
  starting transfers between devices  74.2 us (28%)
  Pallas kernels  27.1 us (10%)
  other arithmetic  15.7 us (6%)
  local copies, waits for them, and re-layouts  8.62 us (3%)
  matrix products  5.73 us (2%)
    ppermute x35, waiting for transfers between devices, send(): return lax.ppermute(value, BOTH, pairs)  127 us
    ppermute x35, starting transfers between devices, send(): return lax.ppermute(value, BOTH, pairs)  74.2 us
    pallas_call x2, Pallas kernels, expert(): pl.pallas_call(functools.partial(expert_kernel, len(earlier) // 2), out_s...  24.3 us
    unnamed x49, local copies, waits for them, and re-layouts  8.26 us
    convert_element_type x9, other arithmetic, added(): return sum((t.astype(F32) for t in terms)).astype(BF)  6.22 us
    dot_general x7, matrix products, dot(): return lax.dot_general(a, b, (dims, ((), ())), preferred_element_type=F32)  5.73 us
  transfers between devices with their start and end apart: 35, of which 20 were waited for; matrix products, arithmetic and copies ran while one was open for 7% of the time, Pallas kernels for 9%

profile of v7, /device:TPU:9, one launch (start us, length us, event | category | flops | bytes accessed | tf_op | source)
XLA Modules:
  0.0 259.2 jit_solution(7541618939537329587)
XLA Ops:
  4.9 3.7 %collective-permute-start = (bf16[768,256]{1,0:T(8,128)(2,1)S(1)}, bf16[768,256]{1,0:T(8,128)(2,1)}, u32[]{:S(2)}, u32[]{:S(2)}) collective-permute-start(bf16[768,256]{1,0:T(8,128)(2,1)S(1)} %get-tuple-element.68), channel_id=1, source_target_pairs={{0,0},{1,4},{2,2},{3,6},{4,1},{5,5},{6,3},{7,7},{8,8},{9,12},{10,1... | collective-permute-start | bytes 1179656 | tf_op jit(solution)/shard_map/ppermute | solution.py:39
  14.2 3.4 %collective-permute-done.1 = bf16[768,256]{1,0:T(8,128)(2,1)} collective-permute-done((bf16[768,256]{1,0:T(8,128)(2,1)S(1)}, bf16[768,256]{1,0:T(8,128)(2,1)}, u32[]{:S(2)}, u32[]{:S(2)}) %collective-permute-start.1) | collective-permute-done | bytes 393248 | tf_op jit(solution)/shard_map/ppermute | solution.py:39
  18.8 2.5 collective-permute-start.4
  21.7 3.2 %collective-permute-start.2 = (bf16[1536,256]{1,0:T(8,128)(2,1)S(1)}, bf16[1536,256]{1,0:T(8,128)(2,1)S(1)}, u32[]{:S(2)}, u32[]{:S(2)}) collective-permute-start(bf16[1536,256]{1,0:T(8,128)(2,1)S(1)} %pad_maximum_fusion.4.own), channel_id=1, source_target_pairs={{0,8},{1,9},{2,10},{3,11},{4,12},{5,13},{6,14},{7,15},{8,16},{9,17... | collective-permute-start | bytes 2359304 | tf_op jit(solution)/shard_map/ppermute | solution.py:39
  24.9 2.1 collective-permute-start.3
  30.1 12.4 %collective-permute-done.2.up = bf16[1536,256]{1,0:T(8,128)(2,1)S(1)} collective-permute-done((bf16[1536,256]{1,0:T(8,128)(2,1)S(1)}, bf16[1536,256]{1,0:T(8,128)(2,1)S(1)}, u32[]{:S(2)}, u32[]{:S(2)}) %collective-permute-start.2) | collective-permute-done | bytes 786464 | tf_op jit(solution)/shard_map/ppermute | solution.py:39
  42.4 2.9 %collective-permute-done.3.down = bf16[1536,256]{1,0:T(8,128)(2,1)S(1)} collective-permute-done((bf16[1536,256]{1,0:T(8,128)(2,1)S(1)}, bf16[1536,256]{1,0:T(8,128)(2,1)S(1)}, u32[]{:S(2)}, u32[]{:S(2)}) %collective-permute-start.3) | collective-permute-done | bytes 786464 | tf_op jit(solution)/shard_map/ppermute | solution.py:39
  45.3 3.2 %collective-permute-start.8 = (bf16[1536,256]{1,0:T(8,128)(2,1)S(1)}, bf16[1536,256]{1,0:T(8,128)(2,1)S(1)}, u32[]{:S(2)}, u32[]{:S(2)}) collective-permute-start(bf16[1536,256]{1,0:T(8,128)(2,1)S(1)} %collective-permute-done.2.up), channel_id=1, source_target_pairs={{8,16},{9,17},{10,18},{11,19},{12,20},{13,21},{14,22},{15,23},{16,... | collective-permute-start | bytes 2359304 | tf_op jit(solution)/shard_map/ppermute | solution.py:39
  50.5 5.7 %collective-permute-done.11 = bf16[72,4096]{1,0:T(8,128)(2,1)S(1)} collective-permute-done((bf16[72,4096]{1,0:T(8,128)(2,1)S(1)}, bf16[72,4096]{1,0:T(8,128)(2,1)S(1)}, u32[]{:S(2)}, u32[]{:S(2)}) %collective-permute-start.11) | collective-permute-done | bytes 589856 | tf_op jit(solution)/shard_map/ppermute | solution.py:39
  57.9 6.0 %collective-permute-done.8.up_2 = bf16[1536,256]{1,0:T(8,128)(2,1)S(1)} collective-permute-done((bf16[1536,256]{1,0:T(8,128)(2,1)S(1)}, bf16[1536,256]{1,0:T(8,128)(2,1)S(1)}, u32[]{:S(2)}, u32[]{:S(2)}) %collective-permute-start.8) | collective-permute-done | bytes 786464 | tf_op jit(solution)/shard_map/ppermute | solution.py:39
  64.8 3.0 %collective-permute-done.9.down_2 = bf16[1536,256]{1,0:T(8,128)(2,1)S(1)} collective-permute-done((bf16[1536,256]{1,0:T(8,128)(2,1)S(1)}, bf16[1536,256]{1,0:T(8,128)(2,1)S(1)}, u32[]{:S(2)}, u32[]{:S(2)}) %collective-permute-start.9) | collective-permute-done | bytes 786464 | tf_op jit(solution)/shard_map/ppermute | solution.py:39
  68.7 2.7 %collective-permute-start.16 = (bf16[288,4096]{1,0:T(8,128)(2,1)}, bf16[288,4096]{1,0:T(8,128)(2,1)}, u32[]{:S(2)}, u32[]{:S(2)}) collective-permute-start(bf16[288,4096]{1,0:T(8,128)(2,1)} %pad_maximum_fusion.1.mine), channel_id=1, source_target_pairs={{0,1},{1,0},{2,3},{3,2},{4,5},{5,4},{6,7},{7,6},{8,9},{9,8},{10,11... | collective-permute-start | bytes 7077896 | tf_op jit(solution)/shard_map/ppermute | solution.py:39
  76.5 3.4 %collective-permute-start.7 = (bf16[768,256]{1,0:T(8,128)(2,1)S(1)}, bf16[768,256]{1,0:T(8,128)(2,1)S(1)}, u32[]{:S(2)}, u32[]{:S(2)}) collective-permute-start(bf16[768,256]{1,0:T(8,128)(2,1)S(1)} %pad_maximum_fusion.5.own), channel_id=1, source_target_pairs={{8,0},{9,1},{10,2},{11,3},{12,4},{13,5},{14,6},{15,7},{16,8},{17,9... | collective-permute-start | bytes 1179656 | tf_op jit(solution)/shard_map/ppermute | solution.py:39
  79.9 7.0 %collective-permute-done.6.up = bf16[768,256]{1,0:T(8,128)(2,1)S(1)} collective-permute-done((bf16[768,256]{1,0:T(8,128)(2,1)S(1)}, bf16[768,256]{1,0:T(8,128)(2,1)S(1)}, u32[]{:S(2)}, u32[]{:S(2)}) %collective-permute-start.6) | collective-permute-done | bytes 393248 | tf_op jit(solution)/shard_map/ppermute | solution.py:39
  86.9 13.0 %collective-permute-done.7.down = bf16[768,256]{1,0:T(8,128)(2,1)S(1)} collective-permute-done((bf16[768,256]{1,0:T(8,128)(2,1)S(1)}, bf16[768,256]{1,0:T(8,128)(2,1)S(1)}, u32[]{:S(2)}, u32[]{:S(2)}) %collective-permute-start.7) | collective-permute-done | bytes 393248 | tf_op jit(solution)/shard_map/ppermute | solution.py:39
  101.2 3.5 %collective-permute-start.14 = (bf16[768,256]{1,0:T(8,128)(2,1)S(1)}, bf16[768,256]{1,0:T(8,128)(2,1)S(1)}, u32[]{:S(2)}, u32[]{:S(2)}) collective-permute-start(bf16[768,256]{1,0:T(8,128)(2,1)S(1)} %collective-permute-done.7.down), channel_id=1, source_target_pairs={{8,0},{9,1},{10,2},{11,3},{12,4},{13,5},{14,6},{15,7},{16,8},{17,9... | collective-permute-start | bytes 1179656 | tf_op jit(solution)/shard_map/ppermute | solution.py:39
  105.6 12.8 %shard_map.119 = (bf16[288,4096]{1,0:T(8,128)(2,1)}, bf16[288,4096]{1,0:T(8,128)(2,1)}, bf16[1536,256]{1,0:T(8,128)(2,1)S(1)}, bf16[1536,256]{1,0:T(8,128)(2,1)S...) custom-call(s32[1]{0:T(128)} %bitcast.z_ref, ...), custom_call_target="tpu_custom_call" | custom-call | flops 5435817984 | bytes 16777216 | tf_op jit(solution)/shard_map/pallas_call | solution.py:304
  120.6 4.1 %collective-permute-start.17 = (bf16[768,256]{1,0:T(8,128)(2,1)S(1)}, bf16[768,256]{1,0:T(8,128)(2,1)S(1)}, u32[]{:S(2)}, u32[]{:S(2)}) collective-permute-start(bf16[768,256]{1,0:T(8,128)(2,1)S(1)} %broadcast_select_fusion.1), channel_id=1, source_target_pairs={{8,0},{9,1},{10,2},{11,3},{12,4},{13,5},{14,6},{15,7},{16,24},{17,... | collective-permute-start | bytes 1179656 | tf_op jit(solution)/shard_map/ppermute | solution.py:39
  124.7 7.0 %collective-permute-done.17.last = bf16[768,256]{1,0:T(8,128)(2,1)S(1)} collective-permute-done((bf16[768,256]{1,0:T(8,128)(2,1)S(1)}, bf16[768,256]{1,0:T(8,128)(2,1)S(1)}, u32[]{:S(2)}, u32[]{:S(2)}) %collective-permute-start.17) | collective-permute-done | bytes 393248 | tf_op jit(solution)/shard_map/ppermute | solution.py:39
  131.7 11.5 %shard_map.120 = (bf16[288,4096]{1,0:T(8,128)(2,1)}, bf16[288,4096]{1,0:T(8,128)(2,1)}, bf16[768,256]{1,0:T(8,128)(2,1)S(1)}, bf16[768,256]{1,0:T(8,128)(2,1)S(1...) custom-call(s32[1]{0:T(128)} %bitcast.z_ref, ...), custom_call_target="tpu_custom_call" | custom-call | flops 2717908992 | bytes 16777216 | tf_op jit(solution)/shard_map/pallas_call | solution.py:304
  143.3 2.3 collective-permute-start.20
  150.4 16.8 %collective-permute-done.21 = bf16[1536,256]{1,0:T(8,128)(2,1)S(1)} collective-permute-done((bf16[1536,256]{1,0:T(8,128)(2,1)S(1)}, bf16[1536,256]{1,0:T(8,128)(2,1)S(1)}, u32[]{:S(2)}, u32[]{:S(2)}) %collective-permute-start.21) | collective-permute-done | bytes 786464 | tf_op jit(solution)/shard_map/ppermute | solution.py:39
  169.7 2.2 collective-permute-start.29
  173.0 4.1 %collective-permute-start.30 = (bf16[1536,256]{1,0:T(8,128)(2,1)}, bf16[1536,256]{1,0:T(8,128)(2,1)}, u32[]{:S(2)}, u32[]{:S(2)}) collective-permute-start(bf16[1536,256]{1,0:T(8,128)(2,1)} %add_convert_fusion.2), channel_id=1, source_target_pairs={{8,0},{9,1},{10,2},{11,3},{12,4},{13,5},{14,6},{15,7},{16,8},{17,9... | collective-permute-start | bytes 2359304 | tf_op jit(solution)/shard_map/ppermute | solution.py:39
  181.8 10.7 %collective-permute-done.29 = bf16[1536,256]{1,0:T(8,128)(2,1)} collective-permute-done((bf16[1536,256]{1,0:T(8,128)(2,1)}, bf16[1536,256]{1,0:T(8,128)(2,1)}, u32[]{:S(2)}, u32[]{:S(2)}) %collective-permute-start.29) | collective-permute-done | bytes 786464 | tf_op jit(solution)/shard_map/ppermute | solution.py:39
  195.1 5.0 %collective-permute-start.31 = (bf16[768,256]{1,0:T(8,128)(2,1)S(1)}, bf16[768,256]{1,0:T(8,128)(2,1)S(1)}, u32[]{:S(2)}, u32[]{:S(2)}) collective-permute-start(bf16[768,256]{1,0:T(8,128)(2,1)S(1)} %get-tuple-element.139), channel_id=1, source_target_pairs={{0,0},{1,4},{2,2},{3,6},{4,1},{5,5},{6,3},{7,7},{8,8},{9,12},{10,1... | collective-permute-start | bytes 1179656 | tf_op jit(solution)/shard_map/ppermute | solution.py:39
  203.3 3.5 %collective-permute-done.25 = bf16[2,72,4096]{2,1,0:T(8,128)(2,1)} collective-permute-done((bf16[2,72,4096]{2,1,0:T(8,128)(2,1)}, bf16[2,72,4096]{2,1,0:T(8,128)(2,1)}, u32[]{:S(2)}, u32[]{:S(2)}) %collective-permute-start.25) | collective-permute-done | bytes 1179680 | tf_op jit(solution)/shard_map/ppermute | solution.py:39
  208.3 4.2 %collective-permute-done.23 = bf16[768,256]{1,0:T(8,128)(2,1)S(1)} collective-permute-done((bf16[768,256]{1,0:T(8,128)(2,1)S(1)}, bf16[768,256]{1,0:T(8,128)(2,1)S(1)}, u32[]{:S(2)}, u32[]{:S(2)}) %collective-permute-start.23) | collective-permute-done | bytes 393248 | tf_op jit(solution)/shard_map/ppermute | solution.py:39
  217.7 3.4 %collective-permute-start.27 = (bf16[768,256]{1,0:T(8,128)(2,1)S(1)}, bf16[768,256]{1,0:T(8,128)(2,1)S(1)}, u32[]{:S(2)}, u32[]{:S(2)}) collective-permute-start(bf16[768,256]{1,0:T(8,128)(2,1)S(1)} %add_convert_fusion.6), channel_id=1, source_target_pairs={{8,0},{9,1},{10,2},{11,3},{12,4},{13,5},{14,6},{15,7},{16,8},{17,9... | collective-permute-start | bytes 1179656 | tf_op jit(solution)/shard_map/ppermute | solution.py:39
  221.3 21.4 %collective-permute-done.28 = bf16[2,72,4096]{2,1,0:T(8,128)(2,1)S(1)} collective-permute-done((bf16[2,72,4096]{2,1,0:T(8,128)(2,1)S(1)}, bf16[2,72,4096]{2,1,0:T(8,128)(2,1)S(1)}, u32[]{:S(2)}, u32[]{:S(2)}) %collective-permute-start.28) | collective-permute-done | bytes 1179680 | tf_op jit(solution)/shard_map/ppermute | solution.py:39
  246.5 5.3 %collective-permute-start.33 = (bf16[384,256]{1,0:T(8,128)(2,1)S(1)}, bf16[384,256]{1,0:T(8,128)(2,1)S(1)}, u32[]{:S(2)}, u32[]{:S(2)}) collective-permute-start(bf16[384,256]{1,0:T(8,128)(2,1)S(1)} %get-tuple-element.143), channel_id=1, source_target_pairs={{0,0},{1,4},{2,2},{3,6},{4,1},{5,5},{6,3},{7,7},{8,8},{9,12},{10,1... | collective-permute-start | bytes 589832 | tf_op jit(solution)/shard_map/ppermute | solution.py:39
  252.9 3.1 %collective-permute-done.33.refs_2_ = bf16[384,256]{1,0:T(8,128)(2,1)S(1)} collective-permute-done((bf16[384,256]{1,0:T(8,128)(2,1)S(1)}, bf16[384,256]{1,0:T(8,128)(2,1)S(1)}, u32[]{:S(2)}, u32[]{:S(2)}) %collective-permute-start.33) | collective-permute-done | bytes 196640 | tf_op jit(solution)/shard_map/ppermute | solution.py:39
  (134 shorter events, 62.9 us)
Async XLA Ops:
  4.9 9.2 %collective-permute-start = (bf16[768,256]{1,0:T(8,128)(2,1)S(1)}, bf16[768,256]{1,0:T(8,128)(2,1)}, u32[]{:S(2)}, u32[]{:S(2)}) collective-permute-start(bf16[768,256]{1,0:T(8,128)(2,1)S(1)} %get-tuple-element.68), channel_id=1, source_target_pairs={{0,0},{1,4},{2,2},{3,6},{4,1},{5,5},{6,3},{7,7},{8,8},{9,12},{10,1... | collective-permute-start | bytes 1179656 | tf_op jit(solution)/shard_map/ppermute | solution.py:39
  8.6 8.9 %collective-permute-start.1 = (bf16[768,256]{1,0:T(8,128)(2,1)S(1)}, bf16[768,256]{1,0:T(8,128)(2,1)}, u32[]{:S(2)}, u32[]{:S(2)}) collective-permute-start(bf16[768,256]{1,0:T(8,128)(2,1)S(1)} %get-tuple-element.69), channel_id=1, source_target_pairs={{0,1},{1,5},{2,3},{3,7},{4,0},{5,4},{6,2},{7,6},{8,9},{9,13},{10,1... | collective-permute-start | bytes 1179656 | tf_op jit(solution)/shard_map/ppermute | solution.py:39
  21.7 20.7 %collective-permute-start.2 = (bf16[1536,256]{1,0:T(8,128)(2,1)S(1)}, bf16[1536,256]{1,0:T(8,128)(2,1)S(1)}, u32[]{:S(2)}, u32[]{:S(2)}) collective-permute-start(bf16[1536,256]{1,0:T(8,128)(2,1)S(1)} %pad_maximum_fusion.4.own), channel_id=1, source_target_pairs={{0,8},{1,9},{2,10},{3,11},{4,12},{5,13},{6,14},{7,15},{8,16},{9,17... | collective-permute-start | bytes 2359304 | tf_op jit(solution)/shard_map/ppermute | solution.py:39
  24.9 20.4 %collective-permute-start.3 = (bf16[1536,256]{1,0:T(8,128)(2,1)S(1)}, bf16[1536,256]{1,0:T(8,128)(2,1)S(1)}, u32[]{:S(2)}, u32[]{:S(2)}) collective-permute-start(bf16[1536,256]{1,0:T(8,128)(2,1)S(1)} %pad_maximum_fusion.4.own), channel_id=1, source_target_pairs={{8,0},{9,1},{10,2},{11,3},{12,4},{13,5},{14,6},{15,7},{16,8},{17,9... | collective-permute-start | bytes 2359304 | tf_op jit(solution)/shard_map/ppermute | solution.py:39
  27.4 23.2 %collective-permute-start.12 = (bf16[72,4096]{1,0:T(8,128)(2,1)S(1)}, bf16[72,4096]{1,0:T(8,128)(2,1)S(1)}, u32[]{:S(2)}, u32[]{:S(2)}) collective-permute-start(bf16[72,4096]{1,0:T(8,128)(2,1)S(1)} %get-tuple-element.135), channel_id=1, source_target_pairs={{0,6},{1,7},{2,4},{3,5},{4,2},{5,3},{6,0},{7,1},{8,14},{9,15},{10,... | collective-permute-start | bytes 1769480 | tf_op jit(solution)/shard_map/ppermute | solution.py:39
  29.5 26.7 %collective-permute-start.11 = (bf16[72,4096]{1,0:T(8,128)(2,1)S(1)}, bf16[72,4096]{1,0:T(8,128)(2,1)S(1)}, u32[]{:S(2)}, u32[]{:S(2)}) collective-permute-start(bf16[72,4096]{1,0:T(8,128)(2,1)S(1)} %get-tuple-element.136), channel_id=1, source_target_pairs={{0,2},{1,3},{2,0},{3,1},{4,6},{5,7},{6,4},{7,5},{8,10},{9,11},{10,... | collective-permute-start | bytes 1769480 | tf_op jit(solution)/shard_map/ppermute | solution.py:39
  29.7 26.5 %collective-permute-start.10 = (bf16[72,4096]{1,0:T(8,128)(2,1)S(1)}, bf16[72,4096]{1,0:T(8,128)(2,1)S(1)}, u32[]{:S(2)}, u32[]{:S(2)}) collective-permute-start(bf16[72,4096]{1,0:T(8,128)(2,1)S(1)} %get-tuple-element.137), channel_id=1, source_target_pairs={{0,4},{1,5},{2,6},{3,7},{4,0},{5,1},{6,2},{7,3},{8,12},{9,13},{10,... | collective-permute-start | bytes 1769480 | tf_op jit(solution)/shard_map/ppermute | solution.py:39
  45.3 18.5 %collective-permute-start.8 = (bf16[1536,256]{1,0:T(8,128)(2,1)S(1)}, bf16[1536,256]{1,0:T(8,128)(2,1)S(1)}, u32[]{:S(2)}, u32[]{:S(2)}) collective-permute-start(bf16[1536,256]{1,0:T(8,128)(2,1)S(1)} %collective-permute-done.2.up), channel_id=1, source_target_pairs={{8,16},{9,17},{10,18},{11,19},{12,20},{13,21},{14,22},{15,23},{16,... | collective-permute-start | bytes 2359304 | tf_op jit(solution)/shard_map/ppermute | solution.py:39
  48.6 19.2 %collective-permute-start.9 = (bf16[1536,256]{1,0:T(8,128)(2,1)S(1)}, bf16[1536,256]{1,0:T(8,128)(2,1)S(1)}, u32[]{:S(2)}, u32[]{:S(2)}) collective-permute-start(bf16[1536,256]{1,0:T(8,128)(2,1)S(1)} %collective-permute-done.3.down), channel_id=1, source_target_pairs={{8,0},{9,1},{10,2},{11,3},{12,4},{13,5},{14,6},{15,7},{16,8},{17,9... | collective-permute-start | bytes 2359304 | tf_op jit(solution)/shard_map/ppermute | solution.py:39
  68.7 36.1 %collective-permute-start.16 = (bf16[288,4096]{1,0:T(8,128)(2,1)}, bf16[288,4096]{1,0:T(8,128)(2,1)}, u32[]{:S(2)}, u32[]{:S(2)}) collective-permute-start(bf16[288,4096]{1,0:T(8,128)(2,1)} %pad_maximum_fusion.1.mine), channel_id=1, source_target_pairs={{0,1},{1,0},{2,3},{3,2},{4,5},{5,4},{6,7},{7,6},{8,9},{9,8},{10,11... | collective-permute-start | bytes 7077896 | tf_op jit(solution)/shard_map/ppermute | solution.py:39
  72.6 32.1 %collective-permute-start.15 = (bf16[1536,256]{1,0:T(8,128)(2,1)S(1)}, bf16[1536,256]{1,0:T(8,128)(2,1)S(1)}, u32[]{:S(2)}, u32[]{:S(2)}) collective-permute-start(bf16[1536,256]{1,0:T(8,128)(2,1)S(1)} %broadcast_select_fusion), channel_id=1, source_target_pairs={{8,0},{9,1},{10,2},{11,3},{12,4},{13,5},{14,6},{15,7},{16,24},{17,... | collective-permute-start | bytes 2359304 | tf_op jit(solution)/shard_map/ppermute | solution.py:39
  74.6 12.3 %collective-permute-start.6 = (bf16[768,256]{1,0:T(8,128)(2,1)S(1)}, bf16[768,256]{1,0:T(8,128)(2,1)S(1)}, u32[]{:S(2)}, u32[]{:S(2)}) collective-permute-start(bf16[768,256]{1,0:T(8,128)(2,1)S(1)} %pad_maximum_fusion.5.own), channel_id=1, source_target_pairs={{0,8},{1,9},{2,10},{3,11},{4,12},{5,13},{6,14},{7,15},{8,16},{9,17... | collective-permute-start | bytes 1179656 | tf_op jit(solution)/shard_map/ppermute | solution.py:39
  76.5 23.4 %collective-permute-start.7 = (bf16[768,256]{1,0:T(8,128)(2,1)S(1)}, bf16[768,256]{1,0:T(8,128)(2,1)S(1)}, u32[]{:S(2)}, u32[]{:S(2)}) collective-permute-start(bf16[768,256]{1,0:T(8,128)(2,1)S(1)} %pad_maximum_fusion.5.own), channel_id=1, source_target_pairs={{8,0},{9,1},{10,2},{11,3},{12,4},{13,5},{14,6},{15,7},{16,8},{17,9... | collective-permute-start | bytes 1179656 | tf_op jit(solution)/shard_map/ppermute | solution.py:39
  99.9 19.4 %collective-permute-start.13 = (bf16[768,256]{1,0:T(8,128)(2,1)S(1)}, bf16[768,256]{1,0:T(8,128)(2,1)S(1)}, u32[]{:S(2)}, u32[]{:S(2)}) collective-permute-start(bf16[768,256]{1,0:T(8,128)(2,1)S(1)} %collective-permute-done.6.up), channel_id=1, source_target_pairs={{8,16},{9,17},{10,18},{11,19},{12,20},{13,21},{14,22},{15,23},{16,... | collective-permute-start | bytes 1179656 | tf_op jit(solution)/shard_map/ppermute | solution.py:39
  101.2 18.1 %collective-permute-start.14 = (bf16[768,256]{1,0:T(8,128)(2,1)S(1)}, bf16[768,256]{1,0:T(8,128)(2,1)S(1)}, u32[]{:S(2)}, u32[]{:S(2)}) collective-permute-start(bf16[768,256]{1,0:T(8,128)(2,1)S(1)} %collective-permute-done.7.down), channel_id=1, source_target_pairs={{8,0},{9,1},{10,2},{11,3},{12,4},{13,5},{14,6},{15,7},{16,8},{17,9... | collective-permute-start | bytes 1179656 | tf_op jit(solution)/shard_map/ppermute | solution.py:39
  119.3 24.0 %collective-permute-start.18 = (bf16[1536,256]{1,0:T(8,128)(2,1)S(1)}, bf16[1536,256]{1,0:T(8,128)(2,1)S(1)}, u32[]{:S(2)}, u32[]{:S(2)}) collective-permute-start(bf16[1536,256]{1,0:T(8,128)(2,1)S(1)} %get-tuple-element.96), channel_id=1, source_target_pairs={{0,8},{1,9},{2,10},{3,11},{4,12},{5,13},{6,14},{7,15},{24,16},{25,... | collective-permute-start | bytes 2359304 | tf_op jit(solution)/shard_map/ppermute | solution.py:39
  120.6 11.1 %collective-permute-start.17 = (bf16[768,256]{1,0:T(8,128)(2,1)S(1)}, bf16[768,256]{1,0:T(8,128)(2,1)S(1)}, u32[]{:S(2)}, u32[]{:S(2)}) collective-permute-start(bf16[768,256]{1,0:T(8,128)(2,1)S(1)} %broadcast_select_fusion.1), channel_id=1, source_target_pairs={{8,0},{9,1},{10,2},{11,3},{12,4},{13,5},{14,6},{15,7},{16,24},{17,... | collective-permute-start | bytes 1179656 | tf_op jit(solution)/shard_map/ppermute | solution.py:39
  143.3 33.8 %collective-permute-start.20 = (bf16[288,4096]{1,0:T(8,128)(2,1)}, bf16[288,4096]{1,0:T(8,128)(2,1)S(1)}, u32[]{:S(2)}, u32[]{:S(2)}) collective-permute-start(bf16[288,4096]{1,0:T(8,128)(2,1)} %get-tuple-element.100), channel_id=1, source_target_pairs={{0,1},{1,0},{2,3},{3,2},{4,5},{5,4},{6,7},{7,6},{8,9},{9,8},{10,11... | collective-permute-start | bytes 7077896 | tf_op jit(solution)/shard_map/ppermute | solution.py:39
  145.8 21.3 %collective-permute-start.21 = (bf16[1536,256]{1,0:T(8,128)(2,1)S(1)}, bf16[1536,256]{1,0:T(8,128)(2,1)S(1)}, u32[]{:S(2)}, u32[]{:S(2)}) collective-permute-start(bf16[1536,256]{1,0:T(8,128)(2,1)S(1)} %add_convert_fusion.4), channel_id=1, source_target_pairs={{0,8},{1,9},{2,10},{3,11},{4,12},{5,13},{6,14},{7,15},{8,16},{9,17... | collective-permute-start | bytes 2359304 | tf_op jit(solution)/shard_map/ppermute | solution.py:39
  147.8 20.8 %collective-permute-start.22 = (bf16[1536,256]{1,0:T(8,128)(2,1)S(1)}, bf16[1536,256]{1,0:T(8,128)(2,1)S(1)}, u32[]{:S(2)}, u32[]{:S(2)}) collective-permute-start(bf16[1536,256]{1,0:T(8,128)(2,1)S(1)} %add_convert_fusion.4), channel_id=1, source_target_pairs={{16,8},{17,9},{18,10},{19,11},{20,12},{21,13},{22,14},{23,15},{24,... | collective-permute-start | bytes 2359304 | tf_op jit(solution)/shard_map/ppermute | solution.py:39
  149.1 28.0 %collective-permute-start.19 = (bf16[768,256]{1,0:T(8,128)(2,1)S(1)}, bf16[768,256]{1,0:T(8,128)(2,1)S(1)}, u32[]{:S(2)}, u32[]{:S(2)}) collective-permute-start(bf16[768,256]{1,0:T(8,128)(2,1)S(1)} %get-tuple-element.99), channel_id=1, source_target_pairs={{0,8},{1,9},{2,10},{3,11},{4,12},{5,13},{6,14},{7,15},{24,16},{25,... | collective-permute-start | bytes 1179656 | tf_op jit(solution)/shard_map/ppermute | solution.py:39
  169.7 22.8 %collective-permute-start.29 = (bf16[1536,256]{1,0:T(8,128)(2,1)}, bf16[1536,256]{1,0:T(8,128)(2,1)}, u32[]{:S(2)}, u32[]{:S(2)}) collective-permute-start(bf16[1536,256]{1,0:T(8,128)(2,1)} %add_convert_fusion.3), channel_id=1, source_target_pairs={{0,8},{1,9},{2,10},{3,11},{4,12},{5,13},{6,14},{7,15},{8,16},{9,17... | collective-permute-start | bytes 2359304 | tf_op jit(solution)/shard_map/ppermute | solution.py:39
  173.0 20.2 %collective-permute-start.30 = (bf16[1536,256]{1,0:T(8,128)(2,1)}, bf16[1536,256]{1,0:T(8,128)(2,1)}, u32[]{:S(2)}, u32[]{:S(2)}) collective-permute-start(bf16[1536,256]{1,0:T(8,128)(2,1)} %add_convert_fusion.2), channel_id=1, source_target_pairs={{8,0},{9,1},{10,2},{11,3},{12,4},{13,5},{14,6},{15,7},{16,8},{17,9... | collective-permute-start | bytes 2359304 | tf_op jit(solution)/shard_map/ppermute | solution.py:39
  180.6 26.2 %collective-permute-start.25 = (bf16[2,72,4096]{2,1,0:T(8,128)(2,1)}, bf16[2,72,4096]{2,1,0:T(8,128)(2,1)}, u32[]{:S(2)}, u32[]{:S(2)}) collective-permute-start(bf16[2,72,4096]{2,1,0:T(8,128)(2,1)} %get-tuple-element.133), channel_id=1, source_target_pairs={{0,4},{1,5},{2,6},{3,7},{4,0},{5,1},{6,2},{7,3},{8,12},{9,13},{10,... | collective-permute-start | bytes 3538952 | tf_op jit(solution)/shard_map/ppermute | solution.py:39
  195.1 47.8 %collective-permute-start.31 = (bf16[768,256]{1,0:T(8,128)(2,1)S(1)}, bf16[768,256]{1,0:T(8,128)(2,1)S(1)}, u32[]{:S(2)}, u32[]{:S(2)}) collective-permute-start(bf16[768,256]{1,0:T(8,128)(2,1)S(1)} %get-tuple-element.139), channel_id=1, source_target_pairs={{0,0},{1,4},{2,2},{3,6},{4,1},{5,5},{6,3},{7,7},{8,8},{9,12},{10,1... | collective-permute-start | bytes 1179656 | tf_op jit(solution)/shard_map/ppermute | solution.py:39
  200.0 42.9 %collective-permute-start.32 = (bf16[768,256]{1,0:T(8,128)(2,1)S(1)}, bf16[768,256]{1,0:T(8,128)(2,1)S(1)}, u32[]{:S(2)}, u32[]{:S(2)}) collective-permute-start(bf16[768,256]{1,0:T(8,128)(2,1)S(1)} %get-tuple-element.138), channel_id=1, source_target_pairs={{0,4},{1,0},{2,6},{3,2},{4,5},{5,1},{6,7},{7,3},{8,12},{9,8},{10,1... | collective-permute-start | bytes 1179656 | tf_op jit(solution)/shard_map/ppermute | solution.py:39
  200.1 12.4 %collective-permute-start.23 = (bf16[768,256]{1,0:T(8,128)(2,1)S(1)}, bf16[768,256]{1,0:T(8,128)(2,1)S(1)}, u32[]{:S(2)}, u32[]{:S(2)}) collective-permute-start(bf16[768,256]{1,0:T(8,128)(2,1)S(1)} %copy-done.16), channel_id=1, source_target_pairs={{0,8},{1,9},{2,10},{3,11},{4,12},{5,13},{6,14},{7,15},{8,16},{9,17... | collective-permute-start | bytes 1179656 | tf_op jit(solution)/shard_map/ppermute | solution.py:39
  202.0 12.2 %collective-permute-start.24 = (bf16[768,256]{1,0:T(8,128)(2,1)S(1)}, bf16[768,256]{1,0:T(8,128)(2,1)S(1)}, u32[]{:S(2)}, u32[]{:S(2)}) collective-permute-start(bf16[768,256]{1,0:T(8,128)(2,1)S(1)} %copy-done.16), channel_id=1, source_target_pairs={{16,8},{17,9},{18,10},{19,11},{20,12},{21,13},{22,14},{23,15},{24,... | collective-permute-start | bytes 1179656 | tf_op jit(solution)/shard_map/ppermute | solution.py:39
  214.3 28.6 %collective-permute-start.26 = (bf16[768,256]{1,0:T(8,128)(2,1)S(1)}, bf16[768,256]{1,0:T(8,128)(2,1)S(1)}, u32[]{:S(2)}, u32[]{:S(2)}) collective-permute-start(bf16[768,256]{1,0:T(8,128)(2,1)S(1)} %add_convert_fusion.7), channel_id=1, source_target_pairs={{0,8},{1,9},{2,10},{3,11},{4,12},{5,13},{6,14},{7,15},{8,16},{9,17... | collective-permute-start | bytes 1179656 | tf_op jit(solution)/shard_map/ppermute | solution.py:39
  216.4 26.3 %collective-permute-start.28 = (bf16[2,72,4096]{2,1,0:T(8,128)(2,1)S(1)}, bf16[2,72,4096]{2,1,0:T(8,128)(2,1)S(1)}, u32[]{:S(2)}, u32[]{:S(2)}) collective-permute-start(bf16[2,72,4096]{2,1,0:T(8,128)(2,1)S(1)} %slice_bitcast_fusion.3), channel_id=1, source_target_pairs={{0,2},{1,3},{2,0},{3,1},{4,6},{5,7},{6,4},{7,5},{8,10},{9,11},{10,... | collective-permute-start | bytes 3538952 | tf_op jit(solution)/shard_map/ppermute | solution.py:39
  217.7 25.2 %collective-permute-start.27 = (bf16[768,256]{1,0:T(8,128)(2,1)S(1)}, bf16[768,256]{1,0:T(8,128)(2,1)S(1)}, u32[]{:S(2)}, u32[]{:S(2)}) collective-permute-start(bf16[768,256]{1,0:T(8,128)(2,1)S(1)} %add_convert_fusion.6), channel_id=1, source_target_pairs={{8,0},{9,1},{10,2},{11,3},{12,4},{13,5},{14,6},{15,7},{16,8},{17,9... | collective-permute-start | bytes 1179656 | tf_op jit(solution)/shard_map/ppermute | solution.py:39
  246.5 9.5 %collective-permute-start.33 = (bf16[384,256]{1,0:T(8,128)(2,1)S(1)}, bf16[384,256]{1,0:T(8,128)(2,1)S(1)}, u32[]{:S(2)}, u32[]{:S(2)}) collective-permute-start(bf16[384,256]{1,0:T(8,128)(2,1)S(1)} %get-tuple-element.143), channel_id=1, source_target_pairs={{0,0},{1,4},{2,2},{3,6},{4,1},{5,5},{6,3},{7,7},{8,8},{9,12},{10,1... | collective-permute-start | bytes 589832 | tf_op jit(solution)/shard_map/ppermute | solution.py:39
  (27 other events, 229.2 us)

commit v8 on v7

--- a/solution.py
+++ b/solution.py
@@ -14,6 +14,10 @@
 
 def dot(a, b, dims=((1,), (0,))):
     return lax.dot_general(a, b, (dims, ((), ())), preferred_element_type=F32)
+
+
+def tie(value, *others):
+    return lax.optimization_barrier((value,) + others)[0]
 
 
 def added(*terms):
@@ -135,13 +139,9 @@
     up_ref[...] = dot(jnp.concatenate(ups[0] + ups[1], axis=1), shuffle, ((1,), (1,)))
 
 
-def expert_kernel(
-    adds, z_ref, own, up, down, up_2, down_2, last, mine, theirs, *refs
-):
-    earlier, refs = refs[:2 * adds], refs[2 * adds:]
-    keep_out, give_out, outer_out, *refs = refs
-    outs, refs = refs[:4], refs[4:]
-    packed, x, grads, gate_up, w_down, pre, d_hidden, hidden, d_both, d_down, keep, give, terms, load, store = refs
+def expert_kernel(z_ref, own, up, down, up_2, down_2, last, mine, theirs, *refs):
+    weight_outs, (hidden_out, d_both_out, outer_out), outs, refs = refs[:2], refs[2:5], refs[5:9], refs[9:]
+    packed, x, grads, gate_up, w_down, pre, d_hidden, hidden, d_both, d_down, terms, load, store = refs
     places, size, _ = packed.shape
     rows, width = x.shape
     slots = rows // 2
@@ -154,14 +154,16 @@
     z = z_ref[0]
 
     loads = [
-        (mine.at[:, :width], x.at[:slots]),
-        (theirs.at[:, :width], x.at[slots:]),
-        (mine.at[:, width:], grads.at[:slots]),
-        (theirs.at[:, width:], grads.at[slots:]),
+        pltpu.make_async_copy(a, b, load.at[places + n])
+        for n, (a, b) in enumerate(
+            (
+                (mine.at[:, :width], x.at[:slots]),
+                (theirs.at[:, :width], x.at[slots:]),
+                (mine.at[:, width:], grads.at[:slots]),
+                (theirs.at[:, width:], grads.at[slots:]),
+            )
+        )
     ]
-    if adds:
-        loads += [(earlier[0], keep), (earlier[1], give)]
-    loads = [pltpu.make_async_copy(a, b, load.at[places + n]) for n, (a, b) in enumerate(loads)]
     for copy in loads[:2]:
         copy.start()
     pltpu.make_async_copy(own, packed.at[0], load.at[0]).start()
@@ -202,6 +204,14 @@
             product = dot(x[:, block], gate_up[block, cols])
             pre[:, cols] = product if s == 0 else pre[:, cols] + product
 
+    stores = []
+
+    def store_to(out, value):
+        stores.append(pltpu.make_async_copy(value, out, store.at[len(stores)]))
+        stores[-1].start()
+
+    store_to(weight_outs[0], gate_up)
+    store_to(weight_outs[1], w_down)
     step = 64 if rows % 64 == 0 else 16
 
     def activate(r, _):
@@ -215,6 +225,7 @@
         return 0
 
     lax.fori_loop(0, rows // step, activate, 0)
+    store_to(hidden_out, hidden)
     for copy in loads[2:]:
         copy.wait()
     d_hidden[...] = dot(grads[...], w_down[...], ((1,), (1,)))
@@ -227,27 +238,12 @@
         return 0
 
     lax.fori_loop(0, rows // step, differentiate, 0)
-
-    def to_tokens(n, _):
-        at = pl.multiple_of(n * LANES, LANES)
-        cols, beyond = pl.ds(at, LANES), pl.ds(at + width, LANES)
-        for to, value in (
-            (cols, dot(hidden[...], w_down[:, cols])),
-            (beyond, dot(d_both[...], gate_up[cols, :], ((1,), (1,)))),
-        ):
-            for ref, part in ((keep, value[:slots]), (give, value[slots:])):
-                ref[:, to] = (part + ref[:, to].astype(F32) if adds else part).astype(BF)
-        d_down[:, cols] = dot(hidden[...], grads[:, cols], ((0,), (0,))).astype(BF)
-        return 0
-
-    lax.fori_loop(0, columns, to_tokens, 0)
-    stores = [pltpu.make_async_copy(keep, keep_out, store.at[0]), pltpu.make_async_copy(give, give_out, store.at[1])]
-    for copy in stores:
-        copy.start()
-
-    def term(k, _):
+    store_to(d_both_out, d_both)
+    d_down[...] = dot(hidden[...], grads[...], ((0,), (0,))).astype(BF)
+
+    for k in (places - 1, 1, 2, 0):
         for h in range(2):
-            from_cols = pl.ds(pl.multiple_of(k * line + h * part_rows, LANES), part_rows)
+            from_cols = slice(k * line + h * part_rows, k * line + (h + 1) * part_rows)
             weights = dot(x[:, from_cols], d_both[...], ((0,), (0,))).astype(BF)
             for i in range(count):
                 to = h * size_half + i * part_rows
@@ -255,16 +251,30 @@
             for j in range(columns):
                 to = h * size_half + count * part_rows + j * piece
                 terms[k, to:to + piece, :] = d_down[down_rows(k, h), j * LANES:(j + 1) * LANES]
-        return 0
-
-    lax.fori_loop(0, places, term, 0)
-    outer_k = jnp.where(z == 0, places - 1, 1)
-    stores.append(pltpu.make_async_copy(terms.at[outer_k], outer_out, store.at[2]))
-    stores += [pltpu.make_async_copy(terms.at[k], out, store.at[3 + k]) for k, out in enumerate(outs)]
-    for copy in stores[2:]:
-        copy.start()
+        store_to(outs[k], terms.at[k])
+        if k == 1:
+            store_to(outer_out, terms.at[jnp.where(z == 0, places - 1, 1)])
     for copy in stores:
         copy.wait()
+
+
+def rows_kernel(chunks, *refs):
+    keep, give = refs[-2:]
+    slots = keep.shape[0]
+
+    def add(pairs, dims):
+        total = sum(dot(a[...], b[...], dims) for a, b in pairs).astype(BF)
+        keep[...], give[...] = total[:slots], total[slots:]
+
+    chunked = [refs[4 * n:4 * n + 4] for n in range(chunks)]
+
+    @pl.when(pl.program_id(0) < pl.num_programs(0) // 2)
+    def _():
+        add([(hidden, w_down) for _, w_down, hidden, _ in chunked], ((1,), (0,)))
+
+    @pl.when(pl.program_id(0) >= pl.num_programs(0) // 2)
+    def _():
+        add([(d_both, gate_up) for gate_up, _, _, d_both in chunked], ((1,), (1,)))
 
 
 def in_vmem(count):
@@ -296,16 +306,18 @@
     )(x, *packed, shuffle)
 
 
-def expert(z, places, units, weights, mine, theirs, earlier=()):
+def expert(z, places, units, weights, mine, theirs):
     size = weights[0].shape[0]
     slots, width = mine.shape[0], mine.shape[1] // 2
     rows = 2 * slots
-    row_shape, term_shape = jax.ShapeDtypeStruct(mine.shape, BF), jax.ShapeDtypeStruct((size, LANES), BF)
-    return pl.pallas_call(
-        functools.partial(expert_kernel, len(earlier) // 2),
-        out_shape=[row_shape] * 2 + [term_shape] * 5,
-        in_specs=[IN_SMEM] + [pl.BlockSpec(memory_space=pl.ANY)] * (8 + len(earlier)),
-        out_specs=[pl.BlockSpec(memory_space=pl.ANY)] * 7,
+    for_rows = [
+        jax.ShapeDtypeStruct(shape, BF) for shape in ((width, 2 * units), (units, width), (rows, units), (rows, 2 * units))
+    ]
+    outs = pl.pallas_call(
+        expert_kernel,
+        out_shape=for_rows + [jax.ShapeDtypeStruct((size, LANES), BF)] * 5,
+        in_specs=[IN_SMEM] + [pl.BlockSpec(memory_space=pl.ANY)] * 8,
+        out_specs=[pl.BlockSpec(memory_space=pl.ANY)] * 9,
         scratch_shapes=[
             pltpu.VMEM((places, size, LANES), BF),
             pltpu.VMEM((rows, width), BF),
@@ -317,17 +329,41 @@
             pltpu.VMEM((rows, units), BF),
             pltpu.VMEM((rows, 2 * units), BF),
             pltpu.VMEM((units, width), BF),
-            pltpu.VMEM((slots, 2 * width), BF),
-            pltpu.VMEM((slots, 2 * width), BF),
             pltpu.VMEM((places, size, LANES), BF),
-            pltpu.SemaphoreType.DMA((places + 6,)),
-            pltpu.SemaphoreType.DMA((7,)),
+            pltpu.SemaphoreType.DMA((places + 4,)),
+            pltpu.SemaphoreType.DMA((9,)),
         ],
         compiler_params=pltpu.CompilerParams(vmem_limit_bytes=VMEM_BYTES),
         cost_estimate=pl.CostEstimate(
-            flops=18 * rows * width * units, bytes_accessed=16 * 2**20, transcendentals=rows * units
+            flops=12 * rows * width * units, bytes_accessed=16 * 2**20, transcendentals=rows * units
         ),
-    )(z, *weights, mine, theirs, *earlier)
+    )(z, *weights, mine, theirs)
+    return outs[:4], outs[4], outs[5:]
+
+
+def token_rows(chunks, slots, width):
+    tile = 2 * LANES
+    tiles = width // tile
+    in_specs = []
+    for gate_up, w_down, hidden, d_both in chunks:
+        in_specs += [
+            pl.BlockSpec((tile, gate_up.shape[1]), lambda n: (jnp.maximum(n - tiles, 0), 0)),
+            pl.BlockSpec((w_down.shape[0], tile), lambda n: (0, jnp.minimum(n, tiles - 1))),
+            pl.BlockSpec(hidden.shape, lambda n: (0, 0)),
+            pl.BlockSpec(d_both.shape, lambda n: (0, 0)),
+        ]
+    units = sum(chunk[1].shape[0] for chunk in chunks)
+    return pl.pallas_call(
+        functools.partial(rows_kernel, len(chunks)),
+        grid=(2 * tiles,),
+        out_shape=[jax.ShapeDtypeStruct((slots, 2 * width), BF)] * 2,
+        in_specs=in_specs,
+        out_specs=[pl.BlockSpec((slots, tile), lambda n: (0, n))] * 2,
+        compiler_params=pltpu.CompilerParams(vmem_limit_bytes=VMEM_BYTES // 2),
+        cost_estimate=pl.CostEstimate(
+            flops=12 * slots * width * units, bytes_accessed=12 * 2**20, transcendentals=0
+        ),
+    )(*(array for chunk in chunks for array in chunk))
 
 
 def local(tokens, expert_ids, gate_probs, w_gate, w_up, w_down, d_out):
@@ -421,45 +457,47 @@
         shard, a2, b2 = together((spread(a, b), a2, b2))
         up, down = g.hop(shard, ups), g.hop(shard, downs)
         shard2, sent = together((spread(a2, b2), sent))
-        up, down, shard2 = together((up, down, shard2))
+        up, down = together((up, down))
         up_2, down_2 = g.hop(up, {1: 2, 2: 3}), g.hop(down, {1: 0, 2: 1})
+        shard2, mine = together((shard2, exchange(sent, 1)))
         up2, down2 = g.hop(shard2, ups), g.hop(shard2, downs)
-        up_2, down_2, mine = together((up_2, down_2, exchange(sent, 1)))
+        up_2, down_2, up2, down2, mine = together((up_2, down_2, up2, down2, mine))
+        last = g.hop(jnp.where(to_last, up_2, down_2), passing)
+        up2_2, down2_2 = g.hop(up2, {1: 2, 2: 3}), g.hop(down2, {1: 0, 2: 1})
         theirs = g.send(mine, other_core)
-        last = g.hop(jnp.where(to_last, up_2, down_2), passing)
-        up2, down2, up_2, down_2 = together((up2, down2, up_2, down_2))
-        up2_2, down2_2 = g.hop(up2, {1: 2, 2: 3}), g.hop(down2, {1: 0, 2: 1})
-        keep, give, outer, *terms = expert(
+        chunk, outer, terms = expert(
             place_z, g.zs, units[0], (shard, up, down, up_2, down_2, last), mine, theirs
         )
-        up2_2, down2_2, outer, keep, give = together((up2_2, down2_2, outer, keep, give))
+        up2_2, down2_2, outer = together((up2_2, down2_2, outer))
         last2 = g.hop(jnp.where(to_last, up2_2, down2_2), passing)
         begun = g.hop(outer, outward)
-        keep, give, outer2, *terms2 = expert(
-            place_z, g.zs, units[1], (shard2, up2, down2, up2_2, down2_2, last2), mine, theirs, (keep, give)
+        chunk2, outer2, terms2 = expert(
+            place_z, g.zs, units[1], (shard2, up2, down2, up2_2, down2_2, last2), mine, theirs
         )
-        begun, give, outer2 = together((begun, give, outer2))
-        middle = added(terms[2], begun)
+        begun, outer2, chunk2 = together((begun, outer2, chunk2))
+        middle, outer2, chunk2 = together((added(terms[2], begun), outer2, chunk2))
         sum_up, sum_down = g.hop(middle, inward_up), g.hop(middle, inward_down)
-        given = g.send(give, other_core)
         begun2 = g.hop(outer2, outward)
-        sum_up, sum_down, keep = together((sum_up, sum_down, keep))
+        keep, give = token_rows((chunk, chunk2), slots, width)
+        sums = added(keep, g.send(give, other_core)).reshape(g.qs, 2, cap, 2 * width)
+        sum_up, sum_down, sums = together((sum_up, sum_down, sums))
+        far_rows = g.send(sums[:, 1], lambda z, x, q, c: (z, 1 - x, q, c))
         sum_up, sum_down = g.hop(added(terms[1], sum_up), ups), g.hop(added(terms[3], sum_down), downs)
-        begun2, given, keep = together((begun2, given, keep))
-        middle2, sums = together((added(terms2[2], begun2), added(keep, given)))
+        middle2 = added(terms2[2], begun2)
         sum_up2, sum_down2 = g.hop(middle2, inward_up), g.hop(middle2, inward_down)
-        sums = sums.reshape(g.qs, 2, cap, 2 * width)
-        near = jnp.stack([sums[:, 0], g.send(sums[:, 1], lambda z, x, q, c: (z, 1 - x, q, c))], axis=1)
-        sum_up, sum_down = together((sum_up, sum_down))
         grad = added(terms[0], sum_up, sum_down)
-        sum_up2, sum_down2, near = together((sum_up2, sum_down2, near))
-        sum_up2, sum_down2 = g.hop(added(terms2[1], sum_up2), ups), g.hop(added(terms2[3], sum_down2), downs)
+        far_rows = tie(far_rows, grad)
+        near = jnp.stack([sums[:, 0], far_rows], axis=1)
         got = jnp.concatenate(
             [near[0]] + [g.send(near[d], lambda z, x, q, c, d=d: (z, x, (q - d) % g.qs, c)) for d in range(1, g.qs)]
         ).reshape(slots, 2 * width)
+        sum_up2, sum_down2 = tie(sum_up2, near), tie(sum_down2, near)
         grads = unspread(grad)
-        sum_up2, sum_down2, got, grads = together((sum_up2, sum_down2, got, grads))
-        grads += unspread(added(terms2[0], sum_up2, sum_down2))
+        sum_up2, sum_down2 = g.hop(added(terms2[1], sum_up2), ups), g.hop(added(terms2[3], sum_down2), downs)
+        sum_up2, sum_down2, grads = together((sum_up2, sum_down2, grads))
+        grad2 = added(terms2[0], sum_up2, sum_down2)
+        got = tie(got, grad2)
+        grads += unspread(grad2)
         d_w_gate, d_w_up, d_w_down = unpack(pieces, place_x, grads, shuffle, *shapes)
     else:
         gate_cols, up_cols = dot(w_gate[0], shuffle).astype(BF), dot(w_up[0], shuffle).astype(BF)

time: 262 us -> 237 us (0.905)
  waiting for transfers between devices: 127 us -> 102 us
  starting transfers between devices: 74.2 us -> 77.5 us
    ppermute x35, waiting for transfers between devices: 127 us -> 102 us  [send(): return lax.ppermute(value, BOTH, pairs)]
    ppermute x35, starting transfers between devices: 74.2 us -> 77.5 us  [send(): return lax.ppermute(value, BOTH, pairs)]
    convert_element_type x9, other arithmetic: 6.22 us -> 3.55 us  [added(): return sum((t.astype(F32) for t in terms)).astype(BF)]
    unnamed x49 -> x44, local copies, waits for them, and re-layouts: 8.26 us -> 6.76 us
    pallas_call x2 -> x3, Pallas kernels: 24.3 us -> 23.1 us  [the longest x2 17.9 us: expert(): pl.pallas_call(expert_kernel, out_shape=for_rows + [jax.ShapeDtypeStruct(...]
  transfers between devices with their start and end apart: 35 -> 35, of which waited for: 20 -> 18; matrix products, arithmetic and copies ran while one was open for 7% -> 5% of each run, Pallas kernels for 9% -> 9%
where the time goes in v8:
time: 237 us; the launch traced here: 234 us
  waiting for transfers between devices  102 us (43%)
  starting transfers between devices  77.5 us (33%)
  Pallas kernels  25.8 us (11%)
  other arithmetic  14.3 us (6%)
  local copies, waits for them, and re-layouts  7.38 us (3%)
  matrix products  5.73 us (2%)
    ppermute x35, waiting for transfers between devices, send(): return lax.ppermute(value, BOTH, pairs)  102 us
    ppermute x35, starting transfers between devices, send(): return lax.ppermute(value, BOTH, pairs)  77.5 us
    pallas_call x2, Pallas kernels, expert(): pl.pallas_call(expert_kernel, out_shape=for_rows + [jax.ShapeDtypeStruct(...  17.9 us
    unnamed x44, local copies, waits for them, and re-layouts  6.76 us
    dot_general x7, matrix products, dot(): return lax.dot_general(a, b, (dims, ((), ())), preferred_element_type=F32)  5.73 us
    pallas_call x1, Pallas kernels, token_rows(): pl.pallas_call(functools.partial(rows_kernel, len(chunks)), grid=(2 * til...  5.11 us
  transfers between devices with their start and end apart: 35, of which 18 were waited for; matrix products, arithmetic and copies ran while one was open for 5% of the time, Pallas kernels for 9%

profile of v8, /device:TPU:9, one launch (start us, length us, event | category | flops | bytes accessed | tf_op | source)
XLA Modules:
  0.0 234.2 jit_solution(8191364591588495898)
XLA Ops:
  4.9 3.7 %collective-permute-start = (bf16[768,256]{1,0:T(8,128)(2,1)S(1)}, bf16[768,256]{1,0:T(8,128)(2,1)}, u32[]{:S(2)}, u32[]{:S(2)}) collective-permute-start(bf16[768,256]{1,0:T(8,128)(2,1)S(1)} %get-tuple-element.73), channel_id=1, source_target_pairs={{0,0},{1,4},{2,2},{3,6},{4,1},{5,5},{6,3},{7,7},{8,8},{9,12},{10,1... | collective-permute-start | bytes 1179656 | tf_op jit(solution)/shard_map/ppermute | solution.py:43
  14.2 3.4 %collective-permute-done.1 = bf16[768,256]{1,0:T(8,128)(2,1)} collective-permute-done((bf16[768,256]{1,0:T(8,128)(2,1)S(1)}, bf16[768,256]{1,0:T(8,128)(2,1)}, u32[]{:S(2)}, u32[]{:S(2)}) %collective-permute-start.1) | collective-permute-done | bytes 393248 | tf_op jit(solution)/shard_map/ppermute | solution.py:43
  18.8 2.5 %collective-permute-start.6 = (bf16[384,256]{1,0:T(8,128)(2,1)S(1)}, bf16[384,256]{1,0:T(8,128)(2,1)S(1)}, u32[]{:S(2)}, u32[]{:S(2)}) collective-permute-start(bf16[384,256]{1,0:T(8,128)(2,1)S(1)} %get-tuple-element.80), channel_id=1, source_target_pairs={{0,0},{1,4},{2,2},{3,6},{4,1},{5,5},{6,3},{7,7},{8,8},{9,12},{10,1... | collective-permute-start | bytes 589832 | tf_op jit(solution)/shard_map/ppermute | solution.py:43
  21.7 3.2 %collective-permute-start.2 = (bf16[1536,256]{1,0:T(8,128)(2,1)S(1)}, bf16[1536,256]{1,0:T(8,128)(2,1)S(1)}, u32[]{:S(2)}, u32[]{:S(2)}) collective-permute-start(bf16[1536,256]{1,0:T(8,128)(2,1)S(1)} %pad_maximum_fusion.4.own), channel_id=1, source_target_pairs={{0,8},{1,9},{2,10},{3,11},{4,12},{5,13},{6,14},{7,15},{8,16},{9,17... | collective-permute-start | bytes 2359304 | tf_op jit(solution)/shard_map/ppermute | solution.py:43
  24.9 2.1 collective-permute-start.3
  27.4 2.1 collective-permute-start.10
  30.1 12.4 %collective-permute-done.2.up = bf16[1536,256]{1,0:T(8,128)(2,1)S(1)} collective-permute-done((bf16[1536,256]{1,0:T(8,128)(2,1)S(1)}, bf16[1536,256]{1,0:T(8,128)(2,1)S(1)}, u32[]{:S(2)}, u32[]{:S(2)}) %collective-permute-start.2) | collective-permute-done | bytes 786464 | tf_op jit(solution)/shard_map/ppermute | solution.py:43
  42.4 2.9 %collective-permute-done.3.down = bf16[1536,256]{1,0:T(8,128)(2,1)S(1)} collective-permute-done((bf16[1536,256]{1,0:T(8,128)(2,1)S(1)}, bf16[1536,256]{1,0:T(8,128)(2,1)S(1)}, u32[]{:S(2)}, u32[]{:S(2)}) %collective-permute-start.3) | collective-permute-done | bytes 786464 | tf_op jit(solution)/shard_map/ppermute | solution.py:43
  45.3 3.2 %collective-permute-start.4 = (bf16[1536,256]{1,0:T(8,128)(2,1)S(1)}, bf16[1536,256]{1,0:T(8,128)(2,1)S(1)}, u32[]{:S(2)}, u32[]{:S(2)}) collective-permute-start(bf16[1536,256]{1,0:T(8,128)(2,1)S(1)} %collective-permute-done.2.up), channel_id=1, source_target_pairs={{8,16},{9,17},{10,18},{11,19},{12,20},{13,21},{14,22},{15,23},{16,... | collective-permute-start | bytes 2359304 | tf_op jit(solution)/shard_map/ppermute | solution.py:43
  50.5 3.9 %collective-permute-done.8 = bf16[72,4096]{1,0:T(8,128)(2,1)S(1)} collective-permute-done((bf16[72,4096]{1,0:T(8,128)(2,1)S(1)}, bf16[72,4096]{1,0:T(8,128)(2,1)S(1)}, u32[]{:S(2)}, u32[]{:S(2)}) %collective-permute-start.8) | collective-permute-done | bytes 589856 | tf_op jit(solution)/shard_map/ppermute | solution.py:43
  57.9 3.1 %collective-permute-start.11 = (bf16[768,256]{1,0:T(8,128)(2,1)S(1)}, bf16[768,256]{1,0:T(8,128)(2,1)S(1)}, u32[]{:S(2)}, u32[]{:S(2)}) collective-permute-start(bf16[768,256]{1,0:T(8,128)(2,1)S(1)} %pad_maximum_fusion.5.own), channel_id=1, source_target_pairs={{0,8},{1,9},{2,10},{3,11},{4,12},{5,13},{6,14},{7,15},{8,16},{9,17... | collective-permute-start | bytes 1179656 | tf_op jit(solution)/shard_map/ppermute | solution.py:43
  61.0 2.1 collective-permute-start.12
  63.2 9.1 %collective-permute-done.11.up = bf16[768,256]{1,0:T(8,128)(2,1)S(1)} collective-permute-done((bf16[768,256]{1,0:T(8,128)(2,1)S(1)}, bf16[768,256]{1,0:T(8,128)(2,1)S(1)}, u32[]{:S(2)}, u32[]{:S(2)}) %collective-permute-start.11) | collective-permute-done | bytes 393248 | tf_op jit(solution)/shard_map/ppermute | solution.py:43
  72.3 3.9 %collective-permute-done.12.down = bf16[768,256]{1,0:T(8,128)(2,1)S(1)} collective-permute-done((bf16[768,256]{1,0:T(8,128)(2,1)S(1)}, bf16[768,256]{1,0:T(8,128)(2,1)S(1)}, u32[]{:S(2)}, u32[]{:S(2)}) %collective-permute-start.12) | collective-permute-done | bytes 393248 | tf_op jit(solution)/shard_map/ppermute | solution.py:43
  78.8 2.7 %collective-permute-start.14 = (bf16[288,4096]{1,0:T(8,128)(2,1)}, bf16[288,4096]{1,0:T(8,128)(2,1)}, u32[]{:S(2)}, u32[]{:S(2)}) collective-permute-start(bf16[288,4096]{1,0:T(8,128)(2,1)} %pad_maximum_fusion.2.mine), channel_id=1, source_target_pairs={{0,1},{1,0},{2,3},{3,2},{4,5},{5,4},{6,7},{7,6},{8,9},{9,8},{10,11... | collective-permute-start | bytes 7077896 | tf_op jit(solution)/shard_map/ppermute | solution.py:43
  88.0 13.6 %collective-permute-done.13.last = bf16[1536,256]{1,0:T(8,128)(2,1)S(1)} collective-permute-done((bf16[1536,256]{1,0:T(8,128)(2,1)S(1)}, bf16[1536,256]{1,0:T(8,128)(2,1)S(1)}, u32[]{:S(2)}, u32[]{:S(2)}) %collective-permute-start.13) | collective-permute-done | bytes 786464 | tf_op jit(solution)/shard_map/ppermute | solution.py:43
  102.5 9.5 %shard_map.119 = (bf16[2048,512]{1,0:T(8,128)(2,1)}, bf16[256,2048]{1,0:T(8,128)(2,1)}, bf16[576,256]{1,0:T(8,128)(2,1)S(1)}, bf16[576,512]{1,0:T(8,128)(2,1)S(1...) custom-call(s32[1]{0:T(128)} %bitcast.z_ref, ...), custom_call_target="tpu_custom_call" | custom-call | flops 3623878656 | bytes 16777216 | tf_op jit(solution)/shard_map/pallas_call | solution.py:316
  113.4 5.0 %collective-permute-start.18 = (bf16[768,256]{1,0:T(8,128)(2,1)S(1)}, bf16[768,256]{1,0:T(8,128)(2,1)S(1)}, u32[]{:S(2)}, u32[]{:S(2)}) collective-permute-start(bf16[768,256]{1,0:T(8,128)(2,1)S(1)} %broadcast_select_fusion.1), channel_id=1, source_target_pairs={{8,0},{9,1},{10,2},{11,3},{12,4},{13,5},{14,6},{15,7},{16,24},{17,... | collective-permute-start | bytes 1179656 | tf_op jit(solution)/shard_map/ppermute | solution.py:43
  118.4 7.0 %collective-permute-done.18.last = bf16[768,256]{1,0:T(8,128)(2,1)S(1)} collective-permute-done((bf16[768,256]{1,0:T(8,128)(2,1)S(1)}, bf16[768,256]{1,0:T(8,128)(2,1)S(1)}, u32[]{:S(2)}, u32[]{:S(2)}) %collective-permute-start.18) | collective-permute-done | bytes 393248 | tf_op jit(solution)/shard_map/ppermute | solution.py:43
  125.5 8.4 %shard_map.120 = (bf16[2048,256]{1,0:T(8,128)(2,1)}, bf16[128,2048]{1,0:T(8,128)(2,1)S(1)}, bf16[576,128]{1,0:T(8,128)(2,1)S(1)}, bf16[576,256]{1,0:T(8,128)(2,1...) custom-call(s32[1]{0:T(128)} %bitcast.z_ref, ...), custom_call_target="tpu_custom_call" | custom-call | flops 1811939328 | bytes 16777216 | tf_op jit(solution)/shard_map/pallas_call | solution.py:316
  135.7 5.1 %shard_map.121 = (bf16[288,4096]{1,0:T(8,128)(2,1)S(1)}, bf16[288,4096]{1,0:T(8,128)(2,1)S(1)}) custom-call(bf16[2048,512]{1,0:T(8,128)(2,1)S(1)} %copy-done.7, bf16[256,2048]{1,0:T(8,128)(2,1)S(1)} %copy-done.8, bf16[576,256]{1,0:T(8,128)(2,1)S(1)} %get-tuple-element.110.refs_2_, bf16[576,512]{1,0:T(8,128)(2,1)S(1)} %get-tuple-element.111.refs_3_, ...), custom_call_target="tpu_custom_call" | custom-call | flops 2717908992 | bytes 12582912 | tf_op jit(solution)/shard_map/pallas_call | solution.py:356
  140.8 2.3 collective-permute-start.21
  148.5 15.8 %collective-permute-done.19 = bf16[1536,256]{1,0:T(8,128)(2,1)S(1)} collective-permute-done((bf16[1536,256]{1,0:T(8,128)(2,1)S(1)}, bf16[1536,256]{1,0:T(8,128)(2,1)S(1)}, u32[]{:S(2)}, u32[]{:S(2)}) %collective-permute-start.19) | collective-permute-done | bytes 786464 | tf_op jit(solution)/shard_map/ppermute | solution.py:43
  168.4 3.4 %collective-permute-start.24 = (bf16[1536,256]{1,0:T(8,128)(2,1)S(1)}, bf16[1536,256]{1,0:T(8,128)(2,1)S(1)}, u32[]{:S(2)}, u32[]{:S(2)}) collective-permute-start(bf16[1536,256]{1,0:T(8,128)(2,1)S(1)} %add_convert_fusion.2), channel_id=1, source_target_pairs={{8,0},{9,1},{10,2},{11,3},{12,4},{13,5},{14,6},{15,7},{16,8},{17,9... | collective-permute-start | bytes 2359304 | tf_op jit(solution)/shard_map/ppermute | solution.py:43
  174.6 4.0 %collective-permute-start.27 = (bf16[768,256]{1,0:T(8,128)(2,1)S(1)}, bf16[768,256]{1,0:T(8,128)(2,1)S(1)}, u32[]{:S(2)}, u32[]{:S(2)}) collective-permute-start(bf16[768,256]{1,0:T(8,128)(2,1)S(1)} %add_convert_fusion.8), channel_id=1, source_target_pairs={{0,8},{1,9},{2,10},{3,11},{4,12},{5,13},{6,14},{7,15},{8,16},{9,17... | collective-permute-start | bytes 1179656 | tf_op jit(solution)/shard_map/ppermute | solution.py:43
  179.0 10.7 %collective-permute-done.23 = bf16[1536,256]{1,0:T(8,128)(2,1)S(1)} collective-permute-done((bf16[1536,256]{1,0:T(8,128)(2,1)S(1)}, bf16[1536,256]{1,0:T(8,128)(2,1)S(1)}, u32[]{:S(2)}, u32[]{:S(2)}) %collective-permute-start.23) | collective-permute-done | bytes 786464 | tf_op jit(solution)/shard_map/ppermute | solution.py:43
  190.0 4.9 %collective-permute-start.31 = (bf16[768,256]{1,0:T(8,128)(2,1)S(1)}, bf16[768,256]{1,0:T(8,128)(2,1)S(1)}, u32[]{:S(2)}, u32[]{:S(2)}) collective-permute-start(bf16[768,256]{1,0:T(8,128)(2,1)S(1)} %get-tuple-element.149), channel_id=1, source_target_pairs={{0,0},{1,4},{2,2},{3,6},{4,1},{5,5},{6,3},{7,7},{8,8},{9,12},{10,1... | collective-permute-start | bytes 1179656 | tf_op jit(solution)/shard_map/ppermute | solution.py:43
  195.0 3.1 %collective-permute-done.22 = bf16[2,72,4096]{2,1,0:T(8,128)(2,1)S(1)} collective-permute-done((bf16[2,72,4096]{2,1,0:T(8,128)(2,1)S(1)}, bf16[2,72,4096]{2,1,0:T(8,128)(2,1)S(1)}, u32[]{:S(2)}, u32[]{:S(2)}) %collective-permute-start.22) | collective-permute-done | bytes 1179680 | tf_op jit(solution)/shard_map/ppermute | solution.py:43
  203.1 3.4 %collective-permute-start.28 = (bf16[768,256]{1,0:T(8,128)(2,1)S(1)}, bf16[768,256]{1,0:T(8,128)(2,1)S(1)}, u32[]{:S(2)}, u32[]{:S(2)}) collective-permute-start(bf16[768,256]{1,0:T(8,128)(2,1)S(1)} %add_convert_fusion.7), channel_id=1, source_target_pairs={{0,8},{1,9},{2,10},{3,11},{4,12},{5,13},{6,14},{7,15},{8,16},{9,17... | collective-permute-start | bytes 1179656 | tf_op jit(solution)/shard_map/ppermute | solution.py:43
  208.4 3.6 %collective-permute-done.28 = bf16[768,256]{1,0:T(8,128)(2,1)S(1)} collective-permute-done((bf16[768,256]{1,0:T(8,128)(2,1)S(1)}, bf16[768,256]{1,0:T(8,128)(2,1)S(1)}, u32[]{:S(2)}, u32[]{:S(2)}) %collective-permute-start.28) | collective-permute-done | bytes 393248 | tf_op jit(solution)/shard_map/ppermute | solution.py:43
  212.2 8.2 %collective-permute-start.33 = (bf16[384,256]{1,0:T(8,128)(2,1)S(1)}, bf16[384,256]{1,0:T(8,128)(2,1)S(1)}, u32[]{:S(2)}, u32[]{:S(2)}) collective-permute-start(bf16[384,256]{1,0:T(8,128)(2,1)S(1)} %get-tuple-element.153), channel_id=1, source_target_pairs={{0,0},{1,4},{2,2},{3,6},{4,1},{5,5},{6,3},{7,7},{8,8},{9,12},{10,1... | collective-permute-start | bytes 589832 | tf_op jit(solution)/shard_map/ppermute | solution.py:43
  220.4 4.6 %collective-permute-done.33.refs_2_ = bf16[384,256]{1,0:T(8,128)(2,1)S(1)} collective-permute-done((bf16[384,256]{1,0:T(8,128)(2,1)S(1)}, bf16[384,256]{1,0:T(8,128)(2,1)S(1)}, u32[]{:S(2)}, u32[]{:S(2)}) %collective-permute-start.33) | collective-permute-done | bytes 196640 | tf_op jit(solution)/shard_map/ppermute | solution.py:43
  (131 shorter events, 59.8 us)
Async XLA Ops:
  4.9 9.2 %collective-permute-start = (bf16[768,256]{1,0:T(8,128)(2,1)S(1)}, bf16[768,256]{1,0:T(8,128)(2,1)}, u32[]{:S(2)}, u32[]{:S(2)}) collective-permute-start(bf16[768,256]{1,0:T(8,128)(2,1)S(1)} %get-tuple-element.73), channel_id=1, source_target_pairs={{0,0},{1,4},{2,2},{3,6},{4,1},{5,5},{6,3},{7,7},{8,8},{9,12},{10,1... | collective-permute-start | bytes 1179656 | tf_op jit(solution)/shard_map/ppermute | solution.py:43
  8.6 8.9 %collective-permute-start.1 = (bf16[768,256]{1,0:T(8,128)(2,1)S(1)}, bf16[768,256]{1,0:T(8,128)(2,1)}, u32[]{:S(2)}, u32[]{:S(2)}) collective-permute-start(bf16[768,256]{1,0:T(8,128)(2,1)S(1)} %get-tuple-element.74), channel_id=1, source_target_pairs={{0,1},{1,5},{2,3},{3,7},{4,0},{5,4},{6,2},{7,6},{8,9},{9,13},{10,1... | collective-permute-start | bytes 1179656 | tf_op jit(solution)/shard_map/ppermute | solution.py:43
  18.8 8.3 %collective-permute-start.6 = (bf16[384,256]{1,0:T(8,128)(2,1)S(1)}, bf16[384,256]{1,0:T(8,128)(2,1)S(1)}, u32[]{:S(2)}, u32[]{:S(2)}) collective-permute-start(bf16[384,256]{1,0:T(8,128)(2,1)S(1)} %get-tuple-element.80), channel_id=1, source_target_pairs={{0,0},{1,4},{2,2},{3,6},{4,1},{5,5},{6,3},{7,7},{8,8},{9,12},{10,1... | collective-permute-start | bytes 589832 | tf_op jit(solution)/shard_map/ppermute | solution.py:43
  21.7 20.7 %collective-permute-start.2 = (bf16[1536,256]{1,0:T(8,128)(2,1)S(1)}, bf16[1536,256]{1,0:T(8,128)(2,1)S(1)}, u32[]{:S(2)}, u32[]{:S(2)}) collective-permute-start(bf16[1536,256]{1,0:T(8,128)(2,1)S(1)} %pad_maximum_fusion.4.own), channel_id=1, source_target_pairs={{0,8},{1,9},{2,10},{3,11},{4,12},{5,13},{6,14},{7,15},{8,16},{9,17... | collective-permute-start | bytes 2359304 | tf_op jit(solution)/shard_map/ppermute | solution.py:43
  24.9 20.4 %collective-permute-start.3 = (bf16[1536,256]{1,0:T(8,128)(2,1)S(1)}, bf16[1536,256]{1,0:T(8,128)(2,1)S(1)}, u32[]{:S(2)}, u32[]{:S(2)}) collective-permute-start(bf16[1536,256]{1,0:T(8,128)(2,1)S(1)} %pad_maximum_fusion.4.own), channel_id=1, source_target_pairs={{8,0},{9,1},{10,2},{11,3},{12,4},{13,5},{14,6},{15,7},{16,8},{17,9... | collective-permute-start | bytes 2359304 | tf_op jit(solution)/shard_map/ppermute | solution.py:43
  27.4 23.2 %collective-permute-start.10 = (bf16[72,4096]{1,0:T(8,128)(2,1)S(1)}, bf16[72,4096]{1,0:T(8,128)(2,1)S(1)}, u32[]{:S(2)}, u32[]{:S(2)}) collective-permute-start(bf16[72,4096]{1,0:T(8,128)(2,1)S(1)} %get-tuple-element.145), channel_id=1, source_target_pairs={{0,6},{1,7},{2,4},{3,5},{4,2},{5,3},{6,0},{7,1},{8,14},{9,15},{10,... | collective-permute-start | bytes 1769480 | tf_op jit(solution)/shard_map/ppermute | solution.py:43
  29.5 25.0 %collective-permute-start.8 = (bf16[72,4096]{1,0:T(8,128)(2,1)S(1)}, bf16[72,4096]{1,0:T(8,128)(2,1)S(1)}, u32[]{:S(2)}, u32[]{:S(2)}) collective-permute-start(bf16[72,4096]{1,0:T(8,128)(2,1)S(1)} %get-tuple-element.147), channel_id=1, source_target_pairs={{0,4},{1,5},{2,6},{3,7},{4,0},{5,1},{6,2},{7,3},{8,12},{9,13},{10,... | collective-permute-start | bytes 1769480 | tf_op jit(solution)/shard_map/ppermute | solution.py:43
  29.8 26.4 %collective-permute-start.9 = (bf16[72,4096]{1,0:T(8,128)(2,1)S(1)}, bf16[72,4096]{1,0:T(8,128)(2,1)S(1)}, u32[]{:S(2)}, u32[]{:S(2)}) collective-permute-start(bf16[72,4096]{1,0:T(8,128)(2,1)S(1)} %get-tuple-element.146), channel_id=1, source_target_pairs={{0,2},{1,3},{2,0},{3,1},{4,6},{5,7},{6,4},{7,5},{8,10},{9,11},{10,... | collective-permute-start | bytes 1769480 | tf_op jit(solution)/shard_map/ppermute | solution.py:43
  45.3 31.6 %collective-permute-start.4 = (bf16[1536,256]{1,0:T(8,128)(2,1)S(1)}, bf16[1536,256]{1,0:T(8,128)(2,1)S(1)}, u32[]{:S(2)}, u32[]{:S(2)}) collective-permute-start(bf16[1536,256]{1,0:T(8,128)(2,1)S(1)} %collective-permute-done.2.up), channel_id=1, source_target_pairs={{8,16},{9,17},{10,18},{11,19},{12,20},{13,21},{14,22},{15,23},{16,... | collective-permute-start | bytes 2359304 | tf_op jit(solution)/shard_map/ppermute | solution.py:43
  48.6 29.2 %collective-permute-start.5 = (bf16[1536,256]{1,0:T(8,128)(2,1)S(1)}, bf16[1536,256]{1,0:T(8,128)(2,1)S(1)}, u32[]{:S(2)}, u32[]{:S(2)}) collective-permute-start(bf16[1536,256]{1,0:T(8,128)(2,1)S(1)} %collective-permute-done.3.down), channel_id=1, source_target_pairs={{8,0},{9,1},{10,2},{11,3},{12,4},{13,5},{14,6},{15,7},{16,8},{17,9... | collective-permute-start | bytes 2359304 | tf_op jit(solution)/shard_map/ppermute | solution.py:43
  57.9 14.4 %collective-permute-start.11 = (bf16[768,256]{1,0:T(8,128)(2,1)S(1)}, bf16[768,256]{1,0:T(8,128)(2,1)S(1)}, u32[]{:S(2)}, u32[]{:S(2)}) collective-permute-start(bf16[768,256]{1,0:T(8,128)(2,1)S(1)} %pad_maximum_fusion.5.own), channel_id=1, source_target_pairs={{0,8},{1,9},{2,10},{3,11},{4,12},{5,13},{6,14},{7,15},{8,16},{9,17... | collective-permute-start | bytes 1179656 | tf_op jit(solution)/shard_map/ppermute | solution.py:43
  61.0 15.2 %collective-permute-start.12 = (bf16[768,256]{1,0:T(8,128)(2,1)S(1)}, bf16[768,256]{1,0:T(8,128)(2,1)S(1)}, u32[]{:S(2)}, u32[]{:S(2)}) collective-permute-start(bf16[768,256]{1,0:T(8,128)(2,1)S(1)} %pad_maximum_fusion.5.own), channel_id=1, source_target_pairs={{8,0},{9,1},{10,2},{11,3},{12,4},{13,5},{14,6},{15,7},{16,8},{17,9... | collective-permute-start | bytes 1179656 | tf_op jit(solution)/shard_map/ppermute | solution.py:43
  78.8 22.8 %collective-permute-start.14 = (bf16[288,4096]{1,0:T(8,128)(2,1)}, bf16[288,4096]{1,0:T(8,128)(2,1)}, u32[]{:S(2)}, u32[]{:S(2)}) collective-permute-start(bf16[288,4096]{1,0:T(8,128)(2,1)} %pad_maximum_fusion.2.mine), channel_id=1, source_target_pairs={{0,1},{1,0},{2,3},{3,2},{4,5},{5,4},{6,7},{7,6},{8,9},{9,8},{10,11... | collective-permute-start | bytes 7077896 | tf_op jit(solution)/shard_map/ppermute | solution.py:43
  82.7 18.9 %collective-permute-start.13 = (bf16[1536,256]{1,0:T(8,128)(2,1)S(1)}, bf16[1536,256]{1,0:T(8,128)(2,1)S(1)}, u32[]{:S(2)}, u32[]{:S(2)}) collective-permute-start(bf16[1536,256]{1,0:T(8,128)(2,1)S(1)} %broadcast_select_fusion), channel_id=1, source_target_pairs={{8,0},{9,1},{10,2},{11,3},{12,4},{13,5},{14,6},{15,7},{16,24},{17,... | collective-permute-start | bytes 2359304 | tf_op jit(solution)/shard_map/ppermute | solution.py:43
  84.7 27.3 %collective-permute-start.15 = (bf16[768,256]{1,0:T(8,128)(2,1)S(1)}, bf16[768,256]{1,0:T(8,128)(2,1)S(1)}, u32[]{:S(2)}, u32[]{:S(2)}) collective-permute-start(bf16[768,256]{1,0:T(8,128)(2,1)S(1)} %collective-permute-done.11.up), channel_id=1, source_target_pairs={{8,16},{9,17},{10,18},{11,19},{12,20},{13,21},{14,22},{15,23},{16,... | collective-permute-start | bytes 1179656 | tf_op jit(solution)/shard_map/ppermute | solution.py:43
  86.0 26.0 %collective-permute-start.16 = (bf16[768,256]{1,0:T(8,128)(2,1)S(1)}, bf16[768,256]{1,0:T(8,128)(2,1)S(1)}, u32[]{:S(2)}, u32[]{:S(2)}) collective-permute-start(bf16[768,256]{1,0:T(8,128)(2,1)S(1)} %copy-done.2), channel_id=1, source_target_pairs={{8,0},{9,1},{10,2},{11,3},{12,4},{13,5},{14,6},{15,7},{16,8},{17,9... | collective-permute-start | bytes 1179656 | tf_op jit(solution)/shard_map/ppermute | solution.py:43
  112.1 21.8 %collective-permute-start.17 = (bf16[1536,256]{1,0:T(8,128)(2,1)S(1)}, bf16[1536,256]{1,0:T(8,128)(2,1)}, u32[]{:S(2)}, u32[]{:S(2)}) collective-permute-start(bf16[1536,256]{1,0:T(8,128)(2,1)S(1)} %get-tuple-element.93), channel_id=1, source_target_pairs={{0,8},{1,9},{2,10},{3,11},{4,12},{5,13},{6,14},{7,15},{24,16},{25,... | collective-permute-start | bytes 2359304 | tf_op jit(solution)/shard_map/ppermute | solution.py:43
  113.4 12.1 %collective-permute-start.18 = (bf16[768,256]{1,0:T(8,128)(2,1)S(1)}, bf16[768,256]{1,0:T(8,128)(2,1)S(1)}, u32[]{:S(2)}, u32[]{:S(2)}) collective-permute-start(bf16[768,256]{1,0:T(8,128)(2,1)S(1)} %broadcast_select_fusion.1), channel_id=1, source_target_pairs={{8,0},{9,1},{10,2},{11,3},{12,4},{13,5},{14,6},{15,7},{16,24},{17,... | collective-permute-start | bytes 1179656 | tf_op jit(solution)/shard_map/ppermute | solution.py:43
  143.1 21.2 %collective-permute-start.19 = (bf16[1536,256]{1,0:T(8,128)(2,1)S(1)}, bf16[1536,256]{1,0:T(8,128)(2,1)S(1)}, u32[]{:S(2)}, u32[]{:S(2)}) collective-permute-start(bf16[1536,256]{1,0:T(8,128)(2,1)S(1)} %add_convert_fusion.4), channel_id=1, source_target_pairs={{0,8},{1,9},{2,10},{3,11},{4,12},{5,13},{6,14},{7,15},{8,16},{9,17... | collective-permute-start | bytes 2359304 | tf_op jit(solution)/shard_map/ppermute | solution.py:43
  145.0 21.0 %collective-permute-start.20 = (bf16[1536,256]{1,0:T(8,128)(2,1)S(1)}, bf16[1536,256]{1,0:T(8,128)(2,1)S(1)}, u32[]{:S(2)}, u32[]{:S(2)}) collective-permute-start(bf16[1536,256]{1,0:T(8,128)(2,1)S(1)} %add_convert_fusion.4), channel_id=1, source_target_pairs={{16,8},{17,9},{18,10},{19,11},{20,12},{21,13},{22,14},{23,15},{24,... | collective-permute-start | bytes 2359304 | tf_op jit(solution)/shard_map/ppermute | solution.py:43
  146.3 26.9 %collective-permute-start.26 = (bf16[768,256]{1,0:T(8,128)(2,1)S(1)}, bf16[768,256]{1,0:T(8,128)(2,1)S(1)}, u32[]{:S(2)}, u32[]{:S(2)}) collective-permute-start(bf16[768,256]{1,0:T(8,128)(2,1)S(1)} %get-tuple-element.128), channel_id=1, source_target_pairs={{0,8},{1,9},{2,10},{3,11},{4,12},{5,13},{6,14},{7,15},{24,16},{25,... | collective-permute-start | bytes 1179656 | tf_op jit(solution)/shard_map/ppermute | solution.py:43
  166.2 23.4 %collective-permute-start.23 = (bf16[1536,256]{1,0:T(8,128)(2,1)S(1)}, bf16[1536,256]{1,0:T(8,128)(2,1)S(1)}, u32[]{:S(2)}, u32[]{:S(2)}) collective-permute-start(bf16[1536,256]{1,0:T(8,128)(2,1)S(1)} %add_convert_fusion.3), channel_id=1, source_target_pairs={{0,8},{1,9},{2,10},{3,11},{4,12},{5,13},{6,14},{7,15},{8,16},{9,17... | collective-permute-start | bytes 2359304 | tf_op jit(solution)/shard_map/ppermute | solution.py:43
  168.4 21.2 %collective-permute-start.24 = (bf16[1536,256]{1,0:T(8,128)(2,1)S(1)}, bf16[1536,256]{1,0:T(8,128)(2,1)S(1)}, u32[]{:S(2)}, u32[]{:S(2)}) collective-permute-start(bf16[1536,256]{1,0:T(8,128)(2,1)S(1)} %add_convert_fusion.2), channel_id=1, source_target_pairs={{8,0},{9,1},{10,2},{11,3},{12,4},{13,5},{14,6},{15,7},{16,8},{17,9... | collective-permute-start | bytes 2359304 | tf_op jit(solution)/shard_map/ppermute | solution.py:43
  171.9 26.2 %collective-permute-start.22 = (bf16[2,72,4096]{2,1,0:T(8,128)(2,1)S(1)}, bf16[2,72,4096]{2,1,0:T(8,128)(2,1)S(1)}, u32[]{:S(2)}, u32[]{:S(2)}) collective-permute-start(bf16[2,72,4096]{2,1,0:T(8,128)(2,1)S(1)} %slice_bitcast_fusion), channel_id=1, source_target_pairs={{0,4},{1,5},{2,6},{3,7},{4,0},{5,1},{6,2},{7,3},{8,12},{9,13},{10,... | collective-permute-start | bytes 3538952 | tf_op jit(solution)/shard_map/ppermute | solution.py:43
  173.3 24.8 %collective-permute-start.29 = (bf16[768,256]{1,0:T(8,128)(2,1)S(1)}, bf16[768,256]{1,0:T(8,128)(2,1)S(1)}, u32[]{:S(2)}, u32[]{:S(2)}) collective-permute-start(bf16[768,256]{1,0:T(8,128)(2,1)S(1)} %add_convert_fusion.8), channel_id=1, source_target_pairs={{16,8},{17,9},{18,10},{19,11},{20,12},{21,13},{22,14},{23,15},{24,... | collective-permute-start | bytes 1179656 | tf_op jit(solution)/shard_map/ppermute | solution.py:43
  174.6 27.1 %collective-permute-start.27 = (bf16[768,256]{1,0:T(8,128)(2,1)S(1)}, bf16[768,256]{1,0:T(8,128)(2,1)S(1)}, u32[]{:S(2)}, u32[]{:S(2)}) collective-permute-start(bf16[768,256]{1,0:T(8,128)(2,1)S(1)} %add_convert_fusion.8), channel_id=1, source_target_pairs={{0,8},{1,9},{2,10},{3,11},{4,12},{5,13},{6,14},{7,15},{8,16},{9,17... | collective-permute-start | bytes 1179656 | tf_op jit(solution)/shard_map/ppermute | solution.py:43
  190.0 18.4 %collective-permute-start.31 = (bf16[768,256]{1,0:T(8,128)(2,1)S(1)}, bf16[768,256]{1,0:T(8,128)(2,1)S(1)}, u32[]{:S(2)}, u32[]{:S(2)}) collective-permute-start(bf16[768,256]{1,0:T(8,128)(2,1)S(1)} %get-tuple-element.149), channel_id=1, source_target_pairs={{0,0},{1,4},{2,2},{3,6},{4,1},{5,5},{6,3},{7,7},{8,8},{9,12},{10,1... | collective-permute-start | bytes 1179656 | tf_op jit(solution)/shard_map/ppermute | solution.py:43
  194.9 13.4 %collective-permute-start.32 = (bf16[768,256]{1,0:T(8,128)(2,1)S(1)}, bf16[768,256]{1,0:T(8,128)(2,1)S(1)}, u32[]{:S(2)}, u32[]{:S(2)}) collective-permute-start(bf16[768,256]{1,0:T(8,128)(2,1)S(1)} %get-tuple-element.148), channel_id=1, source_target_pairs={{0,4},{1,0},{2,6},{3,2},{4,5},{5,1},{6,7},{7,3},{8,12},{9,8},{10,1... | collective-permute-start | bytes 1179656 | tf_op jit(solution)/shard_map/ppermute | solution.py:43
  198.2 10.2 %collective-permute-start.30 = (bf16[768,256]{1,0:T(8,128)(2,1)S(1)}, bf16[768,256]{1,0:T(8,128)(2,1)S(1)}, u32[]{:S(2)}, u32[]{:S(2)}) collective-permute-start(bf16[768,256]{1,0:T(8,128)(2,1)S(1)} %add_convert_fusion.6), channel_id=1, source_target_pairs={{8,0},{9,1},{10,2},{11,3},{12,4},{13,5},{14,6},{15,7},{16,8},{17,9... | collective-permute-start | bytes 1179656 | tf_op jit(solution)/shard_map/ppermute | solution.py:43
  201.7 26.5 %collective-permute-start.25 = (bf16[2,72,4096]{2,1,0:T(8,128)(2,1)}, bf16[2,72,4096]{2,1,0:T(8,128)(2,1)}, u32[]{:S(2)}, u32[]{:S(2)}) collective-permute-start(bf16[2,72,4096]{2,1,0:T(8,128)(2,1)} %get-tuple-element.143), channel_id=1, source_target_pairs={{0,2},{1,3},{2,0},{3,1},{4,6},{5,7},{6,4},{7,5},{8,10},{9,11},{10,... | collective-permute-start | bytes 3538952 | tf_op jit(solution)/shard_map/ppermute | solution.py:43
  203.1 8.9 %collective-permute-start.28 = (bf16[768,256]{1,0:T(8,128)(2,1)S(1)}, bf16[768,256]{1,0:T(8,128)(2,1)S(1)}, u32[]{:S(2)}, u32[]{:S(2)}) collective-permute-start(bf16[768,256]{1,0:T(8,128)(2,1)S(1)} %add_convert_fusion.7), channel_id=1, source_target_pairs={{0,8},{1,9},{2,10},{3,11},{4,12},{5,13},{6,14},{7,15},{8,16},{9,17... | collective-permute-start | bytes 1179656 | tf_op jit(solution)/shard_map/ppermute | solution.py:43
  212.2 12.8 %collective-permute-start.33 = (bf16[384,256]{1,0:T(8,128)(2,1)S(1)}, bf16[384,256]{1,0:T(8,128)(2,1)S(1)}, u32[]{:S(2)}, u32[]{:S(2)}) collective-permute-start(bf16[384,256]{1,0:T(8,128)(2,1)S(1)} %get-tuple-element.153), channel_id=1, source_target_pairs={{0,0},{1,4},{2,2},{3,6},{4,1},{5,5},{6,3},{7,7},{8,8},{9,12},{10,1... | collective-permute-start | bytes 589832 | tf_op jit(solution)/shard_map/ppermute | solution.py:43
  (25 other events, 122.3 us)

commit v9 on v8

--- a/solution.py
+++ b/solution.py
@@ -18,6 +18,10 @@
 
 def tie(value, *others):
     return lax.optimization_barrier((value,) + others)[0]
+
+
+def tie_all(values, *others):
+    return [tie(value, *others) for value in values]
 
 
 def added(*terms):
@@ -91,27 +95,37 @@
     return (jnp.arange(hidden_width, dtype=jnp.int32)[:, None] == source[None, :]).astype(BF)
 
 
-def pack_kernel(pieces, x_ref, gate_ref, up_ref, down_ref, shuffle_ref, *outs):
+def pack_kernel(pieces, x_ref, gate_in, up_in, down_in, shuffle_ref, a_ref, b_ref, gate_ref, up_ref, down_ref, load):
+    loads = [
+        pltpu.make_async_copy(source, target, load.at[n])
+        for n, (source, target) in enumerate(((gate_in, gate_ref), (up_in, up_ref), (down_in, down_ref)))
+    ]
+    for copy in loads:
+        copy.start()
     rows, hidden_width = gate_ref.shape
     half, block = hidden_width // 2, down_ref.shape[0]
     shuffle = shuffle_ref[...]
-    gate, up = dot(gate_ref[...], shuffle).astype(BF), dot(up_ref[...], shuffle).astype(BF)
+    loads[0].wait()
+    gate = dot(gate_ref[...], shuffle).astype(BF)
+    loads[1].wait()
+    up = dot(up_ref[...], shuffle).astype(BF)
+    loads[2].wait()
     x = x_ref[0]
-    done = 0
-    for number, piece in enumerate(pieces):
+    done = base = 0
+    for piece in pieces:
         units = piece * half // sum(pieces)
-        count = 2 * units // LANES
-        for side, start in ((0, x), (1, 1 - x)):
-            ref = outs[2 * number + side]
+        count, columns = 2 * units // LANES, down_ref.shape[1] // LANES
+        for side, (ref, start) in enumerate(((a_ref, x), (b_ref, 1 - x))):
             at = side * half + done * units // piece
             both = jnp.concatenate([gate[:, at:at + units], up[:, at:at + units]], axis=1)
             for i in range(count):
-                ref[i * rows:(i + 1) * rows, :] = both[:, i * LANES:(i + 1) * LANES]
+                ref[base + i * rows:base + (i + 1) * rows, :] = both[:, i * LANES:(i + 1) * LANES]
             source = pl.ds(pl.multiple_of(start * (block // 2) + done, 16), piece)
-            for j in range(down_ref.shape[1] // LANES):
-                to = count * rows + j * piece
+            for j in range(columns):
+                to = base + count * rows + j * piece
                 ref[to:to + piece, :] = down_ref[source, j * LANES:(j + 1) * LANES]
         done += piece
+        base += count * rows + columns * piece
 
 
 def unpack_kernel(pieces, x_ref, *refs):
@@ -139,8 +153,8 @@
     up_ref[...] = dot(jnp.concatenate(ups[0] + ups[1], axis=1), shuffle, ((1,), (1,)))
 
 
-def expert_kernel(z_ref, own, up, down, up_2, down_2, last, mine, theirs, *refs):
-    weight_outs, (hidden_out, d_both_out, outer_out), outs, refs = refs[:2], refs[2:5], refs[5:9], refs[9:]
+def expert_kernel(offset, z_ref, own, up, down, far, up_2, down_2, mine, theirs, *refs):
+    weight_outs, (hidden_out, d_both_out), term_outs, refs = refs[:2], refs[2:4], refs[4:8], refs[8:]
     packed, x, grads, gate_up, w_down, pre, d_hidden, hidden, d_both, d_down, terms, load, store = refs
     places, size, _ = packed.shape
     rows, width = x.shape
@@ -152,6 +166,7 @@
     count, columns = 2 * units // LANES, width // LANES
     size_half = size // 2
     z = z_ref[0]
+    own, up, down = (ref.at[offset:offset + size] for ref in (own, up, down))
 
     loads = [
         pltpu.make_async_copy(a, b, load.at[places + n])
@@ -168,9 +183,9 @@
         copy.start()
     pltpu.make_async_copy(own, packed.at[0], load.at[0]).start()
     for s, is_one, one, other in (
-        (1, z == places - 1, last, down),
+        (1, z == places - 1, far, down),
         (2, z < 2, down_2, up_2),
-        (3, z == 0, last, up),
+        (3, z == 0, far, up),
     ):
         @pl.when(is_one)
         def _():
@@ -251,9 +266,12 @@
             for j in range(columns):
                 to = h * size_half + count * part_rows + j * piece
                 terms[k, to:to + piece, :] = d_down[down_rows(k, h), j * LANES:(j + 1) * LANES]
-        store_to(outs[k], terms.at[k])
         if k == 1:
-            store_to(outer_out, terms.at[jnp.where(z == 0, places - 1, 1)])
+            outer = jnp.where(z < 2, places - 1, 1)
+            store_to(term_outs[0], terms.at[outer])
+            store_to(term_outs[1], terms.at[places - outer])
+        elif k != places - 1:
+            store_to(term_outs[2 if k else 3], terms.at[k])
     for copy in stores:
         copy.wait()
 
@@ -285,13 +303,14 @@
 
 
 def pack(pieces, x, gate, up, down, shuffle):
-    rows, hidden_width = gate.shape
-    sizes = [(rows * hidden_width + down.size // 2) * piece // sum(pieces) // LANES for piece in pieces]
+    size = (gate.size + down.size // 2) // LANES
+    anywhere = pl.BlockSpec(memory_space=pl.ANY)
     return pl.pallas_call(
         functools.partial(pack_kernel, pieces),
-        out_shape=[jax.ShapeDtypeStruct((size, LANES), BF) for size in sizes for _ in range(2)],
-        in_specs=[IN_SMEM] + in_vmem(4),
-        out_specs=in_vmem(2 * len(pieces)),
+        out_shape=[jax.ShapeDtypeStruct((size, LANES), BF)] * 2,
+        in_specs=[IN_SMEM] + [anywhere] * 3 + in_vmem(1),
+        out_specs=in_vmem(2),
+        scratch_shapes=[pltpu.VMEM(w.shape, BF) for w in (gate, up, down)] + [pltpu.SemaphoreType.DMA((3,))],
         compiler_params=pltpu.CompilerParams(vmem_limit_bytes=VMEM_BYTES // 2),
     )(x, gate, up, down, shuffle)
 
@@ -306,18 +325,18 @@
     )(x, *packed, shuffle)
 
 
-def expert(z, places, units, weights, mine, theirs):
-    size = weights[0].shape[0]
+def expert(z, places, units, offset, weights, mine, theirs):
+    size = weights[-1].shape[0]
     slots, width = mine.shape[0], mine.shape[1] // 2
     rows = 2 * slots
     for_rows = [
         jax.ShapeDtypeStruct(shape, BF) for shape in ((width, 2 * units), (units, width), (rows, units), (rows, 2 * units))
     ]
     outs = pl.pallas_call(
-        expert_kernel,
-        out_shape=for_rows + [jax.ShapeDtypeStruct((size, LANES), BF)] * 5,
+        functools.partial(expert_kernel, offset),
+        out_shape=for_rows + [jax.ShapeDtypeStruct((size, LANES), BF)] * 4,
         in_specs=[IN_SMEM] + [pl.BlockSpec(memory_space=pl.ANY)] * 8,
-        out_specs=[pl.BlockSpec(memory_space=pl.ANY)] * 9,
+        out_specs=[pl.BlockSpec(memory_space=pl.ANY)] * 8,
         scratch_shapes=[
             pltpu.VMEM((places, size, LANES), BF),
             pltpu.VMEM((rows, width), BF),
@@ -331,14 +350,14 @@
             pltpu.VMEM((units, width), BF),
             pltpu.VMEM((places, size, LANES), BF),
             pltpu.SemaphoreType.DMA((places + 4,)),
-            pltpu.SemaphoreType.DMA((9,)),
+            pltpu.SemaphoreType.DMA((8,)),
         ],
         compiler_params=pltpu.CompilerParams(vmem_limit_bytes=VMEM_BYTES),
         cost_estimate=pl.CostEstimate(
             flops=12 * rows * width * units, bytes_accessed=16 * 2**20, transcendentals=rows * units
         ),
     )(z, *weights, mine, theirs)
-    return outs[:4], outs[4], outs[5:]
+    return outs[:4], outs[4:]
 
 
 def token_rows(chunks, slots, width):
@@ -398,9 +417,12 @@
     def back_b(z, x, q, c):
         return z, 1 - c, q, x
 
+    def spread_halves(part_a, part_b):
+        got_a, got_b = g.send(part_a, out_a), g.send(part_b, out_b)
+        return jnp.where(first, got_a, got_b), jnp.where(first, got_b, got_a)
+
     def spread(part_a, part_b):
-        got_a, got_b = g.send(part_a, out_a), g.send(part_b, out_b)
-        return jnp.concatenate([jnp.where(first, got_a, got_b), jnp.where(first, got_b, got_a)], axis=0)
+        return jnp.concatenate(spread_halves(part_a, part_b), axis=0)
 
     def unspread(both):
         n = both.shape[0] // 2
@@ -449,54 +471,68 @@
     if in_kernels:
         place_x, place_z = g.x.reshape(1).astype(jnp.int32), g.z.reshape(1).astype(jnp.int32)
         units = [piece * g.dps for piece in pieces]
-        a, b, a2, b2 = pack(pieces, place_x, w_gate[0], w_up[0], w_down[0], shuffle)
-        ups, downs, passing = {0: 1, 1: 2, 2: 3}, {1: 0, 2: 1, 3: 2}, {2: 3, 1: 0}
-        outward, inward_up, inward_down = {0: 1, 3: 2}, {0: 1, 1: 2}, {3: 2, 2: 1}
-        to_last = g.z == 2
-
-        shard, a2, b2 = together((spread(a, b), a2, b2))
+        a, b = pack(pieces, place_x, w_gate[0], w_up[0], w_down[0], shuffle)
+        ups, downs = {0: 1, 1: 2, 2: 3}, {1: 0, 2: 1, 3: 2}
+        split = a.shape[0] * pieces[0] // part
+
+        def forward(up, down):
+            far = g.hop(jnp.where(g.z == 1, up, down), {1: 3, 2: 0})
+            return far, g.hop(up, {1: 2, 2: 3}), g.hop(down, {1: 0, 2: 1})
+
+        def inner_sums(terms, far, from_low, from_high):
+            outer, inner, _, own = terms
+            is_low, is_end = g.z == 1, (g.z == 0) | (g.z == 3)
+            to_end = added(outer, jnp.where(is_low, from_high, from_low), far)
+            to_mid = added(inner, jnp.where(is_low, from_low, from_high))
+            return own, jnp.where(is_end, inner, to_end), to_mid
+
+        def cross(to_end, to_mid):
+            return g.hop(to_end, {0: 1, 1: 0, 2: 3, 3: 2}), g.hop(to_mid, {1: 2, 2: 1})
+
+        outward, inward_up, inward_down = {0: 2, 3: 1}, {0: 1, 1: 2}, {3: 2, 2: 1}
+
+        a, b = spread_halves(a, b)
+        shard = jnp.concatenate([a[:split], b[:split], a[split:], b[split:]], axis=0)
+        shard, sent = together((shard, sent))
         up, down = g.hop(shard, ups), g.hop(shard, downs)
-        shard2, sent = together((spread(a2, b2), sent))
-        up, down = together((up, down))
-        up_2, down_2 = g.hop(up, {1: 2, 2: 3}), g.hop(down, {1: 0, 2: 1})
-        shard2, mine = together((shard2, exchange(sent, 1)))
-        up2, down2 = g.hop(shard2, ups), g.hop(shard2, downs)
-        up_2, down_2, up2, down2, mine = together((up_2, down_2, up2, down2, mine))
-        last = g.hop(jnp.where(to_last, up_2, down_2), passing)
-        up2_2, down2_2 = g.hop(up2, {1: 2, 2: 3}), g.hop(down2, {1: 0, 2: 1})
+        up, down, mine = together((up, down, exchange(sent, 1)))
+        offset = 2 * split
+        passed = forward(up[:offset], down[:offset])
         theirs = g.send(mine, other_core)
-        chunk, outer, terms = expert(
-            place_z, g.zs, units[0], (shard, up, down, up_2, down_2, last), mine, theirs
-        )
-        up2_2, down2_2, outer = together((up2_2, down2_2, outer))
-        last2 = g.hop(jnp.where(to_last, up2_2, down2_2), passing)
-        begun = g.hop(outer, outward)
-        chunk2, outer2, terms2 = expert(
-            place_z, g.zs, units[1], (shard2, up2, down2, up2_2, down2_2, last2), mine, theirs
-        )
-        begun, outer2, chunk2 = together((begun, outer2, chunk2))
-        middle, outer2, chunk2 = together((added(terms[2], begun), outer2, chunk2))
-        sum_up, sum_down = g.hop(middle, inward_up), g.hop(middle, inward_down)
-        begun2 = g.hop(outer2, outward)
-        keep, give = token_rows((chunk, chunk2), slots, width)
+        up2, down2 = tie(up[offset:], *passed), tie(down[offset:], *passed)
+        passed2 = forward(up2, down2)
+        chunk, terms = expert(place_z, g.zs, units[0], 0, (shard, up, down, *passed), mine, theirs)
+        far, from_low = g.hop(terms[0], outward), g.hop(terms[2], inward_up)
+        passed2 = tie_all(passed2, terms[0], terms[2])
+        from_high = g.hop(tie(terms[2], *passed2), inward_down)
+        chunk2, terms2 = expert(place_z, g.zs, units[1], offset, (shard, up, down, *passed2), mine, theirs)
+        far2, from_low2 = g.hop(terms2[0], outward), g.hop(terms2[2], inward_up)
+        far, from_low, from_high, far2, from_low2 = together((far, from_low, from_high, far2, from_low2))
+        own, to_end, to_mid = inner_sums(terms, far, from_low, from_high)
+        middle2, to_end, to_mid = together((terms2[2], to_end, to_mid))
+        end, mid = cross(to_end, to_mid)
+        from_high2 = g.hop(middle2, inward_down)
+        keep, give = token_rows([tie_all(parts, to_end, to_mid) for parts in (chunk, chunk2)], slots, width)
         sums = added(keep, g.send(give, other_core)).reshape(g.qs, 2, cap, 2 * width)
-        sum_up, sum_down, sums = together((sum_up, sum_down, sums))
-        far_rows = g.send(sums[:, 1], lambda z, x, q, c: (z, 1 - x, q, c))
-        sum_up, sum_down = g.hop(added(terms[1], sum_up), ups), g.hop(added(terms[3], sum_down), downs)
-        middle2 = added(terms2[2], begun2)
-        sum_up2, sum_down2 = g.hop(middle2, inward_up), g.hop(middle2, inward_down)
-        grad = added(terms[0], sum_up, sum_down)
-        far_rows = tie(far_rows, grad)
-        near = jnp.stack([sums[:, 0], far_rows], axis=1)
-        got = jnp.concatenate(
-            [near[0]] + [g.send(near[d], lambda z, x, q, c, d=d: (z, x, (q - d) % g.qs, c)) for d in range(1, g.qs)]
-        ).reshape(slots, 2 * width)
-        sum_up2, sum_down2 = tie(sum_up2, near), tie(sum_down2, near)
-        grads = unspread(grad)
-        sum_up2, sum_down2 = g.hop(added(terms2[1], sum_up2), ups), g.hop(added(terms2[3], sum_down2), downs)
-        sum_up2, sum_down2, grads = together((sum_up2, sum_down2, grads))
-        grad2 = added(terms2[0], sum_up2, sum_down2)
-        got = tie(got, grad2)
+        sums = tie(sums, from_high2)
+        own2, to_end2, to_mid2 = inner_sums(terms2, far2, from_low2, from_high2)
+        end2, mid2 = cross(to_end2, to_mid2)
+
+        def along_x(rows):
+            return jnp.stack([rows[:, 0], g.send(rows[:, 1], lambda z, x, q, c: (z, 1 - x, q, c))], axis=1)
+
+        def along_q(rows):
+            return jnp.stack(
+                [rows[0]] + [g.send(rows[d], lambda z, x, q, c, d=d: (z, x, (q - d) % g.qs, c)) for d in range(1, g.qs)]
+            )
+
+        returned, back_rows = together((along_x(sums[..., :width]), along_q(sums[..., width:])))
+        grads = unspread(tie(added(own, end, mid), returned, back_rows))
+        returned, back_rows = along_q(returned), along_x(back_rows)
+        end2, mid2, grads = together((end2, mid2, grads))
+        grad2 = added(own2, end2, mid2)
+        returned, back_rows = tie(returned, grad2), tie(back_rows, grad2)
+        returned, back_rows = returned.reshape(slots, width), back_rows.reshape(slots, width)
         grads += unspread(grad2)
         d_w_gate, d_w_up, d_w_down = unpack(pieces, place_x, grads, shuffle, *shapes)
     else:
@@ -538,7 +574,7 @@
             dot(jnp.concatenate([both_a[:, cols], both_b[:, cols]], axis=1), shuffle, ((1,), (1,)))
             for cols in (slice(0, half), slice(half, None))
         )
-    returned, back_rows = got[:, :width], got[:, width:]
+        returned, back_rows = got[:, :width], got[:, width:]
 
     high = lax.reduce_precision(weighted, 8, 7)
     mixed = (dot(high.astype(BF), returned) + dot((weighted - high).astype(BF), returned)).astype(BF)

time: 237 us -> 272 us (1.15)
  waiting for transfers between devices: 102 us -> 141 us
  starting transfers between devices: 77.5 us -> 61.6 us
  other arithmetic: 14.3 us -> 20.8 us
  local copies, waits for them, and re-layouts: 7.38 us -> 11.3 us
    ppermute x35 -> x33, waiting for transfers between devices: 102 us -> 141 us  [send(): return lax.ppermute(value, BOTH, pairs)]
    ppermute x35 -> x33, starting transfers between devices: 77.5 us -> 61.6 us  [send(): return lax.ppermute(value, BOTH, pairs)]
    select_n x4, other arithmetic: 2.51 us -> 6 us  [the longest x2 4.64 us: inner_sums(): return (own, jnp.where(is_end, inner, to_end), to_mid)]
    convert_element_type x9 -> x5, other arithmetic: 3.55 us -> 6.58 us  [added(): return sum((t.astype(F32) for t in terms)).astype(BF)]
    unnamed x44 -> x58, local copies, waits for them, and re-layouts: 6.76 us -> 9.35 us
  transfers between devices with their start and end apart: 35 -> 33, of which waited for: 18 -> 16; matrix products, arithmetic and copies ran while one was open for 5% -> 8% of each run, Pallas kernels for 9% -> 7%
where the time goes in v9:
time: 272 us; the launch traced here: 271 us
  waiting for transfers between devices  141 us (52%)
  starting transfers between devices  61.6 us (23%)
  Pallas kernels  28.3 us (10%)
  other arithmetic  20.8 us (8%)
  local copies, waits for them, and re-layouts  11.3 us (4%)
  matrix products  5.9 us (2%)
    ppermute x33, waiting for transfers between devices, send(): return lax.ppermute(value, BOTH, pairs)  141 us
    ppermute x33, starting transfers between devices, send(): return lax.ppermute(value, BOTH, pairs)  61.6 us
    pallas_call x2, Pallas kernels, expert(): pl.pallas_call(functools.partial(expert_kernel, offset), out_shape=for_ro...  18.2 us
    unnamed x58, local copies, waits for them, and re-layouts  9.35 us
    convert_element_type x5, other arithmetic, added(): return sum((t.astype(F32) for t in terms)).astype(BF)  6.58 us
    pallas_call x1, Pallas kernels, token_rows(): pl.pallas_call(functools.partial(rows_kernel, len(chunks)), grid=(2 * til...  6.18 us
    dot_general x7, matrix products, dot(): return lax.dot_general(a, b, (dims, ((), ())), preferred_element_type=F32)  5.9 us
  transfers between devices with their start and end apart: 33, of which 16 were waited for; matrix products, arithmetic and copies ran while one was open for 8% of the time, Pallas kernels for 7%

profile of v9, /device:TPU:9, one launch (start us, length us, event | category | flops | bytes accessed | tf_op | source)
XLA Modules:
  0.0 270.9 jit_solution(17066107287289961243)
XLA Ops:
  6.1 3.8 %collective-permute-start = (bf16[1152,256]{1,0:T(8,128)(2,1)S(1)}, bf16[1152,256]{1,0:T(8,128)(2,1)}, u32[]{:S(2)}, u32[]{:S(2)}) collective-permute-start(bf16[1152,256]{1,0:T(8,128)(2,1)S(1)} %get-tuple-element.66), channel_id=1, source_target_pairs={{0,0},{1,4},{2,2},{3,6},{4,1},{5,5},{6,3},{7,7},{8,8},{9,12},{10,1... | collective-permute-start | bytes 1769480 | tf_op jit(solution)/shard_map/ppermute | solution.py:47
  17.6 5.5 %collective-permute-done.1 = bf16[1152,256]{1,0:T(8,128)(2,1)} collective-permute-done((bf16[1152,256]{1,0:T(8,128)(2,1)S(1)}, bf16[1152,256]{1,0:T(8,128)(2,1)}, u32[]{:S(2)}, u32[]{:S(2)}) %collective-permute-start.1) | collective-permute-done | bytes 589856 | tf_op jit(solution)/shard_map/ppermute | solution.py:47
  24.6 3.2 %collective-permute-start.2 = (bf16[2304,256]{1,0:T(8,128)(2,1)S(1)}, bf16[2304,256]{1,0:T(8,128)(2,1)S(1)}, u32[]{:S(2)}, u32[]{:S(2)}) collective-permute-start(bf16[2304,256]{1,0:T(8,128)(2,1)S(1)} %pad_maximum_fusion.2.own), channel_id=1, source_target_pairs={{0,8},{1,9},{2,10},{3,11},{4,12},{5,13},{6,14},{7,15},{8,16},{9,17... | collective-permute-start | bytes 3538952 | tf_op jit(solution)/shard_map/ppermute | solution.py:47
  27.8 2.1 collective-permute-start.3
  30.2 3.0 %collective-permute-start.6 = (bf16[72,4096]{1,0:T(8,128)(2,1)S(1)}, bf16[72,4096]{1,0:T(8,128)(2,1)S(1)}, u32[]{:S(2)}, u32[]{:S(2)}) collective-permute-start(bf16[72,4096]{1,0:T(8,128)(2,1)S(1)} %get-tuple-element.131), channel_id=1, source_target_pairs={{0,6},{1,7},{2,4},{3,5},{4,2},{5,3},{6,0},{7,1},{8,14},{9,15},{10,... | collective-permute-start | bytes 1769480 | tf_op jit(solution)/shard_map/ppermute | solution.py:47
  33.6 12.8 %collective-permute-done.6 = bf16[72,4096]{1,0:T(8,128)(2,1)S(1)} collective-permute-done((bf16[72,4096]{1,0:T(8,128)(2,1)S(1)}, bf16[72,4096]{1,0:T(8,128)(2,1)S(1)}, u32[]{:S(2)}, u32[]{:S(2)}) %collective-permute-start.6) | collective-permute-done | bytes 589856 | tf_op jit(solution)/shard_map/ppermute | solution.py:47
  46.4 13.3 %collective-permute-done.5 = bf16[72,4096]{1,0:T(8,128)(2,1)S(1)} collective-permute-done((bf16[72,4096]{1,0:T(8,128)(2,1)S(1)}, bf16[72,4096]{1,0:T(8,128)(2,1)S(1)}, u32[]{:S(2)}, u32[]{:S(2)}) %collective-permute-start.5) | collective-permute-done | bytes 589856 | tf_op jit(solution)/shard_map/ppermute | solution.py:47
  64.1 4.3 %collective-permute-start.7 = (bf16[1536,256]{1,0:T(8,128)(2,1)S(1)}, bf16[1536,256]{1,0:T(8,128)(2,1)S(1)}, u32[]{:S(2)}, u32[]{:S(2)}) collective-permute-start(bf16[1536,256]{1,0:T(8,128)(2,1)S(1)} %get-tuple-element.137), channel_id=1, source_target_pairs={{8,24},{9,25},{10,26},{11,27},{12,28},{13,29},{14,30},{15,31},{16,... | collective-permute-start | bytes 2359304 | tf_op jit(solution)/shard_map/ppermute | solution.py:47
  72.7 12.4 %collective-permute-done.7.far = bf16[1536,256]{1,0:T(8,128)(2,1)S(1)} collective-permute-done((bf16[1536,256]{1,0:T(8,128)(2,1)S(1)}, bf16[1536,256]{1,0:T(8,128)(2,1)S(1)}, u32[]{:S(2)}, u32[]{:S(2)}) %collective-permute-start.7) | collective-permute-done | bytes 786464 | tf_op jit(solution)/shard_map/ppermute | solution.py:47
  85.2 16.9 %collective-permute-done.8.up_2 = bf16[1536,256]{1,0:T(8,128)(2,1)S(1)} collective-permute-done((bf16[1536,256]{1,0:T(8,128)(2,1)S(1)}, bf16[1536,256]{1,0:T(8,128)(2,1)S(1)}, u32[]{:S(2)}, u32[]{:S(2)}) %collective-permute-start.8) | collective-permute-done | bytes 786464 | tf_op jit(solution)/shard_map/ppermute | solution.py:47
  102.1 5.5 %collective-permute-start.11 = (bf16[768,256]{1,0:T(8,128)(2,1)S(1)}, bf16[768,256]{1,0:T(8,128)(2,1)S(1)}, u32[]{:S(2)}, u32[]{:S(2)}) collective-permute-start(bf16[768,256]{1,0:T(8,128)(2,1)S(1)} %broadcast_select_fusion.5), channel_id=1, source_target_pairs={{8,24},{9,25},{10,26},{11,27},{12,28},{13,29},{14,30},{15,31},{16,... | collective-permute-start | bytes 1179656 | tf_op jit(solution)/shard_map/ppermute | solution.py:47
  110.9 10.5 %shard_map.119 = (bf16[2048,512]{1,0:T(8,128)(2,1)}, bf16[256,2048]{1,0:T(8,128)(2,1)}, bf16[576,256]{1,0:T(8,128)(2,1)S(1)}, bf16[576,512]{1,0:T(8,128)(2,1)S(1...) custom-call(s32[1]{0:T(128)} %bitcast.z_ref, ...), custom_call_target="tpu_custom_call" | custom-call | flops 3623878656 | bytes 16777216 | tf_op jit(solution)/shard_map/pallas_call | solution.py:335
  123.6 3.4 %collective-permute-start.15 = (bf16[1536,256]{1,0:T(8,128)(2,1)}, bf16[1536,256]{1,0:T(8,128)(2,1)}, u32[]{:S(2)}, u32[]{:S(2)}) collective-permute-start(bf16[1536,256]{1,0:T(8,128)(2,1)} %get-tuple-element.83), channel_id=1, source_target_pairs={{0,8},{1,9},{2,10},{3,11},{4,12},{5,13},{6,14},{7,15},{8,16},{9,17... | collective-permute-start | bytes 2359304 | tf_op jit(solution)/shard_map/ppermute | solution.py:47
  128.3 7.7 %shard_map.120 = (bf16[2048,256]{1,0:T(8,128)(2,1)S(1)}, bf16[128,2048]{1,0:T(8,128)(2,1)S(1)}, bf16[576,128]{1,0:T(8,128)(2,1)S(1)}, bf16[576,256]{1,0:T(8,128)...) custom-call(s32[1]{0:T(128)} %bitcast.z_ref, ...), custom_call_target="tpu_custom_call" | custom-call | flops 1811939328 | bytes 16777216 | tf_op jit(solution)/shard_map/pallas_call | solution.py:335
  139.9 4.0 %collective-permute-start.18 = (bf16[768,256]{1,0:T(8,128)(2,1)}, bf16[768,256]{1,0:T(8,128)(2,1)}, u32[]{:S(2)}, u32[]{:S(2)}) collective-permute-start(bf16[768,256]{1,0:T(8,128)(2,1)} %get-tuple-element.107), channel_id=1, source_target_pairs={{0,8},{1,9},{2,10},{3,11},{4,12},{5,13},{6,14},{7,15},{8,16},{9,17... | collective-permute-start | bytes 1179656 | tf_op jit(solution)/shard_map/ppermute | solution.py:47
  144.0 25.1 %collective-permute-done.17 = bf16[768,256]{1,0:T(8,128)(2,1)} collective-permute-done((bf16[768,256]{1,0:T(8,128)(2,1)}, bf16[768,256]{1,0:T(8,128)(2,1)}, u32[]{:S(2)}, u32[]{:S(2)}) %collective-permute-start.17) | collective-permute-done | bytes 393248 | tf_op jit(solution)/shard_map/ppermute | solution.py:47
  169.1 8.8 %collective-permute-done.18 = bf16[768,256]{1,0:T(8,128)(2,1)} collective-permute-done((bf16[768,256]{1,0:T(8,128)(2,1)}, bf16[768,256]{1,0:T(8,128)(2,1)}, u32[]{:S(2)}, u32[]{:S(2)}) %collective-permute-start.18) | collective-permute-done | bytes 393248 | tf_op jit(solution)/shard_map/ppermute | solution.py:47
  177.9 2.4 add_convert_fusion.2
  180.3 3.1 %fusion.3 = bf16[1536,256]{1,0:T(8,128)(2,1)} fusion(bf16[1536,256]{1,0:T(8,128)(2,1)S(1)} %get-tuple-element.82, bf16[1536,256]{1,0:T(8,128)(2,1)} %collective-permute-done.14, bf16[1536,256]{1,0:T(8,128)(2,1)} %get-tuple-element.76, bf16[1536,256]{1,0:T(8,128)(2,1)} %collective-permute-done.16, bf16[1536,256]{1,0:T(8,128)(2,1)} %collective-permute-done.15, ...), kind=kLoop, calls=%fused_computation.24 | loop fusion | flops 3145728 | bytes 4718594 | tf_op jit(solution)/shard_map/jit(_where)/select_n | solution.py:487
  183.5 6.2 %shard_map.121 = (bf16[288,4096]{1,0:T(8,128)(2,1)S(1)}, bf16[288,4096]{1,0:T(8,128)(2,1)}) custom-call(bf16[2048,512]{1,0:T(8,128)(2,1)S(1)} %copy-done.16, bf16[256,2048]{1,0:T(8,128)(2,1)S(1)} %copy-done.17, bf16[576,256]{1,0:T(8,128)(2,1)S(1)} %copy-done.21, bf16[576,512]{1,0:T(8,128)(2,1)S(1)} %copy-done.19, bf16[2048,256]{1,0:T(8,128)(2,1)S(1)} %copy-done.11, ...), custom_call_target="tpu_custom_call" | custom-call | flops 2717908992 | bytes 12582912 | tf_op jit(solution)/shard_map/pallas_call | solution.py:375
  194.0 4.0 %collective-permute-start.27 = (bf16[1536,256]{1,0:T(8,128)(2,1)}, bf16[1536,256]{1,0:T(8,128)(2,1)S(1)}, u32[]{:S(2)}, u32[]{:S(2)}) collective-permute-start(bf16[1536,256]{1,0:T(8,128)(2,1)} %add_convert_fusion.2), channel_id=1, source_target_pairs={{8,16},{9,17},{10,18},{11,19},{12,20},{13,21},{14,22},{15,23},{16,... | collective-permute-start | bytes 2359304 | tf_op jit(solution)/shard_map/ppermute | solution.py:47
  198.1 7.5 %collective-permute-done.20 = bf16[768,256]{1,0:T(8,128)(2,1)S(1)} collective-permute-done((bf16[768,256]{1,0:T(8,128)(2,1)}, bf16[768,256]{1,0:T(8,128)(2,1)S(1)}, u32[]{:S(2)}, u32[]{:S(2)}) %collective-permute-start.20) | collective-permute-done | bytes 393248 | tf_op jit(solution)/shard_map/ppermute | solution.py:47
  208.3 2.1 collective-permute-start.25
  210.4 2.6 add_convert_fusion
  214.1 8.2 %collective-permute-done.27 = bf16[1536,256]{1,0:T(8,128)(2,1)S(1)} collective-permute-done((bf16[1536,256]{1,0:T(8,128)(2,1)}, bf16[1536,256]{1,0:T(8,128)(2,1)S(1)}, u32[]{:S(2)}, u32[]{:S(2)}) %collective-permute-start.27) | collective-permute-done | bytes 786464 | tf_op jit(solution)/shard_map/ppermute | solution.py:47
  223.5 2.9 %collective-permute-done.21 = bf16[2,72,2048]{2,1,0:T(8,128)(2,1)S(1)} collective-permute-done((bf16[2,72,2048]{2,1,0:T(8,128)(2,1)S(1)}, bf16[2,72,2048]{2,1,0:T(8,128)(2,1)S(1)}, u32[]{:S(2)}, u32[]{:S(2)}) %collective-permute-start.21) | collective-permute-done | bytes 589856 | tf_op jit(solution)/shard_map/ppermute | solution.py:47
  226.6 9.4 %collective-permute-done.22 = bf16[2,72,2048]{2,1,0:T(8,128)(2,1)S(1)} collective-permute-done((bf16[2,72,2048]{2,1,0:T(8,128)(2,1)S(1)}, bf16[2,72,2048]{2,1,0:T(8,128)(2,1)S(1)}, u32[]{:S(2)}, u32[]{:S(2)}) %collective-permute-start.22) | collective-permute-done | bytes 589856 | tf_op jit(solution)/shard_map/ppermute | solution.py:47
  237.0 5.4 %collective-permute-start.28 = (bf16[768,256]{1,0:T(8,128)(2,1)S(1)}, bf16[768,256]{1,0:T(8,128)(2,1)S(1)}, u32[]{:S(2)}, u32[]{:S(2)}) collective-permute-start(bf16[768,256]{1,0:T(8,128)(2,1)S(1)} %get-tuple-element.142), channel_id=1, source_target_pairs={{0,0},{1,4},{2,2},{3,6},{4,1},{5,5},{6,3},{7,7},{8,8},{9,12},{10,1... | collective-permute-start | bytes 1179656 | tf_op jit(solution)/shard_map/ppermute | solution.py:47
  244.2 6.9 %collective-permute-done.28.refs_0_ = bf16[768,256]{1,0:T(8,128)(2,1)S(1)} collective-permute-done((bf16[768,256]{1,0:T(8,128)(2,1)S(1)}, bf16[768,256]{1,0:T(8,128)(2,1)S(1)}, u32[]{:S(2)}, u32[]{:S(2)}) %collective-permute-start.28) | collective-permute-done | bytes 393248 | tf_op jit(solution)/shard_map/ppermute | solution.py:47
  251.1 2.5 collective-permute-done.29.refs_1_
  253.7 2.7 collective-permute-start.31
  259.1 6.8 %collective-permute-done.30 = bf16[2,72,2048]{2,1,0:T(8,128)(2,1)S(1)} collective-permute-done((bf16[2,72,2048]{2,1,0:T(8,128)(2,1)S(1)}, bf16[2,72,2048]{2,1,0:T(8,128)(2,1)S(1)}, u32[]{:S(2)}, u32[]{:S(2)}) %collective-permute-start.30) | collective-permute-done | bytes 589856 | tf_op jit(solution)/shard_map/ppermute | solution.py:47
  (150 shorter events, 54.4 us)
Async XLA Ops:
  6.1 11.5 %collective-permute-start = (bf16[1152,256]{1,0:T(8,128)(2,1)S(1)}, bf16[1152,256]{1,0:T(8,128)(2,1)}, u32[]{:S(2)}, u32[]{:S(2)}) collective-permute-start(bf16[1152,256]{1,0:T(8,128)(2,1)S(1)} %get-tuple-element.66), channel_id=1, source_target_pairs={{0,0},{1,4},{2,2},{3,6},{4,1},{5,5},{6,3},{7,7},{8,8},{9,12},{10,1... | collective-permute-start | bytes 1769480 | tf_op jit(solution)/shard_map/ppermute | solution.py:47
  9.9 13.1 %collective-permute-start.1 = (bf16[1152,256]{1,0:T(8,128)(2,1)S(1)}, bf16[1152,256]{1,0:T(8,128)(2,1)}, u32[]{:S(2)}, u32[]{:S(2)}) collective-permute-start(bf16[1152,256]{1,0:T(8,128)(2,1)S(1)} %get-tuple-element.67), channel_id=1, source_target_pairs={{0,1},{1,5},{2,3},{3,7},{4,0},{5,4},{6,2},{7,6},{8,9},{9,13},{10,1... | collective-permute-start | bytes 1769480 | tf_op jit(solution)/shard_map/ppermute | solution.py:47
  24.6 36.8 %collective-permute-start.2 = (bf16[2304,256]{1,0:T(8,128)(2,1)S(1)}, bf16[2304,256]{1,0:T(8,128)(2,1)S(1)}, u32[]{:S(2)}, u32[]{:S(2)}) collective-permute-start(bf16[2304,256]{1,0:T(8,128)(2,1)S(1)} %pad_maximum_fusion.2.own), channel_id=1, source_target_pairs={{0,8},{1,9},{2,10},{3,11},{4,12},{5,13},{6,14},{7,15},{8,16},{9,17... | collective-permute-start | bytes 3538952 | tf_op jit(solution)/shard_map/ppermute | solution.py:47
  27.8 33.6 %collective-permute-start.3 = (bf16[2304,256]{1,0:T(8,128)(2,1)S(1)}, bf16[2304,256]{1,0:T(8,128)(2,1)S(1)}, u32[]{:S(2)}, u32[]{:S(2)}) collective-permute-start(bf16[2304,256]{1,0:T(8,128)(2,1)S(1)} %pad_maximum_fusion.2.own), channel_id=1, source_target_pairs={{8,0},{9,1},{10,2},{11,3},{12,4},{13,5},{14,6},{15,7},{16,8},{17,9... | collective-permute-start | bytes 3538952 | tf_op jit(solution)/shard_map/ppermute | solution.py:47
  30.2 16.2 %collective-permute-start.6 = (bf16[72,4096]{1,0:T(8,128)(2,1)S(1)}, bf16[72,4096]{1,0:T(8,128)(2,1)S(1)}, u32[]{:S(2)}, u32[]{:S(2)}) collective-permute-start(bf16[72,4096]{1,0:T(8,128)(2,1)S(1)} %get-tuple-element.131), channel_id=1, source_target_pairs={{0,6},{1,7},{2,4},{3,5},{4,2},{5,3},{6,0},{7,1},{8,14},{9,15},{10,... | collective-permute-start | bytes 1769480 | tf_op jit(solution)/shard_map/ppermute | solution.py:47
  33.2 26.5 %collective-permute-start.5 = (bf16[72,4096]{1,0:T(8,128)(2,1)S(1)}, bf16[72,4096]{1,0:T(8,128)(2,1)S(1)}, u32[]{:S(2)}, u32[]{:S(2)}) collective-permute-start(bf16[72,4096]{1,0:T(8,128)(2,1)S(1)} %get-tuple-element.132), channel_id=1, source_target_pairs={{0,2},{1,3},{2,0},{3,1},{4,6},{5,7},{6,4},{7,5},{8,10},{9,11},{10,... | collective-permute-start | bytes 1769480 | tf_op jit(solution)/shard_map/ppermute | solution.py:47
  33.4 26.3 %collective-permute-start.4 = (bf16[72,4096]{1,0:T(8,128)(2,1)S(1)}, bf16[72,4096]{1,0:T(8,128)(2,1)S(1)}, u32[]{:S(2)}, u32[]{:S(2)}) collective-permute-start(bf16[72,4096]{1,0:T(8,128)(2,1)S(1)} %get-tuple-element.133), channel_id=1, source_target_pairs={{0,4},{1,5},{2,6},{3,7},{4,0},{5,1},{6,2},{7,3},{8,12},{9,13},{10,... | collective-permute-start | bytes 1769480 | tf_op jit(solution)/shard_map/ppermute | solution.py:47
  62.4 48.4 %collective-permute-start.10 = (bf16[288,4096]{1,0:T(8,128)(2,1)}, bf16[288,4096]{1,0:T(8,128)(2,1)}, u32[]{:S(2)}, u32[]{:S(2)}) collective-permute-start(bf16[288,4096]{1,0:T(8,128)(2,1)} %pad_maximum_fusion.1.mine), channel_id=1, source_target_pairs={{0,1},{1,0},{2,3},{3,2},{4,5},{5,4},{6,7},{7,6},{8,9},{9,8},{10,11... | collective-permute-start | bytes 7077896 | tf_op jit(solution)/shard_map/ppermute | solution.py:47
  64.1 21.1 %collective-permute-start.7 = (bf16[1536,256]{1,0:T(8,128)(2,1)S(1)}, bf16[1536,256]{1,0:T(8,128)(2,1)S(1)}, u32[]{:S(2)}, u32[]{:S(2)}) collective-permute-start(bf16[1536,256]{1,0:T(8,128)(2,1)S(1)} %get-tuple-element.137), channel_id=1, source_target_pairs={{8,24},{9,25},{10,26},{11,27},{12,28},{13,29},{14,30},{15,31},{16,... | collective-permute-start | bytes 2359304 | tf_op jit(solution)/shard_map/ppermute | solution.py:47
  68.4 33.6 %collective-permute-start.8 = (bf16[1536,256]{1,0:T(8,128)(2,1)S(1)}, bf16[1536,256]{1,0:T(8,128)(2,1)S(1)}, u32[]{:S(2)}, u32[]{:S(2)}) collective-permute-start(bf16[1536,256]{1,0:T(8,128)(2,1)S(1)} %get-tuple-element.138), channel_id=1, source_target_pairs={{8,16},{9,17},{10,18},{11,19},{12,20},{13,21},{14,22},{15,23},{16,... | collective-permute-start | bytes 2359304 | tf_op jit(solution)/shard_map/ppermute | solution.py:47
  69.8 32.3 %collective-permute-start.9 = (bf16[1536,256]{1,0:T(8,128)(2,1)S(1)}, bf16[1536,256]{1,0:T(8,128)(2,1)S(1)}, u32[]{:S(2)}, u32[]{:S(2)}) collective-permute-start(bf16[1536,256]{1,0:T(8,128)(2,1)S(1)} %get-tuple-element.136), channel_id=1, source_target_pairs={{8,0},{9,1},{10,2},{11,3},{12,4},{13,5},{14,6},{15,7},{16,8},{17,9... | collective-permute-start | bytes 2359304 | tf_op jit(solution)/shard_map/ppermute | solution.py:47
  102.1 24.9 %collective-permute-start.11 = (bf16[768,256]{1,0:T(8,128)(2,1)S(1)}, bf16[768,256]{1,0:T(8,128)(2,1)S(1)}, u32[]{:S(2)}, u32[]{:S(2)}) collective-permute-start(bf16[768,256]{1,0:T(8,128)(2,1)S(1)} %broadcast_select_fusion.5), channel_id=1, source_target_pairs={{8,24},{9,25},{10,26},{11,27},{12,28},{13,29},{14,30},{15,31},{16,... | collective-permute-start | bytes 1179656 | tf_op jit(solution)/shard_map/ppermute | solution.py:47
  107.6 19.4 %collective-permute-start.12 = (bf16[768,256]{1,0:T(8,128)(2,1)S(1)}, bf16[768,256]{1,0:T(8,128)(2,1)S(1)}, u32[]{:S(2)}, u32[]{:S(2)}) collective-permute-start(bf16[768,256]{1,0:T(8,128)(2,1)S(1)} %slice.88), channel_id=1, source_target_pairs={{8,16},{9,17},{10,18},{11,19},{12,20},{13,21},{14,22},{15,23},{16,... | collective-permute-start | bytes 1179656 | tf_op jit(solution)/shard_map/ppermute | solution.py:47
  108.9 18.1 %collective-permute-start.13 = (bf16[768,256]{1,0:T(8,128)(2,1)S(1)}, bf16[768,256]{1,0:T(8,128)(2,1)S(1)}, u32[]{:S(2)}, u32[]{:S(2)}) collective-permute-start(bf16[768,256]{1,0:T(8,128)(2,1)S(1)} %slice.89), channel_id=1, source_target_pairs={{8,0},{9,1},{10,2},{11,3},{12,4},{13,5},{14,6},{15,7},{16,8},{17,9... | collective-permute-start | bytes 1179656 | tf_op jit(solution)/shard_map/ppermute | solution.py:47
  122.3 55.5 %collective-permute-start.14 = (bf16[1536,256]{1,0:T(8,128)(2,1)}, bf16[1536,256]{1,0:T(8,128)(2,1)}, u32[]{:S(2)}, u32[]{:S(2)}) collective-permute-start(bf16[1536,256]{1,0:T(8,128)(2,1)} %get-tuple-element.76), channel_id=1, source_target_pairs={{0,16},{1,17},{2,18},{3,19},{4,20},{5,21},{6,22},{7,23},{24,8},{25... | collective-permute-start | bytes 2359304 | tf_op jit(solution)/shard_map/ppermute | solution.py:47
  123.6 54.3 %collective-permute-start.15 = (bf16[1536,256]{1,0:T(8,128)(2,1)}, bf16[1536,256]{1,0:T(8,128)(2,1)}, u32[]{:S(2)}, u32[]{:S(2)}) collective-permute-start(bf16[1536,256]{1,0:T(8,128)(2,1)} %get-tuple-element.83), channel_id=1, source_target_pairs={{0,8},{1,9},{2,10},{3,11},{4,12},{5,13},{6,14},{7,15},{8,16},{9,17... | collective-permute-start | bytes 2359304 | tf_op jit(solution)/shard_map/ppermute | solution.py:47
  127.0 50.8 %collective-permute-start.16 = (bf16[1536,256]{1,0:T(8,128)(2,1)}, bf16[1536,256]{1,0:T(8,128)(2,1)}, u32[]{:S(2)}, u32[]{:S(2)}) collective-permute-start(bf16[1536,256]{1,0:T(8,128)(2,1)} %get-tuple-element.83), channel_id=1, source_target_pairs={{16,8},{17,9},{18,10},{19,11},{20,12},{21,13},{22,14},{23,15},{24,... | collective-permute-start | bytes 2359304 | tf_op jit(solution)/shard_map/ppermute | solution.py:47
  138.7 30.4 %collective-permute-start.17 = (bf16[768,256]{1,0:T(8,128)(2,1)}, bf16[768,256]{1,0:T(8,128)(2,1)}, u32[]{:S(2)}, u32[]{:S(2)}) collective-permute-start(bf16[768,256]{1,0:T(8,128)(2,1)} %get-tuple-element.84), channel_id=1, source_target_pairs={{0,16},{1,17},{2,18},{3,19},{4,20},{5,21},{6,22},{7,23},{24,8},{25... | collective-permute-start | bytes 1179656 | tf_op jit(solution)/shard_map/ppermute | solution.py:47
  139.9 37.9 %collective-permute-start.18 = (bf16[768,256]{1,0:T(8,128)(2,1)}, bf16[768,256]{1,0:T(8,128)(2,1)}, u32[]{:S(2)}, u32[]{:S(2)}) collective-permute-start(bf16[768,256]{1,0:T(8,128)(2,1)} %get-tuple-element.107), channel_id=1, source_target_pairs={{0,8},{1,9},{2,10},{3,11},{4,12},{5,13},{6,14},{7,15},{8,16},{9,17... | collective-permute-start | bytes 1179656 | tf_op jit(solution)/shard_map/ppermute | solution.py:47
  191.1 19.3 %collective-permute-start.19 = (bf16[288,4096]{1,0:T(8,128)(2,1)}, bf16[288,4096]{1,0:T(8,128)(2,1)}, u32[]{:S(2)}, u32[]{:S(2)}) collective-permute-start(bf16[288,4096]{1,0:T(8,128)(2,1)} %get-tuple-element.106), channel_id=1, source_target_pairs={{0,1},{1,0},{2,3},{3,2},{4,5},{5,4},{6,7},{7,6},{8,9},{9,8},{10,11... | collective-permute-start | bytes 7077896 | tf_op jit(solution)/shard_map/ppermute | solution.py:47
  192.7 12.8 %collective-permute-start.20 = (bf16[768,256]{1,0:T(8,128)(2,1)}, bf16[768,256]{1,0:T(8,128)(2,1)S(1)}, u32[]{:S(2)}, u32[]{:S(2)}) collective-permute-start(bf16[768,256]{1,0:T(8,128)(2,1)} %get-tuple-element.107), channel_id=1, source_target_pairs={{16,8},{17,9},{18,10},{19,11},{20,12},{21,13},{22,14},{23,15},{24,... | collective-permute-start | bytes 1179656 | tf_op jit(solution)/shard_map/ppermute | solution.py:47
  194.0 28.4 %collective-permute-start.27 = (bf16[1536,256]{1,0:T(8,128)(2,1)}, bf16[1536,256]{1,0:T(8,128)(2,1)S(1)}, u32[]{:S(2)}, u32[]{:S(2)}) collective-permute-start(bf16[1536,256]{1,0:T(8,128)(2,1)} %add_convert_fusion.2), channel_id=1, source_target_pairs={{8,16},{9,17},{10,18},{11,19},{12,20},{13,21},{14,22},{15,23},{16,... | collective-permute-start | bytes 2359304 | tf_op jit(solution)/shard_map/ppermute | solution.py:47
  198.0 25.0 %collective-permute-start.26 = (bf16[1536,256]{1,0:T(8,128)(2,1)}, bf16[1536,256]{1,0:T(8,128)(2,1)S(1)}, u32[]{:S(2)}, u32[]{:S(2)}) collective-permute-start(bf16[1536,256]{1,0:T(8,128)(2,1)} %fusion.3), channel_id=1, source_target_pairs={{0,8},{1,9},{2,10},{3,11},{4,12},{5,13},{6,14},{7,15},{8,0},{9,1},... | collective-permute-start | bytes 2359304 | tf_op jit(solution)/shard_map/ppermute | solution.py:47
  207.0 35.6 %collective-permute-start.24 = (bf16[768,256]{1,0:T(8,128)(2,1)S(1)}, bf16[768,256]{1,0:T(8,128)(2,1)S(1)}, u32[]{:S(2)}, u32[]{:S(2)}) collective-permute-start(bf16[768,256]{1,0:T(8,128)(2,1)S(1)} %fusion.7), channel_id=1, source_target_pairs={{0,8},{1,9},{2,10},{3,11},{4,12},{5,13},{6,14},{7,15},{8,0},{9,1},... | collective-permute-start | bytes 1179656 | tf_op jit(solution)/shard_map/ppermute | solution.py:47
  208.3 35.9 %collective-permute-start.25 = (bf16[768,256]{1,0:T(8,128)(2,1)S(1)}, bf16[768,256]{1,0:T(8,128)(2,1)S(1)}, u32[]{:S(2)}, u32[]{:S(2)}) collective-permute-start(bf16[768,256]{1,0:T(8,128)(2,1)S(1)} %add_convert_fusion.5), channel_id=1, source_target_pairs={{8,16},{9,17},{10,18},{11,19},{12,20},{13,21},{14,22},{15,23},{16,... | collective-permute-start | bytes 1179656 | tf_op jit(solution)/shard_map/ppermute | solution.py:47
  213.1 13.4 %collective-permute-start.21 = (bf16[2,72,2048]{2,1,0:T(8,128)(2,1)S(1)}, bf16[2,72,2048]{2,1,0:T(8,128)(2,1)S(1)}, u32[]{:S(2)}, u32[]{:S(2)}) collective-permute-start(bf16[2,72,2048]{2,1,0:T(8,128)(2,1)S(1)} %slice_bitcast_fusion.5), channel_id=1, source_target_pairs={{0,4},{1,5},{2,6},{3,7},{4,0},{5,1},{6,2},{7,3},{8,12},{9,13},{10,... | collective-permute-start | bytes 1769480 | tf_op jit(solution)/shard_map/ppermute | solution.py:47
  222.4 13.7 %collective-permute-start.22 = (bf16[2,72,2048]{2,1,0:T(8,128)(2,1)S(1)}, bf16[2,72,2048]{2,1,0:T(8,128)(2,1)S(1)}, u32[]{:S(2)}, u32[]{:S(2)}) collective-permute-start(bf16[2,72,2048]{2,1,0:T(8,128)(2,1)S(1)} %get-tuple-element.129), channel_id=1, source_target_pairs={{0,2},{1,3},{2,0},{3,1},{4,6},{5,7},{6,4},{7,5},{8,10},{9,11},{10,... | collective-permute-start | bytes 1769480 | tf_op jit(solution)/shard_map/ppermute | solution.py:47
  236.2 20.2 %collective-permute-start.23 = (bf16[2,72,2048]{2,1,0:T(8,128)(2,1)S(1)}, bf16[2,72,2048]{2,1,0:T(8,128)(2,1)S(1)}, u32[]{:S(2)}, u32[]{:S(2)}) collective-permute-start(bf16[2,72,2048]{2,1,0:T(8,128)(2,1)S(1)} %slice_bitcast_fusion.2), channel_id=1, source_target_pairs={{0,2},{1,3},{2,0},{3,1},{4,6},{5,7},{6,4},{7,5},{8,10},{9,11},{10,... | collective-permute-start | bytes 1769480 | tf_op jit(solution)/shard_map/ppermute | solution.py:47
  237.0 14.1 %collective-permute-start.28 = (bf16[768,256]{1,0:T(8,128)(2,1)S(1)}, bf16[768,256]{1,0:T(8,128)(2,1)S(1)}, u32[]{:S(2)}, u32[]{:S(2)}) collective-permute-start(bf16[768,256]{1,0:T(8,128)(2,1)S(1)} %get-tuple-element.142), channel_id=1, source_target_pairs={{0,0},{1,4},{2,2},{3,6},{4,1},{5,5},{6,3},{7,7},{8,8},{9,12},{10,1... | collective-permute-start | bytes 1179656 | tf_op jit(solution)/shard_map/ppermute | solution.py:47
  242.7 23.2 %collective-permute-start.30 = (bf16[2,72,2048]{2,1,0:T(8,128)(2,1)S(1)}, bf16[2,72,2048]{2,1,0:T(8,128)(2,1)S(1)}, u32[]{:S(2)}, u32[]{:S(2)}) collective-permute-start(bf16[2,72,2048]{2,1,0:T(8,128)(2,1)S(1)} %get-tuple-element.135), channel_id=1, source_target_pairs={{0,4},{1,5},{2,6},{3,7},{4,0},{5,1},{6,2},{7,3},{8,12},{9,13},{10,... | collective-permute-start | bytes 1769480 | tf_op jit(solution)/shard_map/ppermute | solution.py:47
  253.7 14.5 %collective-permute-start.31 = (bf16[384,256]{1,0:T(8,128)(2,1)S(1)}, bf16[384,256]{1,0:T(8,128)(2,1)S(1)}, u32[]{:S(2)}, u32[]{:S(2)}) collective-permute-start(bf16[384,256]{1,0:T(8,128)(2,1)S(1)} %get-tuple-element.144), channel_id=1, source_target_pairs={{0,0},{1,4},{2,2},{3,6},{4,1},{5,5},{6,3},{7,7},{8,8},{9,12},{10,1... | collective-permute-start | bytes 589832 | tf_op jit(solution)/shard_map/ppermute | solution.py:47
  256.4 12.5 %collective-permute-start.32 = (bf16[384,256]{1,0:T(8,128)(2,1)S(1)}, bf16[384,256]{1,0:T(8,128)(2,1)S(1)}, u32[]{:S(2)}, u32[]{:S(2)}) collective-permute-start(bf16[384,256]{1,0:T(8,128)(2,1)S(1)} %get-tuple-element.143), channel_id=1, source_target_pairs={{0,4},{1,0},{2,6},{3,2},{4,5},{5,1},{6,7},{7,3},{8,12},{9,8},{10,1... | collective-permute-start | bytes 589832 | tf_op jit(solution)/shard_map/ppermute | solution.py:47
  (30 other events, 207.2 us)

commit v10 on v8

--- a/solution.py
+++ b/solution.py
@@ -463,12 +463,13 @@
         up2, down2 = g.hop(shard2, ups), g.hop(shard2, downs)
         up_2, down_2, up2, down2, mine = together((up_2, down_2, up2, down2, mine))
         last = g.hop(jnp.where(to_last, up_2, down_2), passing)
+        theirs = g.send(mine, other_core)
+        up2, down2 = tie(up2, last), tie(down2, last)
         up2_2, down2_2 = g.hop(up2, {1: 2, 2: 3}), g.hop(down2, {1: 0, 2: 1})
-        theirs = g.send(mine, other_core)
         chunk, outer, terms = expert(
             place_z, g.zs, units[0], (shard, up, down, up_2, down_2, last), mine, theirs
         )
-        up2_2, down2_2, outer = together((up2_2, down2_2, outer))
+        up2_2, down2_2 = tie(up2_2, outer), tie(down2_2, outer)
         last2 = g.hop(jnp.where(to_last, up2_2, down2_2), passing)
         begun = g.hop(outer, outward)
         chunk2, outer2, terms2 = expert(
@@ -481,22 +482,28 @@
         keep, give = token_rows((chunk, chunk2), slots, width)
         sums = added(keep, g.send(give, other_core)).reshape(g.qs, 2, cap, 2 * width)
         sum_up, sum_down, sums = together((sum_up, sum_down, sums))
-        far_rows = g.send(sums[:, 1], lambda z, x, q, c: (z, 1 - x, q, c))
+
+        def along_x(rows):
+            return jnp.stack([rows[:, 0], g.send(rows[:, 1], lambda z, x, q, c: (z, 1 - x, q, c))], axis=1)
+
+        def along_q(rows):
+            return jnp.stack(
+                [rows[0]] + [g.send(rows[d], lambda z, x, q, c, d=d: (z, x, (q - d) % g.qs, c)) for d in range(1, g.qs)]
+            )
+
+        returned, back_rows = along_x(sums[..., :width]), along_q(sums[..., width:])
         sum_up, sum_down = g.hop(added(terms[1], sum_up), ups), g.hop(added(terms[3], sum_down), downs)
         middle2 = added(terms2[2], begun2)
         sum_up2, sum_down2 = g.hop(middle2, inward_up), g.hop(middle2, inward_down)
+        returned, back_rows, sum_up, sum_down = together((returned, back_rows, sum_up, sum_down))
+        returned, back_rows = along_q(returned), along_x(back_rows)
         grad = added(terms[0], sum_up, sum_down)
-        far_rows = tie(far_rows, grad)
-        near = jnp.stack([sums[:, 0], far_rows], axis=1)
-        got = jnp.concatenate(
-            [near[0]] + [g.send(near[d], lambda z, x, q, c, d=d: (z, x, (q - d) % g.qs, c)) for d in range(1, g.qs)]
-        ).reshape(slots, 2 * width)
-        sum_up2, sum_down2 = tie(sum_up2, near), tie(sum_down2, near)
         grads = unspread(grad)
         sum_up2, sum_down2 = g.hop(added(terms2[1], sum_up2), ups), g.hop(added(terms2[3], sum_down2), downs)
         sum_up2, sum_down2, grads = together((sum_up2, sum_down2, grads))
         grad2 = added(terms2[0], sum_up2, sum_down2)
-        got = tie(got, grad2)
+        returned, back_rows = tie(returned, grad2), tie(back_rows, grad2)
+        returned, back_rows = returned.reshape(slots, width), back_rows.reshape(slots, width)
         grads += unspread(grad2)
         d_w_gate, d_w_up, d_w_down = unpack(pieces, place_x, grads, shuffle, *shapes)
     else:
@@ -538,7 +545,7 @@
             dot(jnp.concatenate([both_a[:, cols], both_b[:, cols]], axis=1), shuffle, ((1,), (1,)))
             for cols in (slice(0, half), slice(half, None))
         )
-    returned, back_rows = got[:, :width], got[:, width:]
+        returned, back_rows = got[:, :width], got[:, width:]
 
     high = lax.reduce_precision(weighted, 8, 7)
     mixed = (dot(high.astype(BF), returned) + dot((weighted - high).astype(BF), returned)).astype(BF)

time: 237 us -> 246 us (1.038)
  local copies, waits for them, and re-layouts: 7.38 us -> 14.3 us
  waiting for transfers between devices: 102 us -> 105 us
    unnamed x44 -> x62, local copies, waits for them, and re-layouts: 6.76 us -> 13 us
    ppermute x35 -> x37, waiting for transfers between devices: 102 us -> 105 us  [send(): return lax.ppermute(value, BOTH, pairs)]
    ppermute x35 -> x37, starting transfers between devices: 77.5 us -> 77.2 us  [send(): return lax.ppermute(value, BOTH, pairs)]
  transfers between devices with their start and end apart: 35 -> 37, of which waited for: 18 -> 18; matrix products, arithmetic and copies ran while one was open for 5% -> 7% of each run, Pallas kernels for 9% -> 7%
where the time goes in v10:
time: 246 us; the launch traced here: 244 us
  waiting for transfers between devices  105 us (43%)
  starting transfers between devices  77.2 us (31%)
  Pallas kernels  26.7 us (11%)
  local copies, waits for them, and re-layouts  14.3 us (6%)
  other arithmetic  13.1 us (5%)
  matrix products  5.89 us (2%)
    ppermute x37, waiting for transfers between devices, send(): return lax.ppermute(value, BOTH, pairs)  105 us
    ppermute x37, starting transfers between devices, send(): return lax.ppermute(value, BOTH, pairs)  77.2 us
    pallas_call x2, Pallas kernels, expert(): pl.pallas_call(expert_kernel, out_shape=for_rows + [jax.ShapeDtypeStruct(...  17.8 us
    unnamed x62, local copies, waits for them, and re-layouts  13 us
    pallas_call x1, Pallas kernels, token_rows(): pl.pallas_call(functools.partial(rows_kernel, len(chunks)), grid=(2 * til...  6.18 us
    dot_general x7, matrix products, dot(): return lax.dot_general(a, b, (dims, ((), ())), preferred_element_type=F32)  5.89 us
    convert_element_type x9, other arithmetic, added(): return sum((t.astype(F32) for t in terms)).astype(BF)  5.79 us
  transfers between devices with their start and end apart: 37, of which 18 were waited for; matrix products, arithmetic and copies ran while one was open for 7% of the time, Pallas kernels for 7%

profile of v10, /device:TPU:9, one launch (start us, length us, event | category | flops | bytes accessed | tf_op | source)
XLA Modules:
  0.0 244.2 jit_solution(15841811007832324292)
XLA Ops:
  4.9 3.7 %collective-permute-start = (bf16[768,256]{1,0:T(8,128)(2,1)S(1)}, bf16[768,256]{1,0:T(8,128)(2,1)S(1)}, u32[]{:S(2)}, u32[]{:S(2)}) collective-permute-start(bf16[768,256]{1,0:T(8,128)(2,1)S(1)} %get-tuple-element.76), channel_id=1, source_target_pairs={{0,0},{1,4},{2,2},{3,6},{4,1},{5,5},{6,3},{7,7},{8,8},{9,12},{10,1... | collective-permute-start | bytes 1179656 | tf_op jit(solution)/shard_map/ppermute | solution.py:43
  9.0 2.6 %convolution_convert_fusion = bf16[288,2048]{1,0:T(8,128)(2,1)} fusion(pred[128,288]{0,1:T(8,128)(4,1)S(1)} %fusion.6, s32[]{:T(128)S(6)} %select_n.146, bf16[128,2048]{1,0:T(8,128)(2,1)} %param.7), kind=kOutput, calls=%fused_computation.3 | convolution fusion | flops 152633344 | bytes 1740804 | tf_op jit(solution)/shard_map/dot_general | solution.py:16
  14.1 3.5 %collective-permute-done.1 = bf16[768,256]{1,0:T(8,128)(2,1)} collective-permute-done((bf16[768,256]{1,0:T(8,128)(2,1)S(1)}, bf16[768,256]{1,0:T(8,128)(2,1)}, u32[]{:S(2)}, u32[]{:S(2)}) %collective-permute-start.1) | collective-permute-done | bytes 393248 | tf_op jit(solution)/shard_map/ppermute | solution.py:43
  18.6 2.5 %collective-permute-start.6 = (bf16[384,256]{1,0:T(8,128)(2,1)S(1)}, bf16[384,256]{1,0:T(8,128)(2,1)S(1)}, u32[]{:S(2)}, u32[]{:S(2)}) collective-permute-start(bf16[384,256]{1,0:T(8,128)(2,1)S(1)} %get-tuple-element.83), channel_id=1, source_target_pairs={{0,0},{1,4},{2,2},{3,6},{4,1},{5,5},{6,3},{7,7},{8,8},{9,12},{10,1... | collective-permute-start | bytes 589832 | tf_op jit(solution)/shard_map/ppermute | solution.py:43
  21.6 3.2 %collective-permute-start.2 = (bf16[1536,256]{1,0:T(8,128)(2,1)S(1)}, bf16[1536,256]{1,0:T(8,128)(2,1)S(1)}, u32[]{:S(2)}, u32[]{:S(2)}) collective-permute-start(bf16[1536,256]{1,0:T(8,128)(2,1)S(1)} %pad_maximum_fusion.6.own), channel_id=1, source_target_pairs={{0,8},{1,9},{2,10},{3,11},{4,12},{5,13},{6,14},{7,15},{8,16},{9,17... | collective-permute-start | bytes 2359304 | tf_op jit(solution)/shard_map/ppermute | solution.py:43
  30.0 12.3 %collective-permute-done.2.up = bf16[1536,256]{1,0:T(8,128)(2,1)S(1)} collective-permute-done((bf16[1536,256]{1,0:T(8,128)(2,1)S(1)}, bf16[1536,256]{1,0:T(8,128)(2,1)S(1)}, u32[]{:S(2)}, u32[]{:S(2)}) %collective-permute-start.2) | collective-permute-done | bytes 786464 | tf_op jit(solution)/shard_map/ppermute | solution.py:43
  42.3 2.9 %collective-permute-done.3.down = bf16[1536,256]{1,0:T(8,128)(2,1)S(1)} collective-permute-done((bf16[1536,256]{1,0:T(8,128)(2,1)S(1)}, bf16[1536,256]{1,0:T(8,128)(2,1)S(1)}, u32[]{:S(2)}, u32[]{:S(2)}) %collective-permute-start.3) | collective-permute-done | bytes 786464 | tf_op jit(solution)/shard_map/ppermute | solution.py:43
  45.2 3.2 %collective-permute-start.4 = (bf16[1536,256]{1,0:T(8,128)(2,1)S(1)}, bf16[1536,256]{1,0:T(8,128)(2,1)S(1)}, u32[]{:S(2)}, u32[]{:S(2)}) collective-permute-start(bf16[1536,256]{1,0:T(8,128)(2,1)S(1)} %collective-permute-done.2.up), channel_id=1, source_target_pairs={{8,16},{9,17},{10,18},{11,19},{12,20},{13,21},{14,22},{15,23},{16,... | collective-permute-start | bytes 2359304 | tf_op jit(solution)/shard_map/ppermute | solution.py:43
  50.4 3.9 %collective-permute-done.8 = bf16[72,4096]{1,0:T(8,128)(2,1)S(1)} collective-permute-done((bf16[72,4096]{1,0:T(8,128)(2,1)S(1)}, bf16[72,4096]{1,0:T(8,128)(2,1)S(1)}, u32[]{:S(2)}, u32[]{:S(2)}) %collective-permute-start.8) | collective-permute-done | bytes 589856 | tf_op jit(solution)/shard_map/ppermute | solution.py:43
  57.8 3.1 %collective-permute-start.11 = (bf16[768,256]{1,0:T(8,128)(2,1)S(1)}, bf16[768,256]{1,0:T(8,128)(2,1)S(1)}, u32[]{:S(2)}, u32[]{:S(2)}) collective-permute-start(bf16[768,256]{1,0:T(8,128)(2,1)S(1)} %pad_maximum_fusion.7.own), channel_id=1, source_target_pairs={{0,8},{1,9},{2,10},{3,11},{4,12},{5,13},{6,14},{7,15},{8,16},{9,17... | collective-permute-start | bytes 1179656 | tf_op jit(solution)/shard_map/ppermute | solution.py:43
  63.1 9.1 %collective-permute-done.11.up = bf16[768,256]{1,0:T(8,128)(2,1)S(1)} collective-permute-done((bf16[768,256]{1,0:T(8,128)(2,1)S(1)}, bf16[768,256]{1,0:T(8,128)(2,1)S(1)}, u32[]{:S(2)}, u32[]{:S(2)}) %collective-permute-start.11) | collective-permute-done | bytes 393248 | tf_op jit(solution)/shard_map/ppermute | solution.py:43
  72.2 3.9 %collective-permute-done.12.down = bf16[768,256]{1,0:T(8,128)(2,1)S(1)} collective-permute-done((bf16[768,256]{1,0:T(8,128)(2,1)S(1)}, bf16[768,256]{1,0:T(8,128)(2,1)S(1)}, u32[]{:S(2)}, u32[]{:S(2)}) %collective-permute-start.12) | collective-permute-done | bytes 393248 | tf_op jit(solution)/shard_map/ppermute | solution.py:43
  78.6 2.7 %collective-permute-start.14 = (bf16[288,4096]{1,0:T(8,128)(2,1)}, bf16[288,4096]{1,0:T(8,128)(2,1)}, u32[]{:S(2)}, u32[]{:S(2)}) collective-permute-start(bf16[288,4096]{1,0:T(8,128)(2,1)} %pad_maximum_fusion.1.mine), channel_id=1, source_target_pairs={{0,1},{1,0},{2,3},{3,2},{4,5},{5,4},{6,7},{7,6},{8,9},{9,8},{10,11... | collective-permute-start | bytes 7077896 | tf_op jit(solution)/shard_map/ppermute | solution.py:43
  84.5 16.9 %collective-permute-done.13.last = bf16[1536,256]{1,0:T(8,128)(2,1)S(1)} collective-permute-done((bf16[1536,256]{1,0:T(8,128)(2,1)S(1)}, bf16[1536,256]{1,0:T(8,128)(2,1)S(1)}, u32[]{:S(2)}, u32[]{:S(2)}) %collective-permute-start.13) | collective-permute-done | bytes 786464 | tf_op jit(solution)/shard_map/ppermute | solution.py:43
  101.4 4.1 %collective-permute-start.17 = (bf16[768,256]{1,0:T(8,128)(2,1)S(1)}, bf16[768,256]{1,0:T(8,128)(2,1)S(1)}, u32[]{:S(2)}, u32[]{:S(2)}) collective-permute-start(bf16[768,256]{1,0:T(8,128)(2,1)S(1)} %copy-done.9), channel_id=1, source_target_pairs={{8,0},{9,1},{10,2},{11,3},{12,4},{13,5},{14,6},{15,7},{16,8},{17,9... | collective-permute-start | bytes 1179656 | tf_op jit(solution)/shard_map/ppermute | solution.py:43
  106.9 9.6 %shard_map.119 = (bf16[2048,512]{1,0:T(8,128)(2,1)}, bf16[256,2048]{1,0:T(8,128)(2,1)}, bf16[576,256]{1,0:T(8,128)(2,1)S(1)}, bf16[576,512]{1,0:T(8,128)(2,1)S(1...) custom-call(s32[1]{0:T(128)} %bitcast.z_ref, ...), custom_call_target="tpu_custom_call" | custom-call | flops 3623878656 | bytes 16777216 | tf_op jit(solution)/shard_map/pallas_call | solution.py:316
  120.5 4.1 %collective-permute-start.18 = (bf16[768,256]{1,0:T(8,128)(2,1)S(1)}, bf16[768,256]{1,0:T(8,128)(2,1)S(1)}, u32[]{:S(2)}, u32[]{:S(2)}) collective-permute-start(bf16[768,256]{1,0:T(8,128)(2,1)S(1)} %broadcast_select_fusion.1), channel_id=1, source_target_pairs={{8,0},{9,1},{10,2},{11,3},{12,4},{13,5},{14,6},{15,7},{16,24},{17,... | collective-permute-start | bytes 1179656 | tf_op jit(solution)/shard_map/ppermute | solution.py:43
  124.5 6.8 %collective-permute-done.18.last = bf16[768,256]{1,0:T(8,128)(2,1)S(1)} collective-permute-done((bf16[768,256]{1,0:T(8,128)(2,1)S(1)}, bf16[768,256]{1,0:T(8,128)(2,1)S(1)}, u32[]{:S(2)}, u32[]{:S(2)}) %collective-permute-start.18) | collective-permute-done | bytes 393248 | tf_op jit(solution)/shard_map/ppermute | solution.py:43
  131.4 8.2 %shard_map.120 = (bf16[2048,256]{1,0:T(8,128)(2,1)}, bf16[128,2048]{1,0:T(8,128)(2,1)S(1)}, bf16[576,128]{1,0:T(8,128)(2,1)S(1)}, bf16[576,256]{1,0:T(8,128)(2,1...) custom-call(s32[1]{0:T(128)} %bitcast.z_ref, ...), custom_call_target="tpu_custom_call" | custom-call | flops 1811939328 | bytes 16777216 | tf_op jit(solution)/shard_map/pallas_call | solution.py:316
  141.6 6.2 %shard_map.121 = (bf16[288,4096]{1,0:T(8,128)(2,1)S(1)}, bf16[288,4096]{1,0:T(8,128)(2,1)}) custom-call(bf16[2048,512]{1,0:T(8,128)(2,1)S(1)} %copy-done.19, bf16[256,2048]{1,0:T(8,128)(2,1)S(1)} %copy-done.20, bf16[576,256]{1,0:T(8,128)(2,1)S(1)} %get-tuple-element.114.refs_2_, bf16[576,512]{1,0:T(8,128)(2,1)S(1)} %get-tuple-element.115.refs_3_, ...), custom_call_target="tpu_custom_call" | custom-call | flops 2717908992 | bytes 12582912 | tf_op jit(solution)/shard_map/pallas_call | solution.py:356
  156.1 8.5 %collective-permute-done.27 = bf16[768,256]{1,0:T(8,128)(2,1)S(1)} collective-permute-done((bf16[768,256]{1,0:T(8,128)(2,1)}, bf16[768,256]{1,0:T(8,128)(2,1)S(1)}, u32[]{:S(2)}, u32[]{:S(2)}) %collective-permute-start.27) | collective-permute-done | bytes 393248 | tf_op jit(solution)/shard_map/ppermute | solution.py:43
  167.9 4.0 %collective-permute-start.28 = (bf16[768,256]{1,0:T(8,128)(2,1)S(1)}, bf16[768,256]{1,0:T(8,128)(2,1)S(1)}, u32[]{:S(2)}, u32[]{:S(2)}) collective-permute-start(bf16[768,256]{1,0:T(8,128)(2,1)S(1)} %add_convert_fusion.8), channel_id=1, source_target_pairs={{0,8},{1,9},{2,10},{3,11},{4,12},{5,13},{6,14},{7,15},{8,16},{9,17... | collective-permute-start | bytes 1179656 | tf_op jit(solution)/shard_map/ppermute | solution.py:43
  171.9 3.3 %add_convert_fusion = bf16[288,4096]{1,0:T(8,128)(2,1)S(1)} fusion(bf16[288,4096]{1,0:T(8,128)(2,1)} %collective-permute-done.21, bf16[288,4096]{1,0:T(8,128)(2,1)} %copy-done.1), kind=kLoop, calls=%fused_computation | loop fusion | flops 4718592 | bytes 7077888 | tf_op jit(solution)/shard_map/convert_element_type | solution.py:24
  175.2 6.3 %collective-permute-done.19 = bf16[1536,256]{1,0:T(8,128)(2,1)S(1)} collective-permute-done((bf16[1536,256]{1,0:T(8,128)(2,1)S(1)}, bf16[1536,256]{1,0:T(8,128)(2,1)S(1)}, u32[]{:S(2)}, u32[]{:S(2)}) %collective-permute-start.19) | collective-permute-done | bytes 786464 | tf_op jit(solution)/shard_map/ppermute | solution.py:43
  186.4 3.4 %collective-permute-start.24 = (bf16[1536,256]{1,0:T(8,128)(2,1)S(1)}, bf16[1536,256]{1,0:T(8,128)(2,1)S(1)}, u32[]{:S(2)}, u32[]{:S(2)}) collective-permute-start(bf16[1536,256]{1,0:T(8,128)(2,1)S(1)} %add_convert_fusion.3), channel_id=1, source_target_pairs={{0,8},{1,9},{2,10},{3,11},{4,12},{5,13},{6,14},{7,15},{8,16},{9,17... | collective-permute-start | bytes 2359304 | tf_op jit(solution)/shard_map/ppermute | solution.py:43
  193.5 5.2 %collective-permute-done.23 = bf16[2,72,2048]{2,1,0:T(8,128)(2,1)S(1)} collective-permute-done((bf16[2,72,2048]{2,1,0:T(8,128)(2,1)S(1)}, bf16[2,72,2048]{2,1,0:T(8,128)(2,1)S(1)}, u32[]{:S(2)}, u32[]{:S(2)}) %collective-permute-start.23) | collective-permute-done | bytes 589856 | tf_op jit(solution)/shard_map/ppermute | solution.py:43
  198.7 3.1 %collective-permute-start.29 = (bf16[768,256]{1,0:T(8,128)(2,1)S(1)}, bf16[768,256]{1,0:T(8,128)(2,1)S(1)}, u32[]{:S(2)}, u32[]{:S(2)}) collective-permute-start(bf16[768,256]{1,0:T(8,128)(2,1)S(1)} %add_convert_fusion.7), channel_id=1, source_target_pairs={{0,8},{1,9},{2,10},{3,11},{4,12},{5,13},{6,14},{7,15},{8,16},{9,17... | collective-permute-start | bytes 1179656 | tf_op jit(solution)/shard_map/ppermute | solution.py:43
  202.9 3.1 %collective-permute-done.24 = bf16[1536,256]{1,0:T(8,128)(2,1)S(1)} collective-permute-done((bf16[1536,256]{1,0:T(8,128)(2,1)S(1)}, bf16[1536,256]{1,0:T(8,128)(2,1)S(1)}, u32[]{:S(2)}, u32[]{:S(2)}) %collective-permute-start.24) | collective-permute-done | bytes 786464 | tf_op jit(solution)/shard_map/ppermute | solution.py:43
  206.4 7.1 %collective-permute-start.32 = (bf16[768,256]{1,0:T(8,128)(2,1)S(1)}, bf16[768,256]{1,0:T(8,128)(2,1)S(1)}, u32[]{:S(2)}, u32[]{:S(2)}) collective-permute-start(bf16[768,256]{1,0:T(8,128)(2,1)S(1)} %get-tuple-element.157), channel_id=1, source_target_pairs={{0,0},{1,4},{2,2},{3,6},{4,1},{5,5},{6,3},{7,7},{8,8},{9,12},{10,1... | collective-permute-start | bytes 1179656 | tf_op jit(solution)/shard_map/ppermute | solution.py:43
  215.7 6.6 %collective-permute-done.32.refs_0_ = bf16[768,256]{1,0:T(8,128)(2,1)S(1)} collective-permute-done((bf16[768,256]{1,0:T(8,128)(2,1)S(1)}, bf16[768,256]{1,0:T(8,128)(2,1)S(1)}, u32[]{:S(2)}, u32[]{:S(2)}) %collective-permute-start.32) | collective-permute-done | bytes 393248 | tf_op jit(solution)/shard_map/ppermute | solution.py:43
  224.9 2.7 %collective-permute-start.35 = (bf16[384,256]{1,0:T(8,128)(2,1)S(1)}, bf16[384,256]{1,0:T(8,128)(2,1)S(1)}, u32[]{:S(2)}, u32[]{:S(2)}) collective-permute-start(bf16[384,256]{1,0:T(8,128)(2,1)S(1)} %get-tuple-element.161), channel_id=1, source_target_pairs={{0,0},{1,4},{2,2},{3,6},{4,1},{5,5},{6,3},{7,7},{8,8},{9,12},{10,1... | collective-permute-start | bytes 589832 | tf_op jit(solution)/shard_map/ppermute | solution.py:43
  227.7 9.4 %collective-permute-done.34 = bf16[2,72,2048]{2,1,0:T(8,128)(2,1)S(1)} collective-permute-done((bf16[2,72,2048]{2,1,0:T(8,128)(2,1)S(1)}, bf16[2,72,2048]{2,1,0:T(8,128)(2,1)S(1)}, u32[]{:S(2)}, u32[]{:S(2)}) %collective-permute-start.34) | collective-permute-done | bytes 589856 | tf_op jit(solution)/shard_map/ppermute | solution.py:43
  (161 shorter events, 67.6 us)
Async XLA Ops:
  21.6 20.7 %collective-permute-start.2 = (bf16[1536,256]{1,0:T(8,128)(2,1)S(1)}, bf16[1536,256]{1,0:T(8,128)(2,1)S(1)}, u32[]{:S(2)}, u32[]{:S(2)}) collective-permute-start(bf16[1536,256]{1,0:T(8,128)(2,1)S(1)} %pad_maximum_fusion.6.own), channel_id=1, source_target_pairs={{0,8},{1,9},{2,10},{3,11},{4,12},{5,13},{6,14},{7,15},{8,16},{9,17... | collective-permute-start | bytes 2359304 | tf_op jit(solution)/shard_map/ppermute | solution.py:43
  24.8 20.4 %collective-permute-start.3 = (bf16[1536,256]{1,0:T(8,128)(2,1)S(1)}, bf16[1536,256]{1,0:T(8,128)(2,1)S(1)}, u32[]{:S(2)}, u32[]{:S(2)}) collective-permute-start(bf16[1536,256]{1,0:T(8,128)(2,1)S(1)} %pad_maximum_fusion.6.own), channel_id=1, source_target_pairs={{8,0},{9,1},{10,2},{11,3},{12,4},{13,5},{14,6},{15,7},{16,8},{17,9... | collective-permute-start | bytes 2359304 | tf_op jit(solution)/shard_map/ppermute | solution.py:43
  27.3 23.1 %collective-permute-start.10 = (bf16[72,4096]{1,0:T(8,128)(2,1)S(1)}, bf16[72,4096]{1,0:T(8,128)(2,1)S(1)}, u32[]{:S(2)}, u32[]{:S(2)}) collective-permute-start(bf16[72,4096]{1,0:T(8,128)(2,1)S(1)} %get-tuple-element.151), channel_id=1, source_target_pairs={{0,6},{1,7},{2,4},{3,5},{4,2},{5,3},{6,0},{7,1},{8,14},{9,15},{10,... | collective-permute-start | bytes 1769480 | tf_op jit(solution)/shard_map/ppermute | solution.py:43
  29.4 25.0 %collective-permute-start.8 = (bf16[72,4096]{1,0:T(8,128)(2,1)S(1)}, bf16[72,4096]{1,0:T(8,128)(2,1)S(1)}, u32[]{:S(2)}, u32[]{:S(2)}) collective-permute-start(bf16[72,4096]{1,0:T(8,128)(2,1)S(1)} %get-tuple-element.153), channel_id=1, source_target_pairs={{0,4},{1,5},{2,6},{3,7},{4,0},{5,1},{6,2},{7,3},{8,12},{9,13},{10,... | collective-permute-start | bytes 1769480 | tf_op jit(solution)/shard_map/ppermute | solution.py:43
  29.8 26.4 %collective-permute-start.9 = (bf16[72,4096]{1,0:T(8,128)(2,1)S(1)}, bf16[72,4096]{1,0:T(8,128)(2,1)S(1)}, u32[]{:S(2)}, u32[]{:S(2)}) collective-permute-start(bf16[72,4096]{1,0:T(8,128)(2,1)S(1)} %get-tuple-element.152), channel_id=1, source_target_pairs={{0,2},{1,3},{2,0},{3,1},{4,6},{5,7},{6,4},{7,5},{8,10},{9,11},{10,... | collective-permute-start | bytes 1769480 | tf_op jit(solution)/shard_map/ppermute | solution.py:43
  45.2 31.6 %collective-permute-start.4 = (bf16[1536,256]{1,0:T(8,128)(2,1)S(1)}, bf16[1536,256]{1,0:T(8,128)(2,1)S(1)}, u32[]{:S(2)}, u32[]{:S(2)}) collective-permute-start(bf16[1536,256]{1,0:T(8,128)(2,1)S(1)} %collective-permute-done.2.up), channel_id=1, source_target_pairs={{8,16},{9,17},{10,18},{11,19},{12,20},{13,21},{14,22},{15,23},{16,... | collective-permute-start | bytes 2359304 | tf_op jit(solution)/shard_map/ppermute | solution.py:43
  48.5 29.2 %collective-permute-start.5 = (bf16[1536,256]{1,0:T(8,128)(2,1)S(1)}, bf16[1536,256]{1,0:T(8,128)(2,1)S(1)}, u32[]{:S(2)}, u32[]{:S(2)}) collective-permute-start(bf16[1536,256]{1,0:T(8,128)(2,1)S(1)} %collective-permute-done.3.down), channel_id=1, source_target_pairs={{8,0},{9,1},{10,2},{11,3},{12,4},{13,5},{14,6},{15,7},{16,8},{17,9... | collective-permute-start | bytes 2359304 | tf_op jit(solution)/shard_map/ppermute | solution.py:43
  57.8 14.4 %collective-permute-start.11 = (bf16[768,256]{1,0:T(8,128)(2,1)S(1)}, bf16[768,256]{1,0:T(8,128)(2,1)S(1)}, u32[]{:S(2)}, u32[]{:S(2)}) collective-permute-start(bf16[768,256]{1,0:T(8,128)(2,1)S(1)} %pad_maximum_fusion.7.own), channel_id=1, source_target_pairs={{0,8},{1,9},{2,10},{3,11},{4,12},{5,13},{6,14},{7,15},{8,16},{9,17... | collective-permute-start | bytes 1179656 | tf_op jit(solution)/shard_map/ppermute | solution.py:43
  61.0 15.1 %collective-permute-start.12 = (bf16[768,256]{1,0:T(8,128)(2,1)S(1)}, bf16[768,256]{1,0:T(8,128)(2,1)S(1)}, u32[]{:S(2)}, u32[]{:S(2)}) collective-permute-start(bf16[768,256]{1,0:T(8,128)(2,1)S(1)} %pad_maximum_fusion.7.own), channel_id=1, source_target_pairs={{8,0},{9,1},{10,2},{11,3},{12,4},{13,5},{14,6},{15,7},{16,8},{17,9... | collective-permute-start | bytes 1179656 | tf_op jit(solution)/shard_map/ppermute | solution.py:43
  78.6 28.3 %collective-permute-start.14 = (bf16[288,4096]{1,0:T(8,128)(2,1)}, bf16[288,4096]{1,0:T(8,128)(2,1)}, u32[]{:S(2)}, u32[]{:S(2)}) collective-permute-start(bf16[288,4096]{1,0:T(8,128)(2,1)} %pad_maximum_fusion.1.mine), channel_id=1, source_target_pairs={{0,1},{1,0},{2,3},{3,2},{4,5},{5,4},{6,7},{7,6},{8,9},{9,8},{10,11... | collective-permute-start | bytes 7077896 | tf_op jit(solution)/shard_map/ppermute | solution.py:43
  82.6 18.9 %collective-permute-start.13 = (bf16[1536,256]{1,0:T(8,128)(2,1)S(1)}, bf16[1536,256]{1,0:T(8,128)(2,1)S(1)}, u32[]{:S(2)}, u32[]{:S(2)}) collective-permute-start(bf16[1536,256]{1,0:T(8,128)(2,1)S(1)} %broadcast_select_fusion), channel_id=1, source_target_pairs={{8,0},{9,1},{10,2},{11,3},{12,4},{13,5},{14,6},{15,7},{16,24},{17,... | collective-permute-start | bytes 2359304 | tf_op jit(solution)/shard_map/ppermute | solution.py:43
  101.4 18.9 %collective-permute-start.17 = (bf16[768,256]{1,0:T(8,128)(2,1)S(1)}, bf16[768,256]{1,0:T(8,128)(2,1)S(1)}, u32[]{:S(2)}, u32[]{:S(2)}) collective-permute-start(bf16[768,256]{1,0:T(8,128)(2,1)S(1)} %copy-done.9), channel_id=1, source_target_pairs={{8,0},{9,1},{10,2},{11,3},{12,4},{13,5},{14,6},{15,7},{16,8},{17,9... | collective-permute-start | bytes 1179656 | tf_op jit(solution)/shard_map/ppermute | solution.py:43
  105.5 14.8 %collective-permute-start.16 = (bf16[768,256]{1,0:T(8,128)(2,1)S(1)}, bf16[768,256]{1,0:T(8,128)(2,1)S(1)}, u32[]{:S(2)}, u32[]{:S(2)}) collective-permute-start(bf16[768,256]{1,0:T(8,128)(2,1)S(1)} %collective-permute-done.11.up), channel_id=1, source_target_pairs={{8,16},{9,17},{10,18},{11,19},{12,20},{13,21},{14,22},{15,23},{16,... | collective-permute-start | bytes 1179656 | tf_op jit(solution)/shard_map/ppermute | solution.py:43
  119.1 20.5 %collective-permute-start.15 = (bf16[1536,256]{1,0:T(8,128)(2,1)S(1)}, bf16[1536,256]{1,0:T(8,128)(2,1)S(1)}, u32[]{:S(2)}, u32[]{:S(2)}) collective-permute-start(bf16[1536,256]{1,0:T(8,128)(2,1)S(1)} %get-tuple-element.93), channel_id=1, source_target_pairs={{0,8},{1,9},{2,10},{3,11},{4,12},{5,13},{6,14},{7,15},{24,16},{25,... | collective-permute-start | bytes 2359304 | tf_op jit(solution)/shard_map/ppermute | solution.py:43
  149.2 22.7 %collective-permute-start.21 = (bf16[288,4096]{1,0:T(8,128)(2,1)}, bf16[288,4096]{1,0:T(8,128)(2,1)}, u32[]{:S(2)}, u32[]{:S(2)}) collective-permute-start(bf16[288,4096]{1,0:T(8,128)(2,1)} %get-tuple-element.121), channel_id=1, source_target_pairs={{0,1},{1,0},{2,3},{3,2},{4,5},{5,4},{6,7},{7,6},{8,9},{9,8},{10,11... | collective-permute-start | bytes 7077896 | tf_op jit(solution)/shard_map/ppermute | solution.py:43
  151.6 13.0 %collective-permute-start.27 = (bf16[768,256]{1,0:T(8,128)(2,1)}, bf16[768,256]{1,0:T(8,128)(2,1)S(1)}, u32[]{:S(2)}, u32[]{:S(2)}) collective-permute-start(bf16[768,256]{1,0:T(8,128)(2,1)} %get-tuple-element.131), channel_id=1, source_target_pairs={{0,8},{1,9},{2,10},{3,11},{4,12},{5,13},{6,14},{7,15},{24,16},{25,... | collective-permute-start | bytes 1179656 | tf_op jit(solution)/shard_map/ppermute | solution.py:43
  152.9 28.6 %collective-permute-start.19 = (bf16[1536,256]{1,0:T(8,128)(2,1)S(1)}, bf16[1536,256]{1,0:T(8,128)(2,1)S(1)}, u32[]{:S(2)}, u32[]{:S(2)}) collective-permute-start(bf16[1536,256]{1,0:T(8,128)(2,1)S(1)} %add_convert_fusion.4), channel_id=1, source_target_pairs={{0,8},{1,9},{2,10},{3,11},{4,12},{5,13},{6,14},{7,15},{8,16},{9,17... | collective-permute-start | bytes 2359304 | tf_op jit(solution)/shard_map/ppermute | solution.py:43
  154.8 26.7 %collective-permute-start.20 = (bf16[1536,256]{1,0:T(8,128)(2,1)S(1)}, bf16[1536,256]{1,0:T(8,128)(2,1)S(1)}, u32[]{:S(2)}, u32[]{:S(2)}) collective-permute-start(bf16[1536,256]{1,0:T(8,128)(2,1)S(1)} %add_convert_fusion.4), channel_id=1, source_target_pairs={{16,8},{17,9},{18,10},{19,11},{20,12},{21,13},{22,14},{23,15},{24,... | collective-permute-start | bytes 2359304 | tf_op jit(solution)/shard_map/ppermute | solution.py:43
  166.6 23.2 %collective-permute-start.30 = (bf16[768,256]{1,0:T(8,128)(2,1)S(1)}, bf16[768,256]{1,0:T(8,128)(2,1)S(1)}, u32[]{:S(2)}, u32[]{:S(2)}) collective-permute-start(bf16[768,256]{1,0:T(8,128)(2,1)S(1)} %add_convert_fusion.8), channel_id=1, source_target_pairs={{16,8},{17,9},{18,10},{19,11},{20,12},{21,13},{22,14},{23,15},{24,... | collective-permute-start | bytes 1179656 | tf_op jit(solution)/shard_map/ppermute | solution.py:43
  167.9 23.3 %collective-permute-start.28 = (bf16[768,256]{1,0:T(8,128)(2,1)S(1)}, bf16[768,256]{1,0:T(8,128)(2,1)S(1)}, u32[]{:S(2)}, u32[]{:S(2)}) collective-permute-start(bf16[768,256]{1,0:T(8,128)(2,1)S(1)} %add_convert_fusion.8), channel_id=1, source_target_pairs={{0,8},{1,9},{2,10},{3,11},{4,12},{5,13},{6,14},{7,15},{8,16},{9,17... | collective-permute-start | bytes 1179656 | tf_op jit(solution)/shard_map/ppermute | solution.py:43
  182.8 20.1 %collective-permute-start.25 = (bf16[1536,256]{1,0:T(8,128)(2,1)S(1)}, bf16[1536,256]{1,0:T(8,128)(2,1)S(1)}, u32[]{:S(2)}, u32[]{:S(2)}) collective-permute-start(bf16[1536,256]{1,0:T(8,128)(2,1)S(1)} %add_convert_fusion.2), channel_id=1, source_target_pairs={{8,0},{9,1},{10,2},{11,3},{12,4},{13,5},{14,6},{15,7},{16,8},{17,9... | collective-permute-start | bytes 2359304 | tf_op jit(solution)/shard_map/ppermute | solution.py:43
  184.9 13.8 %collective-permute-start.23 = (bf16[2,72,2048]{2,1,0:T(8,128)(2,1)S(1)}, bf16[2,72,2048]{2,1,0:T(8,128)(2,1)S(1)}, u32[]{:S(2)}, u32[]{:S(2)}) collective-permute-start(bf16[2,72,2048]{2,1,0:T(8,128)(2,1)S(1)} %get-tuple-element.149), channel_id=1, source_target_pairs={{0,2},{1,3},{2,0},{3,1},{4,6},{5,7},{6,4},{7,5},{8,10},{9,11},{10,... | collective-permute-start | bytes 1769480 | tf_op jit(solution)/shard_map/ppermute | solution.py:43
  186.4 19.6 %collective-permute-start.24 = (bf16[1536,256]{1,0:T(8,128)(2,1)S(1)}, bf16[1536,256]{1,0:T(8,128)(2,1)S(1)}, u32[]{:S(2)}, u32[]{:S(2)}) collective-permute-start(bf16[1536,256]{1,0:T(8,128)(2,1)S(1)} %add_convert_fusion.3), channel_id=1, source_target_pairs={{0,8},{1,9},{2,10},{3,11},{4,12},{5,13},{6,14},{7,15},{8,16},{9,17... | collective-permute-start | bytes 2359304 | tf_op jit(solution)/shard_map/ppermute | solution.py:43
  189.8 13.0 %collective-permute-start.22 = (bf16[2,72,2048]{2,1,0:T(8,128)(2,1)S(1)}, bf16[2,72,2048]{2,1,0:T(8,128)(2,1)S(1)}, u32[]{:S(2)}, u32[]{:S(2)}) collective-permute-start(bf16[2,72,2048]{2,1,0:T(8,128)(2,1)S(1)} %slice_bitcast_fusion.5), channel_id=1, source_target_pairs={{0,4},{1,5},{2,6},{3,7},{4,0},{5,1},{6,2},{7,3},{8,12},{9,13},{10,... | collective-permute-start | bytes 1769480 | tf_op jit(solution)/shard_map/ppermute | solution.py:43
  191.2 24.2 %collective-permute-start.31 = (bf16[768,256]{1,0:T(8,128)(2,1)S(1)}, bf16[768,256]{1,0:T(8,128)(2,1)S(1)}, u32[]{:S(2)}, u32[]{:S(2)}) collective-permute-start(bf16[768,256]{1,0:T(8,128)(2,1)S(1)} %add_convert_fusion.6), channel_id=1, source_target_pairs={{8,0},{9,1},{10,2},{11,3},{12,4},{13,5},{14,6},{15,7},{16,8},{17,9... | collective-permute-start | bytes 1179656 | tf_op jit(solution)/shard_map/ppermute | solution.py:43
  198.7 17.0 %collective-permute-start.29 = (bf16[768,256]{1,0:T(8,128)(2,1)S(1)}, bf16[768,256]{1,0:T(8,128)(2,1)S(1)}, u32[]{:S(2)}, u32[]{:S(2)}) collective-permute-start(bf16[768,256]{1,0:T(8,128)(2,1)S(1)} %add_convert_fusion.7), channel_id=1, source_target_pairs={{0,8},{1,9},{2,10},{3,11},{4,12},{5,13},{6,14},{7,15},{8,16},{9,17... | collective-permute-start | bytes 1179656 | tf_op jit(solution)/shard_map/ppermute | solution.py:43
  206.4 15.9 %collective-permute-start.32 = (bf16[768,256]{1,0:T(8,128)(2,1)S(1)}, bf16[768,256]{1,0:T(8,128)(2,1)S(1)}, u32[]{:S(2)}, u32[]{:S(2)}) collective-permute-start(bf16[768,256]{1,0:T(8,128)(2,1)S(1)} %get-tuple-element.157), channel_id=1, source_target_pairs={{0,0},{1,4},{2,2},{3,6},{4,1},{5,5},{6,3},{7,7},{8,8},{9,12},{10,1... | collective-permute-start | bytes 1179656 | tf_op jit(solution)/shard_map/ppermute | solution.py:43
  213.6 11.2 %collective-permute-start.33 = (bf16[768,256]{1,0:T(8,128)(2,1)S(1)}, bf16[768,256]{1,0:T(8,128)(2,1)S(1)}, u32[]{:S(2)}, u32[]{:S(2)}) collective-permute-start(bf16[768,256]{1,0:T(8,128)(2,1)S(1)} %get-tuple-element.156), channel_id=1, source_target_pairs={{0,4},{1,0},{2,6},{3,2},{4,5},{5,1},{6,7},{7,3},{8,12},{9,8},{10,1... | collective-permute-start | bytes 1179656 | tf_op jit(solution)/shard_map/ppermute | solution.py:43
  213.7 23.4 %collective-permute-start.34 = (bf16[2,72,2048]{2,1,0:T(8,128)(2,1)S(1)}, bf16[2,72,2048]{2,1,0:T(8,128)(2,1)S(1)}, u32[]{:S(2)}, u32[]{:S(2)}) collective-permute-start(bf16[2,72,2048]{2,1,0:T(8,128)(2,1)S(1)} %get-tuple-element.155), channel_id=1, source_target_pairs={{0,4},{1,5},{2,6},{3,7},{4,0},{5,1},{6,2},{7,3},{8,12},{9,13},{10,... | collective-permute-start | bytes 1769480 | tf_op jit(solution)/shard_map/ppermute | solution.py:43
  215.4 22.3 %collective-permute-start.26 = (bf16[2,72,2048]{2,1,0:T(8,128)(2,1)S(1)}, bf16[2,72,2048]{2,1,0:T(8,128)(2,1)S(1)}, u32[]{:S(2)}, u32[]{:S(2)}) collective-permute-start(bf16[2,72,2048]{2,1,0:T(8,128)(2,1)S(1)} %slice_bitcast_fusion.2), channel_id=1, source_target_pairs={{0,2},{1,3},{2,0},{3,1},{4,6},{5,7},{6,4},{7,5},{8,10},{9,11},{10,... | collective-permute-start | bytes 1769480 | tf_op jit(solution)/shard_map/ppermute | solution.py:43
  224.9 17.2 %collective-permute-start.35 = (bf16[384,256]{1,0:T(8,128)(2,1)S(1)}, bf16[384,256]{1,0:T(8,128)(2,1)S(1)}, u32[]{:S(2)}, u32[]{:S(2)}) collective-permute-start(bf16[384,256]{1,0:T(8,128)(2,1)S(1)} %get-tuple-element.161), channel_id=1, source_target_pairs={{0,0},{1,4},{2,2},{3,6},{4,1},{5,5},{6,3},{7,7},{8,8},{9,12},{10,1... | collective-permute-start | bytes 589832 | tf_op jit(solution)/shard_map/ppermute | solution.py:43
  227.6 14.5 %collective-permute-start.36 = (bf16[384,256]{1,0:T(8,128)(2,1)S(1)}, bf16[384,256]{1,0:T(8,128)(2,1)S(1)}, u32[]{:S(2)}, u32[]{:S(2)}) collective-permute-start(bf16[384,256]{1,0:T(8,128)(2,1)S(1)} %get-tuple-element.160), channel_id=1, source_target_pairs={{0,4},{1,0},{2,6},{3,2},{4,5},{5,1},{6,7},{7,3},{8,12},{9,8},{10,1... | collective-permute-start | bytes 589832 | tf_op jit(solution)/shard_map/ppermute | solution.py:43
  (37 other events, 214.9 us)

commit v11 on v10

--- a/solution.py
+++ b/solution.py
@@ -335,7 +335,7 @@
         ],
         compiler_params=pltpu.CompilerParams(vmem_limit_bytes=VMEM_BYTES),
         cost_estimate=pl.CostEstimate(
-            flops=12 * rows * width * units, bytes_accessed=16 * 2**20, transcendentals=rows * units
+            flops=12 * rows * width * units, bytes_accessed=4 * 2**20, transcendentals=rows * units
         ),
     )(z, *weights, mine, theirs)
     return outs[:4], outs[4], outs[5:]
@@ -361,7 +361,7 @@
         out_specs=[pl.BlockSpec((slots, tile), lambda n: (0, n))] * 2,
         compiler_params=pltpu.CompilerParams(vmem_limit_bytes=VMEM_BYTES // 2),
         cost_estimate=pl.CostEstimate(
-            flops=12 * slots * width * units, bytes_accessed=12 * 2**20, transcendentals=0
+            flops=12 * slots * width * units, bytes_accessed=2 * 2**20, transcendentals=0
         ),
     )(*(array for chunk in chunks for array in chunk))
 
@@ -444,6 +444,17 @@
         ],
         axis=1,
     )
+    def combine(returned, back_rows):
+        high = lax.reduce_precision(weighted, 8, 7)
+        mixed = (dot(high.astype(BF), returned) + dot((weighted - high).astype(BF), returned)).astype(BF)
+        products = dot(d_out, returned, ((1,), (1,)))
+        d_probs = jnp.sum(jnp.where(pair, products[:, None, :], 0.0), axis=2)
+        d_turned = dot(placing, back_rows).astype(BF)
+        d_tokens = lax.dynamic_slice(
+            jnp.concatenate([d_turned, d_turned], axis=1), (0, (g.zs - g.z) * line_width), (rows, width)
+        )
+        return mixed, d_tokens, d_probs
+
     shapes = w_gate.shape[1:], w_down.shape[1:]
     together = lax.optimization_barrier
     if in_kernels:
@@ -458,30 +469,30 @@
         up, down = g.hop(shard, ups), g.hop(shard, downs)
         shard2, sent = together((spread(a2, b2), sent))
         up, down = together((up, down))
+        far = g.hop(jnp.where(g.z == 1, up, down), {1: 3, 2: 0})
         up_2, down_2 = g.hop(up, {1: 2, 2: 3}), g.hop(down, {1: 0, 2: 1})
-        shard2, mine = together((shard2, exchange(sent, 1)))
+        mine = tie(exchange(sent, 1), far, up_2, down_2)
+        theirs = g.send(mine, other_core)
+        shard2 = tie(shard2, mine)
         up2, down2 = g.hop(shard2, ups), g.hop(shard2, downs)
-        up_2, down_2, up2, down2, mine = together((up_2, down_2, up2, down2, mine))
-        last = g.hop(jnp.where(to_last, up_2, down_2), passing)
-        theirs = g.send(mine, other_core)
-        up2, down2 = tie(up2, last), tie(down2, last)
+        chunk, outer, terms = expert(place_z, g.zs, units[0], (shard, up, down, up_2, down_2, far), mine, theirs)
+        begun = g.hop(outer, outward)
+        up2, down2 = tie(up2, outer), tie(down2, outer)
         up2_2, down2_2 = g.hop(up2, {1: 2, 2: 3}), g.hop(down2, {1: 0, 2: 1})
-        chunk, outer, terms = expert(
-            place_z, g.zs, units[0], (shard, up, down, up_2, down_2, last), mine, theirs
+        passed = jnp.where(to_last, up2_2, down2_2)
+        last2 = g.hop(passed, passing)
+        middle = added(terms[2], tie(begun, passed))
+        sum_up, sum_down = g.hop(middle, inward_up), g.hop(middle, inward_down)
+        chunk2, outer2, terms2 = expert(
+            place_z, g.zs, units[1], (shard2, up2, down2, up2_2, down2_2, tie(last2, middle)), mine, theirs
         )
-        up2_2, down2_2 = tie(up2_2, outer), tie(down2_2, outer)
-        last2 = g.hop(jnp.where(to_last, up2_2, down2_2), passing)
-        begun = g.hop(outer, outward)
-        chunk2, outer2, terms2 = expert(
-            place_z, g.zs, units[1], (shard2, up2, down2, up2_2, down2_2, last2), mine, theirs
-        )
-        begun, outer2, chunk2 = together((begun, outer2, chunk2))
-        middle, outer2, chunk2 = together((added(terms[2], begun), outer2, chunk2))
-        sum_up, sum_down = g.hop(middle, inward_up), g.hop(middle, inward_down)
+        keep, give = token_rows((chunk, chunk2), slots, width)
+        sum_up, sum_down = tie(sum_up, keep, give), tie(sum_down, keep, give)
+        sum_up, sum_down = added(terms[1], sum_up), added(terms[3], sum_down)
+        give, outer2 = tie(give, sum_up, sum_down), tie(outer2, sum_up, sum_down)
+        sum_up, sum_down = g.hop(sum_up, ups), g.hop(sum_down, downs)
         begun2 = g.hop(outer2, outward)
-        keep, give = token_rows((chunk, chunk2), slots, width)
         sums = added(keep, g.send(give, other_core)).reshape(g.qs, 2, cap, 2 * width)
-        sum_up, sum_down, sums = together((sum_up, sum_down, sums))
 
         def along_x(rows):
             return jnp.stack([rows[:, 0], g.send(rows[:, 1], lambda z, x, q, c: (z, 1 - x, q, c))], axis=1)
@@ -492,19 +503,18 @@
             )
 
         returned, back_rows = along_x(sums[..., :width]), along_q(sums[..., width:])
-        sum_up, sum_down = g.hop(added(terms[1], sum_up), ups), g.hop(added(terms[3], sum_down), downs)
+        grad = added(terms[0], tie(sum_up, sums), tie(sum_down, sums))
+        begun2, returned, back_rows, grad = together((begun2, returned, back_rows, grad))
         middle2 = added(terms2[2], begun2)
         sum_up2, sum_down2 = g.hop(middle2, inward_up), g.hop(middle2, inward_down)
-        returned, back_rows, sum_up, sum_down = together((returned, back_rows, sum_up, sum_down))
         returned, back_rows = along_q(returned), along_x(back_rows)
-        grad = added(terms[0], sum_up, sum_down)
-        grads = unspread(grad)
-        sum_up2, sum_down2 = g.hop(added(terms2[1], sum_up2), ups), g.hop(added(terms2[3], sum_down2), downs)
-        sum_up2, sum_down2, grads = together((sum_up2, sum_down2, grads))
-        grad2 = added(terms2[0], sum_up2, sum_down2)
-        returned, back_rows = tie(returned, grad2), tie(back_rows, grad2)
-        returned, back_rows = returned.reshape(slots, width), back_rows.reshape(slots, width)
-        grads += unspread(grad2)
+        sum_up2, sum_down2 = tie(sum_up2, grad), tie(sum_down2, grad)
+        sum_up2, sum_down2 = added(terms2[1], sum_up2), added(terms2[3], sum_down2)
+        grads = unspread(tie(grad, sum_up2, sum_down2))
+        sum_up2, sum_down2 = g.hop(sum_up2, ups), g.hop(sum_down2, downs)
+        mixed, d_tokens, d_probs = combine(returned.reshape(slots, width), back_rows.reshape(slots, width))
+        sum_up2, sum_down2 = (tie(value, mixed, d_tokens, d_probs, *grads) for value in (sum_up2, sum_down2))
+        grads += unspread(added(terms2[0], sum_up2, sum_down2))
         d_w_gate, d_w_up, d_w_down = unpack(pieces, place_x, grads, shuffle, *shapes)
     else:
         gate_cols, up_cols = dot(w_gate[0], shuffle).astype(BF), dot(w_up[0], shuffle).astype(BF)
@@ -545,17 +555,7 @@
             dot(jnp.concatenate([both_a[:, cols], both_b[:, cols]], axis=1), shuffle, ((1,), (1,)))
             for cols in (slice(0, half), slice(half, None))
         )
-        returned, back_rows = got[:, :width], got[:, width:]
-
-    high = lax.reduce_precision(weighted, 8, 7)
-    mixed = (dot(high.astype(BF), returned) + dot((weighted - high).astype(BF), returned)).astype(BF)
-    products = dot(d_out, returned, ((1,), (1,)))
-    d_probs = jnp.sum(jnp.where(pair, products[:, None, :], 0.0), axis=2)
-    d_turned = dot(placing, back_rows).astype(BF)
-    d_tokens = lax.dynamic_slice(
-        jnp.concatenate([d_turned, d_turned], axis=1), (0, (g.zs - g.z) * line_width), (rows, width)
-    )
-
+        mixed, d_tokens, d_probs = combine(got[:, :width], got[:, width:])
     return (mixed, d_tokens, d_probs, d_w_gate[None], d_w_up[None], d_w_down[None])
 
 

time: 246 us -> 241 us (0.980)
  waiting for transfers between devices: 105 us -> 96.6 us
    ppermute x37, waiting for transfers between devices: 105 us -> 96.6 us  [send(): return lax.ppermute(value, BOTH, pairs)]
    unnamed x62 -> x81, local copies, waits for them, and re-layouts: 13 us -> 13.4 us
  transfers between devices with their start and end apart: 37 -> 37, of which waited for: 18 -> 19; matrix products, arithmetic and copies ran while one was open for 7% -> 8% of each run, Pallas kernels for 7% -> 10%
where the time goes in v11:
time: 241 us; the launch traced here: 239 us
  waiting for transfers between devices  96.6 us (40%)
  starting transfers between devices  78.7 us (33%)
  Pallas kernels  26.6 us (11%)
  local copies, waits for them, and re-layouts  15.4 us (6%)
  other arithmetic  14.2 us (6%)
  matrix products  5.84 us (2%)
    ppermute x37, waiting for transfers between devices, send(): return lax.ppermute(value, BOTH, pairs)  96.6 us
    ppermute x37, starting transfers between devices, send(): return lax.ppermute(value, BOTH, pairs)  78.7 us
    pallas_call x2, Pallas kernels, expert(): pl.pallas_call(expert_kernel, out_shape=for_rows + [jax.ShapeDtypeStruct(...  17.7 us
    unnamed x81, local copies, waits for them, and re-layouts  13.4 us
    convert_element_type x9, other arithmetic, added(): return sum((t.astype(F32) for t in terms)).astype(BF)  6.73 us
    pallas_call x1, Pallas kernels, token_rows(): pl.pallas_call(functools.partial(rows_kernel, len(chunks)), grid=(2 * til...  6.11 us
    dot_general x7, matrix products, dot(): return lax.dot_general(a, b, (dims, ((), ())), preferred_element_type=F32)  5.84 us
  transfers between devices with their start and end apart: 37, of which 19 were waited for; matrix products, arithmetic and copies ran while one was open for 8% of the time, Pallas kernels for 10%

profile of v11, /device:TPU:9, one launch (start us, length us, event | category | flops | bytes accessed | tf_op | source)
XLA Modules:
  0.0 239.0 jit_solution(9898784412615479189)
XLA Ops:
  4.9 3.7 %collective-permute-start = (bf16[768,256]{1,0:T(8,128)(2,1)S(1)}, bf16[768,256]{1,0:T(8,128)(2,1)S(1)}, u32[]{:S(2)}, u32[]{:S(2)}) collective-permute-start(bf16[768,256]{1,0:T(8,128)(2,1)S(1)} %get-tuple-element.61), channel_id=1, source_target_pairs={{0,0},{1,4},{2,2},{3,6},{4,1},{5,5},{6,3},{7,7},{8,8},{9,12},{10,1... | collective-permute-start | bytes 1179656 | tf_op jit(solution)/shard_map/ppermute | solution.py:43
  9.0 2.6 %convolution_convert_fusion = bf16[288,2048]{1,0:T(8,128)(2,1)} fusion(pred[128,288]{0,1:T(8,128)(4,1)S(1)} %fusion.6, s32[]{:T(128)S(6)} %select_n.146, bf16[128,2048]{1,0:T(8,128)(2,1)} %param.7), kind=kOutput, calls=%fused_computation.3 | convolution fusion | flops 152633344 | bytes 1740804 | tf_op jit(solution)/shard_map/dot_general | solution.py:16
  14.1 3.5 %collective-permute-done.1 = bf16[768,256]{1,0:T(8,128)(2,1)} collective-permute-done((bf16[768,256]{1,0:T(8,128)(2,1)S(1)}, bf16[768,256]{1,0:T(8,128)(2,1)}, u32[]{:S(2)}, u32[]{:S(2)}) %collective-permute-start.1) | collective-permute-done | bytes 393248 | tf_op jit(solution)/shard_map/ppermute | solution.py:43
  18.6 2.5 %collective-permute-start.2 = (bf16[384,256]{1,0:T(8,128)(2,1)S(1)}, bf16[384,256]{1,0:T(8,128)(2,1)S(1)}, u32[]{:S(2)}, u32[]{:S(2)}) collective-permute-start(bf16[384,256]{1,0:T(8,128)(2,1)S(1)} %get-tuple-element.65), channel_id=1, source_target_pairs={{0,0},{1,4},{2,2},{3,6},{4,1},{5,5},{6,3},{7,7},{8,8},{9,12},{10,1... | collective-permute-start | bytes 589832 | tf_op jit(solution)/shard_map/ppermute | solution.py:43
  21.6 3.2 %collective-permute-start.7 = (bf16[1536,256]{1,0:T(8,128)(2,1)S(1)}, bf16[1536,256]{1,0:T(8,128)(2,1)}, u32[]{:S(2)}, u32[]{:S(2)}) collective-permute-start(bf16[1536,256]{1,0:T(8,128)(2,1)S(1)} %pad_maximum_fusion.6.own), channel_id=1, source_target_pairs={{0,8},{1,9},{2,10},{3,11},{4,12},{5,13},{6,14},{7,15},{8,16},{9,17... | collective-permute-start | bytes 2359304 | tf_op jit(solution)/shard_map/ppermute | solution.py:43
  24.8 3.0 %collective-permute-start.8 = (bf16[1536,256]{1,0:T(8,128)(2,1)S(1)}, bf16[1536,256]{1,0:T(8,128)(2,1)}, u32[]{:S(2)}, u32[]{:S(2)}) collective-permute-start(bf16[1536,256]{1,0:T(8,128)(2,1)S(1)} %pad_maximum_fusion.6.own), channel_id=1, source_target_pairs={{8,0},{9,1},{10,2},{11,3},{12,4},{13,5},{14,6},{15,7},{16,8},{17,9... | collective-permute-start | bytes 2359304 | tf_op jit(solution)/shard_map/ppermute | solution.py:43
  31.8 10.6 %collective-permute-done.7.up = bf16[1536,256]{1,0:T(8,128)(2,1)} collective-permute-done((bf16[1536,256]{1,0:T(8,128)(2,1)S(1)}, bf16[1536,256]{1,0:T(8,128)(2,1)}, u32[]{:S(2)}, u32[]{:S(2)}) %collective-permute-start.7) | collective-permute-done | bytes 786464 | tf_op jit(solution)/shard_map/ppermute | solution.py:43
  42.4 2.9 %collective-permute-done.8.down = bf16[1536,256]{1,0:T(8,128)(2,1)} collective-permute-done((bf16[1536,256]{1,0:T(8,128)(2,1)S(1)}, bf16[1536,256]{1,0:T(8,128)(2,1)}, u32[]{:S(2)}, u32[]{:S(2)}) %collective-permute-start.8) | collective-permute-done | bytes 786464 | tf_op jit(solution)/shard_map/ppermute | solution.py:43
  45.3 3.2 %collective-permute-start.10 = (bf16[1536,256]{1,0:T(8,128)(2,1)}, bf16[1536,256]{1,0:T(8,128)(2,1)S(1)}, u32[]{:S(2)}, u32[]{:S(2)}) collective-permute-start(bf16[1536,256]{1,0:T(8,128)(2,1)} %collective-permute-done.7.up), channel_id=1, source_target_pairs={{8,16},{9,17},{10,18},{11,19},{12,20},{13,21},{14,22},{15,23},{16,... | collective-permute-start | bytes 2359304 | tf_op jit(solution)/shard_map/ppermute | solution.py:43
  53.1 3.9 %collective-permute-done.6 = bf16[72,4096]{1,0:T(8,128)(2,1)S(1)} collective-permute-done((bf16[72,4096]{1,0:T(8,128)(2,1)}, bf16[72,4096]{1,0:T(8,128)(2,1)S(1)}, u32[]{:S(2)}, u32[]{:S(2)}) %collective-permute-start.6) | collective-permute-done | bytes 589856 | tf_op jit(solution)/shard_map/ppermute | solution.py:43
  58.3 22.6 %collective-permute-done.9.last = bf16[1536,256]{1,0:T(8,128)(2,1)S(1)} collective-permute-done((bf16[1536,256]{1,0:T(8,128)(2,1)S(1)}, bf16[1536,256]{1,0:T(8,128)(2,1)S(1)}, u32[]{:S(2)}, u32[]{:S(2)}) %collective-permute-start.9) | collective-permute-done | bytes 786464 | tf_op jit(solution)/shard_map/ppermute | solution.py:43
  80.9 4.4 %collective-permute-done.11.down_2 = bf16[1536,256]{1,0:T(8,128)(2,1)S(1)} collective-permute-done((bf16[1536,256]{1,0:T(8,128)(2,1)}, bf16[1536,256]{1,0:T(8,128)(2,1)S(1)}, u32[]{:S(2)}, u32[]{:S(2)}) %collective-permute-start.11) | collective-permute-done | bytes 786464 | tf_op jit(solution)/shard_map/ppermute | solution.py:43
  86.8 3.0 %collective-permute-start.14 = (bf16[768,256]{1,0:T(8,128)(2,1)S(1)}, bf16[768,256]{1,0:T(8,128)(2,1)S(1)}, u32[]{:S(2)}, u32[]{:S(2)}) collective-permute-start(bf16[768,256]{1,0:T(8,128)(2,1)S(1)} %pad_maximum_fusion.7.own), channel_id=1, source_target_pairs={{8,0},{9,1},{10,2},{11,3},{12,4},{13,5},{14,6},{15,7},{16,8},{17,9... | collective-permute-start | bytes 1179656 | tf_op jit(solution)/shard_map/ppermute | solution.py:43
  93.6 9.5 %shard_map.119 = (bf16[2048,512]{1,0:T(8,128)(2,1)}, bf16[256,2048]{1,0:T(8,128)(2,1)}, bf16[576,256]{1,0:T(8,128)(2,1)S(1)}, bf16[576,512]{1,0:T(8,128)(2,1)S(1...) custom-call(s32[1]{0:T(128)} %bitcast.z_ref, ...), custom_call_target="tpu_custom_call" | custom-call | flops 3623878656 | bytes 4194304 | tf_op jit(solution)/shard_map/pallas_call | solution.py:316
  109.5 4.9 %collective-permute-start.16 = (bf16[768,256]{1,0:T(8,128)(2,1)S(1)}, bf16[768,256]{1,0:T(8,128)(2,1)S(1)}, u32[]{:S(2)}, u32[]{:S(2)}) collective-permute-start(bf16[768,256]{1,0:T(8,128)(2,1)S(1)} %collective-permute-done.14.down), channel_id=1, source_target_pairs={{8,0},{9,1},{10,2},{11,3},{12,4},{13,5},{14,6},{15,7},{16,8},{17,9... | collective-permute-start | bytes 1179656 | tf_op jit(solution)/shard_map/ppermute | solution.py:43
  115.7 6.2 %collective-permute-done.16.down_2 = bf16[768,256]{1,0:T(8,128)(2,1)S(1)} collective-permute-done((bf16[768,256]{1,0:T(8,128)(2,1)S(1)}, bf16[768,256]{1,0:T(8,128)(2,1)S(1)}, u32[]{:S(2)}, u32[]{:S(2)}) %collective-permute-start.16) | collective-permute-done | bytes 393248 | tf_op jit(solution)/shard_map/ppermute | solution.py:43
  123.6 2.5 %collective-permute-start.17 = (bf16[768,256]{1,0:T(8,128)(2,1)S(1)}, bf16[768,256]{1,0:T(8,128)(2,1)S(1)}, u32[]{:S(2)}, u32[]{:S(2)}) collective-permute-start(bf16[768,256]{1,0:T(8,128)(2,1)S(1)} %broadcast_select_fusion.1), channel_id=1, source_target_pairs={{8,0},{9,1},{10,2},{11,3},{12,4},{13,5},{14,6},{15,7},{16,24},{17,... | collective-permute-start | bytes 1179656 | tf_op jit(solution)/shard_map/ppermute | solution.py:43
  126.1 2.8 %collective-permute-done.18 = bf16[1536,256]{1,0:T(8,128)(2,1)} collective-permute-done((bf16[1536,256]{1,0:T(8,128)(2,1)}, bf16[1536,256]{1,0:T(8,128)(2,1)}, u32[]{:S(2)}, u32[]{:S(2)}) %collective-permute-start.18) | collective-permute-done | bytes 786464 | tf_op jit(solution)/shard_map/ppermute | solution.py:43
  131.9 4.0 %collective-permute-start.19 = (bf16[1536,256]{1,0:T(8,128)(2,1)S(1)}, bf16[1536,256]{1,0:T(8,128)(2,1)S(1)}, u32[]{:S(2)}, u32[]{:S(2)}) collective-permute-start(bf16[1536,256]{1,0:T(8,128)(2,1)S(1)} %add_convert_fusion.4), channel_id=1, source_target_pairs={{0,8},{1,9},{2,10},{3,11},{4,12},{5,13},{6,14},{7,15},{8,16},{9,17... | collective-permute-start | bytes 2359304 | tf_op jit(solution)/shard_map/ppermute | solution.py:43
  135.9 8.3 %shard_map.120 = (bf16[2048,256]{1,0:T(8,128)(2,1)}, bf16[128,2048]{1,0:T(8,128)(2,1)S(1)}, bf16[576,128]{1,0:T(8,128)(2,1)S(1)}, bf16[576,256]{1,0:T(8,128)(2,1...) custom-call(s32[1]{0:T(128)} %bitcast.z_ref, ...), custom_call_target="tpu_custom_call" | custom-call | flops 1811939328 | bytes 4194304 | tf_op jit(solution)/shard_map/pallas_call | solution.py:316
  146.1 6.1 %shard_map.121 = (bf16[288,4096]{1,0:T(8,128)(2,1)S(1)}, bf16[288,4096]{1,0:T(8,128)(2,1)}) custom-call(bf16[2048,512]{1,0:T(8,128)(2,1)S(1)} %copy-done.24, bf16[256,2048]{1,0:T(8,128)(2,1)S(1)} %copy-done.25, bf16[576,256]{1,0:T(8,128)(2,1)S(1)} %copy-done.29, bf16[576,512]{1,0:T(8,128)(2,1)S(1)} %copy-done.27, bf16[2048,256]{1,0:T(8,128)(2,1)S(1)} %copy-done.21, ...), custom_call_target="tpu_custom_call" | custom-call | flops 2717908992 | bytes 2097152 | tf_op jit(solution)/shard_map/pallas_call | solution.py:356
  159.1 3.3 %collective-permute-start.26 = (bf16[1536,256]{1,0:T(8,128)(2,1)S(1)}, bf16[1536,256]{1,0:T(8,128)(2,1)S(1)}, u32[]{:S(2)}, u32[]{:S(2)}) collective-permute-start(bf16[1536,256]{1,0:T(8,128)(2,1)S(1)} %add_convert_fusion.2), channel_id=1, source_target_pairs={{8,0},{9,1},{10,2},{11,3},{12,4},{13,5},{14,6},{15,7},{16,8},{17,9... | collective-permute-start | bytes 2359304 | tf_op jit(solution)/shard_map/ppermute | solution.py:43
  163.7 3.3 %add_convert_fusion = bf16[288,4096]{1,0:T(8,128)(2,1)S(1)} fusion(bf16[288,4096]{1,0:T(8,128)(2,1)} %collective-permute-done.22, bf16[288,4096]{1,0:T(8,128)(2,1)} %copy-done.1), kind=kLoop, calls=%fused_computation | loop fusion | flops 4718592 | bytes 7077888 | tf_op jit(solution)/shard_map/convert_element_type | solution.py:24
  168.5 9.8 %collective-permute-done.25 = bf16[1536,256]{1,0:T(8,128)(2,1)S(1)} collective-permute-done((bf16[1536,256]{1,0:T(8,128)(2,1)}, bf16[1536,256]{1,0:T(8,128)(2,1)S(1)}, u32[]{:S(2)}, u32[]{:S(2)}) %collective-permute-start.25) | collective-permute-done | bytes 786464 | tf_op jit(solution)/shard_map/ppermute | solution.py:43
  181.6 11.9 %collective-permute-done.23 = bf16[2,72,2048]{2,1,0:T(8,128)(2,1)S(1)} collective-permute-done((bf16[2,72,2048]{2,1,0:T(8,128)(2,1)S(1)}, bf16[2,72,2048]{2,1,0:T(8,128)(2,1)S(1)}, u32[]{:S(2)}, u32[]{:S(2)}) %collective-permute-start.23) | collective-permute-done | bytes 589856 | tf_op jit(solution)/shard_map/ppermute | solution.py:43
  195.1 4.0 %collective-permute-start.29 = (bf16[768,256]{1,0:T(8,128)(2,1)S(1)}, bf16[768,256]{1,0:T(8,128)(2,1)S(1)}, u32[]{:S(2)}, u32[]{:S(2)}) collective-permute-start(bf16[768,256]{1,0:T(8,128)(2,1)S(1)} %add_convert_fusion.8), channel_id=1, source_target_pairs={{0,8},{1,9},{2,10},{3,11},{4,12},{5,13},{6,14},{7,15},{8,16},{9,17... | collective-permute-start | bytes 1179656 | tf_op jit(solution)/shard_map/ppermute | solution.py:43
  201.9 3.6 %collective-permute-done.29 = bf16[768,256]{1,0:T(8,128)(2,1)S(1)} collective-permute-done((bf16[768,256]{1,0:T(8,128)(2,1)S(1)}, bf16[768,256]{1,0:T(8,128)(2,1)S(1)}, u32[]{:S(2)}, u32[]{:S(2)}) %collective-permute-start.29) | collective-permute-done | bytes 393248 | tf_op jit(solution)/shard_map/ppermute | solution.py:43
  205.7 3.7 %collective-permute-start.33 = (bf16[768,256]{1,0:T(8,128)(2,1)S(1)}, bf16[768,256]{1,0:T(8,128)(2,1)S(1)}, u32[]{:S(2)}, u32[]{:S(2)}) collective-permute-start(bf16[768,256]{1,0:T(8,128)(2,1)S(1)} %add_convert_fusion.7), channel_id=1, source_target_pairs={{0,8},{1,9},{2,10},{3,11},{4,12},{5,13},{6,14},{7,15},{8,16},{9,17... | collective-permute-start | bytes 1179656 | tf_op jit(solution)/shard_map/ppermute | solution.py:43
  211.5 6.5 %collective-permute-start.31 = (bf16[768,256]{1,0:T(8,128)(2,1)S(1)}, bf16[768,256]{1,0:T(8,128)(2,1)S(1)}, u32[]{:S(2)}, u32[]{:S(2)}) collective-permute-start(bf16[768,256]{1,0:T(8,128)(2,1)S(1)} %get-tuple-element.129), channel_id=1, source_target_pairs={{0,0},{1,4},{2,2},{3,6},{4,1},{5,5},{6,3},{7,7},{8,8},{9,12},{10,1... | collective-permute-start | bytes 1179656 | tf_op jit(solution)/shard_map/ppermute | solution.py:43
  223.5 3.0 %collective-permute-done.31.refs_0_ = bf16[768,256]{1,0:T(8,128)(2,1)S(1)} collective-permute-done((bf16[768,256]{1,0:T(8,128)(2,1)S(1)}, bf16[768,256]{1,0:T(8,128)(2,1)S(1)}, u32[]{:S(2)}, u32[]{:S(2)}) %collective-permute-start.31) | collective-permute-done | bytes 393248 | tf_op jit(solution)/shard_map/ppermute | solution.py:43
  227.9 3.6 %collective-permute-start.35 = (bf16[384,256]{1,0:T(8,128)(2,1)S(1)}, bf16[384,256]{1,0:T(8,128)(2,1)S(1)}, u32[]{:S(2)}, u32[]{:S(2)}) collective-permute-start(bf16[384,256]{1,0:T(8,128)(2,1)S(1)} %get-tuple-element.133), channel_id=1, source_target_pairs={{0,0},{1,4},{2,2},{3,6},{4,1},{5,5},{6,3},{7,7},{8,8},{9,12},{10,1... | collective-permute-start | bytes 589832 | tf_op jit(solution)/shard_map/ppermute | solution.py:43
  231.6 4.2 %collective-permute-done.35.refs_2_ = bf16[384,256]{1,0:T(8,128)(2,1)S(1)} collective-permute-done((bf16[384,256]{1,0:T(8,128)(2,1)S(1)}, bf16[384,256]{1,0:T(8,128)(2,1)S(1)}, u32[]{:S(2)}, u32[]{:S(2)}) %collective-permute-start.35) | collective-permute-done | bytes 196640 | tf_op jit(solution)/shard_map/ppermute | solution.py:43
  (177 shorter events, 67.2 us)
Async XLA Ops:
  4.9 9.1 %collective-permute-start = (bf16[768,256]{1,0:T(8,128)(2,1)S(1)}, bf16[768,256]{1,0:T(8,128)(2,1)S(1)}, u32[]{:S(2)}, u32[]{:S(2)}) collective-permute-start(bf16[768,256]{1,0:T(8,128)(2,1)S(1)} %get-tuple-element.61), channel_id=1, source_target_pairs={{0,0},{1,4},{2,2},{3,6},{4,1},{5,5},{6,3},{7,7},{8,8},{9,12},{10,1... | collective-permute-start | bytes 1179656 | tf_op jit(solution)/shard_map/ppermute | solution.py:43
  8.6 8.9 %collective-permute-start.1 = (bf16[768,256]{1,0:T(8,128)(2,1)S(1)}, bf16[768,256]{1,0:T(8,128)(2,1)}, u32[]{:S(2)}, u32[]{:S(2)}) collective-permute-start(bf16[768,256]{1,0:T(8,128)(2,1)S(1)} %get-tuple-element.62), channel_id=1, source_target_pairs={{0,1},{1,5},{2,3},{3,7},{4,0},{5,4},{6,2},{7,6},{8,9},{9,13},{10,1... | collective-permute-start | bytes 1179656 | tf_op jit(solution)/shard_map/ppermute | solution.py:43
  18.6 9.2 %collective-permute-start.2 = (bf16[384,256]{1,0:T(8,128)(2,1)S(1)}, bf16[384,256]{1,0:T(8,128)(2,1)S(1)}, u32[]{:S(2)}, u32[]{:S(2)}) collective-permute-start(bf16[384,256]{1,0:T(8,128)(2,1)S(1)} %get-tuple-element.65), channel_id=1, source_target_pairs={{0,0},{1,4},{2,2},{3,6},{4,1},{5,5},{6,3},{7,7},{8,8},{9,12},{10,1... | collective-permute-start | bytes 589832 | tf_op jit(solution)/shard_map/ppermute | solution.py:43
  21.6 20.8 %collective-permute-start.7 = (bf16[1536,256]{1,0:T(8,128)(2,1)S(1)}, bf16[1536,256]{1,0:T(8,128)(2,1)}, u32[]{:S(2)}, u32[]{:S(2)}) collective-permute-start(bf16[1536,256]{1,0:T(8,128)(2,1)S(1)} %pad_maximum_fusion.6.own), channel_id=1, source_target_pairs={{0,8},{1,9},{2,10},{3,11},{4,12},{5,13},{6,14},{7,15},{8,16},{9,17... | collective-permute-start | bytes 2359304 | tf_op jit(solution)/shard_map/ppermute | solution.py:43
  24.8 20.5 %collective-permute-start.8 = (bf16[1536,256]{1,0:T(8,128)(2,1)S(1)}, bf16[1536,256]{1,0:T(8,128)(2,1)}, u32[]{:S(2)}, u32[]{:S(2)}) collective-permute-start(bf16[1536,256]{1,0:T(8,128)(2,1)S(1)} %pad_maximum_fusion.6.own), channel_id=1, source_target_pairs={{8,0},{9,1},{10,2},{11,3},{12,4},{13,5},{14,6},{15,7},{16,8},{17,9... | collective-permute-start | bytes 2359304 | tf_op jit(solution)/shard_map/ppermute | solution.py:43
  29.1 22.0 %collective-permute-start.4 = (bf16[72,4096]{1,0:T(8,128)(2,1)}, bf16[72,4096]{1,0:T(8,128)(2,1)}, u32[]{:S(2)}, u32[]{:S(2)}) collective-permute-start(bf16[72,4096]{1,0:T(8,128)(2,1)} %get-tuple-element.125), channel_id=1, source_target_pairs={{0,4},{1,5},{2,6},{3,7},{4,0},{5,1},{6,2},{7,3},{8,12},{9,13},{10,... | collective-permute-start | bytes 1769480 | tf_op jit(solution)/shard_map/ppermute | solution.py:43
  30.2 22.8 %collective-permute-start.5 = (bf16[72,4096]{1,0:T(8,128)(2,1)}, bf16[72,4096]{1,0:T(8,128)(2,1)S(1)}, u32[]{:S(2)}, u32[]{:S(2)}) collective-permute-start(bf16[72,4096]{1,0:T(8,128)(2,1)} %get-tuple-element.124), channel_id=1, source_target_pairs={{0,2},{1,3},{2,0},{3,1},{4,6},{5,7},{6,4},{7,5},{8,10},{9,11},{10,... | collective-permute-start | bytes 1769480 | tf_op jit(solution)/shard_map/ppermute | solution.py:43
  31.5 25.5 %collective-permute-start.6 = (bf16[72,4096]{1,0:T(8,128)(2,1)}, bf16[72,4096]{1,0:T(8,128)(2,1)S(1)}, u32[]{:S(2)}, u32[]{:S(2)}) collective-permute-start(bf16[72,4096]{1,0:T(8,128)(2,1)} %get-tuple-element.123), channel_id=1, source_target_pairs={{0,6},{1,7},{2,4},{3,5},{4,2},{5,3},{6,0},{7,1},{8,14},{9,15},{10,... | collective-permute-start | bytes 1769480 | tf_op jit(solution)/shard_map/ppermute | solution.py:43
  45.3 35.6 %collective-permute-start.10 = (bf16[1536,256]{1,0:T(8,128)(2,1)}, bf16[1536,256]{1,0:T(8,128)(2,1)S(1)}, u32[]{:S(2)}, u32[]{:S(2)}) collective-permute-start(bf16[1536,256]{1,0:T(8,128)(2,1)} %collective-permute-done.7.up), channel_id=1, source_target_pairs={{8,16},{9,17},{10,18},{11,19},{12,20},{13,21},{14,22},{15,23},{16,... | collective-permute-start | bytes 2359304 | tf_op jit(solution)/shard_map/ppermute | solution.py:43
  49.8 31.1 %collective-permute-start.9 = (bf16[1536,256]{1,0:T(8,128)(2,1)S(1)}, bf16[1536,256]{1,0:T(8,128)(2,1)S(1)}, u32[]{:S(2)}, u32[]{:S(2)}) collective-permute-start(bf16[1536,256]{1,0:T(8,128)(2,1)S(1)} %broadcast_select_fusion), channel_id=1, source_target_pairs={{8,24},{9,25},{10,26},{11,27},{12,28},{13,29},{14,30},{15,31},{16,... | collective-permute-start | bytes 2359304 | tf_op jit(solution)/shard_map/ppermute | solution.py:43
  51.1 34.2 %collective-permute-start.11 = (bf16[1536,256]{1,0:T(8,128)(2,1)}, bf16[1536,256]{1,0:T(8,128)(2,1)S(1)}, u32[]{:S(2)}, u32[]{:S(2)}) collective-permute-start(bf16[1536,256]{1,0:T(8,128)(2,1)} %collective-permute-done.8.down), channel_id=1, source_target_pairs={{8,0},{9,1},{10,2},{11,3},{12,4},{13,5},{14,6},{15,7},{16,8},{17,9... | collective-permute-start | bytes 2359304 | tf_op jit(solution)/shard_map/ppermute | solution.py:43
  86.8 22.7 %collective-permute-start.14 = (bf16[768,256]{1,0:T(8,128)(2,1)S(1)}, bf16[768,256]{1,0:T(8,128)(2,1)S(1)}, u32[]{:S(2)}, u32[]{:S(2)}) collective-permute-start(bf16[768,256]{1,0:T(8,128)(2,1)S(1)} %pad_maximum_fusion.7.own), channel_id=1, source_target_pairs={{8,0},{9,1},{10,2},{11,3},{12,4},{13,5},{14,6},{15,7},{16,8},{17,9... | collective-permute-start | bytes 1179656 | tf_op jit(solution)/shard_map/ppermute | solution.py:43
  89.8 24.5 %collective-permute-start.12 = (bf16[768,256]{1,0:T(8,128)(2,1)S(1)}, bf16[768,256]{1,0:T(8,128)(2,1)}, u32[]{:S(2)}, u32[]{:S(2)}) collective-permute-start(bf16[768,256]{1,0:T(8,128)(2,1)S(1)} %pad_maximum_fusion.7.own), channel_id=1, source_target_pairs={{0,8},{1,9},{2,10},{3,11},{4,12},{5,13},{6,14},{7,15},{8,16},{9,17... | collective-permute-start | bytes 1179656 | tf_op jit(solution)/shard_map/ppermute | solution.py:43
  108.2 20.7 %collective-permute-start.18 = (bf16[1536,256]{1,0:T(8,128)(2,1)}, bf16[1536,256]{1,0:T(8,128)(2,1)}, u32[]{:S(2)}, u32[]{:S(2)}) collective-permute-start(bf16[1536,256]{1,0:T(8,128)(2,1)} %get-tuple-element.74), channel_id=1, source_target_pairs={{0,8},{1,9},{2,10},{3,11},{4,12},{5,13},{6,14},{7,15},{24,16},{25,... | collective-permute-start | bytes 2359304 | tf_op jit(solution)/shard_map/ppermute | solution.py:43
  109.5 12.4 %collective-permute-start.16 = (bf16[768,256]{1,0:T(8,128)(2,1)S(1)}, bf16[768,256]{1,0:T(8,128)(2,1)S(1)}, u32[]{:S(2)}, u32[]{:S(2)}) collective-permute-start(bf16[768,256]{1,0:T(8,128)(2,1)S(1)} %collective-permute-done.14.down), channel_id=1, source_target_pairs={{8,0},{9,1},{10,2},{11,3},{12,4},{13,5},{14,6},{15,7},{16,8},{17,9... | collective-permute-start | bytes 1179656 | tf_op jit(solution)/shard_map/ppermute | solution.py:43
  114.4 9.2 %collective-permute-start.15 = (bf16[768,256]{1,0:T(8,128)(2,1)}, bf16[768,256]{1,0:T(8,128)(2,1)S(1)}, u32[]{:S(2)}, u32[]{:S(2)}) collective-permute-start(bf16[768,256]{1,0:T(8,128)(2,1)} %collective-permute-done.12.up), channel_id=1, source_target_pairs={{8,16},{9,17},{10,18},{11,19},{12,20},{13,21},{14,22},{15,23},{16,... | collective-permute-start | bytes 1179656 | tf_op jit(solution)/shard_map/ppermute | solution.py:43
  123.6 12.3 %collective-permute-start.17 = (bf16[768,256]{1,0:T(8,128)(2,1)S(1)}, bf16[768,256]{1,0:T(8,128)(2,1)S(1)}, u32[]{:S(2)}, u32[]{:S(2)}) collective-permute-start(bf16[768,256]{1,0:T(8,128)(2,1)S(1)} %broadcast_select_fusion.1), channel_id=1, source_target_pairs={{8,0},{9,1},{10,2},{11,3},{12,4},{13,5},{14,6},{15,7},{16,24},{17,... | collective-permute-start | bytes 1179656 | tf_op jit(solution)/shard_map/ppermute | solution.py:43
  130.3 22.0 %collective-permute-start.20 = (bf16[1536,256]{1,0:T(8,128)(2,1)S(1)}, bf16[1536,256]{1,0:T(8,128)(2,1)S(1)}, u32[]{:S(2)}, u32[]{:S(2)}) collective-permute-start(bf16[1536,256]{1,0:T(8,128)(2,1)S(1)} %add_convert_fusion.4), channel_id=1, source_target_pairs={{16,8},{17,9},{18,10},{19,11},{20,12},{21,13},{22,14},{23,15},{24,... | collective-permute-start | bytes 2359304 | tf_op jit(solution)/shard_map/ppermute | solution.py:43
  131.9 20.4 %collective-permute-start.19 = (bf16[1536,256]{1,0:T(8,128)(2,1)S(1)}, bf16[1536,256]{1,0:T(8,128)(2,1)S(1)}, u32[]{:S(2)}, u32[]{:S(2)}) collective-permute-start(bf16[1536,256]{1,0:T(8,128)(2,1)S(1)} %add_convert_fusion.4), channel_id=1, source_target_pairs={{0,8},{1,9},{2,10},{3,11},{4,12},{5,13},{6,14},{7,15},{8,16},{9,17... | collective-permute-start | bytes 2359304 | tf_op jit(solution)/shard_map/ppermute | solution.py:43
  157.0 21.3 %collective-permute-start.25 = (bf16[1536,256]{1,0:T(8,128)(2,1)}, bf16[1536,256]{1,0:T(8,128)(2,1)S(1)}, u32[]{:S(2)}, u32[]{:S(2)}) collective-permute-start(bf16[1536,256]{1,0:T(8,128)(2,1)} %add_convert_fusion.3), channel_id=1, source_target_pairs={{0,8},{1,9},{2,10},{3,11},{4,12},{5,13},{6,14},{7,15},{8,16},{9,17... | collective-permute-start | bytes 2359304 | tf_op jit(solution)/shard_map/ppermute | solution.py:43
  159.1 20.7 %collective-permute-start.26 = (bf16[1536,256]{1,0:T(8,128)(2,1)S(1)}, bf16[1536,256]{1,0:T(8,128)(2,1)S(1)}, u32[]{:S(2)}, u32[]{:S(2)}) collective-permute-start(bf16[1536,256]{1,0:T(8,128)(2,1)S(1)} %add_convert_fusion.2), channel_id=1, source_target_pairs={{8,0},{9,1},{10,2},{11,3},{12,4},{13,5},{14,6},{15,7},{16,8},{17,9... | collective-permute-start | bytes 2359304 | tf_op jit(solution)/shard_map/ppermute | solution.py:43
  162.4 31.3 %collective-permute-start.21 = (bf16[768,256]{1,0:T(8,128)(2,1)S(1)}, bf16[768,256]{1,0:T(8,128)(2,1)S(1)}, u32[]{:S(2)}, u32[]{:S(2)}) collective-permute-start(bf16[768,256]{1,0:T(8,128)(2,1)S(1)} %copy-done.23), channel_id=1, source_target_pairs={{0,8},{1,9},{2,10},{3,11},{4,12},{5,13},{6,14},{7,15},{24,16},{25,... | collective-permute-start | bytes 1179656 | tf_op jit(solution)/shard_map/ppermute | solution.py:43
  167.1 14.4 %collective-permute-start.24 = (bf16[2,72,2048]{2,1,0:T(8,128)(2,1)S(1)}, bf16[2,72,2048]{2,1,0:T(8,128)(2,1)S(1)}, u32[]{:S(2)}, u32[]{:S(2)}) collective-permute-start(bf16[2,72,2048]{2,1,0:T(8,128)(2,1)S(1)} %get-tuple-element.119), channel_id=1, source_target_pairs={{0,2},{1,3},{2,0},{3,1},{4,6},{5,7},{6,4},{7,5},{8,10},{9,11},{10,... | collective-permute-start | bytes 1769480 | tf_op jit(solution)/shard_map/ppermute | solution.py:43
  179.8 13.7 %collective-permute-start.23 = (bf16[2,72,2048]{2,1,0:T(8,128)(2,1)S(1)}, bf16[2,72,2048]{2,1,0:T(8,128)(2,1)S(1)}, u32[]{:S(2)}, u32[]{:S(2)}) collective-permute-start(bf16[2,72,2048]{2,1,0:T(8,128)(2,1)S(1)} %get-tuple-element.121), channel_id=1, source_target_pairs={{0,4},{1,5},{2,6},{3,7},{4,0},{5,1},{6,2},{7,3},{8,12},{9,13},{10,... | collective-permute-start | bytes 1769480 | tf_op jit(solution)/shard_map/ppermute | solution.py:43
  193.8 11.9 %collective-permute-start.30 = (bf16[768,256]{1,0:T(8,128)(2,1)S(1)}, bf16[768,256]{1,0:T(8,128)(2,1)S(1)}, u32[]{:S(2)}, u32[]{:S(2)}) collective-permute-start(bf16[768,256]{1,0:T(8,128)(2,1)S(1)} %add_convert_fusion.8), channel_id=1, source_target_pairs={{16,8},{17,9},{18,10},{19,11},{20,12},{21,13},{22,14},{23,15},{24,... | collective-permute-start | bytes 1179656 | tf_op jit(solution)/shard_map/ppermute | solution.py:43
  195.1 10.5 %collective-permute-start.29 = (bf16[768,256]{1,0:T(8,128)(2,1)S(1)}, bf16[768,256]{1,0:T(8,128)(2,1)S(1)}, u32[]{:S(2)}, u32[]{:S(2)}) collective-permute-start(bf16[768,256]{1,0:T(8,128)(2,1)S(1)} %add_convert_fusion.8), channel_id=1, source_target_pairs={{0,8},{1,9},{2,10},{3,11},{4,12},{5,13},{6,14},{7,15},{8,16},{9,17... | collective-permute-start | bytes 1179656 | tf_op jit(solution)/shard_map/ppermute | solution.py:43
  199.4 18.7 %collective-permute-start.28 = (bf16[2,72,2048]{2,1,0:T(8,128)(2,1)S(1)}, bf16[2,72,2048]{2,1,0:T(8,128)(2,1)S(1)}, u32[]{:S(2)}, u32[]{:S(2)}) collective-permute-start(bf16[2,72,2048]{2,1,0:T(8,128)(2,1)S(1)} %get-tuple-element.127), channel_id=1, source_target_pairs={{0,4},{1,5},{2,6},{3,7},{4,0},{5,1},{6,2},{7,3},{8,12},{9,13},{10,... | collective-permute-start | bytes 1769480 | tf_op jit(solution)/shard_map/ppermute | solution.py:43
  200.7 18.0 %collective-permute-start.27 = (bf16[2,72,2048]{2,1,0:T(8,128)(2,1)S(1)}, bf16[2,72,2048]{2,1,0:T(8,128)(2,1)S(1)}, u32[]{:S(2)}, u32[]{:S(2)}) collective-permute-start(bf16[2,72,2048]{2,1,0:T(8,128)(2,1)S(1)} %slice_bitcast_fusion.6), channel_id=1, source_target_pairs={{0,2},{1,3},{2,0},{3,1},{4,6},{5,7},{6,4},{7,5},{8,10},{9,11},{10,... | collective-permute-start | bytes 1769480 | tf_op jit(solution)/shard_map/ppermute | solution.py:43
  205.7 22.0 %collective-permute-start.33 = (bf16[768,256]{1,0:T(8,128)(2,1)S(1)}, bf16[768,256]{1,0:T(8,128)(2,1)S(1)}, u32[]{:S(2)}, u32[]{:S(2)}) collective-permute-start(bf16[768,256]{1,0:T(8,128)(2,1)S(1)} %add_convert_fusion.7), channel_id=1, source_target_pairs={{0,8},{1,9},{2,10},{3,11},{4,12},{5,13},{6,14},{7,15},{8,16},{9,17... | collective-permute-start | bytes 1179656 | tf_op jit(solution)/shard_map/ppermute | solution.py:43
  209.5 18.2 %collective-permute-start.34 = (bf16[768,256]{1,0:T(8,128)(2,1)S(1)}, bf16[768,256]{1,0:T(8,128)(2,1)S(1)}, u32[]{:S(2)}, u32[]{:S(2)}) collective-permute-start(bf16[768,256]{1,0:T(8,128)(2,1)S(1)} %add_convert_fusion.6), channel_id=1, source_target_pairs={{8,0},{9,1},{10,2},{11,3},{12,4},{13,5},{14,6},{15,7},{16,8},{17,9... | collective-permute-start | bytes 1179656 | tf_op jit(solution)/shard_map/ppermute | solution.py:43
  211.5 15.0 %collective-permute-start.31 = (bf16[768,256]{1,0:T(8,128)(2,1)S(1)}, bf16[768,256]{1,0:T(8,128)(2,1)S(1)}, u32[]{:S(2)}, u32[]{:S(2)}) collective-permute-start(bf16[768,256]{1,0:T(8,128)(2,1)S(1)} %get-tuple-element.129), channel_id=1, source_target_pairs={{0,0},{1,4},{2,2},{3,6},{4,1},{5,5},{6,3},{7,7},{8,8},{9,12},{10,1... | collective-permute-start | bytes 1179656 | tf_op jit(solution)/shard_map/ppermute | solution.py:43
  218.1 9.6 %collective-permute-start.32 = (bf16[768,256]{1,0:T(8,128)(2,1)S(1)}, bf16[768,256]{1,0:T(8,128)(2,1)S(1)}, u32[]{:S(2)}, u32[]{:S(2)}) collective-permute-start(bf16[768,256]{1,0:T(8,128)(2,1)S(1)} %get-tuple-element.128), channel_id=1, source_target_pairs={{0,4},{1,0},{2,6},{3,2},{4,5},{5,1},{6,7},{7,3},{8,12},{9,8},{10,1... | collective-permute-start | bytes 1179656 | tf_op jit(solution)/shard_map/ppermute | solution.py:43
  (46 other events, 335.7 us)

commit v12 on v11

--- a/solution.py
+++ b/solution.py
@@ -76,7 +76,7 @@
 
 
 LANES = 256
-VMEM_BYTES = 48 * 2**20
+MIB = 2**20
 
 
 def shuffle_matrix(x, dps, hidden_width, pieces):
@@ -292,7 +292,7 @@
         out_shape=[jax.ShapeDtypeStruct((size, LANES), BF) for size in sizes for _ in range(2)],
         in_specs=[IN_SMEM] + in_vmem(4),
         out_specs=in_vmem(2 * len(pieces)),
-        compiler_params=pltpu.CompilerParams(vmem_limit_bytes=VMEM_BYTES // 2),
+        compiler_params=pltpu.CompilerParams(vmem_limit_bytes=58 * MIB),
     )(x, gate, up, down, shuffle)
 
 
@@ -302,7 +302,7 @@
         out_shape=[jax.ShapeDtypeStruct(shape, F32) for shape in (gate_shape, gate_shape, down_shape)],
         in_specs=[IN_SMEM] + in_vmem(len(packed) + 1),
         out_specs=in_vmem(3),
-        compiler_params=pltpu.CompilerParams(vmem_limit_bytes=VMEM_BYTES // 2),
+        compiler_params=pltpu.CompilerParams(vmem_limit_bytes=24 * MIB),
     )(x, *packed, shuffle)
 
 
@@ -333,7 +333,7 @@
             pltpu.SemaphoreType.DMA((places + 4,)),
             pltpu.SemaphoreType.DMA((9,)),
         ],
-        compiler_params=pltpu.CompilerParams(vmem_limit_bytes=VMEM_BYTES),
+        compiler_params=pltpu.CompilerParams(vmem_limit_bytes=24 * MIB),
         cost_estimate=pl.CostEstimate(
             flops=12 * rows * width * units, bytes_accessed=4 * 2**20, transcendentals=rows * units
         ),
@@ -359,7 +359,7 @@
         out_shape=[jax.ShapeDtypeStruct((slots, 2 * width), BF)] * 2,
         in_specs=in_specs,
         out_specs=[pl.BlockSpec((slots, tile), lambda n: (0, n))] * 2,
-        compiler_params=pltpu.CompilerParams(vmem_limit_bytes=VMEM_BYTES // 2),
+        compiler_params=pltpu.CompilerParams(vmem_limit_bytes=24 * MIB),
         cost_estimate=pl.CostEstimate(
             flops=12 * slots * width * units, bytes_accessed=2 * 2**20, transcendentals=0
         ),
@@ -504,7 +504,7 @@
 
         returned, back_rows = along_x(sums[..., :width]), along_q(sums[..., width:])
         grad = added(terms[0], tie(sum_up, sums), tie(sum_down, sums))
-        begun2, returned, back_rows, grad = together((begun2, returned, back_rows, grad))
+        begun2, grad = together((begun2, grad))
         middle2 = added(terms2[2], begun2)
         sum_up2, sum_down2 = g.hop(middle2, inward_up), g.hop(middle2, inward_down)
         returned, back_rows = along_q(returned), along_x(back_rows)

time: 241 us -> 249 us (1.033)
  starting transfers between devices: 78.7 us -> 87.9 us
  local copies, waits for them, and re-layouts: 15.4 us -> 12.8 us
    ppermute x37, starting transfers between devices: 78.7 us -> 87.9 us  [send(): return lax.ppermute(value, BOTH, pairs)]
    pallas_call x1, Pallas kernels: 0.78 us -> 3.37 us  [pack(): pl.pallas_call(functools.partial(pack_kernel, pieces), out_shape=[jax.Sha...]
    unnamed x81 -> x77, local copies, waits for them, and re-layouts: 13.4 us -> 11.4 us
  transfers between devices with their start and end apart: 37 -> 37, of which waited for: 19 -> 20; matrix products, arithmetic and copies ran while one was open for 8% -> 7% of each run, Pallas kernels for 10% -> 10%
where the time goes in v12:
time: 249 us; the launch traced here: 248 us
  waiting for transfers between devices  96.5 us (39%)
  starting transfers between devices  87.9 us (35%)
  Pallas kernels  29 us (12%)
  other arithmetic  16.1 us (6%)
  local copies, waits for them, and re-layouts  12.8 us (5%)
  matrix products  3.81 us (2%)
    ppermute x37, waiting for transfers between devices, send(): return lax.ppermute(value, BOTH, pairs)  96.5 us
    ppermute x37, starting transfers between devices, send(): return lax.ppermute(value, BOTH, pairs)  87.9 us
    pallas_call x2, Pallas kernels, expert(): pl.pallas_call(expert_kernel, out_shape=for_rows + [jax.ShapeDtypeStruct(...  17.4 us
    unnamed x77, local copies, waits for them, and re-layouts  11.4 us
    convert_element_type x9, other arithmetic, added(): return sum((t.astype(F32) for t in terms)).astype(BF)  7.03 us
    pallas_call x1, Pallas kernels, token_rows(): pl.pallas_call(functools.partial(rows_kernel, len(chunks)), grid=(2 * til...  6.19 us
  transfers between devices with their start and end apart: 37, of which 20 were waited for; matrix products, arithmetic and copies ran while one was open for 7% of the time, Pallas kernels for 10%

profile of v12, /device:TPU:9, one launch (start us, length us, event | category | flops | bytes accessed | tf_op | source)
XLA Modules:
  0.0 247.7 jit_solution(3415680095397368579)
XLA Ops:
  2.2 3.4 %shard_map.118 = (bf16[768,256]{1,0:T(8,128)(2,1)}, bf16[768,256]{1,0:T(8,128)(2,1)}, bf16[384,256]{1,0:T(8,128)(2,1)}, bf16[384,256]{1,0:T(8,128)(2,1)}) custom-call(s32[1]{0:T(128)} %bitcast.1.x_ref, bf16[256,768]{1,0:T(8,128)(2,1)} %bitcast.53, bf16[256,768]{1,0:T(8,128)(2,1)} %bitcast.54, bf16[96,2048]{1,0:T(8,128)(2,1)} %bitcast.55, ...), custom_call_target="tpu_custom_call" | custom-call | tf_op jit(solution)/shard_map/pallas_call | solution.py:290
  5.6 3.7 %collective-permute-start = (bf16[768,256]{1,0:T(8,128)(2,1)}, bf16[768,256]{1,0:T(8,128)(2,1)S(1)}, u32[]{:S(2)}, u32[]{:S(2)}) collective-permute-start(bf16[768,256]{1,0:T(8,128)(2,1)} %get-tuple-element.59), channel_id=1, source_target_pairs={{0,0},{1,4},{2,2},{3,6},{4,1},{5,5},{6,3},{7,7},{8,8},{9,12},{10,1... | collective-permute-start | bytes 1179656 | tf_op jit(solution)/shard_map/ppermute | solution.py:43
  10.8 4.1 %collective-permute-done = bf16[768,256]{1,0:T(8,128)(2,1)S(1)} collective-permute-done((bf16[768,256]{1,0:T(8,128)(2,1)}, bf16[768,256]{1,0:T(8,128)(2,1)S(1)}, u32[]{:S(2)}, u32[]{:S(2)}) %collective-permute-start) | collective-permute-done | bytes 393248 | tf_op jit(solution)/shard_map/ppermute | solution.py:43
  14.9 3.6 %collective-permute-done.1 = bf16[768,256]{1,0:T(8,128)(2,1)S(1)} collective-permute-done((bf16[768,256]{1,0:T(8,128)(2,1)}, bf16[768,256]{1,0:T(8,128)(2,1)S(1)}, u32[]{:S(2)}, u32[]{:S(2)}) %collective-permute-start.1) | collective-permute-done | bytes 393248 | tf_op jit(solution)/shard_map/ppermute | solution.py:43
  21.4 3.2 %collective-permute-start.2 = (bf16[1536,256]{1,0:T(8,128)(2,1)S(1)}, bf16[1536,256]{1,0:T(8,128)(2,1)}, u32[]{:S(2)}, u32[]{:S(2)}) collective-permute-start(bf16[1536,256]{1,0:T(8,128)(2,1)S(1)} %pad_maximum_fusion.4.own), channel_id=1, source_target_pairs={{0,8},{1,9},{2,10},{3,11},{4,12},{5,13},{6,14},{7,15},{8,16},{9,17... | collective-permute-start | bytes 2359304 | tf_op jit(solution)/shard_map/ppermute | solution.py:43
  24.6 3.0 %collective-permute-start.3 = (bf16[1536,256]{1,0:T(8,128)(2,1)S(1)}, bf16[1536,256]{1,0:T(8,128)(2,1)}, u32[]{:S(2)}, u32[]{:S(2)}) collective-permute-start(bf16[1536,256]{1,0:T(8,128)(2,1)S(1)} %pad_maximum_fusion.4.own), channel_id=1, source_target_pairs={{8,0},{9,1},{10,2},{11,3},{12,4},{13,5},{14,6},{15,7},{16,8},{17,9... | collective-permute-start | bytes 2359304 | tf_op jit(solution)/shard_map/ppermute | solution.py:43
  31.6 10.4 %collective-permute-done.2.up = bf16[1536,256]{1,0:T(8,128)(2,1)} collective-permute-done((bf16[1536,256]{1,0:T(8,128)(2,1)S(1)}, bf16[1536,256]{1,0:T(8,128)(2,1)}, u32[]{:S(2)}, u32[]{:S(2)}) %collective-permute-start.2) | collective-permute-done | bytes 786464 | tf_op jit(solution)/shard_map/ppermute | solution.py:43
  42.0 2.9 %collective-permute-done.3.down = bf16[1536,256]{1,0:T(8,128)(2,1)} collective-permute-done((bf16[1536,256]{1,0:T(8,128)(2,1)S(1)}, bf16[1536,256]{1,0:T(8,128)(2,1)}, u32[]{:S(2)}, u32[]{:S(2)}) %collective-permute-start.3) | collective-permute-done | bytes 786464 | tf_op jit(solution)/shard_map/ppermute | solution.py:43
  44.9 3.2 %collective-permute-start.4 = (bf16[1536,256]{1,0:T(8,128)(2,1)}, bf16[1536,256]{1,0:T(8,128)(2,1)S(1)}, u32[]{:S(2)}, u32[]{:S(2)}) collective-permute-start(bf16[1536,256]{1,0:T(8,128)(2,1)} %collective-permute-done.2.up), channel_id=1, source_target_pairs={{8,16},{9,17},{10,18},{11,19},{12,20},{13,21},{14,22},{15,23},{16,... | collective-permute-start | bytes 2359304 | tf_op jit(solution)/shard_map/ppermute | solution.py:43
  50.8 4.8 %collective-permute-done.10 = bf16[72,4096]{1,0:T(8,128)(2,1)S(1)} collective-permute-done((bf16[72,4096]{1,0:T(8,128)(2,1)}, bf16[72,4096]{1,0:T(8,128)(2,1)S(1)}, u32[]{:S(2)}, u32[]{:S(2)}) %collective-permute-start.10) | collective-permute-done | bytes 589856 | tf_op jit(solution)/shard_map/ppermute | solution.py:43
  60.0 20.3 %collective-permute-done.6.last = bf16[1536,256]{1,0:T(8,128)(2,1)S(1)} collective-permute-done((bf16[1536,256]{1,0:T(8,128)(2,1)S(1)}, bf16[1536,256]{1,0:T(8,128)(2,1)S(1)}, u32[]{:S(2)}, u32[]{:S(2)}) %collective-permute-start.6) | collective-permute-done | bytes 786464 | tf_op jit(solution)/shard_map/ppermute | solution.py:43
  80.4 4.6 %collective-permute-done.5.down_2 = bf16[1536,256]{1,0:T(8,128)(2,1)S(1)} collective-permute-done((bf16[1536,256]{1,0:T(8,128)(2,1)}, bf16[1536,256]{1,0:T(8,128)(2,1)S(1)}, u32[]{:S(2)}, u32[]{:S(2)}) %collective-permute-start.5) | collective-permute-done | bytes 786464 | tf_op jit(solution)/shard_map/ppermute | solution.py:43
  86.4 3.0 %collective-permute-start.14 = (bf16[768,256]{1,0:T(8,128)(2,1)S(1)}, bf16[768,256]{1,0:T(8,128)(2,1)}, u32[]{:S(2)}, u32[]{:S(2)}) collective-permute-start(bf16[768,256]{1,0:T(8,128)(2,1)S(1)} %pad_maximum_fusion.7.own), channel_id=1, source_target_pairs={{8,0},{9,1},{10,2},{11,3},{12,4},{13,5},{14,6},{15,7},{16,8},{17,9... | collective-permute-start | bytes 1179656 | tf_op jit(solution)/shard_map/ppermute | solution.py:43
  91.7 9.7 %shard_map.119 = (bf16[2048,512]{1,0:T(8,128)(2,1)S(1)}, bf16[256,2048]{1,0:T(8,128)(2,1)S(1)}, bf16[576,256]{1,0:T(8,128)(2,1)S(1)}, bf16[576,512]{1,0:T(8,128)...) custom-call(s32[1]{0:T(128)} %bitcast.z_ref, ...), custom_call_target="tpu_custom_call" | custom-call | flops 3623878656 | bytes 4194304 | tf_op jit(solution)/shard_map/pallas_call | solution.py:316
  110.1 4.9 %collective-permute-start.16 = (bf16[768,256]{1,0:T(8,128)(2,1)}, bf16[768,256]{1,0:T(8,128)(2,1)}, u32[]{:S(2)}, u32[]{:S(2)}) collective-permute-start(bf16[768,256]{1,0:T(8,128)(2,1)} %collective-permute-done.14.down), channel_id=1, source_target_pairs={{8,0},{9,1},{10,2},{11,3},{12,4},{13,5},{14,6},{15,7},{16,8},{17,9... | collective-permute-start | bytes 1179656 | tf_op jit(solution)/shard_map/ppermute | solution.py:43
  117.1 5.8 %collective-permute-done.16.down_2 = bf16[768,256]{1,0:T(8,128)(2,1)} collective-permute-done((bf16[768,256]{1,0:T(8,128)(2,1)}, bf16[768,256]{1,0:T(8,128)(2,1)}, u32[]{:S(2)}, u32[]{:S(2)}) %collective-permute-start.16) | collective-permute-done | bytes 393248 | tf_op jit(solution)/shard_map/ppermute | solution.py:43
  125.2 2.8 %collective-permute-start.17 = (bf16[768,256]{1,0:T(8,128)(2,1)S(1)}, bf16[768,256]{1,0:T(8,128)(2,1)S(1)}, u32[]{:S(2)}, u32[]{:S(2)}) collective-permute-start(bf16[768,256]{1,0:T(8,128)(2,1)S(1)} %broadcast_select_fusion.1), channel_id=1, source_target_pairs={{8,0},{9,1},{10,2},{11,3},{12,4},{13,5},{14,6},{15,7},{16,24},{17,... | collective-permute-start | bytes 1179656 | tf_op jit(solution)/shard_map/ppermute | solution.py:43
  132.7 4.0 %collective-permute-start.19 = (bf16[1536,256]{1,0:T(8,128)(2,1)S(1)}, bf16[1536,256]{1,0:T(8,128)(2,1)S(1)}, u32[]{:S(2)}, u32[]{:S(2)}) collective-permute-start(bf16[1536,256]{1,0:T(8,128)(2,1)S(1)} %add_convert_fusion.4), channel_id=1, source_target_pairs={{0,8},{1,9},{2,10},{3,11},{4,12},{5,13},{6,14},{7,15},{8,16},{9,17... | collective-permute-start | bytes 2359304 | tf_op jit(solution)/shard_map/ppermute | solution.py:43
  136.7 7.8 %shard_map.120 = (bf16[2048,256]{1,0:T(8,128)(2,1)S(1)}, bf16[128,2048]{1,0:T(8,128)(2,1)S(1)}, bf16[576,128]{1,0:T(8,128)(2,1)S(1)}, bf16[576,256]{1,0:T(8,128)...) custom-call(s32[1]{0:T(128)} %bitcast.z_ref, ...), custom_call_target="tpu_custom_call" | custom-call | flops 1811939328 | bytes 4194304 | tf_op jit(solution)/shard_map/pallas_call | solution.py:316
  148.4 6.2 %shard_map.121 = (bf16[288,4096]{1,0:T(8,128)(2,1)S(1)}, bf16[288,4096]{1,0:T(8,128)(2,1)}) custom-call(bf16[2048,512]{1,0:T(8,128)(2,1)S(1)} %copy-done.24, bf16[256,2048]{1,0:T(8,128)(2,1)S(1)} %copy-done.26, bf16[576,256]{1,0:T(8,128)(2,1)S(1)} %copy-done.30, bf16[576,512]{1,0:T(8,128)(2,1)S(1)} %copy-done.28, ...), custom_call_target="tpu_custom_call" | custom-call | flops 2717908992 | bytes 2097152 | tf_op jit(solution)/shard_map/pallas_call | solution.py:356
  160.8 3.2 %collective-permute-start.28 = (bf16[1536,256]{1,0:T(8,128)(2,1)}, bf16[1536,256]{1,0:T(8,128)(2,1)S(1)}, u32[]{:S(2)}, u32[]{:S(2)}) collective-permute-start(bf16[1536,256]{1,0:T(8,128)(2,1)} %add_convert_fusion.2), channel_id=1, source_target_pairs={{8,0},{9,1},{10,2},{11,3},{12,4},{13,5},{14,6},{15,7},{16,8},{17,9... | collective-permute-start | bytes 2359304 | tf_op jit(solution)/shard_map/ppermute | solution.py:43
  168.1 11.9 %collective-permute-done.27 = bf16[1536,256]{1,0:T(8,128)(2,1)S(1)} collective-permute-done((bf16[1536,256]{1,0:T(8,128)(2,1)}, bf16[1536,256]{1,0:T(8,128)(2,1)S(1)}, u32[]{:S(2)}, u32[]{:S(2)}) %collective-permute-start.27) | collective-permute-done | bytes 786464 | tf_op jit(solution)/shard_map/ppermute | solution.py:43
  180.0 2.8 %collective-permute-done.28 = bf16[1536,256]{1,0:T(8,128)(2,1)S(1)} collective-permute-done((bf16[1536,256]{1,0:T(8,128)(2,1)}, bf16[1536,256]{1,0:T(8,128)(2,1)S(1)}, u32[]{:S(2)}, u32[]{:S(2)}) %collective-permute-start.28) | collective-permute-done | bytes 786464 | tf_op jit(solution)/shard_map/ppermute | solution.py:43
  183.1 5.4 %collective-permute-done.26 = bf16[768,256]{1,0:T(8,128)(2,1)S(1)} collective-permute-done((bf16[768,256]{1,0:T(8,128)(2,1)S(1)}, bf16[768,256]{1,0:T(8,128)(2,1)S(1)}, u32[]{:S(2)}, u32[]{:S(2)}) %collective-permute-start.26) | collective-permute-done | bytes 393248 | tf_op jit(solution)/shard_map/ppermute | solution.py:43
  189.9 6.5 %collective-permute-start.29 = (bf16[768,256]{1,0:T(8,128)(2,1)S(1)}, bf16[768,256]{1,0:T(8,128)(2,1)S(1)}, u32[]{:S(2)}, u32[]{:S(2)}) collective-permute-start(bf16[768,256]{1,0:T(8,128)(2,1)S(1)} %add_convert_fusion.8), channel_id=1, source_target_pairs={{0,8},{1,9},{2,10},{3,11},{4,12},{5,13},{6,14},{7,15},{8,16},{9,17... | collective-permute-start | bytes 1179656 | tf_op jit(solution)/shard_map/ppermute | solution.py:43
  199.7 3.9 %collective-permute-done.29 = bf16[768,256]{1,0:T(8,128)(2,1)S(1)} collective-permute-done((bf16[768,256]{1,0:T(8,128)(2,1)S(1)}, bf16[768,256]{1,0:T(8,128)(2,1)S(1)}, u32[]{:S(2)}, u32[]{:S(2)}) %collective-permute-start.29) | collective-permute-done | bytes 393248 | tf_op jit(solution)/shard_map/ppermute | solution.py:43
  203.7 4.1 %collective-permute-start.33 = (bf16[768,256]{1,0:T(8,128)(2,1)S(1)}, bf16[768,256]{1,0:T(8,128)(2,1)S(1)}, u32[]{:S(2)}, u32[]{:S(2)}) collective-permute-start(bf16[768,256]{1,0:T(8,128)(2,1)S(1)} %add_convert_fusion.7), channel_id=1, source_target_pairs={{0,8},{1,9},{2,10},{3,11},{4,12},{5,13},{6,14},{7,15},{8,16},{9,17... | collective-permute-start | bytes 1179656 | tf_op jit(solution)/shard_map/ppermute | solution.py:43
  215.4 4.4 %collective-permute-start.31 = (bf16[768,256]{1,0:T(8,128)(2,1)S(1)}, bf16[768,256]{1,0:T(8,128)(2,1)S(1)}, u32[]{:S(2)}, u32[]{:S(2)}) collective-permute-start(bf16[768,256]{1,0:T(8,128)(2,1)S(1)} %get-tuple-element.127), channel_id=1, source_target_pairs={{0,0},{1,4},{2,2},{3,6},{4,1},{5,5},{6,3},{7,7},{8,8},{9,12},{10,1... | collective-permute-start | bytes 1179656 | tf_op jit(solution)/shard_map/ppermute | solution.py:43
  219.9 4.3 %collective-permute-done.25 = bf16[2,72,2048]{2,1,0:T(8,128)(2,1)S(1)} collective-permute-done((bf16[2,72,2048]{2,1,0:T(8,128)(2,1)S(1)}, bf16[2,72,2048]{2,1,0:T(8,128)(2,1)S(1)}, u32[]{:S(2)}, u32[]{:S(2)}) %collective-permute-start.25) | collective-permute-done | bytes 589856 | tf_op jit(solution)/shard_map/ppermute | solution.py:43
  224.1 4.2 %collective-permute-start.32 = (bf16[768,256]{1,0:T(8,128)(2,1)S(1)}, bf16[768,256]{1,0:T(8,128)(2,1)S(1)}, u32[]{:S(2)}, u32[]{:S(2)}) collective-permute-start(bf16[768,256]{1,0:T(8,128)(2,1)S(1)} %get-tuple-element.126), channel_id=1, source_target_pairs={{0,4},{1,0},{2,6},{3,2},{4,5},{5,1},{6,7},{7,3},{8,12},{9,8},{10,1... | collective-permute-start | bytes 1179656 | tf_op jit(solution)/shard_map/ppermute | solution.py:43
  234.6 5.7 %collective-permute-start.35 = (bf16[384,256]{1,0:T(8,128)(2,1)S(1)}, bf16[384,256]{1,0:T(8,128)(2,1)S(1)}, u32[]{:S(2)}, u32[]{:S(2)}) collective-permute-start(bf16[384,256]{1,0:T(8,128)(2,1)S(1)} %get-tuple-element.131), channel_id=1, source_target_pairs={{0,0},{1,4},{2,2},{3,6},{4,1},{5,5},{6,3},{7,7},{8,8},{9,12},{10,1... | collective-permute-start | bytes 589832 | tf_op jit(solution)/shard_map/ppermute | solution.py:43
  240.3 4.2 %collective-permute-done.35.refs_2_ = bf16[384,256]{1,0:T(8,128)(2,1)S(1)} collective-permute-done((bf16[384,256]{1,0:T(8,128)(2,1)S(1)}, bf16[384,256]{1,0:T(8,128)(2,1)S(1)}, u32[]{:S(2)}, u32[]{:S(2)}) %collective-permute-start.35) | collective-permute-done | bytes 196640 | tf_op jit(solution)/shard_map/ppermute | solution.py:43
  (168 shorter events, 74.4 us)
Async XLA Ops:
  5.6 9.3 %collective-permute-start = (bf16[768,256]{1,0:T(8,128)(2,1)}, bf16[768,256]{1,0:T(8,128)(2,1)S(1)}, u32[]{:S(2)}, u32[]{:S(2)}) collective-permute-start(bf16[768,256]{1,0:T(8,128)(2,1)} %get-tuple-element.59), channel_id=1, source_target_pairs={{0,0},{1,4},{2,2},{3,6},{4,1},{5,5},{6,3},{7,7},{8,8},{9,12},{10,1... | collective-permute-start | bytes 1179656 | tf_op jit(solution)/shard_map/ppermute | solution.py:43
  9.3 9.2 %collective-permute-start.1 = (bf16[768,256]{1,0:T(8,128)(2,1)}, bf16[768,256]{1,0:T(8,128)(2,1)S(1)}, u32[]{:S(2)}, u32[]{:S(2)}) collective-permute-start(bf16[768,256]{1,0:T(8,128)(2,1)} %get-tuple-element.60), channel_id=1, source_target_pairs={{0,1},{1,5},{2,3},{3,7},{4,0},{5,4},{6,2},{7,6},{8,9},{9,13},{10,1... | collective-permute-start | bytes 1179656 | tf_op jit(solution)/shard_map/ppermute | solution.py:43
  21.4 20.6 %collective-permute-start.2 = (bf16[1536,256]{1,0:T(8,128)(2,1)S(1)}, bf16[1536,256]{1,0:T(8,128)(2,1)}, u32[]{:S(2)}, u32[]{:S(2)}) collective-permute-start(bf16[1536,256]{1,0:T(8,128)(2,1)S(1)} %pad_maximum_fusion.4.own), channel_id=1, source_target_pairs={{0,8},{1,9},{2,10},{3,11},{4,12},{5,13},{6,14},{7,15},{8,16},{9,17... | collective-permute-start | bytes 2359304 | tf_op jit(solution)/shard_map/ppermute | solution.py:43
  24.6 20.3 %collective-permute-start.3 = (bf16[1536,256]{1,0:T(8,128)(2,1)S(1)}, bf16[1536,256]{1,0:T(8,128)(2,1)}, u32[]{:S(2)}, u32[]{:S(2)}) collective-permute-start(bf16[1536,256]{1,0:T(8,128)(2,1)S(1)} %pad_maximum_fusion.4.own), channel_id=1, source_target_pairs={{8,0},{9,1},{10,2},{11,3},{12,4},{13,5},{14,6},{15,7},{16,8},{17,9... | collective-permute-start | bytes 2359304 | tf_op jit(solution)/shard_map/ppermute | solution.py:43
  29.0 26.6 %collective-permute-start.10 = (bf16[72,4096]{1,0:T(8,128)(2,1)}, bf16[72,4096]{1,0:T(8,128)(2,1)S(1)}, u32[]{:S(2)}, u32[]{:S(2)}) collective-permute-start(bf16[72,4096]{1,0:T(8,128)(2,1)} %get-tuple-element.120), channel_id=1, source_target_pairs={{0,2},{1,3},{2,0},{3,1},{4,6},{5,7},{6,4},{7,5},{8,10},{9,11},{10,... | collective-permute-start | bytes 1769480 | tf_op jit(solution)/shard_map/ppermute | solution.py:43
  30.2 27.3 %collective-permute-start.11 = (bf16[72,4096]{1,0:T(8,128)(2,1)}, bf16[72,4096]{1,0:T(8,128)(2,1)S(1)}, u32[]{:S(2)}, u32[]{:S(2)}) collective-permute-start(bf16[72,4096]{1,0:T(8,128)(2,1)} %get-tuple-element.119), channel_id=1, source_target_pairs={{0,6},{1,7},{2,4},{3,5},{4,2},{5,3},{6,0},{7,1},{8,14},{9,15},{10,... | collective-permute-start | bytes 1769480 | tf_op jit(solution)/shard_map/ppermute | solution.py:43
  31.4 26.1 %collective-permute-start.9 = (bf16[72,4096]{1,0:T(8,128)(2,1)S(1)}, bf16[72,4096]{1,0:T(8,128)(2,1)S(1)}, u32[]{:S(2)}, u32[]{:S(2)}) collective-permute-start(bf16[72,4096]{1,0:T(8,128)(2,1)S(1)} %get-tuple-element.121), channel_id=1, source_target_pairs={{0,4},{1,5},{2,6},{3,7},{4,0},{5,1},{6,2},{7,3},{8,12},{9,13},{10,... | collective-permute-start | bytes 1769480 | tf_op jit(solution)/shard_map/ppermute | solution.py:43
  44.9 35.4 %collective-permute-start.4 = (bf16[1536,256]{1,0:T(8,128)(2,1)}, bf16[1536,256]{1,0:T(8,128)(2,1)S(1)}, u32[]{:S(2)}, u32[]{:S(2)}) collective-permute-start(bf16[1536,256]{1,0:T(8,128)(2,1)} %collective-permute-done.2.up), channel_id=1, source_target_pairs={{8,16},{9,17},{10,18},{11,19},{12,20},{13,21},{14,22},{15,23},{16,... | collective-permute-start | bytes 2359304 | tf_op jit(solution)/shard_map/ppermute | solution.py:43
  49.4 30.9 %collective-permute-start.6 = (bf16[1536,256]{1,0:T(8,128)(2,1)S(1)}, bf16[1536,256]{1,0:T(8,128)(2,1)S(1)}, u32[]{:S(2)}, u32[]{:S(2)}) collective-permute-start(bf16[1536,256]{1,0:T(8,128)(2,1)S(1)} %broadcast_select_fusion), channel_id=1, source_target_pairs={{8,24},{9,25},{10,26},{11,27},{12,28},{13,29},{14,30},{15,31},{16,... | collective-permute-start | bytes 2359304 | tf_op jit(solution)/shard_map/ppermute | solution.py:43
  55.6 29.4 %collective-permute-start.5 = (bf16[1536,256]{1,0:T(8,128)(2,1)}, bf16[1536,256]{1,0:T(8,128)(2,1)S(1)}, u32[]{:S(2)}, u32[]{:S(2)}) collective-permute-start(bf16[1536,256]{1,0:T(8,128)(2,1)} %collective-permute-done.3.down), channel_id=1, source_target_pairs={{8,0},{9,1},{10,2},{11,3},{12,4},{13,5},{14,6},{15,7},{16,8},{17,9... | collective-permute-start | bytes 2359304 | tf_op jit(solution)/shard_map/ppermute | solution.py:43
  86.4 23.7 %collective-permute-start.14 = (bf16[768,256]{1,0:T(8,128)(2,1)S(1)}, bf16[768,256]{1,0:T(8,128)(2,1)}, u32[]{:S(2)}, u32[]{:S(2)}) collective-permute-start(bf16[768,256]{1,0:T(8,128)(2,1)S(1)} %pad_maximum_fusion.7.own), channel_id=1, source_target_pairs={{8,0},{9,1},{10,2},{11,3},{12,4},{13,5},{14,6},{15,7},{16,8},{17,9... | collective-permute-start | bytes 1179656 | tf_op jit(solution)/shard_map/ppermute | solution.py:43
  89.4 25.6 %collective-permute-start.13 = (bf16[768,256]{1,0:T(8,128)(2,1)S(1)}, bf16[768,256]{1,0:T(8,128)(2,1)}, u32[]{:S(2)}, u32[]{:S(2)}) collective-permute-start(bf16[768,256]{1,0:T(8,128)(2,1)S(1)} %pad_maximum_fusion.7.own), channel_id=1, source_target_pairs={{0,8},{1,9},{2,10},{3,11},{4,12},{5,13},{6,14},{7,15},{8,16},{9,17... | collective-permute-start | bytes 1179656 | tf_op jit(solution)/shard_map/ppermute | solution.py:43
  108.8 20.7 %collective-permute-start.18 = (bf16[1536,256]{1,0:T(8,128)(2,1)}, bf16[1536,256]{1,0:T(8,128)(2,1)}, u32[]{:S(2)}, u32[]{:S(2)}) collective-permute-start(bf16[1536,256]{1,0:T(8,128)(2,1)} %get-tuple-element.76), channel_id=1, source_target_pairs={{0,8},{1,9},{2,10},{3,11},{4,12},{5,13},{6,14},{7,15},{24,16},{25,... | collective-permute-start | bytes 2359304 | tf_op jit(solution)/shard_map/ppermute | solution.py:43
  110.1 12.8 %collective-permute-start.16 = (bf16[768,256]{1,0:T(8,128)(2,1)}, bf16[768,256]{1,0:T(8,128)(2,1)}, u32[]{:S(2)}, u32[]{:S(2)}) collective-permute-start(bf16[768,256]{1,0:T(8,128)(2,1)} %collective-permute-done.14.down), channel_id=1, source_target_pairs={{8,0},{9,1},{10,2},{11,3},{12,4},{13,5},{14,6},{15,7},{16,8},{17,9... | collective-permute-start | bytes 1179656 | tf_op jit(solution)/shard_map/ppermute | solution.py:43
  115.0 9.2 %collective-permute-start.15 = (bf16[768,256]{1,0:T(8,128)(2,1)}, bf16[768,256]{1,0:T(8,128)(2,1)}, u32[]{:S(2)}, u32[]{:S(2)}) collective-permute-start(bf16[768,256]{1,0:T(8,128)(2,1)} %collective-permute-done.13.up), channel_id=1, source_target_pairs={{8,16},{9,17},{10,18},{11,19},{12,20},{13,21},{14,22},{15,23},{16,... | collective-permute-start | bytes 1179656 | tf_op jit(solution)/shard_map/ppermute | solution.py:43
  125.2 11.5 %collective-permute-start.17 = (bf16[768,256]{1,0:T(8,128)(2,1)S(1)}, bf16[768,256]{1,0:T(8,128)(2,1)S(1)}, u32[]{:S(2)}, u32[]{:S(2)}) collective-permute-start(bf16[768,256]{1,0:T(8,128)(2,1)S(1)} %broadcast_select_fusion.1), channel_id=1, source_target_pairs={{8,0},{9,1},{10,2},{11,3},{12,4},{13,5},{14,6},{15,7},{16,24},{17,... | collective-permute-start | bytes 1179656 | tf_op jit(solution)/shard_map/ppermute | solution.py:43
  131.2 23.4 %collective-permute-start.20 = (bf16[1536,256]{1,0:T(8,128)(2,1)S(1)}, bf16[1536,256]{1,0:T(8,128)(2,1)S(1)}, u32[]{:S(2)}, u32[]{:S(2)}) collective-permute-start(bf16[1536,256]{1,0:T(8,128)(2,1)S(1)} %add_convert_fusion.4), channel_id=1, source_target_pairs={{16,8},{17,9},{18,10},{19,11},{20,12},{21,13},{22,14},{23,15},{24,... | collective-permute-start | bytes 2359304 | tf_op jit(solution)/shard_map/ppermute | solution.py:43
  132.7 21.8 %collective-permute-start.19 = (bf16[1536,256]{1,0:T(8,128)(2,1)S(1)}, bf16[1536,256]{1,0:T(8,128)(2,1)S(1)}, u32[]{:S(2)}, u32[]{:S(2)}) collective-permute-start(bf16[1536,256]{1,0:T(8,128)(2,1)S(1)} %add_convert_fusion.4), channel_id=1, source_target_pairs={{0,8},{1,9},{2,10},{3,11},{4,12},{5,13},{6,14},{7,15},{8,16},{9,17... | collective-permute-start | bytes 2359304 | tf_op jit(solution)/shard_map/ppermute | solution.py:43
  158.7 21.3 %collective-permute-start.27 = (bf16[1536,256]{1,0:T(8,128)(2,1)}, bf16[1536,256]{1,0:T(8,128)(2,1)S(1)}, u32[]{:S(2)}, u32[]{:S(2)}) collective-permute-start(bf16[1536,256]{1,0:T(8,128)(2,1)} %add_convert_fusion.3), channel_id=1, source_target_pairs={{0,8},{1,9},{2,10},{3,11},{4,12},{5,13},{6,14},{7,15},{8,16},{9,17... | collective-permute-start | bytes 2359304 | tf_op jit(solution)/shard_map/ppermute | solution.py:43
  160.8 22.0 %collective-permute-start.28 = (bf16[1536,256]{1,0:T(8,128)(2,1)}, bf16[1536,256]{1,0:T(8,128)(2,1)S(1)}, u32[]{:S(2)}, u32[]{:S(2)}) collective-permute-start(bf16[1536,256]{1,0:T(8,128)(2,1)} %add_convert_fusion.2), channel_id=1, source_target_pairs={{8,0},{9,1},{10,2},{11,3},{12,4},{13,5},{14,6},{15,7},{16,8},{17,9... | collective-permute-start | bytes 2359304 | tf_op jit(solution)/shard_map/ppermute | solution.py:43
  164.1 24.3 %collective-permute-start.26 = (bf16[768,256]{1,0:T(8,128)(2,1)S(1)}, bf16[768,256]{1,0:T(8,128)(2,1)S(1)}, u32[]{:S(2)}, u32[]{:S(2)}) collective-permute-start(bf16[768,256]{1,0:T(8,128)(2,1)S(1)} %copy-done.22), channel_id=1, source_target_pairs={{0,8},{1,9},{2,10},{3,11},{4,12},{5,13},{6,14},{7,15},{24,16},{25,... | collective-permute-start | bytes 1179656 | tf_op jit(solution)/shard_map/ppermute | solution.py:43
  188.6 15.2 %collective-permute-start.30 = (bf16[768,256]{1,0:T(8,128)(2,1)S(1)}, bf16[768,256]{1,0:T(8,128)(2,1)S(1)}, u32[]{:S(2)}, u32[]{:S(2)}) collective-permute-start(bf16[768,256]{1,0:T(8,128)(2,1)S(1)} %add_convert_fusion.8), channel_id=1, source_target_pairs={{16,8},{17,9},{18,10},{19,11},{20,12},{21,13},{22,14},{23,15},{24,... | collective-permute-start | bytes 1179656 | tf_op jit(solution)/shard_map/ppermute | solution.py:43
  189.9 13.7 %collective-permute-start.29 = (bf16[768,256]{1,0:T(8,128)(2,1)S(1)}, bf16[768,256]{1,0:T(8,128)(2,1)S(1)}, u32[]{:S(2)}, u32[]{:S(2)}) collective-permute-start(bf16[768,256]{1,0:T(8,128)(2,1)S(1)} %add_convert_fusion.8), channel_id=1, source_target_pairs={{0,8},{1,9},{2,10},{3,11},{4,12},{5,13},{6,14},{7,15},{8,16},{9,17... | collective-permute-start | bytes 1179656 | tf_op jit(solution)/shard_map/ppermute | solution.py:43
  196.4 13.5 %collective-permute-start.24 = (bf16[2,72,2048]{2,1,0:T(8,128)(2,1)S(1)}, bf16[2,72,2048]{2,1,0:T(8,128)(2,1)S(1)}, u32[]{:S(2)}, u32[]{:S(2)}) collective-permute-start(bf16[2,72,2048]{2,1,0:T(8,128)(2,1)S(1)} %get-tuple-element.115), channel_id=1, source_target_pairs={{0,2},{1,3},{2,0},{3,1},{4,6},{5,7},{6,4},{7,5},{8,10},{9,11},{10,... | collective-permute-start | bytes 1769480 | tf_op jit(solution)/shard_map/ppermute | solution.py:43
  197.8 16.1 %collective-permute-start.22 = (bf16[2,72,2048]{2,1,0:T(8,128)(2,1)S(1)}, bf16[2,72,2048]{2,1,0:T(8,128)(2,1)S(1)}, u32[]{:S(2)}, u32[]{:S(2)}) collective-permute-start(bf16[2,72,2048]{2,1,0:T(8,128)(2,1)S(1)} %get-tuple-element.117), channel_id=1, source_target_pairs={{0,4},{1,5},{2,6},{3,7},{4,0},{5,1},{6,2},{7,3},{8,12},{9,13},{10,... | collective-permute-start | bytes 1769480 | tf_op jit(solution)/shard_map/ppermute | solution.py:43
  203.7 30.7 %collective-permute-start.33 = (bf16[768,256]{1,0:T(8,128)(2,1)S(1)}, bf16[768,256]{1,0:T(8,128)(2,1)S(1)}, u32[]{:S(2)}, u32[]{:S(2)}) collective-permute-start(bf16[768,256]{1,0:T(8,128)(2,1)S(1)} %add_convert_fusion.7), channel_id=1, source_target_pairs={{0,8},{1,9},{2,10},{3,11},{4,12},{5,13},{6,14},{7,15},{8,16},{9,17... | collective-permute-start | bytes 1179656 | tf_op jit(solution)/shard_map/ppermute | solution.py:43
  210.0 14.1 %collective-permute-start.25 = (bf16[2,72,2048]{2,1,0:T(8,128)(2,1)S(1)}, bf16[2,72,2048]{2,1,0:T(8,128)(2,1)S(1)}, u32[]{:S(2)}, u32[]{:S(2)}) collective-permute-start(bf16[2,72,2048]{2,1,0:T(8,128)(2,1)S(1)} %get-tuple-element.123), channel_id=1, source_target_pairs={{0,4},{1,5},{2,6},{3,7},{4,0},{5,1},{6,2},{7,3},{8,12},{9,13},{10,... | collective-permute-start | bytes 1769480 | tf_op jit(solution)/shard_map/ppermute | solution.py:43
  212.0 22.3 %collective-permute-start.34 = (bf16[768,256]{1,0:T(8,128)(2,1)S(1)}, bf16[768,256]{1,0:T(8,128)(2,1)S(1)}, u32[]{:S(2)}, u32[]{:S(2)}) collective-permute-start(bf16[768,256]{1,0:T(8,128)(2,1)S(1)} %add_convert_fusion.6), channel_id=1, source_target_pairs={{8,0},{9,1},{10,2},{11,3},{12,4},{13,5},{14,6},{15,7},{16,8},{17,9... | collective-permute-start | bytes 1179656 | tf_op jit(solution)/shard_map/ppermute | solution.py:43
  214.1 14.8 %collective-permute-start.23 = (bf16[2,72,2048]{2,1,0:T(8,128)(2,1)S(1)}, bf16[2,72,2048]{2,1,0:T(8,128)(2,1)S(1)}, u32[]{:S(2)}, u32[]{:S(2)}) collective-permute-start(bf16[2,72,2048]{2,1,0:T(8,128)(2,1)S(1)} %get-tuple-element.125), channel_id=1, source_target_pairs={{0,2},{1,3},{2,0},{3,1},{4,6},{5,7},{6,4},{7,5},{8,10},{9,11},{10,... | collective-permute-start | bytes 1769480 | tf_op jit(solution)/shard_map/ppermute | solution.py:43
  215.4 18.3 %collective-permute-start.31 = (bf16[768,256]{1,0:T(8,128)(2,1)S(1)}, bf16[768,256]{1,0:T(8,128)(2,1)S(1)}, u32[]{:S(2)}, u32[]{:S(2)}) collective-permute-start(bf16[768,256]{1,0:T(8,128)(2,1)S(1)} %get-tuple-element.127), channel_id=1, source_target_pairs={{0,0},{1,4},{2,2},{3,6},{4,1},{5,5},{6,3},{7,7},{8,8},{9,12},{10,1... | collective-permute-start | bytes 1179656 | tf_op jit(solution)/shard_map/ppermute | solution.py:43
  224.1 10.2 %collective-permute-start.32 = (bf16[768,256]{1,0:T(8,128)(2,1)S(1)}, bf16[768,256]{1,0:T(8,128)(2,1)S(1)}, u32[]{:S(2)}, u32[]{:S(2)}) collective-permute-start(bf16[768,256]{1,0:T(8,128)(2,1)S(1)} %get-tuple-element.126), channel_id=1, source_target_pairs={{0,4},{1,0},{2,6},{3,2},{4,5},{5,1},{6,7},{7,3},{8,12},{9,8},{10,1... | collective-permute-start | bytes 1179656 | tf_op jit(solution)/shard_map/ppermute | solution.py:43
  234.6 9.9 %collective-permute-start.35 = (bf16[384,256]{1,0:T(8,128)(2,1)S(1)}, bf16[384,256]{1,0:T(8,128)(2,1)S(1)}, u32[]{:S(2)}, u32[]{:S(2)}) collective-permute-start(bf16[384,256]{1,0:T(8,128)(2,1)S(1)} %get-tuple-element.131), channel_id=1, source_target_pairs={{0,0},{1,4},{2,2},{3,6},{4,1},{5,5},{6,3},{7,7},{8,8},{9,12},{10,1... | collective-permute-start | bytes 589832 | tf_op jit(solution)/shard_map/ppermute | solution.py:43
  (43 other events, 340.3 us)

commit v13 on v12

--- a/solution.py
+++ b/solution.py
@@ -140,8 +140,9 @@
 
 
 def expert_kernel(z_ref, own, up, down, up_2, down_2, last, mine, theirs, *refs):
-    weight_outs, (hidden_out, d_both_out, outer_out), outs, refs = refs[:2], refs[2:5], refs[5:9], refs[9:]
-    packed, x, grads, gate_up, w_down, pre, d_hidden, hidden, d_both, d_down, terms, load, store = refs
+    gate_up, w_down, hidden, d_both, outer = refs[:5]
+    terms, refs = refs[5:9], refs[9:]
+    packed, x, grads, pre, d_hidden, d_down, load = refs
     places, size, _ = packed.shape
     rows, width = x.shape
     slots = rows // 2
@@ -204,14 +205,6 @@
             product = dot(x[:, block], gate_up[block, cols])
             pre[:, cols] = product if s == 0 else pre[:, cols] + product
 
-    stores = []
-
-    def store_to(out, value):
-        stores.append(pltpu.make_async_copy(value, out, store.at[len(stores)]))
-        stores[-1].start()
-
-    store_to(weight_outs[0], gate_up)
-    store_to(weight_outs[1], w_down)
     step = 64 if rows % 64 == 0 else 16
 
     def activate(r, _):
@@ -225,7 +218,6 @@
         return 0
 
     lax.fori_loop(0, rows // step, activate, 0)
-    store_to(hidden_out, hidden)
     for copy in loads[2:]:
         copy.wait()
     d_hidden[...] = dot(grads[...], w_down[...], ((1,), (1,)))
@@ -238,24 +230,26 @@
         return 0
 
     lax.fori_loop(0, rows // step, differentiate, 0)
-    store_to(d_both_out, d_both)
     d_down[...] = dot(hidden[...], grads[...], ((0,), (0,))).astype(BF)
 
-    for k in (places - 1, 1, 2, 0):
+    for k, term in enumerate(terms):
         for h in range(2):
             from_cols = slice(k * line + h * part_rows, k * line + (h + 1) * part_rows)
             weights = dot(x[:, from_cols], d_both[...], ((0,), (0,))).astype(BF)
             for i in range(count):
                 to = h * size_half + i * part_rows
-                terms[k, to:to + part_rows, :] = weights[:, i * LANES:(i + 1) * LANES]
+                term[to:to + part_rows, :] = weights[:, i * LANES:(i + 1) * LANES]
             for j in range(columns):
                 to = h * size_half + count * part_rows + j * piece
-                terms[k, to:to + piece, :] = d_down[down_rows(k, h), j * LANES:(j + 1) * LANES]
-        store_to(outs[k], terms.at[k])
-        if k == 1:
-            store_to(outer_out, terms.at[jnp.where(z == 0, places - 1, 1)])
-    for copy in stores:
-        copy.wait()
+                term[to:to + piece, :] = d_down[down_rows(k, h), j * LANES:(j + 1) * LANES]
+
+    @pl.when(z == 0)
+    def _():
+        outer[...] = terms[places - 1][...]
+
+    @pl.when(z != 0)
+    def _():
+        outer[...] = terms[1][...]
 
 
 def rows_kernel(chunks, *refs):
@@ -317,21 +311,15 @@
         expert_kernel,
         out_shape=for_rows + [jax.ShapeDtypeStruct((size, LANES), BF)] * 5,
         in_specs=[IN_SMEM] + [pl.BlockSpec(memory_space=pl.ANY)] * 8,
-        out_specs=[pl.BlockSpec(memory_space=pl.ANY)] * 9,
+        out_specs=in_vmem(9),
         scratch_shapes=[
             pltpu.VMEM((places, size, LANES), BF),
             pltpu.VMEM((rows, width), BF),
             pltpu.VMEM((rows, width), BF),
-            pltpu.VMEM((width, 2 * units), BF),
-            pltpu.VMEM((units, width), BF),
             pltpu.VMEM((rows, 2 * units), F32),
             pltpu.VMEM((rows, units), F32),
-            pltpu.VMEM((rows, units), BF),
-            pltpu.VMEM((rows, 2 * units), BF),
             pltpu.VMEM((units, width), BF),
-            pltpu.VMEM((places, size, LANES), BF),
             pltpu.SemaphoreType.DMA((places + 4,)),
-            pltpu.SemaphoreType.DMA((9,)),
         ],
         compiler_params=pltpu.CompilerParams(vmem_limit_bytes=24 * MIB),
         cost_estimate=pl.CostEstimate(
@@ -490,30 +478,25 @@
         sum_up, sum_down = tie(sum_up, keep, give), tie(sum_down, keep, give)
         sum_up, sum_down = added(terms[1], sum_up), added(terms[3], sum_down)
         give, outer2 = tie(give, sum_up, sum_down), tie(outer2, sum_up, sum_down)
+        sums = added(keep, g.send(give, other_core)).reshape(g.qs, 2, cap, 2 * width)
+        sum_up, sum_down, sums = together((sum_up, sum_down, sums))
         sum_up, sum_down = g.hop(sum_up, ups), g.hop(sum_down, downs)
         begun2 = g.hop(outer2, outward)
-        sums = added(keep, g.send(give, other_core)).reshape(g.qs, 2, cap, 2 * width)
-
-        def along_x(rows):
-            return jnp.stack([rows[:, 0], g.send(rows[:, 1], lambda z, x, q, c: (z, 1 - x, q, c))], axis=1)
-
-        def along_q(rows):
-            return jnp.stack(
-                [rows[0]] + [g.send(rows[d], lambda z, x, q, c, d=d: (z, x, (q - d) % g.qs, c)) for d in range(1, g.qs)]
-            )
-
-        returned, back_rows = along_x(sums[..., :width]), along_q(sums[..., width:])
-        grad = added(terms[0], tie(sum_up, sums), tie(sum_down, sums))
+        far_rows = g.send(sums[:, 1], lambda z, x, q, c: (z, 1 - x, q, c))
+        grad = added(terms[0], sum_up, sum_down)
         begun2, grad = together((begun2, grad))
         middle2 = added(terms2[2], begun2)
         sum_up2, sum_down2 = g.hop(middle2, inward_up), g.hop(middle2, inward_down)
-        returned, back_rows = along_q(returned), along_x(back_rows)
+        near = jnp.stack([sums[:, 0], far_rows], axis=1)
+        got = jnp.concatenate(
+            [near[0]] + [g.send(near[d], lambda z, x, q, c, d=d: (z, x, (q - d) % g.qs, c)) for d in range(1, g.qs)]
+        ).reshape(slots, 2 * width)
         sum_up2, sum_down2 = tie(sum_up2, grad), tie(sum_down2, grad)
         sum_up2, sum_down2 = added(terms2[1], sum_up2), added(terms2[3], sum_down2)
         grads = unspread(tie(grad, sum_up2, sum_down2))
         sum_up2, sum_down2 = g.hop(sum_up2, ups), g.hop(sum_down2, downs)
-        mixed, d_tokens, d_probs = combine(returned.reshape(slots, width), back_rows.reshape(slots, width))
-        sum_up2, sum_down2 = (tie(value, mixed, d_tokens, d_probs, *grads) for value in (sum_up2, sum_down2))
+        mixed, d_tokens, d_probs = combine(got[:, :width], got[:, width:])
+        sum_up2, sum_down2 = (tie(value, *grads) for value in (sum_up2, sum_down2))
         grads += unspread(added(terms2[0], sum_up2, sum_down2))
         d_w_gate, d_w_up, d_w_down = unpack(pieces, place_x, grads, shuffle, *shapes)
     else:

time: 249 us -> 245 us (0.984)
  waiting for transfers between devices: 96.5 us -> 107 us
  starting transfers between devices: 87.9 us -> 80.8 us
  local copies, waits for them, and re-layouts: 12.8 us -> 9.2 us
  Pallas kernels: 29 us -> 25.8 us
    ppermute x37 -> x35, waiting for transfers between devices: 96.5 us -> 107 us  [send(): return lax.ppermute(value, BOTH, pairs)]
    ppermute x37 -> x35, starting transfers between devices: 87.9 us -> 80.8 us  [send(): return lax.ppermute(value, BOTH, pairs)]
    unnamed x77 -> x58, local copies, waits for them, and re-layouts: 11.4 us -> 7.53 us
    convert_element_type x9, other arithmetic: 7.03 us -> 3.69 us  [added(): return sum((t.astype(F32) for t in terms)).astype(BF)]
  transfers between devices with their start and end apart: 37 -> 35, of which waited for: 20 -> 24; matrix products, arithmetic and copies ran while one was open for 7% -> 5% of each run, Pallas kernels for 10% -> 9%
where the time goes in v13:
time: 245 us; the launch traced here: 244 us
  waiting for transfers between devices  107 us (44%)
  starting transfers between devices  80.8 us (33%)
  Pallas kernels  25.8 us (11%)
  other arithmetic  15.4 us (6%)
  local copies, waits for them, and re-layouts  9.2 us (4%)
  matrix products  3.8 us (2%)
    ppermute x35, waiting for transfers between devices, send(): return lax.ppermute(value, BOTH, pairs)  107 us
    ppermute x35, starting transfers between devices, send(): return lax.ppermute(value, BOTH, pairs)  80.8 us
    pallas_call x2, Pallas kernels, expert(): pl.pallas_call(expert_kernel, out_shape=for_rows + [jax.ShapeDtypeStruct(...  15.3 us
    unnamed x58, local copies, waits for them, and re-layouts  7.53 us
    pallas_call x1, Pallas kernels, token_rows(): pl.pallas_call(functools.partial(rows_kernel, len(chunks)), grid=(2 * til...  5.13 us
  transfers between devices with their start and end apart: 35, of which 24 were waited for; matrix products, arithmetic and copies ran while one was open for 5% of the time, Pallas kernels for 9%

profile of v13, /device:TPU:9, one launch (start us, length us, event | category | flops | bytes accessed | tf_op | source)
XLA Modules:
  0.0 243.7 jit_solution(2509401694758782154)
XLA Ops:
  2.2 3.4 %shard_map.118 = (bf16[768,256]{1,0:T(8,128)(2,1)}, bf16[768,256]{1,0:T(8,128)(2,1)}, bf16[384,256]{1,0:T(8,128)(2,1)}, bf16[384,256]{1,0:T(8,128)(2,1)}) custom-call(s32[1]{0:T(128)} %bitcast.1.x_ref, bf16[256,768]{1,0:T(8,128)(2,1)} %bitcast.34, bf16[256,768]{1,0:T(8,128)(2,1)} %bitcast.35, bf16[96,2048]{1,0:T(8,128)(2,1)} %bitcast.36, ...), custom_call_target="tpu_custom_call" | custom-call | tf_op jit(solution)/shard_map/pallas_call | solution.py:284
  5.6 3.7 %collective-permute-start = (bf16[768,256]{1,0:T(8,128)(2,1)}, bf16[768,256]{1,0:T(8,128)(2,1)S(1)}, u32[]{:S(2)}, u32[]{:S(2)}) collective-permute-start(bf16[768,256]{1,0:T(8,128)(2,1)} %get-tuple-element.60), channel_id=1, source_target_pairs={{0,0},{1,4},{2,2},{3,6},{4,1},{5,5},{6,3},{7,7},{8,8},{9,12},{10,1... | collective-permute-start | bytes 1179656 | tf_op jit(solution)/shard_map/ppermute | solution.py:43
  10.8 4.1 %collective-permute-done = bf16[768,256]{1,0:T(8,128)(2,1)S(1)} collective-permute-done((bf16[768,256]{1,0:T(8,128)(2,1)}, bf16[768,256]{1,0:T(8,128)(2,1)S(1)}, u32[]{:S(2)}, u32[]{:S(2)}) %collective-permute-start) | collective-permute-done | bytes 393248 | tf_op jit(solution)/shard_map/ppermute | solution.py:43
  14.9 3.6 %collective-permute-done.1 = bf16[768,256]{1,0:T(8,128)(2,1)S(1)} collective-permute-done((bf16[768,256]{1,0:T(8,128)(2,1)}, bf16[768,256]{1,0:T(8,128)(2,1)S(1)}, u32[]{:S(2)}, u32[]{:S(2)}) %collective-permute-start.1) | collective-permute-done | bytes 393248 | tf_op jit(solution)/shard_map/ppermute | solution.py:43
  21.4 3.2 %collective-permute-start.2 = (bf16[1536,256]{1,0:T(8,128)(2,1)S(1)}, bf16[1536,256]{1,0:T(8,128)(2,1)}, u32[]{:S(2)}, u32[]{:S(2)}) collective-permute-start(bf16[1536,256]{1,0:T(8,128)(2,1)S(1)} %pad_maximum_fusion.4.own), channel_id=1, source_target_pairs={{0,8},{1,9},{2,10},{3,11},{4,12},{5,13},{6,14},{7,15},{8,16},{9,17... | collective-permute-start | bytes 2359304 | tf_op jit(solution)/shard_map/ppermute | solution.py:43
  24.7 3.0 %collective-permute-start.3 = (bf16[1536,256]{1,0:T(8,128)(2,1)S(1)}, bf16[1536,256]{1,0:T(8,128)(2,1)}, u32[]{:S(2)}, u32[]{:S(2)}) collective-permute-start(bf16[1536,256]{1,0:T(8,128)(2,1)S(1)} %pad_maximum_fusion.4.own), channel_id=1, source_target_pairs={{8,0},{9,1},{10,2},{11,3},{12,4},{13,5},{14,6},{15,7},{16,8},{17,9... | collective-permute-start | bytes 2359304 | tf_op jit(solution)/shard_map/ppermute | solution.py:43
  31.6 10.4 %collective-permute-done.2.up = bf16[1536,256]{1,0:T(8,128)(2,1)} collective-permute-done((bf16[1536,256]{1,0:T(8,128)(2,1)S(1)}, bf16[1536,256]{1,0:T(8,128)(2,1)}, u32[]{:S(2)}, u32[]{:S(2)}) %collective-permute-start.2) | collective-permute-done | bytes 786464 | tf_op jit(solution)/shard_map/ppermute | solution.py:43
  42.0 2.9 %collective-permute-done.3.down = bf16[1536,256]{1,0:T(8,128)(2,1)} collective-permute-done((bf16[1536,256]{1,0:T(8,128)(2,1)S(1)}, bf16[1536,256]{1,0:T(8,128)(2,1)}, u32[]{:S(2)}, u32[]{:S(2)}) %collective-permute-start.3) | collective-permute-done | bytes 786464 | tf_op jit(solution)/shard_map/ppermute | solution.py:43
  44.9 3.2 %collective-permute-start.4 = (bf16[1536,256]{1,0:T(8,128)(2,1)}, bf16[1536,256]{1,0:T(8,128)(2,1)S(1)}, u32[]{:S(2)}, u32[]{:S(2)}) collective-permute-start(bf16[1536,256]{1,0:T(8,128)(2,1)} %collective-permute-done.2.up), channel_id=1, source_target_pairs={{8,16},{9,17},{10,18},{11,19},{12,20},{13,21},{14,22},{15,23},{16,... | collective-permute-start | bytes 2359304 | tf_op jit(solution)/shard_map/ppermute | solution.py:43
  50.8 4.8 %collective-permute-done.10 = bf16[72,4096]{1,0:T(8,128)(2,1)S(1)} collective-permute-done((bf16[72,4096]{1,0:T(8,128)(2,1)}, bf16[72,4096]{1,0:T(8,128)(2,1)S(1)}, u32[]{:S(2)}, u32[]{:S(2)}) %collective-permute-start.10) | collective-permute-done | bytes 589856 | tf_op jit(solution)/shard_map/ppermute | solution.py:43
  60.0 20.3 %collective-permute-done.6.last = bf16[1536,256]{1,0:T(8,128)(2,1)S(1)} collective-permute-done((bf16[1536,256]{1,0:T(8,128)(2,1)S(1)}, bf16[1536,256]{1,0:T(8,128)(2,1)S(1)}, u32[]{:S(2)}, u32[]{:S(2)}) %collective-permute-start.6) | collective-permute-done | bytes 786464 | tf_op jit(solution)/shard_map/ppermute | solution.py:43
  80.4 4.6 %collective-permute-done.5.down_2 = bf16[1536,256]{1,0:T(8,128)(2,1)S(1)} collective-permute-done((bf16[1536,256]{1,0:T(8,128)(2,1)}, bf16[1536,256]{1,0:T(8,128)(2,1)S(1)}, u32[]{:S(2)}, u32[]{:S(2)}) %collective-permute-start.5) | collective-permute-done | bytes 786464 | tf_op jit(solution)/shard_map/ppermute | solution.py:43
  86.4 3.0 %collective-permute-start.16 = (bf16[768,256]{1,0:T(8,128)(2,1)S(1)}, bf16[768,256]{1,0:T(8,128)(2,1)}, u32[]{:S(2)}, u32[]{:S(2)}) collective-permute-start(bf16[768,256]{1,0:T(8,128)(2,1)S(1)} %pad_maximum_fusion.5.own), channel_id=1, source_target_pairs={{8,0},{9,1},{10,2},{11,3},{12,4},{13,5},{14,6},{15,7},{16,8},{17,9... | collective-permute-start | bytes 1179656 | tf_op jit(solution)/shard_map/ppermute | solution.py:43
  91.7 9.4 %shard_map.119 = (bf16[2048,512]{1,0:T(8,128)(2,1)S(1)}, bf16[256,2048]{1,0:T(8,128)(2,1)S(1)}, bf16[576,256]{1,0:T(8,128)(2,1)S(1)}, bf16[576,512]{1,0:T(8,128)...) custom-call(s32[1]{0:T(128)} %bitcast.z_ref, ...), custom_call_target="tpu_custom_call" | custom-call | flops 3623878656 | bytes 4194304 | tf_op jit(solution)/shard_map/pallas_call | solution.py:310
  109.9 4.9 %collective-permute-start.17 = (bf16[768,256]{1,0:T(8,128)(2,1)}, bf16[768,256]{1,0:T(8,128)(2,1)}, u32[]{:S(2)}, u32[]{:S(2)}) collective-permute-start(bf16[768,256]{1,0:T(8,128)(2,1)} %collective-permute-done.16.down), channel_id=1, source_target_pairs={{8,0},{9,1},{10,2},{11,3},{12,4},{13,5},{14,6},{15,7},{16,8},{17,9... | collective-permute-start | bytes 1179656 | tf_op jit(solution)/shard_map/ppermute | solution.py:43
  116.8 5.8 %collective-permute-done.17.down_2 = bf16[768,256]{1,0:T(8,128)(2,1)} collective-permute-done((bf16[768,256]{1,0:T(8,128)(2,1)}, bf16[768,256]{1,0:T(8,128)(2,1)}, u32[]{:S(2)}, u32[]{:S(2)}) %collective-permute-start.17) | collective-permute-done | bytes 393248 | tf_op jit(solution)/shard_map/ppermute | solution.py:43
  132.5 4.0 %collective-permute-start.18 = (bf16[1536,256]{1,0:T(8,128)(2,1)S(1)}, bf16[1536,256]{1,0:T(8,128)(2,1)S(1)}, u32[]{:S(2)}, u32[]{:S(2)}) collective-permute-start(bf16[1536,256]{1,0:T(8,128)(2,1)S(1)} %add_convert_fusion.4), channel_id=1, source_target_pairs={{0,8},{1,9},{2,10},{3,11},{4,12},{5,13},{6,14},{7,15},{8,16},{9,17... | collective-permute-start | bytes 2359304 | tf_op jit(solution)/shard_map/ppermute | solution.py:43
  136.5 5.8 %shard_map.120 = (bf16[2048,256]{1,0:T(8,128)(2,1)S(1)}, bf16[128,2048]{1,0:T(8,128)(2,1)S(1)}, bf16[576,128]{1,0:T(8,128)(2,1)S(1)}, bf16[576,256]{1,0:T(8,128)...) custom-call(s32[1]{0:T(128)} %bitcast.z_ref, ...), custom_call_target="tpu_custom_call" | custom-call | flops 1811939328 | bytes 4194304 | tf_op jit(solution)/shard_map/pallas_call | solution.py:310
  142.4 5.1 %shard_map.121 = (bf16[288,4096]{1,0:T(8,128)(2,1)S(1)}, bf16[288,4096]{1,0:T(8,128)(2,1)S(1)}) custom-call(bf16[2048,512]{1,0:T(8,128)(2,1)S(1)} %copy-done.14, bf16[256,2048]{1,0:T(8,128)(2,1)S(1)} %copy-done.16, bf16[576,256]{1,0:T(8,128)(2,1)S(1)} %copy-done.20, bf16[576,512]{1,0:T(8,128)(2,1)S(1)} %copy-done.18, ...), custom_call_target="tpu_custom_call" | custom-call | flops 2717908992 | bytes 2097152 | tf_op jit(solution)/shard_map/pallas_call | solution.py:344
  147.6 3.2 %collective-permute-done.20 = bf16[1536,256]{1,0:T(8,128)(2,1)S(1)} collective-permute-done((bf16[1536,256]{1,0:T(8,128)(2,1)S(1)}, bf16[1536,256]{1,0:T(8,128)(2,1)S(1)}, u32[]{:S(2)}, u32[]{:S(2)}) %collective-permute-start.20) | collective-permute-done | bytes 786464 | tf_op jit(solution)/shard_map/ppermute | solution.py:43
  154.9 4.2 %collective-permute-done.21 = bf16[288,4096]{1,0:T(8,128)(2,1)S(1)} collective-permute-done((bf16[288,4096]{1,0:T(8,128)(2,1)S(1)}, bf16[288,4096]{1,0:T(8,128)(2,1)S(1)}, u32[]{:S(2)}, u32[]{:S(2)}) %collective-permute-start.21) | collective-permute-done | bytes 2359328 | tf_op jit(solution)/shard_map/ppermute | solution.py:43
  159.9 4.0 %collective-permute-start.25 = (bf16[1536,256]{1,0:T(8,128)(2,1)S(1)}, bf16[1536,256]{1,0:T(8,128)(2,1)S(1)}, u32[]{:S(2)}, u32[]{:S(2)}) collective-permute-start(bf16[1536,256]{1,0:T(8,128)(2,1)S(1)} %add_convert_fusion.3), channel_id=1, source_target_pairs={{0,8},{1,9},{2,10},{3,11},{4,12},{5,13},{6,14},{7,15},{8,16},{9,17... | collective-permute-start | bytes 2359304 | tf_op jit(solution)/shard_map/ppermute | solution.py:43
  169.5 11.1 %collective-permute-done.25 = bf16[1536,256]{1,0:T(8,128)(2,1)S(1)} collective-permute-done((bf16[1536,256]{1,0:T(8,128)(2,1)S(1)}, bf16[1536,256]{1,0:T(8,128)(2,1)S(1)}, u32[]{:S(2)}, u32[]{:S(2)}) %collective-permute-start.25) | collective-permute-done | bytes 786464 | tf_op jit(solution)/shard_map/ppermute | solution.py:43
  180.6 3.7 %collective-permute-done.26 = bf16[1536,256]{1,0:T(8,128)(2,1)S(1)} collective-permute-done((bf16[1536,256]{1,0:T(8,128)(2,1)S(1)}, bf16[1536,256]{1,0:T(8,128)(2,1)S(1)}, u32[]{:S(2)}, u32[]{:S(2)}) %collective-permute-start.26) | collective-permute-done | bytes 786464 | tf_op jit(solution)/shard_map/ppermute | solution.py:43
  184.6 4.4 %collective-permute-done.24 = bf16[768,256]{1,0:T(8,128)(2,1)S(1)} collective-permute-done((bf16[768,256]{1,0:T(8,128)(2,1)S(1)}, bf16[768,256]{1,0:T(8,128)(2,1)S(1)}, u32[]{:S(2)}, u32[]{:S(2)}) %collective-permute-start.24) | collective-permute-done | bytes 393248 | tf_op jit(solution)/shard_map/ppermute | solution.py:43
  190.4 6.5 %collective-permute-start.27 = (bf16[768,256]{1,0:T(8,128)(2,1)S(1)}, bf16[768,256]{1,0:T(8,128)(2,1)S(1)}, u32[]{:S(2)}, u32[]{:S(2)}) collective-permute-start(bf16[768,256]{1,0:T(8,128)(2,1)S(1)} %add_convert_fusion.8), channel_id=1, source_target_pairs={{0,8},{1,9},{2,10},{3,11},{4,12},{5,13},{6,14},{7,15},{8,16},{9,17... | collective-permute-start | bytes 1179656 | tf_op jit(solution)/shard_map/ppermute | solution.py:43
  199.8 3.4 %collective-permute-done.28 = bf16[768,256]{1,0:T(8,128)(2,1)S(1)} collective-permute-done((bf16[768,256]{1,0:T(8,128)(2,1)S(1)}, bf16[768,256]{1,0:T(8,128)(2,1)S(1)}, u32[]{:S(2)}, u32[]{:S(2)}) %collective-permute-start.28) | collective-permute-done | bytes 393248 | tf_op jit(solution)/shard_map/ppermute | solution.py:43
  204.5 5.9 %collective-permute-start.29 = (bf16[768,256]{1,0:T(8,128)(2,1)S(1)}, bf16[768,256]{1,0:T(8,128)(2,1)S(1)}, u32[]{:S(2)}, u32[]{:S(2)}) collective-permute-start(bf16[768,256]{1,0:T(8,128)(2,1)S(1)} %get-tuple-element.123), channel_id=1, source_target_pairs={{0,0},{1,4},{2,2},{3,6},{4,1},{5,5},{6,3},{7,7},{8,8},{9,12},{10,1... | collective-permute-start | bytes 1179656 | tf_op jit(solution)/shard_map/ppermute | solution.py:43
  210.4 4.1 %collective-permute-start.31 = (bf16[768,256]{1,0:T(8,128)(2,1)S(1)}, bf16[768,256]{1,0:T(8,128)(2,1)S(1)}, u32[]{:S(2)}, u32[]{:S(2)}) collective-permute-start(bf16[768,256]{1,0:T(8,128)(2,1)S(1)} %add_convert_fusion.7), channel_id=1, source_target_pairs={{0,8},{1,9},{2,10},{3,11},{4,12},{5,13},{6,14},{7,15},{8,16},{9,17... | collective-permute-start | bytes 1179656 | tf_op jit(solution)/shard_map/ppermute | solution.py:43
  222.7 3.8 %collective-permute-done.32 = bf16[768,256]{1,0:T(8,128)(2,1)S(1)} collective-permute-done((bf16[768,256]{1,0:T(8,128)(2,1)S(1)}, bf16[768,256]{1,0:T(8,128)(2,1)S(1)}, u32[]{:S(2)}, u32[]{:S(2)}) %collective-permute-start.32) | collective-permute-done | bytes 393248 | tf_op jit(solution)/shard_map/ppermute | solution.py:43
  226.7 3.6 %collective-permute-start.33 = (bf16[384,256]{1,0:T(8,128)(2,1)S(1)}, bf16[384,256]{1,0:T(8,128)(2,1)S(1)}, u32[]{:S(2)}, u32[]{:S(2)}) collective-permute-start(bf16[384,256]{1,0:T(8,128)(2,1)S(1)} %get-tuple-element.127), channel_id=1, source_target_pairs={{0,0},{1,4},{2,2},{3,6},{4,1},{5,5},{6,3},{7,7},{8,8},{9,12},{10,1... | collective-permute-start | bytes 589832 | tf_op jit(solution)/shard_map/ppermute | solution.py:43
  230.3 4.3 %collective-permute-done.33.refs_2_ = bf16[384,256]{1,0:T(8,128)(2,1)S(1)} collective-permute-done((bf16[384,256]{1,0:T(8,128)(2,1)S(1)}, bf16[384,256]{1,0:T(8,128)(2,1)S(1)}, u32[]{:S(2)}, u32[]{:S(2)}) %collective-permute-start.33) | collective-permute-done | bytes 196640 | tf_op jit(solution)/shard_map/ppermute | solution.py:43
  (145 shorter events, 74.7 us)
Async XLA Ops:
  5.6 9.3 %collective-permute-start = (bf16[768,256]{1,0:T(8,128)(2,1)}, bf16[768,256]{1,0:T(8,128)(2,1)S(1)}, u32[]{:S(2)}, u32[]{:S(2)}) collective-permute-start(bf16[768,256]{1,0:T(8,128)(2,1)} %get-tuple-element.60), channel_id=1, source_target_pairs={{0,0},{1,4},{2,2},{3,6},{4,1},{5,5},{6,3},{7,7},{8,8},{9,12},{10,1... | collective-permute-start | bytes 1179656 | tf_op jit(solution)/shard_map/ppermute | solution.py:43
  9.3 9.2 %collective-permute-start.1 = (bf16[768,256]{1,0:T(8,128)(2,1)}, bf16[768,256]{1,0:T(8,128)(2,1)S(1)}, u32[]{:S(2)}, u32[]{:S(2)}) collective-permute-start(bf16[768,256]{1,0:T(8,128)(2,1)} %get-tuple-element.61), channel_id=1, source_target_pairs={{0,1},{1,5},{2,3},{3,7},{4,0},{5,4},{6,2},{7,6},{8,9},{9,13},{10,1... | collective-permute-start | bytes 1179656 | tf_op jit(solution)/shard_map/ppermute | solution.py:43
  18.6 9.0 %collective-permute-start.7 = (bf16[384,256]{1,0:T(8,128)(2,1)S(1)}, bf16[384,256]{1,0:T(8,128)(2,1)S(1)}, u32[]{:S(2)}, u32[]{:S(2)}) collective-permute-start(bf16[384,256]{1,0:T(8,128)(2,1)S(1)} %copy-done.28), channel_id=1, source_target_pairs={{0,0},{1,4},{2,2},{3,6},{4,1},{5,5},{6,3},{7,7},{8,8},{9,12},{10,1... | collective-permute-start | bytes 589832 | tf_op jit(solution)/shard_map/ppermute | solution.py:43
  21.4 20.6 %collective-permute-start.2 = (bf16[1536,256]{1,0:T(8,128)(2,1)S(1)}, bf16[1536,256]{1,0:T(8,128)(2,1)}, u32[]{:S(2)}, u32[]{:S(2)}) collective-permute-start(bf16[1536,256]{1,0:T(8,128)(2,1)S(1)} %pad_maximum_fusion.4.own), channel_id=1, source_target_pairs={{0,8},{1,9},{2,10},{3,11},{4,12},{5,13},{6,14},{7,15},{8,16},{9,17... | collective-permute-start | bytes 2359304 | tf_op jit(solution)/shard_map/ppermute | solution.py:43
  24.7 20.3 %collective-permute-start.3 = (bf16[1536,256]{1,0:T(8,128)(2,1)S(1)}, bf16[1536,256]{1,0:T(8,128)(2,1)}, u32[]{:S(2)}, u32[]{:S(2)}) collective-permute-start(bf16[1536,256]{1,0:T(8,128)(2,1)S(1)} %pad_maximum_fusion.4.own), channel_id=1, source_target_pairs={{8,0},{9,1},{10,2},{11,3},{12,4},{13,5},{14,6},{15,7},{16,8},{17,9... | collective-permute-start | bytes 2359304 | tf_op jit(solution)/shard_map/ppermute | solution.py:43
  29.0 26.6 %collective-permute-start.10 = (bf16[72,4096]{1,0:T(8,128)(2,1)}, bf16[72,4096]{1,0:T(8,128)(2,1)S(1)}, u32[]{:S(2)}, u32[]{:S(2)}) collective-permute-start(bf16[72,4096]{1,0:T(8,128)(2,1)} %get-tuple-element.120), channel_id=1, source_target_pairs={{0,2},{1,3},{2,0},{3,1},{4,6},{5,7},{6,4},{7,5},{8,10},{9,11},{10,... | collective-permute-start | bytes 1769480 | tf_op jit(solution)/shard_map/ppermute | solution.py:43
  30.2 27.3 %collective-permute-start.11 = (bf16[72,4096]{1,0:T(8,128)(2,1)}, bf16[72,4096]{1,0:T(8,128)(2,1)S(1)}, u32[]{:S(2)}, u32[]{:S(2)}) collective-permute-start(bf16[72,4096]{1,0:T(8,128)(2,1)} %get-tuple-element.119), channel_id=1, source_target_pairs={{0,6},{1,7},{2,4},{3,5},{4,2},{5,3},{6,0},{7,1},{8,14},{9,15},{10,... | collective-permute-start | bytes 1769480 | tf_op jit(solution)/shard_map/ppermute | solution.py:43
  31.4 26.1 %collective-permute-start.9 = (bf16[72,4096]{1,0:T(8,128)(2,1)S(1)}, bf16[72,4096]{1,0:T(8,128)(2,1)S(1)}, u32[]{:S(2)}, u32[]{:S(2)}) collective-permute-start(bf16[72,4096]{1,0:T(8,128)(2,1)S(1)} %get-tuple-element.121), channel_id=1, source_target_pairs={{0,4},{1,5},{2,6},{3,7},{4,0},{5,1},{6,2},{7,3},{8,12},{9,13},{10,... | collective-permute-start | bytes 1769480 | tf_op jit(solution)/shard_map/ppermute | solution.py:43
  44.9 35.4 %collective-permute-start.4 = (bf16[1536,256]{1,0:T(8,128)(2,1)}, bf16[1536,256]{1,0:T(8,128)(2,1)S(1)}, u32[]{:S(2)}, u32[]{:S(2)}) collective-permute-start(bf16[1536,256]{1,0:T(8,128)(2,1)} %collective-permute-done.2.up), channel_id=1, source_target_pairs={{8,16},{9,17},{10,18},{11,19},{12,20},{13,21},{14,22},{15,23},{16,... | collective-permute-start | bytes 2359304 | tf_op jit(solution)/shard_map/ppermute | solution.py:43
  49.4 30.9 %collective-permute-start.6 = (bf16[1536,256]{1,0:T(8,128)(2,1)S(1)}, bf16[1536,256]{1,0:T(8,128)(2,1)S(1)}, u32[]{:S(2)}, u32[]{:S(2)}) collective-permute-start(bf16[1536,256]{1,0:T(8,128)(2,1)S(1)} %broadcast_select_fusion), channel_id=1, source_target_pairs={{8,24},{9,25},{10,26},{11,27},{12,28},{13,29},{14,30},{15,31},{16,... | collective-permute-start | bytes 2359304 | tf_op jit(solution)/shard_map/ppermute | solution.py:43
  55.6 29.3 %collective-permute-start.5 = (bf16[1536,256]{1,0:T(8,128)(2,1)}, bf16[1536,256]{1,0:T(8,128)(2,1)S(1)}, u32[]{:S(2)}, u32[]{:S(2)}) collective-permute-start(bf16[1536,256]{1,0:T(8,128)(2,1)} %collective-permute-done.3.down), channel_id=1, source_target_pairs={{8,0},{9,1},{10,2},{11,3},{12,4},{13,5},{14,6},{15,7},{16,8},{17,9... | collective-permute-start | bytes 2359304 | tf_op jit(solution)/shard_map/ppermute | solution.py:43
  84.9 6.7 %collective-permute-start.12 = (bf16[288,4096]{1,0:T(8,128)(2,1)S(1)}, bf16[288,4096]{1,0:T(8,128)(2,1)S(1)}, u32[]{:S(2)}, u32[]{:S(2)}) collective-permute-start(bf16[288,4096]{1,0:T(8,128)(2,1)S(1)} %pad_maximum_fusion.1.mine), channel_id=1, source_target_pairs={{0,1},{1,0},{2,3},{3,2},{4,5},{5,4},{6,7},{7,6},{8,9},{9,8},{10,11... | collective-permute-start | bytes 7077896 | tf_op jit(solution)/shard_map/ppermute | solution.py:43
  86.4 23.5 %collective-permute-start.16 = (bf16[768,256]{1,0:T(8,128)(2,1)S(1)}, bf16[768,256]{1,0:T(8,128)(2,1)}, u32[]{:S(2)}, u32[]{:S(2)}) collective-permute-start(bf16[768,256]{1,0:T(8,128)(2,1)S(1)} %pad_maximum_fusion.5.own), channel_id=1, source_target_pairs={{8,0},{9,1},{10,2},{11,3},{12,4},{13,5},{14,6},{15,7},{16,8},{17,9... | collective-permute-start | bytes 1179656 | tf_op jit(solution)/shard_map/ppermute | solution.py:43
  89.4 25.3 %collective-permute-start.14 = (bf16[768,256]{1,0:T(8,128)(2,1)S(1)}, bf16[768,256]{1,0:T(8,128)(2,1)}, u32[]{:S(2)}, u32[]{:S(2)}) collective-permute-start(bf16[768,256]{1,0:T(8,128)(2,1)S(1)} %pad_maximum_fusion.5.own), channel_id=1, source_target_pairs={{0,8},{1,9},{2,10},{3,11},{4,12},{5,13},{6,14},{7,15},{8,16},{9,17... | collective-permute-start | bytes 1179656 | tf_op jit(solution)/shard_map/ppermute | solution.py:43
  108.6 20.7 %collective-permute-start.13 = (bf16[1536,256]{1,0:T(8,128)(2,1)}, bf16[1536,256]{1,0:T(8,128)(2,1)}, u32[]{:S(2)}, u32[]{:S(2)}) collective-permute-start(bf16[1536,256]{1,0:T(8,128)(2,1)} %get-tuple-element.73), channel_id=1, source_target_pairs={{0,8},{1,9},{2,10},{3,11},{4,12},{5,13},{6,14},{7,15},{24,16},{25,... | collective-permute-start | bytes 2359304 | tf_op jit(solution)/shard_map/ppermute | solution.py:43
  109.9 12.8 %collective-permute-start.17 = (bf16[768,256]{1,0:T(8,128)(2,1)}, bf16[768,256]{1,0:T(8,128)(2,1)}, u32[]{:S(2)}, u32[]{:S(2)}) collective-permute-start(bf16[768,256]{1,0:T(8,128)(2,1)} %collective-permute-done.16.down), channel_id=1, source_target_pairs={{8,0},{9,1},{10,2},{11,3},{12,4},{13,5},{14,6},{15,7},{16,8},{17,9... | collective-permute-start | bytes 1179656 | tf_op jit(solution)/shard_map/ppermute | solution.py:43
  114.8 9.2 %collective-permute-start.15 = (bf16[768,256]{1,0:T(8,128)(2,1)}, bf16[768,256]{1,0:T(8,128)(2,1)}, u32[]{:S(2)}, u32[]{:S(2)}) collective-permute-start(bf16[768,256]{1,0:T(8,128)(2,1)} %collective-permute-done.14.up), channel_id=1, source_target_pairs={{8,16},{9,17},{10,18},{11,19},{12,20},{13,21},{14,22},{15,23},{16,... | collective-permute-start | bytes 1179656 | tf_op jit(solution)/shard_map/ppermute | solution.py:43
  125.0 11.5 %collective-permute-start.19 = (bf16[768,256]{1,0:T(8,128)(2,1)S(1)}, bf16[768,256]{1,0:T(8,128)(2,1)S(1)}, u32[]{:S(2)}, u32[]{:S(2)}) collective-permute-start(bf16[768,256]{1,0:T(8,128)(2,1)S(1)} %broadcast_select_fusion.1), channel_id=1, source_target_pairs={{8,0},{9,1},{10,2},{11,3},{12,4},{13,5},{14,6},{15,7},{16,24},{17,... | collective-permute-start | bytes 1179656 | tf_op jit(solution)/shard_map/ppermute | solution.py:43
  131.0 19.8 %collective-permute-start.20 = (bf16[1536,256]{1,0:T(8,128)(2,1)S(1)}, bf16[1536,256]{1,0:T(8,128)(2,1)S(1)}, u32[]{:S(2)}, u32[]{:S(2)}) collective-permute-start(bf16[1536,256]{1,0:T(8,128)(2,1)S(1)} %add_convert_fusion.4), channel_id=1, source_target_pairs={{16,8},{17,9},{18,10},{19,11},{20,12},{21,13},{22,14},{23,15},{24,... | collective-permute-start | bytes 2359304 | tf_op jit(solution)/shard_map/ppermute | solution.py:43
  132.5 19.5 %collective-permute-start.18 = (bf16[1536,256]{1,0:T(8,128)(2,1)S(1)}, bf16[1536,256]{1,0:T(8,128)(2,1)S(1)}, u32[]{:S(2)}, u32[]{:S(2)}) collective-permute-start(bf16[1536,256]{1,0:T(8,128)(2,1)S(1)} %add_convert_fusion.4), channel_id=1, source_target_pairs={{0,8},{1,9},{2,10},{3,11},{4,12},{5,13},{6,14},{7,15},{8,16},{9,17... | collective-permute-start | bytes 2359304 | tf_op jit(solution)/shard_map/ppermute | solution.py:43
  159.9 20.6 %collective-permute-start.25 = (bf16[1536,256]{1,0:T(8,128)(2,1)S(1)}, bf16[1536,256]{1,0:T(8,128)(2,1)S(1)}, u32[]{:S(2)}, u32[]{:S(2)}) collective-permute-start(bf16[1536,256]{1,0:T(8,128)(2,1)S(1)} %add_convert_fusion.3), channel_id=1, source_target_pairs={{0,8},{1,9},{2,10},{3,11},{4,12},{5,13},{6,14},{7,15},{8,16},{9,17... | collective-permute-start | bytes 2359304 | tf_op jit(solution)/shard_map/ppermute | solution.py:43
  163.9 20.3 %collective-permute-start.26 = (bf16[1536,256]{1,0:T(8,128)(2,1)S(1)}, bf16[1536,256]{1,0:T(8,128)(2,1)S(1)}, u32[]{:S(2)}, u32[]{:S(2)}) collective-permute-start(bf16[1536,256]{1,0:T(8,128)(2,1)S(1)} %add_convert_fusion.2), channel_id=1, source_target_pairs={{8,0},{9,1},{10,2},{11,3},{12,4},{13,5},{14,6},{15,7},{16,8},{17,9... | collective-permute-start | bytes 2359304 | tf_op jit(solution)/shard_map/ppermute | solution.py:43
  165.9 31.0 %collective-permute-start.22 = (bf16[2,72,4096]{2,1,0:T(8,128)(2,1)S(1)}, bf16[2,72,4096]{2,1,0:T(8,128)(2,1)S(1)}, u32[]{:S(2)}, u32[]{:S(2)}) collective-permute-start(bf16[2,72,4096]{2,1,0:T(8,128)(2,1)S(1)} %slice_bitcast_fusion), channel_id=1, source_target_pairs={{0,4},{1,5},{2,6},{3,7},{4,0},{5,1},{6,2},{7,3},{8,12},{9,13},{10,... | collective-permute-start | bytes 3538952 | tf_op jit(solution)/shard_map/ppermute | solution.py:43
  167.8 21.2 %collective-permute-start.24 = (bf16[768,256]{1,0:T(8,128)(2,1)S(1)}, bf16[768,256]{1,0:T(8,128)(2,1)S(1)}, u32[]{:S(2)}, u32[]{:S(2)}) collective-permute-start(bf16[768,256]{1,0:T(8,128)(2,1)S(1)} %get-tuple-element.96), channel_id=1, source_target_pairs={{0,8},{1,9},{2,10},{3,11},{4,12},{5,13},{6,14},{7,15},{24,16},{25,... | collective-permute-start | bytes 1179656 | tf_op jit(solution)/shard_map/ppermute | solution.py:43
  189.1 14.2 %collective-permute-start.28 = (bf16[768,256]{1,0:T(8,128)(2,1)S(1)}, bf16[768,256]{1,0:T(8,128)(2,1)S(1)}, u32[]{:S(2)}, u32[]{:S(2)}) collective-permute-start(bf16[768,256]{1,0:T(8,128)(2,1)S(1)} %add_convert_fusion.8), channel_id=1, source_target_pairs={{16,8},{17,9},{18,10},{19,11},{20,12},{21,13},{22,14},{23,15},{24,... | collective-permute-start | bytes 1179656 | tf_op jit(solution)/shard_map/ppermute | solution.py:43
  190.4 13.7 %collective-permute-start.27 = (bf16[768,256]{1,0:T(8,128)(2,1)S(1)}, bf16[768,256]{1,0:T(8,128)(2,1)S(1)}, u32[]{:S(2)}, u32[]{:S(2)}) collective-permute-start(bf16[768,256]{1,0:T(8,128)(2,1)S(1)} %add_convert_fusion.8), channel_id=1, source_target_pairs={{0,8},{1,9},{2,10},{3,11},{4,12},{5,13},{6,14},{7,15},{8,16},{9,17... | collective-permute-start | bytes 1179656 | tf_op jit(solution)/shard_map/ppermute | solution.py:43
  198.6 39.2 %collective-permute-start.23 = (bf16[2,72,4096]{2,1,0:T(8,128)(2,1)}, bf16[2,72,4096]{2,1,0:T(8,128)(2,1)}, u32[]{:S(2)}, u32[]{:S(2)}) collective-permute-start(bf16[2,72,4096]{2,1,0:T(8,128)(2,1)} %get-tuple-element.117), channel_id=1, source_target_pairs={{0,2},{1,3},{2,0},{3,1},{4,6},{5,7},{6,4},{7,5},{8,10},{9,11},{10,... | collective-permute-start | bytes 3538952 | tf_op jit(solution)/shard_map/ppermute | solution.py:43
  204.5 14.7 %collective-permute-start.29 = (bf16[768,256]{1,0:T(8,128)(2,1)S(1)}, bf16[768,256]{1,0:T(8,128)(2,1)S(1)}, u32[]{:S(2)}, u32[]{:S(2)}) collective-permute-start(bf16[768,256]{1,0:T(8,128)(2,1)S(1)} %get-tuple-element.123), channel_id=1, source_target_pairs={{0,0},{1,4},{2,2},{3,6},{4,1},{5,5},{6,3},{7,7},{8,8},{9,12},{10,1... | collective-permute-start | bytes 1179656 | tf_op jit(solution)/shard_map/ppermute | solution.py:43
  210.3 10.1 %collective-permute-start.30 = (bf16[768,256]{1,0:T(8,128)(2,1)S(1)}, bf16[768,256]{1,0:T(8,128)(2,1)S(1)}, u32[]{:S(2)}, u32[]{:S(2)}) collective-permute-start(bf16[768,256]{1,0:T(8,128)(2,1)S(1)} %get-tuple-element.122), channel_id=1, source_target_pairs={{0,4},{1,0},{2,6},{3,2},{4,5},{5,1},{6,7},{7,3},{8,12},{9,8},{10,1... | collective-permute-start | bytes 1179656 | tf_op jit(solution)/shard_map/ppermute | solution.py:43
  210.4 12.3 %collective-permute-start.31 = (bf16[768,256]{1,0:T(8,128)(2,1)S(1)}, bf16[768,256]{1,0:T(8,128)(2,1)S(1)}, u32[]{:S(2)}, u32[]{:S(2)}) collective-permute-start(bf16[768,256]{1,0:T(8,128)(2,1)S(1)} %add_convert_fusion.7), channel_id=1, source_target_pairs={{0,8},{1,9},{2,10},{3,11},{4,12},{5,13},{6,14},{7,15},{8,16},{9,17... | collective-permute-start | bytes 1179656 | tf_op jit(solution)/shard_map/ppermute | solution.py:43
  214.5 12.0 %collective-permute-start.32 = (bf16[768,256]{1,0:T(8,128)(2,1)S(1)}, bf16[768,256]{1,0:T(8,128)(2,1)S(1)}, u32[]{:S(2)}, u32[]{:S(2)}) collective-permute-start(bf16[768,256]{1,0:T(8,128)(2,1)S(1)} %add_convert_fusion.6), channel_id=1, source_target_pairs={{8,0},{9,1},{10,2},{11,3},{12,4},{13,5},{14,6},{15,7},{16,8},{17,9... | collective-permute-start | bytes 1179656 | tf_op jit(solution)/shard_map/ppermute | solution.py:43
  226.7 7.9 %collective-permute-start.33 = (bf16[384,256]{1,0:T(8,128)(2,1)S(1)}, bf16[384,256]{1,0:T(8,128)(2,1)S(1)}, u32[]{:S(2)}, u32[]{:S(2)}) collective-permute-start(bf16[384,256]{1,0:T(8,128)(2,1)S(1)} %get-tuple-element.127), channel_id=1, source_target_pairs={{0,0},{1,4},{2,2},{3,6},{4,1},{5,5},{6,3},{7,7},{8,8},{9,12},{10,1... | collective-permute-start | bytes 589832 | tf_op jit(solution)/shard_map/ppermute | solution.py:43
  (32 other events, 293.0 us)

commit v14 on v12

--- a/solution.py
+++ b/solution.py
@@ -18,6 +18,10 @@
 
 def tie(value, *others):
     return lax.optimization_barrier((value,) + others)[0]
+
+
+def tie_all(values, *others):
+    return [tie(value, *others) for value in values]
 
 
 def added(*terms):
@@ -317,7 +321,7 @@
         expert_kernel,
         out_shape=for_rows + [jax.ShapeDtypeStruct((size, LANES), BF)] * 5,
         in_specs=[IN_SMEM] + [pl.BlockSpec(memory_space=pl.ANY)] * 8,
-        out_specs=[pl.BlockSpec(memory_space=pl.ANY)] * 9,
+        out_specs=[pl.BlockSpec(memory_space=pltpu.HBM)] * 9,
         scratch_shapes=[
             pltpu.VMEM((places, size, LANES), BF),
             pltpu.VMEM((rows, width), BF),
@@ -490,31 +494,26 @@
         sum_up, sum_down = tie(sum_up, keep, give), tie(sum_down, keep, give)
         sum_up, sum_down = added(terms[1], sum_up), added(terms[3], sum_down)
         give, outer2 = tie(give, sum_up, sum_down), tie(outer2, sum_up, sum_down)
+        sums = added(keep, g.send(give, other_core)).reshape(g.qs, 2, cap, 2 * width)
+        sum_up, sum_down, sums = together((sum_up, sum_down, sums))
         sum_up, sum_down = g.hop(sum_up, ups), g.hop(sum_down, downs)
         begun2 = g.hop(outer2, outward)
-        sums = added(keep, g.send(give, other_core)).reshape(g.qs, 2, cap, 2 * width)
-
-        def along_x(rows):
-            return jnp.stack([rows[:, 0], g.send(rows[:, 1], lambda z, x, q, c: (z, 1 - x, q, c))], axis=1)
-
-        def along_q(rows):
-            return jnp.stack(
-                [rows[0]] + [g.send(rows[d], lambda z, x, q, c, d=d: (z, x, (q - d) % g.qs, c)) for d in range(1, g.qs)]
-            )
-
-        returned, back_rows = along_x(sums[..., :width]), along_q(sums[..., width:])
-        grad = added(terms[0], tie(sum_up, sums), tie(sum_down, sums))
+        far_rows = g.send(sums[:, 1], lambda z, x, q, c: (z, 1 - x, q, c))
+        grad = added(terms[0], sum_up, sum_down)
         begun2, grad = together((begun2, grad))
         middle2 = added(terms2[2], begun2)
         sum_up2, sum_down2 = g.hop(middle2, inward_up), g.hop(middle2, inward_down)
-        returned, back_rows = along_q(returned), along_x(back_rows)
+        near = jnp.stack([sums[:, 0], far_rows], axis=1)
+        got = jnp.concatenate(
+            [near[0]] + [g.send(near[d], lambda z, x, q, c, d=d: (z, x, (q - d) % g.qs, c)) for d in range(1, g.qs)]
+        ).reshape(slots, 2 * width)
         sum_up2, sum_down2 = tie(sum_up2, grad), tie(sum_down2, grad)
         sum_up2, sum_down2 = added(terms2[1], sum_up2), added(terms2[3], sum_down2)
         grads = unspread(tie(grad, sum_up2, sum_down2))
         sum_up2, sum_down2 = g.hop(sum_up2, ups), g.hop(sum_down2, downs)
-        mixed, d_tokens, d_probs = combine(returned.reshape(slots, width), back_rows.reshape(slots, width))
-        sum_up2, sum_down2 = (tie(value, mixed, d_tokens, d_probs, *grads) for value in (sum_up2, sum_down2))
-        grads += unspread(added(terms2[0], sum_up2, sum_down2))
+        mixed, d_tokens, d_probs = combine(got[:, :width], got[:, width:])
+        grads = tie_all(grads, sum_up2, sum_down2)
+        grads += tie_all(unspread(added(terms2[0], sum_up2, sum_down2)), mixed, d_tokens, d_probs)
         d_w_gate, d_w_up, d_w_down = unpack(pieces, place_x, grads, shuffle, *shapes)
     else:
         gate_cols, up_cols = dot(w_gate[0], shuffle).astype(BF), dot(w_up[0], shuffle).astype(BF)

time: 249 us -> 236 us (0.948)
  waiting for transfers between devices: 96.5 us -> 90.2 us
  starting transfers between devices: 87.9 us -> 82.8 us
  local copies, waits for them, and re-layouts: 12.8 us -> 9.96 us
    ppermute x37 -> x35, waiting for transfers between devices: 96.5 us -> 90.2 us  [send(): return lax.ppermute(value, BOTH, pairs)]
    ppermute x37 -> x35, starting transfers between devices: 87.9 us -> 82.8 us  [send(): return lax.ppermute(value, BOTH, pairs)]
    unnamed x77 -> x60, local copies, waits for them, and re-layouts: 11.4 us -> 8.3 us
  transfers between devices with their start and end apart: 37 -> 35, of which waited for: 20 -> 18; matrix products, arithmetic and copies ran while one was open for 7% -> 9% of each run, Pallas kernels for 10% -> 10%
where the time goes in v14:
time: 236 us; the launch traced here: 234 us
  waiting for transfers between devices  90.2 us (38%)
  starting transfers between devices  82.8 us (35%)
  Pallas kernels  28 us (12%)
  other arithmetic  17.5 us (7%)
  local copies, waits for them, and re-layouts  9.96 us (4%)
  matrix products  3.8 us (2%)
    ppermute x35, waiting for transfers between devices, send(): return lax.ppermute(value, BOTH, pairs)  90.2 us
    ppermute x35, starting transfers between devices, send(): return lax.ppermute(value, BOTH, pairs)  82.8 us
    pallas_call x2, Pallas kernels, expert(): pl.pallas_call(expert_kernel, out_shape=for_rows + [jax.ShapeDtypeStruct(...  17.4 us
    unnamed x60, local copies, waits for them, and re-layouts  8.3 us
    convert_element_type x9, other arithmetic, added(): return sum((t.astype(F32) for t in terms)).astype(BF)  6.14 us
    pallas_call x1, Pallas kernels, token_rows(): pl.pallas_call(functools.partial(rows_kernel, len(chunks)), grid=(2 * til...  5.14 us
  transfers between devices with their start and end apart: 35, of which 18 were waited for; matrix products, arithmetic and copies ran while one was open for 9% of the time, Pallas kernels for 10%

profile of v14, /device:TPU:9, one launch (start us, length us, event | category | flops | bytes accessed | tf_op | source)
XLA Modules:
  0.0 233.8 jit_solution(8770866657866298616)
XLA Ops:
  2.2 3.4 %shard_map.118 = (bf16[768,256]{1,0:T(8,128)(2,1)}, bf16[768,256]{1,0:T(8,128)(2,1)}, bf16[384,256]{1,0:T(8,128)(2,1)}, bf16[384,256]{1,0:T(8,128)(2,1)}) custom-call(s32[1]{0:T(128)} %bitcast.1.x_ref, bf16[256,768]{1,0:T(8,128)(2,1)} %bitcast.34, bf16[256,768]{1,0:T(8,128)(2,1)} %bitcast.35, bf16[96,2048]{1,0:T(8,128)(2,1)} %bitcast.36, ...), custom_call_target="tpu_custom_call" | custom-call | tf_op jit(solution)/shard_map/pallas_call | solution.py:294
  5.6 3.7 %collective-permute-start = (bf16[768,256]{1,0:T(8,128)(2,1)}, bf16[768,256]{1,0:T(8,128)(2,1)S(1)}, u32[]{:S(2)}, u32[]{:S(2)}) collective-permute-start(bf16[768,256]{1,0:T(8,128)(2,1)} %get-tuple-element.62), channel_id=1, source_target_pairs={{0,0},{1,4},{2,2},{3,6},{4,1},{5,5},{6,3},{7,7},{8,8},{9,12},{10,1... | collective-permute-start | bytes 1179656 | tf_op jit(solution)/shard_map/ppermute | solution.py:47
  10.8 4.1 %collective-permute-done = bf16[768,256]{1,0:T(8,128)(2,1)S(1)} collective-permute-done((bf16[768,256]{1,0:T(8,128)(2,1)}, bf16[768,256]{1,0:T(8,128)(2,1)S(1)}, u32[]{:S(2)}, u32[]{:S(2)}) %collective-permute-start) | collective-permute-done | bytes 393248 | tf_op jit(solution)/shard_map/ppermute | solution.py:47
  14.9 3.6 %collective-permute-done.1 = bf16[768,256]{1,0:T(8,128)(2,1)S(1)} collective-permute-done((bf16[768,256]{1,0:T(8,128)(2,1)}, bf16[768,256]{1,0:T(8,128)(2,1)S(1)}, u32[]{:S(2)}, u32[]{:S(2)}) %collective-permute-start.1) | collective-permute-done | bytes 393248 | tf_op jit(solution)/shard_map/ppermute | solution.py:47
  18.6 2.5 %collective-permute-start.7 = (bf16[384,256]{1,0:T(8,128)(2,1)S(1)}, bf16[384,256]{1,0:T(8,128)(2,1)S(1)}, u32[]{:S(2)}, u32[]{:S(2)}) collective-permute-start(bf16[384,256]{1,0:T(8,128)(2,1)S(1)} %copy-done.29), channel_id=1, source_target_pairs={{0,0},{1,4},{2,2},{3,6},{4,1},{5,5},{6,3},{7,7},{8,8},{9,12},{10,1... | collective-permute-start | bytes 589832 | tf_op jit(solution)/shard_map/ppermute | solution.py:47
  21.4 3.2 %collective-permute-start.2 = (bf16[1536,256]{1,0:T(8,128)(2,1)S(1)}, bf16[1536,256]{1,0:T(8,128)(2,1)}, u32[]{:S(2)}, u32[]{:S(2)}) collective-permute-start(bf16[1536,256]{1,0:T(8,128)(2,1)S(1)} %pad_maximum_fusion.4.own), channel_id=1, source_target_pairs={{0,8},{1,9},{2,10},{3,11},{4,12},{5,13},{6,14},{7,15},{8,16},{9,17... | collective-permute-start | bytes 2359304 | tf_op jit(solution)/shard_map/ppermute | solution.py:47
  24.6 3.0 %collective-permute-start.3 = (bf16[1536,256]{1,0:T(8,128)(2,1)S(1)}, bf16[1536,256]{1,0:T(8,128)(2,1)}, u32[]{:S(2)}, u32[]{:S(2)}) collective-permute-start(bf16[1536,256]{1,0:T(8,128)(2,1)S(1)} %pad_maximum_fusion.4.own), channel_id=1, source_target_pairs={{8,0},{9,1},{10,2},{11,3},{12,4},{13,5},{14,6},{15,7},{16,8},{17,9... | collective-permute-start | bytes 2359304 | tf_op jit(solution)/shard_map/ppermute | solution.py:47
  31.6 10.4 %collective-permute-done.2.up = bf16[1536,256]{1,0:T(8,128)(2,1)} collective-permute-done((bf16[1536,256]{1,0:T(8,128)(2,1)S(1)}, bf16[1536,256]{1,0:T(8,128)(2,1)}, u32[]{:S(2)}, u32[]{:S(2)}) %collective-permute-start.2) | collective-permute-done | bytes 786464 | tf_op jit(solution)/shard_map/ppermute | solution.py:47
  42.0 2.9 %collective-permute-done.3.down = bf16[1536,256]{1,0:T(8,128)(2,1)} collective-permute-done((bf16[1536,256]{1,0:T(8,128)(2,1)S(1)}, bf16[1536,256]{1,0:T(8,128)(2,1)}, u32[]{:S(2)}, u32[]{:S(2)}) %collective-permute-start.3) | collective-permute-done | bytes 786464 | tf_op jit(solution)/shard_map/ppermute | solution.py:47
  44.9 3.2 %collective-permute-start.4 = (bf16[1536,256]{1,0:T(8,128)(2,1)}, bf16[1536,256]{1,0:T(8,128)(2,1)S(1)}, u32[]{:S(2)}, u32[]{:S(2)}) collective-permute-start(bf16[1536,256]{1,0:T(8,128)(2,1)} %collective-permute-done.2.up), channel_id=1, source_target_pairs={{8,16},{9,17},{10,18},{11,19},{12,20},{13,21},{14,22},{15,23},{16,... | collective-permute-start | bytes 2359304 | tf_op jit(solution)/shard_map/ppermute | solution.py:47
  50.8 4.8 %collective-permute-done.10 = bf16[72,4096]{1,0:T(8,128)(2,1)S(1)} collective-permute-done((bf16[72,4096]{1,0:T(8,128)(2,1)}, bf16[72,4096]{1,0:T(8,128)(2,1)S(1)}, u32[]{:S(2)}, u32[]{:S(2)}) %collective-permute-start.10) | collective-permute-done | bytes 589856 | tf_op jit(solution)/shard_map/ppermute | solution.py:47
  60.0 20.3 %collective-permute-done.6.last = bf16[1536,256]{1,0:T(8,128)(2,1)S(1)} collective-permute-done((bf16[1536,256]{1,0:T(8,128)(2,1)S(1)}, bf16[1536,256]{1,0:T(8,128)(2,1)S(1)}, u32[]{:S(2)}, u32[]{:S(2)}) %collective-permute-start.6) | collective-permute-done | bytes 786464 | tf_op jit(solution)/shard_map/ppermute | solution.py:47
  80.4 4.6 %collective-permute-done.5.down_2 = bf16[1536,256]{1,0:T(8,128)(2,1)S(1)} collective-permute-done((bf16[1536,256]{1,0:T(8,128)(2,1)}, bf16[1536,256]{1,0:T(8,128)(2,1)S(1)}, u32[]{:S(2)}, u32[]{:S(2)}) %collective-permute-start.5) | collective-permute-done | bytes 786464 | tf_op jit(solution)/shard_map/ppermute | solution.py:47
  86.4 3.0 %collective-permute-start.16 = (bf16[768,256]{1,0:T(8,128)(2,1)S(1)}, bf16[768,256]{1,0:T(8,128)(2,1)}, u32[]{:S(2)}, u32[]{:S(2)}) collective-permute-start(bf16[768,256]{1,0:T(8,128)(2,1)S(1)} %pad_maximum_fusion.5.own), channel_id=1, source_target_pairs={{8,0},{9,1},{10,2},{11,3},{12,4},{13,5},{14,6},{15,7},{16,8},{17,9... | collective-permute-start | bytes 1179656 | tf_op jit(solution)/shard_map/ppermute | solution.py:47
  91.7 9.7 %shard_map.119 = (bf16[2048,512]{1,0:T(8,128)(2,1)S(1)}, bf16[256,2048]{1,0:T(8,128)(2,1)S(1)}, bf16[576,256]{1,0:T(8,128)(2,1)S(1)}, bf16[576,512]{1,0:T(8,128)...) custom-call(s32[1]{0:T(128)} %bitcast.z_ref, ...), custom_call_target="tpu_custom_call" | custom-call | flops 3623878656 | bytes 4194304 | tf_op jit(solution)/shard_map/pallas_call | solution.py:320
  110.2 4.8 %collective-permute-start.17 = (bf16[768,256]{1,0:T(8,128)(2,1)}, bf16[768,256]{1,0:T(8,128)(2,1)}, u32[]{:S(2)}, u32[]{:S(2)}) collective-permute-start(bf16[768,256]{1,0:T(8,128)(2,1)} %collective-permute-done.16.down), channel_id=1, source_target_pairs={{8,0},{9,1},{10,2},{11,3},{12,4},{13,5},{14,6},{15,7},{16,8},{17,9... | collective-permute-start | bytes 1179656 | tf_op jit(solution)/shard_map/ppermute | solution.py:47
  117.1 5.8 %collective-permute-done.17.down_2 = bf16[768,256]{1,0:T(8,128)(2,1)} collective-permute-done((bf16[768,256]{1,0:T(8,128)(2,1)}, bf16[768,256]{1,0:T(8,128)(2,1)}, u32[]{:S(2)}, u32[]{:S(2)}) %collective-permute-start.17) | collective-permute-done | bytes 393248 | tf_op jit(solution)/shard_map/ppermute | solution.py:47
  125.3 2.8 %collective-permute-start.19 = (bf16[768,256]{1,0:T(8,128)(2,1)S(1)}, bf16[768,256]{1,0:T(8,128)(2,1)S(1)}, u32[]{:S(2)}, u32[]{:S(2)}) collective-permute-start(bf16[768,256]{1,0:T(8,128)(2,1)S(1)} %broadcast_select_fusion.1), channel_id=1, source_target_pairs={{8,0},{9,1},{10,2},{11,3},{12,4},{13,5},{14,6},{15,7},{16,24},{17,... | collective-permute-start | bytes 1179656 | tf_op jit(solution)/shard_map/ppermute | solution.py:47
  132.8 4.0 %collective-permute-start.18 = (bf16[1536,256]{1,0:T(8,128)(2,1)S(1)}, bf16[1536,256]{1,0:T(8,128)(2,1)S(1)}, u32[]{:S(2)}, u32[]{:S(2)}) collective-permute-start(bf16[1536,256]{1,0:T(8,128)(2,1)S(1)} %add_convert_fusion.4), channel_id=1, source_target_pairs={{0,8},{1,9},{2,10},{3,11},{4,12},{5,13},{6,14},{7,15},{8,16},{9,17... | collective-permute-start | bytes 2359304 | tf_op jit(solution)/shard_map/ppermute | solution.py:47
  136.8 7.8 %shard_map.120 = (bf16[2048,256]{1,0:T(8,128)(2,1)S(1)}, bf16[128,2048]{1,0:T(8,128)(2,1)S(1)}, bf16[576,128]{1,0:T(8,128)(2,1)S(1)}, bf16[576,256]{1,0:T(8,128)...) custom-call(s32[1]{0:T(128)} %bitcast.z_ref, ...), custom_call_target="tpu_custom_call" | custom-call | flops 1811939328 | bytes 4194304 | tf_op jit(solution)/shard_map/pallas_call | solution.py:320
  145.4 5.1 %shard_map.121 = (bf16[288,4096]{1,0:T(8,128)(2,1)S(1)}, bf16[288,4096]{1,0:T(8,128)(2,1)S(1)}) custom-call(bf16[2048,512]{1,0:T(8,128)(2,1)S(1)} %copy-done.16, bf16[256,2048]{1,0:T(8,128)(2,1)S(1)} %copy-done.18, bf16[576,256]{1,0:T(8,128)(2,1)S(1)} %copy-done.22, bf16[576,512]{1,0:T(8,128)(2,1)S(1)} %copy-done.20, ...), custom_call_target="tpu_custom_call" | custom-call | flops 2717908992 | bytes 2097152 | tf_op jit(solution)/shard_map/pallas_call | solution.py:360
  155.1 4.2 %collective-permute-done.21 = bf16[288,4096]{1,0:T(8,128)(2,1)S(1)} collective-permute-done((bf16[288,4096]{1,0:T(8,128)(2,1)S(1)}, bf16[288,4096]{1,0:T(8,128)(2,1)S(1)}, u32[]{:S(2)}, u32[]{:S(2)}) %collective-permute-start.21) | collective-permute-done | bytes 2359328 | tf_op jit(solution)/shard_map/ppermute | solution.py:47
  160.2 4.0 %collective-permute-start.25 = (bf16[1536,256]{1,0:T(8,128)(2,1)S(1)}, bf16[1536,256]{1,0:T(8,128)(2,1)S(1)}, u32[]{:S(2)}, u32[]{:S(2)}) collective-permute-start(bf16[1536,256]{1,0:T(8,128)(2,1)S(1)} %add_convert_fusion.3), channel_id=1, source_target_pairs={{0,8},{1,9},{2,10},{3,11},{4,12},{5,13},{6,14},{7,15},{8,16},{9,17... | collective-permute-start | bytes 2359304 | tf_op jit(solution)/shard_map/ppermute | solution.py:47
  169.7 11.1 %collective-permute-done.25 = bf16[1536,256]{1,0:T(8,128)(2,1)S(1)} collective-permute-done((bf16[1536,256]{1,0:T(8,128)(2,1)S(1)}, bf16[1536,256]{1,0:T(8,128)(2,1)S(1)}, u32[]{:S(2)}, u32[]{:S(2)}) %collective-permute-start.25) | collective-permute-done | bytes 786464 | tf_op jit(solution)/shard_map/ppermute | solution.py:47
  180.8 3.7 %collective-permute-done.26 = bf16[1536,256]{1,0:T(8,128)(2,1)S(1)} collective-permute-done((bf16[1536,256]{1,0:T(8,128)(2,1)S(1)}, bf16[1536,256]{1,0:T(8,128)(2,1)S(1)}, u32[]{:S(2)}, u32[]{:S(2)}) %collective-permute-start.26) | collective-permute-done | bytes 786464 | tf_op jit(solution)/shard_map/ppermute | solution.py:47
  184.8 4.4 %collective-permute-done.24 = bf16[768,256]{1,0:T(8,128)(2,1)S(1)} collective-permute-done((bf16[768,256]{1,0:T(8,128)(2,1)S(1)}, bf16[768,256]{1,0:T(8,128)(2,1)S(1)}, u32[]{:S(2)}, u32[]{:S(2)}) %collective-permute-start.24) | collective-permute-done | bytes 393248 | tf_op jit(solution)/shard_map/ppermute | solution.py:47
  190.7 6.5 %collective-permute-start.27 = (bf16[768,256]{1,0:T(8,128)(2,1)S(1)}, bf16[768,256]{1,0:T(8,128)(2,1)S(1)}, u32[]{:S(2)}, u32[]{:S(2)}) collective-permute-start(bf16[768,256]{1,0:T(8,128)(2,1)S(1)} %add_convert_fusion.8), channel_id=1, source_target_pairs={{0,8},{1,9},{2,10},{3,11},{4,12},{5,13},{6,14},{7,15},{8,16},{9,17... | collective-permute-start | bytes 1179656 | tf_op jit(solution)/shard_map/ppermute | solution.py:47
  199.7 3.9 %collective-permute-done.28 = bf16[768,256]{1,0:T(8,128)(2,1)S(1)} collective-permute-done((bf16[768,256]{1,0:T(8,128)(2,1)S(1)}, bf16[768,256]{1,0:T(8,128)(2,1)S(1)}, u32[]{:S(2)}, u32[]{:S(2)}) %collective-permute-start.28) | collective-permute-done | bytes 393248 | tf_op jit(solution)/shard_map/ppermute | solution.py:47
  207.3 3.4 %collective-permute-start.30 = (bf16[768,256]{1,0:T(8,128)(2,1)}, bf16[768,256]{1,0:T(8,128)(2,1)}, u32[]{:S(2)}, u32[]{:S(2)}) collective-permute-start(bf16[768,256]{1,0:T(8,128)(2,1)} %add_convert_fusion.7), channel_id=1, source_target_pairs={{0,8},{1,9},{2,10},{3,11},{4,12},{5,13},{6,14},{7,15},{8,16},{9,17... | collective-permute-start | bytes 1179656 | tf_op jit(solution)/shard_map/ppermute | solution.py:47
  213.0 3.6 %collective-permute-start.29 = (bf16[768,256]{1,0:T(8,128)(2,1)S(1)}, bf16[768,256]{1,0:T(8,128)(2,1)S(1)}, u32[]{:S(2)}, u32[]{:S(2)}) collective-permute-start(bf16[768,256]{1,0:T(8,128)(2,1)S(1)} %get-tuple-element.127), channel_id=1, source_target_pairs={{0,0},{1,4},{2,2},{3,6},{4,1},{5,5},{6,3},{7,7},{8,8},{9,12},{10,1... | collective-permute-start | bytes 1179656 | tf_op jit(solution)/shard_map/ppermute | solution.py:47
  219.5 2.7 %collective-permute-start.34 = (bf16[384,256]{1,0:T(8,128)(2,1)S(1)}, bf16[384,256]{1,0:T(8,128)(2,1)S(1)}, u32[]{:S(2)}, u32[]{:S(2)}) collective-permute-start(bf16[384,256]{1,0:T(8,128)(2,1)S(1)} %get-tuple-element.130), channel_id=1, source_target_pairs={{0,4},{1,0},{2,6},{3,2},{4,5},{5,1},{6,7},{7,3},{8,12},{9,8},{10,1... | collective-permute-start | bytes 589832 | tf_op jit(solution)/shard_map/ppermute | solution.py:47
  222.2 3.6 %collective-permute-start.33 = (bf16[384,256]{1,0:T(8,128)(2,1)S(1)}, bf16[384,256]{1,0:T(8,128)(2,1)S(1)}, u32[]{:S(2)}, u32[]{:S(2)}) collective-permute-start(bf16[384,256]{1,0:T(8,128)(2,1)S(1)} %get-tuple-element.131), channel_id=1, source_target_pairs={{0,0},{1,4},{2,2},{3,6},{4,1},{5,5},{6,3},{7,7},{8,8},{9,12},{10,1... | collective-permute-start | bytes 589832 | tf_op jit(solution)/shard_map/ppermute | solution.py:47
  (147 shorter events, 68.4 us)
Async XLA Ops:
  5.6 9.3 %collective-permute-start = (bf16[768,256]{1,0:T(8,128)(2,1)}, bf16[768,256]{1,0:T(8,128)(2,1)S(1)}, u32[]{:S(2)}, u32[]{:S(2)}) collective-permute-start(bf16[768,256]{1,0:T(8,128)(2,1)} %get-tuple-element.62), channel_id=1, source_target_pairs={{0,0},{1,4},{2,2},{3,6},{4,1},{5,5},{6,3},{7,7},{8,8},{9,12},{10,1... | collective-permute-start | bytes 1179656 | tf_op jit(solution)/shard_map/ppermute | solution.py:47
  9.3 9.2 %collective-permute-start.1 = (bf16[768,256]{1,0:T(8,128)(2,1)}, bf16[768,256]{1,0:T(8,128)(2,1)S(1)}, u32[]{:S(2)}, u32[]{:S(2)}) collective-permute-start(bf16[768,256]{1,0:T(8,128)(2,1)} %get-tuple-element.63), channel_id=1, source_target_pairs={{0,1},{1,5},{2,3},{3,7},{4,0},{5,4},{6,2},{7,6},{8,9},{9,13},{10,1... | collective-permute-start | bytes 1179656 | tf_op jit(solution)/shard_map/ppermute | solution.py:47
  18.6 9.0 %collective-permute-start.7 = (bf16[384,256]{1,0:T(8,128)(2,1)S(1)}, bf16[384,256]{1,0:T(8,128)(2,1)S(1)}, u32[]{:S(2)}, u32[]{:S(2)}) collective-permute-start(bf16[384,256]{1,0:T(8,128)(2,1)S(1)} %copy-done.29), channel_id=1, source_target_pairs={{0,0},{1,4},{2,2},{3,6},{4,1},{5,5},{6,3},{7,7},{8,8},{9,12},{10,1... | collective-permute-start | bytes 589832 | tf_op jit(solution)/shard_map/ppermute | solution.py:47
  21.4 20.6 %collective-permute-start.2 = (bf16[1536,256]{1,0:T(8,128)(2,1)S(1)}, bf16[1536,256]{1,0:T(8,128)(2,1)}, u32[]{:S(2)}, u32[]{:S(2)}) collective-permute-start(bf16[1536,256]{1,0:T(8,128)(2,1)S(1)} %pad_maximum_fusion.4.own), channel_id=1, source_target_pairs={{0,8},{1,9},{2,10},{3,11},{4,12},{5,13},{6,14},{7,15},{8,16},{9,17... | collective-permute-start | bytes 2359304 | tf_op jit(solution)/shard_map/ppermute | solution.py:47
  24.6 20.3 %collective-permute-start.3 = (bf16[1536,256]{1,0:T(8,128)(2,1)S(1)}, bf16[1536,256]{1,0:T(8,128)(2,1)}, u32[]{:S(2)}, u32[]{:S(2)}) collective-permute-start(bf16[1536,256]{1,0:T(8,128)(2,1)S(1)} %pad_maximum_fusion.4.own), channel_id=1, source_target_pairs={{8,0},{9,1},{10,2},{11,3},{12,4},{13,5},{14,6},{15,7},{16,8},{17,9... | collective-permute-start | bytes 2359304 | tf_op jit(solution)/shard_map/ppermute | solution.py:47
  29.0 26.6 %collective-permute-start.10 = (bf16[72,4096]{1,0:T(8,128)(2,1)}, bf16[72,4096]{1,0:T(8,128)(2,1)S(1)}, u32[]{:S(2)}, u32[]{:S(2)}) collective-permute-start(bf16[72,4096]{1,0:T(8,128)(2,1)} %get-tuple-element.124), channel_id=1, source_target_pairs={{0,2},{1,3},{2,0},{3,1},{4,6},{5,7},{6,4},{7,5},{8,10},{9,11},{10,... | collective-permute-start | bytes 1769480 | tf_op jit(solution)/shard_map/ppermute | solution.py:47
  30.2 27.3 %collective-permute-start.11 = (bf16[72,4096]{1,0:T(8,128)(2,1)}, bf16[72,4096]{1,0:T(8,128)(2,1)S(1)}, u32[]{:S(2)}, u32[]{:S(2)}) collective-permute-start(bf16[72,4096]{1,0:T(8,128)(2,1)} %get-tuple-element.123), channel_id=1, source_target_pairs={{0,6},{1,7},{2,4},{3,5},{4,2},{5,3},{6,0},{7,1},{8,14},{9,15},{10,... | collective-permute-start | bytes 1769480 | tf_op jit(solution)/shard_map/ppermute | solution.py:47
  31.4 26.1 %collective-permute-start.9 = (bf16[72,4096]{1,0:T(8,128)(2,1)S(1)}, bf16[72,4096]{1,0:T(8,128)(2,1)S(1)}, u32[]{:S(2)}, u32[]{:S(2)}) collective-permute-start(bf16[72,4096]{1,0:T(8,128)(2,1)S(1)} %get-tuple-element.125), channel_id=1, source_target_pairs={{0,4},{1,5},{2,6},{3,7},{4,0},{5,1},{6,2},{7,3},{8,12},{9,13},{10,... | collective-permute-start | bytes 1769480 | tf_op jit(solution)/shard_map/ppermute | solution.py:47
  44.9 35.4 %collective-permute-start.4 = (bf16[1536,256]{1,0:T(8,128)(2,1)}, bf16[1536,256]{1,0:T(8,128)(2,1)S(1)}, u32[]{:S(2)}, u32[]{:S(2)}) collective-permute-start(bf16[1536,256]{1,0:T(8,128)(2,1)} %collective-permute-done.2.up), channel_id=1, source_target_pairs={{8,16},{9,17},{10,18},{11,19},{12,20},{13,21},{14,22},{15,23},{16,... | collective-permute-start | bytes 2359304 | tf_op jit(solution)/shard_map/ppermute | solution.py:47
  49.4 30.9 %collective-permute-start.6 = (bf16[1536,256]{1,0:T(8,128)(2,1)S(1)}, bf16[1536,256]{1,0:T(8,128)(2,1)S(1)}, u32[]{:S(2)}, u32[]{:S(2)}) collective-permute-start(bf16[1536,256]{1,0:T(8,128)(2,1)S(1)} %broadcast_select_fusion), channel_id=1, source_target_pairs={{8,24},{9,25},{10,26},{11,27},{12,28},{13,29},{14,30},{15,31},{16,... | collective-permute-start | bytes 2359304 | tf_op jit(solution)/shard_map/ppermute | solution.py:47
  55.6 29.3 %collective-permute-start.5 = (bf16[1536,256]{1,0:T(8,128)(2,1)}, bf16[1536,256]{1,0:T(8,128)(2,1)S(1)}, u32[]{:S(2)}, u32[]{:S(2)}) collective-permute-start(bf16[1536,256]{1,0:T(8,128)(2,1)} %collective-permute-done.3.down), channel_id=1, source_target_pairs={{8,0},{9,1},{10,2},{11,3},{12,4},{13,5},{14,6},{15,7},{16,8},{17,9... | collective-permute-start | bytes 2359304 | tf_op jit(solution)/shard_map/ppermute | solution.py:47
  86.4 23.8 %collective-permute-start.16 = (bf16[768,256]{1,0:T(8,128)(2,1)S(1)}, bf16[768,256]{1,0:T(8,128)(2,1)}, u32[]{:S(2)}, u32[]{:S(2)}) collective-permute-start(bf16[768,256]{1,0:T(8,128)(2,1)S(1)} %pad_maximum_fusion.5.own), channel_id=1, source_target_pairs={{8,0},{9,1},{10,2},{11,3},{12,4},{13,5},{14,6},{15,7},{16,8},{17,9... | collective-permute-start | bytes 1179656 | tf_op jit(solution)/shard_map/ppermute | solution.py:47
  89.4 25.6 %collective-permute-start.14 = (bf16[768,256]{1,0:T(8,128)(2,1)S(1)}, bf16[768,256]{1,0:T(8,128)(2,1)}, u32[]{:S(2)}, u32[]{:S(2)}) collective-permute-start(bf16[768,256]{1,0:T(8,128)(2,1)S(1)} %pad_maximum_fusion.5.own), channel_id=1, source_target_pairs={{0,8},{1,9},{2,10},{3,11},{4,12},{5,13},{6,14},{7,15},{8,16},{9,17... | collective-permute-start | bytes 1179656 | tf_op jit(solution)/shard_map/ppermute | solution.py:47
  108.9 20.7 %collective-permute-start.13 = (bf16[1536,256]{1,0:T(8,128)(2,1)}, bf16[1536,256]{1,0:T(8,128)(2,1)}, u32[]{:S(2)}, u32[]{:S(2)}) collective-permute-start(bf16[1536,256]{1,0:T(8,128)(2,1)} %get-tuple-element.75), channel_id=1, source_target_pairs={{0,8},{1,9},{2,10},{3,11},{4,12},{5,13},{6,14},{7,15},{24,16},{25,... | collective-permute-start | bytes 2359304 | tf_op jit(solution)/shard_map/ppermute | solution.py:47
  110.2 12.7 %collective-permute-start.17 = (bf16[768,256]{1,0:T(8,128)(2,1)}, bf16[768,256]{1,0:T(8,128)(2,1)}, u32[]{:S(2)}, u32[]{:S(2)}) collective-permute-start(bf16[768,256]{1,0:T(8,128)(2,1)} %collective-permute-done.16.down), channel_id=1, source_target_pairs={{8,0},{9,1},{10,2},{11,3},{12,4},{13,5},{14,6},{15,7},{16,8},{17,9... | collective-permute-start | bytes 1179656 | tf_op jit(solution)/shard_map/ppermute | solution.py:47
  115.0 9.2 %collective-permute-start.15 = (bf16[768,256]{1,0:T(8,128)(2,1)}, bf16[768,256]{1,0:T(8,128)(2,1)}, u32[]{:S(2)}, u32[]{:S(2)}) collective-permute-start(bf16[768,256]{1,0:T(8,128)(2,1)} %collective-permute-done.14.up), channel_id=1, source_target_pairs={{8,16},{9,17},{10,18},{11,19},{12,20},{13,21},{14,22},{15,23},{16,... | collective-permute-start | bytes 1179656 | tf_op jit(solution)/shard_map/ppermute | solution.py:47
  125.3 11.5 %collective-permute-start.19 = (bf16[768,256]{1,0:T(8,128)(2,1)S(1)}, bf16[768,256]{1,0:T(8,128)(2,1)S(1)}, u32[]{:S(2)}, u32[]{:S(2)}) collective-permute-start(bf16[768,256]{1,0:T(8,128)(2,1)S(1)} %broadcast_select_fusion.1), channel_id=1, source_target_pairs={{8,0},{9,1},{10,2},{11,3},{12,4},{13,5},{14,6},{15,7},{16,24},{17,... | collective-permute-start | bytes 1179656 | tf_op jit(solution)/shard_map/ppermute | solution.py:47
  131.2 19.8 %collective-permute-start.20 = (bf16[1536,256]{1,0:T(8,128)(2,1)S(1)}, bf16[1536,256]{1,0:T(8,128)(2,1)S(1)}, u32[]{:S(2)}, u32[]{:S(2)}) collective-permute-start(bf16[1536,256]{1,0:T(8,128)(2,1)S(1)} %add_convert_fusion.4), channel_id=1, source_target_pairs={{16,8},{17,9},{18,10},{19,11},{20,12},{21,13},{22,14},{23,15},{24,... | collective-permute-start | bytes 2359304 | tf_op jit(solution)/shard_map/ppermute | solution.py:47
  132.8 19.5 %collective-permute-start.18 = (bf16[1536,256]{1,0:T(8,128)(2,1)S(1)}, bf16[1536,256]{1,0:T(8,128)(2,1)S(1)}, u32[]{:S(2)}, u32[]{:S(2)}) collective-permute-start(bf16[1536,256]{1,0:T(8,128)(2,1)S(1)} %add_convert_fusion.4), channel_id=1, source_target_pairs={{0,8},{1,9},{2,10},{3,11},{4,12},{5,13},{6,14},{7,15},{8,16},{9,17... | collective-permute-start | bytes 2359304 | tf_op jit(solution)/shard_map/ppermute | solution.py:47
  160.2 20.6 %collective-permute-start.25 = (bf16[1536,256]{1,0:T(8,128)(2,1)S(1)}, bf16[1536,256]{1,0:T(8,128)(2,1)S(1)}, u32[]{:S(2)}, u32[]{:S(2)}) collective-permute-start(bf16[1536,256]{1,0:T(8,128)(2,1)S(1)} %add_convert_fusion.3), channel_id=1, source_target_pairs={{0,8},{1,9},{2,10},{3,11},{4,12},{5,13},{6,14},{7,15},{8,16},{9,17... | collective-permute-start | bytes 2359304 | tf_op jit(solution)/shard_map/ppermute | solution.py:47
  164.2 20.3 %collective-permute-start.26 = (bf16[1536,256]{1,0:T(8,128)(2,1)S(1)}, bf16[1536,256]{1,0:T(8,128)(2,1)S(1)}, u32[]{:S(2)}, u32[]{:S(2)}) collective-permute-start(bf16[1536,256]{1,0:T(8,128)(2,1)S(1)} %add_convert_fusion.2), channel_id=1, source_target_pairs={{8,0},{9,1},{10,2},{11,3},{12,4},{13,5},{14,6},{15,7},{16,8},{17,9... | collective-permute-start | bytes 2359304 | tf_op jit(solution)/shard_map/ppermute | solution.py:47
  166.2 31.0 %collective-permute-start.22 = (bf16[2,72,4096]{2,1,0:T(8,128)(2,1)S(1)}, bf16[2,72,4096]{2,1,0:T(8,128)(2,1)S(1)}, u32[]{:S(2)}, u32[]{:S(2)}) collective-permute-start(bf16[2,72,4096]{2,1,0:T(8,128)(2,1)S(1)} %slice_bitcast_fusion), channel_id=1, source_target_pairs={{0,4},{1,5},{2,6},{3,7},{4,0},{5,1},{6,2},{7,3},{8,12},{9,13},{10,... | collective-permute-start | bytes 3538952 | tf_op jit(solution)/shard_map/ppermute | solution.py:47
  168.1 21.2 %collective-permute-start.24 = (bf16[768,256]{1,0:T(8,128)(2,1)S(1)}, bf16[768,256]{1,0:T(8,128)(2,1)S(1)}, u32[]{:S(2)}, u32[]{:S(2)}) collective-permute-start(bf16[768,256]{1,0:T(8,128)(2,1)S(1)} %get-tuple-element.98), channel_id=1, source_target_pairs={{0,8},{1,9},{2,10},{3,11},{4,12},{5,13},{6,14},{7,15},{24,16},{25,... | collective-permute-start | bytes 1179656 | tf_op jit(solution)/shard_map/ppermute | solution.py:47
  189.4 14.3 %collective-permute-start.28 = (bf16[768,256]{1,0:T(8,128)(2,1)S(1)}, bf16[768,256]{1,0:T(8,128)(2,1)S(1)}, u32[]{:S(2)}, u32[]{:S(2)}) collective-permute-start(bf16[768,256]{1,0:T(8,128)(2,1)S(1)} %add_convert_fusion.8), channel_id=1, source_target_pairs={{16,8},{17,9},{18,10},{19,11},{20,12},{21,13},{22,14},{23,15},{24,... | collective-permute-start | bytes 1179656 | tf_op jit(solution)/shard_map/ppermute | solution.py:47
  190.7 15.7 %collective-permute-start.27 = (bf16[768,256]{1,0:T(8,128)(2,1)S(1)}, bf16[768,256]{1,0:T(8,128)(2,1)S(1)}, u32[]{:S(2)}, u32[]{:S(2)}) collective-permute-start(bf16[768,256]{1,0:T(8,128)(2,1)S(1)} %add_convert_fusion.8), channel_id=1, source_target_pairs={{0,8},{1,9},{2,10},{3,11},{4,12},{5,13},{6,14},{7,15},{8,16},{9,17... | collective-permute-start | bytes 1179656 | tf_op jit(solution)/shard_map/ppermute | solution.py:47
  198.5 27.4 %collective-permute-start.23 = (bf16[2,72,4096]{2,1,0:T(8,128)(2,1)}, bf16[2,72,4096]{2,1,0:T(8,128)(2,1)}, u32[]{:S(2)}, u32[]{:S(2)}) collective-permute-start(bf16[2,72,4096]{2,1,0:T(8,128)(2,1)} %get-tuple-element.121), channel_id=1, source_target_pairs={{0,2},{1,3},{2,0},{3,1},{4,6},{5,7},{6,4},{7,5},{8,10},{9,11},{10,... | collective-permute-start | bytes 3538952 | tf_op jit(solution)/shard_map/ppermute | solution.py:47
  204.5 12.1 %collective-permute-start.31 = (bf16[768,256]{1,0:T(8,128)(2,1)}, bf16[768,256]{1,0:T(8,128)(2,1)S(1)}, u32[]{:S(2)}, u32[]{:S(2)}) collective-permute-start(bf16[768,256]{1,0:T(8,128)(2,1)} %add_convert_fusion.6), channel_id=1, source_target_pairs={{8,0},{9,1},{10,2},{11,3},{12,4},{13,5},{14,6},{15,7},{16,8},{17,9... | collective-permute-start | bytes 1179656 | tf_op jit(solution)/shard_map/ppermute | solution.py:47
  207.3 11.1 %collective-permute-start.30 = (bf16[768,256]{1,0:T(8,128)(2,1)}, bf16[768,256]{1,0:T(8,128)(2,1)}, u32[]{:S(2)}, u32[]{:S(2)}) collective-permute-start(bf16[768,256]{1,0:T(8,128)(2,1)} %add_convert_fusion.7), channel_id=1, source_target_pairs={{0,8},{1,9},{2,10},{3,11},{4,12},{5,13},{6,14},{7,15},{8,16},{9,17... | collective-permute-start | bytes 1179656 | tf_op jit(solution)/shard_map/ppermute | solution.py:47
  210.7 15.1 %collective-permute-start.32 = (bf16[768,256]{1,0:T(8,128)(2,1)S(1)}, bf16[768,256]{1,0:T(8,128)(2,1)S(1)}, u32[]{:S(2)}, u32[]{:S(2)}) collective-permute-start(bf16[768,256]{1,0:T(8,128)(2,1)S(1)} %get-tuple-element.126), channel_id=1, source_target_pairs={{0,4},{1,0},{2,6},{3,2},{4,5},{5,1},{6,7},{7,3},{8,12},{9,8},{10,1... | collective-permute-start | bytes 1179656 | tf_op jit(solution)/shard_map/ppermute | solution.py:47
  213.0 12.8 %collective-permute-start.29 = (bf16[768,256]{1,0:T(8,128)(2,1)S(1)}, bf16[768,256]{1,0:T(8,128)(2,1)S(1)}, u32[]{:S(2)}, u32[]{:S(2)}) collective-permute-start(bf16[768,256]{1,0:T(8,128)(2,1)S(1)} %get-tuple-element.127), channel_id=1, source_target_pairs={{0,0},{1,4},{2,2},{3,6},{4,1},{5,5},{6,3},{7,7},{8,8},{9,12},{10,1... | collective-permute-start | bytes 1179656 | tf_op jit(solution)/shard_map/ppermute | solution.py:47
  219.5 12.2 %collective-permute-start.34 = (bf16[384,256]{1,0:T(8,128)(2,1)S(1)}, bf16[384,256]{1,0:T(8,128)(2,1)S(1)}, u32[]{:S(2)}, u32[]{:S(2)}) collective-permute-start(bf16[384,256]{1,0:T(8,128)(2,1)S(1)} %get-tuple-element.130), channel_id=1, source_target_pairs={{0,4},{1,0},{2,6},{3,2},{4,5},{5,1},{6,7},{7,3},{8,12},{9,8},{10,1... | collective-permute-start | bytes 589832 | tf_op jit(solution)/shard_map/ppermute | solution.py:47
  222.2 9.6 %collective-permute-start.33 = (bf16[384,256]{1,0:T(8,128)(2,1)S(1)}, bf16[384,256]{1,0:T(8,128)(2,1)S(1)}, u32[]{:S(2)}, u32[]{:S(2)}) collective-permute-start(bf16[384,256]{1,0:T(8,128)(2,1)S(1)} %get-tuple-element.131), channel_id=1, source_target_pairs={{0,0},{1,4},{2,2},{3,6},{4,1},{5,5},{6,3},{7,7},{8,8},{9,12},{10,1... | collective-permute-start | bytes 589832 | tf_op jit(solution)/shard_map/ppermute | solution.py:47
  (33 other events, 284.5 us)

commit v15 on v14

--- a/solution.py
+++ b/solution.py
@@ -310,7 +310,7 @@
     )(x, *packed, shuffle)
 
 
-def expert(z, places, units, weights, mine, theirs):
+def expert(z, places, units, weights, mine, theirs, vmem):
     size = weights[0].shape[0]
     slots, width = mine.shape[0], mine.shape[1] // 2
     rows = 2 * slots
@@ -337,7 +337,7 @@
             pltpu.SemaphoreType.DMA((places + 4,)),
             pltpu.SemaphoreType.DMA((9,)),
         ],
-        compiler_params=pltpu.CompilerParams(vmem_limit_bytes=24 * MIB),
+        compiler_params=pltpu.CompilerParams(vmem_limit_bytes=vmem),
         cost_estimate=pl.CostEstimate(
             flops=12 * rows * width * units, bytes_accessed=4 * 2**20, transcendentals=rows * units
         ),
@@ -479,7 +479,7 @@
         theirs = g.send(mine, other_core)
         shard2 = tie(shard2, mine)
         up2, down2 = g.hop(shard2, ups), g.hop(shard2, downs)
-        chunk, outer, terms = expert(place_z, g.zs, units[0], (shard, up, down, up_2, down_2, far), mine, theirs)
+        chunk, outer, terms = expert(place_z, g.zs, units[0], (shard, up, down, up_2, down_2, far), mine, theirs, 52 * MIB)
         begun = g.hop(outer, outward)
         up2, down2 = tie(up2, outer), tie(down2, outer)
         up2_2, down2_2 = g.hop(up2, {1: 2, 2: 3}), g.hop(down2, {1: 0, 2: 1})
@@ -488,7 +488,7 @@
         middle = added(terms[2], tie(begun, passed))
         sum_up, sum_down = g.hop(middle, inward_up), g.hop(middle, inward_down)
         chunk2, outer2, terms2 = expert(
-            place_z, g.zs, units[1], (shard2, up2, down2, up2_2, down2_2, tie(last2, middle)), mine, theirs
+            place_z, g.zs, units[1], (shard2, up2, down2, up2_2, down2_2, tie(last2, middle)), mine, theirs, 24 * MIB
         )
         keep, give = token_rows((chunk, chunk2), slots, width)
         sum_up, sum_down = tie(sum_up, keep, give), tie(sum_down, keep, give)

time: 236 us -> 234 us (level)
    unnamed x60 -> x54, local copies, waits for them, and re-layouts: 8.3 us -> 6.34 us
  transfers between devices with their start and end apart: 35 -> 35, of which waited for: 18 -> 16; matrix products, arithmetic and copies ran while one was open for 9% -> 8% of each run, Pallas kernels for 10% -> 10%
where the time goes in v15:
time: 234 us; the launch traced here: 231 us
  waiting for transfers between devices  89.3 us (38%)
  starting transfers between devices  82.6 us (35%)
  Pallas kernels  28.4 us (12%)
  other arithmetic  16.3 us (7%)
  local copies, waits for them, and re-layouts  7.78 us (3%)
  matrix products  4.87 us (2%)
    ppermute x35, waiting for transfers between devices, send(): return lax.ppermute(value, BOTH, pairs)  89.3 us
    ppermute x35, starting transfers between devices, send(): return lax.ppermute(value, BOTH, pairs)  82.6 us
    pallas_call x2, Pallas kernels, expert(): pl.pallas_call(expert_kernel, out_shape=for_rows + [jax.ShapeDtypeStruct(...  17.9 us
    unnamed x54, local copies, waits for them, and re-layouts  6.34 us
    convert_element_type x9, other arithmetic, added(): return sum((t.astype(F32) for t in terms)).astype(BF)  6.23 us
    pallas_call x1, Pallas kernels, token_rows(): pl.pallas_call(functools.partial(rows_kernel, len(chunks)), grid=(2 * til...  5.14 us
    dot_general x7, matrix products, dot(): return lax.dot_general(a, b, (dims, ((), ())), preferred_element_type=F32)  4.87 us
  transfers between devices with their start and end apart: 35, of which 16 were waited for; matrix products, arithmetic and copies ran while one was open for 8% of the time, Pallas kernels for 10%

profile of v15, /device:TPU:9, one launch (start us, length us, event | category | flops | bytes accessed | tf_op | source)
XLA Modules:
  0.0 230.8 jit_solution(4403561240072537428)
XLA Ops:
  2.3 3.4 %shard_map.118 = (bf16[768,256]{1,0:T(8,128)(2,1)}, bf16[768,256]{1,0:T(8,128)(2,1)}, bf16[384,256]{1,0:T(8,128)(2,1)}, bf16[384,256]{1,0:T(8,128)(2,1)}) custom-call(s32[1]{0:T(128)} %bitcast.1.x_ref, bf16[256,768]{1,0:T(8,128)(2,1)} %bitcast.34, bf16[256,768]{1,0:T(8,128)(2,1)} %bitcast.35, bf16[96,2048]{1,0:T(8,128)(2,1)} %bitcast.36, ...), custom_call_target="tpu_custom_call" | custom-call | tf_op jit(solution)/shard_map/pallas_call | solution.py:294
  5.7 3.7 %collective-permute-start = (bf16[768,256]{1,0:T(8,128)(2,1)}, bf16[768,256]{1,0:T(8,128)(2,1)S(1)}, u32[]{:S(2)}, u32[]{:S(2)}) collective-permute-start(bf16[768,256]{1,0:T(8,128)(2,1)} %get-tuple-element.62), channel_id=1, source_target_pairs={{0,0},{1,4},{2,2},{3,6},{4,1},{5,5},{6,3},{7,7},{8,8},{9,12},{10,1... | collective-permute-start | bytes 1179656 | tf_op jit(solution)/shard_map/ppermute | solution.py:47
  11.9 3.1 %collective-permute-done = bf16[768,256]{1,0:T(8,128)(2,1)S(1)} collective-permute-done((bf16[768,256]{1,0:T(8,128)(2,1)}, bf16[768,256]{1,0:T(8,128)(2,1)S(1)}, u32[]{:S(2)}, u32[]{:S(2)}) %collective-permute-start) | collective-permute-done | bytes 393248 | tf_op jit(solution)/shard_map/ppermute | solution.py:47
  15.0 3.6 %collective-permute-done.1 = bf16[768,256]{1,0:T(8,128)(2,1)S(1)} collective-permute-done((bf16[768,256]{1,0:T(8,128)(2,1)}, bf16[768,256]{1,0:T(8,128)(2,1)S(1)}, u32[]{:S(2)}, u32[]{:S(2)}) %collective-permute-start.1) | collective-permute-done | bytes 393248 | tf_op jit(solution)/shard_map/ppermute | solution.py:47
  22.3 3.2 %collective-permute-start.2 = (bf16[1536,256]{1,0:T(8,128)(2,1)}, bf16[1536,256]{1,0:T(8,128)(2,1)}, u32[]{:S(2)}, u32[]{:S(2)}) collective-permute-start(bf16[1536,256]{1,0:T(8,128)(2,1)} %pad_maximum_fusion.4.own), channel_id=1, source_target_pairs={{0,8},{1,9},{2,10},{3,11},{4,12},{5,13},{6,14},{7,15},{8,16},{9,17... | collective-permute-start | bytes 2359304 | tf_op jit(solution)/shard_map/ppermute | solution.py:47
  25.6 3.0 %collective-permute-start.3 = (bf16[1536,256]{1,0:T(8,128)(2,1)}, bf16[1536,256]{1,0:T(8,128)(2,1)}, u32[]{:S(2)}, u32[]{:S(2)}) collective-permute-start(bf16[1536,256]{1,0:T(8,128)(2,1)} %pad_maximum_fusion.4.own), channel_id=1, source_target_pairs={{8,0},{9,1},{10,2},{11,3},{12,4},{13,5},{14,6},{15,7},{16,8},{17,9... | collective-permute-start | bytes 2359304 | tf_op jit(solution)/shard_map/ppermute | solution.py:47
  32.3 10.8 %collective-permute-done.2.up = bf16[1536,256]{1,0:T(8,128)(2,1)} collective-permute-done((bf16[1536,256]{1,0:T(8,128)(2,1)}, bf16[1536,256]{1,0:T(8,128)(2,1)}, u32[]{:S(2)}, u32[]{:S(2)}) %collective-permute-start.2) | collective-permute-done | bytes 786464 | tf_op jit(solution)/shard_map/ppermute | solution.py:47
  43.2 2.9 %collective-permute-done.3.down = bf16[1536,256]{1,0:T(8,128)(2,1)} collective-permute-done((bf16[1536,256]{1,0:T(8,128)(2,1)}, bf16[1536,256]{1,0:T(8,128)(2,1)}, u32[]{:S(2)}, u32[]{:S(2)}) %collective-permute-start.3) | collective-permute-done | bytes 786464 | tf_op jit(solution)/shard_map/ppermute | solution.py:47
  46.1 3.2 %collective-permute-start.4 = (bf16[1536,256]{1,0:T(8,128)(2,1)}, bf16[1536,256]{1,0:T(8,128)(2,1)S(1)}, u32[]{:S(2)}, u32[]{:S(2)}) collective-permute-start(bf16[1536,256]{1,0:T(8,128)(2,1)} %collective-permute-done.2.up), channel_id=1, source_target_pairs={{8,16},{9,17},{10,18},{11,19},{12,20},{13,21},{14,22},{15,23},{16,... | collective-permute-start | bytes 2359304 | tf_op jit(solution)/shard_map/ppermute | solution.py:47
  51.9 4.2 %collective-permute-done.10 = bf16[72,4096]{1,0:T(8,128)(2,1)S(1)} collective-permute-done((bf16[72,4096]{1,0:T(8,128)(2,1)S(1)}, bf16[72,4096]{1,0:T(8,128)(2,1)S(1)}, u32[]{:S(2)}, u32[]{:S(2)}) %collective-permute-start.10) | collective-permute-done | bytes 589856 | tf_op jit(solution)/shard_map/ppermute | solution.py:47
  58.3 23.2 %collective-permute-done.6.last = bf16[1536,256]{1,0:T(8,128)(2,1)S(1)} collective-permute-done((bf16[1536,256]{1,0:T(8,128)(2,1)S(1)}, bf16[1536,256]{1,0:T(8,128)(2,1)S(1)}, u32[]{:S(2)}, u32[]{:S(2)}) %collective-permute-start.6) | collective-permute-done | bytes 786464 | tf_op jit(solution)/shard_map/ppermute | solution.py:47
  81.5 4.6 %collective-permute-done.5.down_2 = bf16[1536,256]{1,0:T(8,128)(2,1)S(1)} collective-permute-done((bf16[1536,256]{1,0:T(8,128)(2,1)}, bf16[1536,256]{1,0:T(8,128)(2,1)S(1)}, u32[]{:S(2)}, u32[]{:S(2)}) %collective-permute-start.5) | collective-permute-done | bytes 786464 | tf_op jit(solution)/shard_map/ppermute | solution.py:47
  87.5 3.0 %collective-permute-start.16 = (bf16[768,256]{1,0:T(8,128)(2,1)S(1)}, bf16[768,256]{1,0:T(8,128)(2,1)}, u32[]{:S(2)}, u32[]{:S(2)}) collective-permute-start(bf16[768,256]{1,0:T(8,128)(2,1)S(1)} %pad_maximum_fusion.5.own), channel_id=1, source_target_pairs={{8,0},{9,1},{10,2},{11,3},{12,4},{13,5},{14,6},{15,7},{16,8},{17,9... | collective-permute-start | bytes 1179656 | tf_op jit(solution)/shard_map/ppermute | solution.py:47
  94.3 9.9 %shard_map.119 = (bf16[2048,512]{1,0:T(8,128)(2,1)}, bf16[256,2048]{1,0:T(8,128)(2,1)}, bf16[576,256]{1,0:T(8,128)(2,1)S(1)}, bf16[576,512]{1,0:T(8,128)(2,1)S(1...) custom-call(s32[1]{0:T(128)} %bitcast.z_ref, ...), custom_call_target="tpu_custom_call" | custom-call | flops 3623878656 | bytes 4194304 | tf_op jit(solution)/shard_map/pallas_call | solution.py:320
  107.2 4.9 %collective-permute-start.17 = (bf16[768,256]{1,0:T(8,128)(2,1)}, bf16[768,256]{1,0:T(8,128)(2,1)}, u32[]{:S(2)}, u32[]{:S(2)}) collective-permute-start(bf16[768,256]{1,0:T(8,128)(2,1)} %collective-permute-done.16.down), channel_id=1, source_target_pairs={{8,0},{9,1},{10,2},{11,3},{12,4},{13,5},{14,6},{15,7},{16,8},{17,9... | collective-permute-start | bytes 1179656 | tf_op jit(solution)/shard_map/ppermute | solution.py:47
  114.2 5.8 %collective-permute-done.17.down_2 = bf16[768,256]{1,0:T(8,128)(2,1)} collective-permute-done((bf16[768,256]{1,0:T(8,128)(2,1)}, bf16[768,256]{1,0:T(8,128)(2,1)}, u32[]{:S(2)}, u32[]{:S(2)}) %collective-permute-start.17) | collective-permute-done | bytes 393248 | tf_op jit(solution)/shard_map/ppermute | solution.py:47
  122.3 2.8 %collective-permute-start.19 = (bf16[768,256]{1,0:T(8,128)(2,1)S(1)}, bf16[768,256]{1,0:T(8,128)(2,1)S(1)}, u32[]{:S(2)}, u32[]{:S(2)}) collective-permute-start(bf16[768,256]{1,0:T(8,128)(2,1)S(1)} %broadcast_select_fusion.1), channel_id=1, source_target_pairs={{8,0},{9,1},{10,2},{11,3},{12,4},{13,5},{14,6},{15,7},{16,24},{17,... | collective-permute-start | bytes 1179656 | tf_op jit(solution)/shard_map/ppermute | solution.py:47
  129.6 4.0 %collective-permute-start.18 = (bf16[1536,256]{1,0:T(8,128)(2,1)S(1)}, bf16[1536,256]{1,0:T(8,128)(2,1)S(1)}, u32[]{:S(2)}, u32[]{:S(2)}) collective-permute-start(bf16[1536,256]{1,0:T(8,128)(2,1)S(1)} %add_convert_fusion.4), channel_id=1, source_target_pairs={{0,8},{1,9},{2,10},{3,11},{4,12},{5,13},{6,14},{7,15},{8,16},{9,17... | collective-permute-start | bytes 2359304 | tf_op jit(solution)/shard_map/ppermute | solution.py:47
  135.3 8.0 %shard_map.120 = (bf16[2048,256]{1,0:T(8,128)(2,1)S(1)}, bf16[128,2048]{1,0:T(8,128)(2,1)S(1)}, bf16[576,128]{1,0:T(8,128)(2,1)S(1)}, bf16[576,256]{1,0:T(8,128)...) custom-call(s32[1]{0:T(128)} %bitcast.z_ref, ...), custom_call_target="tpu_custom_call" | custom-call | flops 1811939328 | bytes 4194304 | tf_op jit(solution)/shard_map/pallas_call | solution.py:320
  144.0 5.1 %shard_map.121 = (bf16[288,4096]{1,0:T(8,128)(2,1)S(1)}, bf16[288,4096]{1,0:T(8,128)(2,1)S(1)}) custom-call(bf16[2048,512]{1,0:T(8,128)(2,1)S(1)} %copy-done.8, bf16[256,2048]{1,0:T(8,128)(2,1)S(1)} %copy-done.9, bf16[576,256]{1,0:T(8,128)(2,1)S(1)} %copy-done.13, bf16[576,512]{1,0:T(8,128)(2,1)S(1)} %copy-done.11, ...), custom_call_target="tpu_custom_call" | custom-call | flops 2717908992 | bytes 2097152 | tf_op jit(solution)/shard_map/pallas_call | solution.py:360
  152.6 4.2 %collective-permute-done.21 = bf16[288,4096]{1,0:T(8,128)(2,1)S(1)} collective-permute-done((bf16[288,4096]{1,0:T(8,128)(2,1)S(1)}, bf16[288,4096]{1,0:T(8,128)(2,1)S(1)}, u32[]{:S(2)}, u32[]{:S(2)}) %collective-permute-start.21) | collective-permute-done | bytes 2359328 | tf_op jit(solution)/shard_map/ppermute | solution.py:47
  157.6 3.3 %collective-permute-start.25 = (bf16[1536,256]{1,0:T(8,128)(2,1)S(1)}, bf16[1536,256]{1,0:T(8,128)(2,1)S(1)}, u32[]{:S(2)}, u32[]{:S(2)}) collective-permute-start(bf16[1536,256]{1,0:T(8,128)(2,1)S(1)} %add_convert_fusion.3), channel_id=1, source_target_pairs={{0,8},{1,9},{2,10},{3,11},{4,12},{5,13},{6,14},{7,15},{8,16},{9,17... | collective-permute-start | bytes 2359304 | tf_op jit(solution)/shard_map/ppermute | solution.py:47
  166.6 11.7 %collective-permute-done.25 = bf16[1536,256]{1,0:T(8,128)(2,1)S(1)} collective-permute-done((bf16[1536,256]{1,0:T(8,128)(2,1)S(1)}, bf16[1536,256]{1,0:T(8,128)(2,1)S(1)}, u32[]{:S(2)}, u32[]{:S(2)}) %collective-permute-start.25) | collective-permute-done | bytes 786464 | tf_op jit(solution)/shard_map/ppermute | solution.py:47
  178.3 3.0 %collective-permute-done.26 = bf16[1536,256]{1,0:T(8,128)(2,1)S(1)} collective-permute-done((bf16[1536,256]{1,0:T(8,128)(2,1)S(1)}, bf16[1536,256]{1,0:T(8,128)(2,1)S(1)}, u32[]{:S(2)}, u32[]{:S(2)}) %collective-permute-start.26) | collective-permute-done | bytes 786464 | tf_op jit(solution)/shard_map/ppermute | solution.py:47
  181.7 5.1 %collective-permute-done.24 = bf16[768,256]{1,0:T(8,128)(2,1)S(1)} collective-permute-done((bf16[768,256]{1,0:T(8,128)(2,1)S(1)}, bf16[768,256]{1,0:T(8,128)(2,1)S(1)}, u32[]{:S(2)}, u32[]{:S(2)}) %collective-permute-start.24) | collective-permute-done | bytes 393248 | tf_op jit(solution)/shard_map/ppermute | solution.py:47
  188.1 6.6 %collective-permute-start.27 = (bf16[768,256]{1,0:T(8,128)(2,1)S(1)}, bf16[768,256]{1,0:T(8,128)(2,1)S(1)}, u32[]{:S(2)}, u32[]{:S(2)}) collective-permute-start(bf16[768,256]{1,0:T(8,128)(2,1)S(1)} %add_convert_fusion.8), channel_id=1, source_target_pairs={{0,8},{1,9},{2,10},{3,11},{4,12},{5,13},{6,14},{7,15},{8,16},{9,17... | collective-permute-start | bytes 1179656 | tf_op jit(solution)/shard_map/ppermute | solution.py:47
  197.3 3.4 %collective-permute-done.28 = bf16[768,256]{1,0:T(8,128)(2,1)S(1)} collective-permute-done((bf16[768,256]{1,0:T(8,128)(2,1)S(1)}, bf16[768,256]{1,0:T(8,128)(2,1)S(1)}, u32[]{:S(2)}, u32[]{:S(2)}) %collective-permute-start.28) | collective-permute-done | bytes 393248 | tf_op jit(solution)/shard_map/ppermute | solution.py:47
  204.3 3.4 %collective-permute-start.30 = (bf16[768,256]{1,0:T(8,128)(2,1)}, bf16[768,256]{1,0:T(8,128)(2,1)}, u32[]{:S(2)}, u32[]{:S(2)}) collective-permute-start(bf16[768,256]{1,0:T(8,128)(2,1)} %add_convert_fusion.7), channel_id=1, source_target_pairs={{0,8},{1,9},{2,10},{3,11},{4,12},{5,13},{6,14},{7,15},{8,16},{9,17... | collective-permute-start | bytes 1179656 | tf_op jit(solution)/shard_map/ppermute | solution.py:47
  207.8 2.7 %collective-permute-start.32 = (bf16[768,256]{1,0:T(8,128)(2,1)S(1)}, bf16[768,256]{1,0:T(8,128)(2,1)S(1)}, u32[]{:S(2)}, u32[]{:S(2)}) collective-permute-start(bf16[768,256]{1,0:T(8,128)(2,1)S(1)} %get-tuple-element.126), channel_id=1, source_target_pairs={{0,4},{1,0},{2,6},{3,2},{4,5},{5,1},{6,7},{7,3},{8,12},{9,8},{10,1... | collective-permute-start | bytes 1179656 | tf_op jit(solution)/shard_map/ppermute | solution.py:47
  210.5 3.6 %collective-permute-start.29 = (bf16[768,256]{1,0:T(8,128)(2,1)S(1)}, bf16[768,256]{1,0:T(8,128)(2,1)S(1)}, u32[]{:S(2)}, u32[]{:S(2)}) collective-permute-start(bf16[768,256]{1,0:T(8,128)(2,1)S(1)} %get-tuple-element.127), channel_id=1, source_target_pairs={{0,0},{1,4},{2,2},{3,6},{4,1},{5,5},{6,3},{7,7},{8,8},{9,12},{10,1... | collective-permute-start | bytes 1179656 | tf_op jit(solution)/shard_map/ppermute | solution.py:47
  216.2 3.1 %collective-permute-start.34 = (bf16[384,256]{1,0:T(8,128)(2,1)S(1)}, bf16[384,256]{1,0:T(8,128)(2,1)S(1)}, u32[]{:S(2)}, u32[]{:S(2)}) collective-permute-start(bf16[384,256]{1,0:T(8,128)(2,1)S(1)} %get-tuple-element.130), channel_id=1, source_target_pairs={{0,4},{1,0},{2,6},{3,2},{4,5},{5,1},{6,7},{7,3},{8,12},{9,8},{10,1... | collective-permute-start | bytes 589832 | tf_op jit(solution)/shard_map/ppermute | solution.py:47
  219.3 3.6 %collective-permute-start.33 = (bf16[384,256]{1,0:T(8,128)(2,1)S(1)}, bf16[384,256]{1,0:T(8,128)(2,1)S(1)}, u32[]{:S(2)}, u32[]{:S(2)}) collective-permute-start(bf16[384,256]{1,0:T(8,128)(2,1)S(1)} %get-tuple-element.131), channel_id=1, source_target_pairs={{0,0},{1,4},{2,2},{3,6},{4,1},{5,5},{6,3},{7,7},{8,8},{9,12},{10,1... | collective-permute-start | bytes 589832 | tf_op jit(solution)/shard_map/ppermute | solution.py:47
  (141 shorter events, 63.2 us)
Async XLA Ops:
  5.7 9.3 %collective-permute-start = (bf16[768,256]{1,0:T(8,128)(2,1)}, bf16[768,256]{1,0:T(8,128)(2,1)S(1)}, u32[]{:S(2)}, u32[]{:S(2)}) collective-permute-start(bf16[768,256]{1,0:T(8,128)(2,1)} %get-tuple-element.62), channel_id=1, source_target_pairs={{0,0},{1,4},{2,2},{3,6},{4,1},{5,5},{6,3},{7,7},{8,8},{9,12},{10,1... | collective-permute-start | bytes 1179656 | tf_op jit(solution)/shard_map/ppermute | solution.py:47
  9.3 9.2 %collective-permute-start.1 = (bf16[768,256]{1,0:T(8,128)(2,1)}, bf16[768,256]{1,0:T(8,128)(2,1)S(1)}, u32[]{:S(2)}, u32[]{:S(2)}) collective-permute-start(bf16[768,256]{1,0:T(8,128)(2,1)} %get-tuple-element.63), channel_id=1, source_target_pairs={{0,1},{1,5},{2,3},{3,7},{4,0},{5,4},{6,2},{7,6},{8,9},{9,13},{10,1... | collective-permute-start | bytes 1179656 | tf_op jit(solution)/shard_map/ppermute | solution.py:47
  19.5 9.0 %collective-permute-start.7 = (bf16[384,256]{1,0:T(8,128)(2,1)S(1)}, bf16[384,256]{1,0:T(8,128)(2,1)S(1)}, u32[]{:S(2)}, u32[]{:S(2)}) collective-permute-start(bf16[384,256]{1,0:T(8,128)(2,1)S(1)} %copy-done.26), channel_id=1, source_target_pairs={{0,0},{1,4},{2,2},{3,6},{4,1},{5,5},{6,3},{7,7},{8,8},{9,12},{10,1... | collective-permute-start | bytes 589832 | tf_op jit(solution)/shard_map/ppermute | solution.py:47
  22.3 20.8 %collective-permute-start.2 = (bf16[1536,256]{1,0:T(8,128)(2,1)}, bf16[1536,256]{1,0:T(8,128)(2,1)}, u32[]{:S(2)}, u32[]{:S(2)}) collective-permute-start(bf16[1536,256]{1,0:T(8,128)(2,1)} %pad_maximum_fusion.4.own), channel_id=1, source_target_pairs={{0,8},{1,9},{2,10},{3,11},{4,12},{5,13},{6,14},{7,15},{8,16},{9,17... | collective-permute-start | bytes 2359304 | tf_op jit(solution)/shard_map/ppermute | solution.py:47
  25.6 20.5 %collective-permute-start.3 = (bf16[1536,256]{1,0:T(8,128)(2,1)}, bf16[1536,256]{1,0:T(8,128)(2,1)}, u32[]{:S(2)}, u32[]{:S(2)}) collective-permute-start(bf16[1536,256]{1,0:T(8,128)(2,1)} %pad_maximum_fusion.4.own), channel_id=1, source_target_pairs={{8,0},{9,1},{10,2},{11,3},{12,4},{13,5},{14,6},{15,7},{16,8},{17,9... | collective-permute-start | bytes 2359304 | tf_op jit(solution)/shard_map/ppermute | solution.py:47
  29.7 26.4 %collective-permute-start.10 = (bf16[72,4096]{1,0:T(8,128)(2,1)S(1)}, bf16[72,4096]{1,0:T(8,128)(2,1)S(1)}, u32[]{:S(2)}, u32[]{:S(2)}) collective-permute-start(bf16[72,4096]{1,0:T(8,128)(2,1)S(1)} %get-tuple-element.124), channel_id=1, source_target_pairs={{0,2},{1,3},{2,0},{3,1},{4,6},{5,7},{6,4},{7,5},{8,10},{9,11},{10,... | collective-permute-start | bytes 1769480 | tf_op jit(solution)/shard_map/ppermute | solution.py:47
  30.9 27.1 %collective-permute-start.11 = (bf16[72,4096]{1,0:T(8,128)(2,1)S(1)}, bf16[72,4096]{1,0:T(8,128)(2,1)S(1)}, u32[]{:S(2)}, u32[]{:S(2)}) collective-permute-start(bf16[72,4096]{1,0:T(8,128)(2,1)S(1)} %get-tuple-element.123), channel_id=1, source_target_pairs={{0,6},{1,7},{2,4},{3,5},{4,2},{5,3},{6,0},{7,1},{8,14},{9,15},{10,... | collective-permute-start | bytes 1769480 | tf_op jit(solution)/shard_map/ppermute | solution.py:47
  32.1 25.9 %collective-permute-start.9 = (bf16[72,4096]{1,0:T(8,128)(2,1)S(1)}, bf16[72,4096]{1,0:T(8,128)(2,1)S(1)}, u32[]{:S(2)}, u32[]{:S(2)}) collective-permute-start(bf16[72,4096]{1,0:T(8,128)(2,1)S(1)} %get-tuple-element.125), channel_id=1, source_target_pairs={{0,4},{1,5},{2,6},{3,7},{4,0},{5,1},{6,2},{7,3},{8,12},{9,13},{10,... | collective-permute-start | bytes 1769480 | tf_op jit(solution)/shard_map/ppermute | solution.py:47
  46.1 35.4 %collective-permute-start.4 = (bf16[1536,256]{1,0:T(8,128)(2,1)}, bf16[1536,256]{1,0:T(8,128)(2,1)S(1)}, u32[]{:S(2)}, u32[]{:S(2)}) collective-permute-start(bf16[1536,256]{1,0:T(8,128)(2,1)} %collective-permute-done.2.up), channel_id=1, source_target_pairs={{8,16},{9,17},{10,18},{11,19},{12,20},{13,21},{14,22},{15,23},{16,... | collective-permute-start | bytes 2359304 | tf_op jit(solution)/shard_map/ppermute | solution.py:47
  50.5 31.0 %collective-permute-start.6 = (bf16[1536,256]{1,0:T(8,128)(2,1)S(1)}, bf16[1536,256]{1,0:T(8,128)(2,1)S(1)}, u32[]{:S(2)}, u32[]{:S(2)}) collective-permute-start(bf16[1536,256]{1,0:T(8,128)(2,1)S(1)} %broadcast_select_fusion), channel_id=1, source_target_pairs={{8,24},{9,25},{10,26},{11,27},{12,28},{13,29},{14,30},{15,31},{16,... | collective-permute-start | bytes 2359304 | tf_op jit(solution)/shard_map/ppermute | solution.py:47
  56.1 30.0 %collective-permute-start.5 = (bf16[1536,256]{1,0:T(8,128)(2,1)}, bf16[1536,256]{1,0:T(8,128)(2,1)S(1)}, u32[]{:S(2)}, u32[]{:S(2)}) collective-permute-start(bf16[1536,256]{1,0:T(8,128)(2,1)} %collective-permute-done.3.down), channel_id=1, source_target_pairs={{8,0},{9,1},{10,2},{11,3},{12,4},{13,5},{14,6},{15,7},{16,8},{17,9... | collective-permute-start | bytes 2359304 | tf_op jit(solution)/shard_map/ppermute | solution.py:47
  87.5 19.6 %collective-permute-start.16 = (bf16[768,256]{1,0:T(8,128)(2,1)S(1)}, bf16[768,256]{1,0:T(8,128)(2,1)}, u32[]{:S(2)}, u32[]{:S(2)}) collective-permute-start(bf16[768,256]{1,0:T(8,128)(2,1)S(1)} %pad_maximum_fusion.5.own), channel_id=1, source_target_pairs={{8,0},{9,1},{10,2},{11,3},{12,4},{13,5},{14,6},{15,7},{16,8},{17,9... | collective-permute-start | bytes 1179656 | tf_op jit(solution)/shard_map/ppermute | solution.py:47
  90.6 21.5 %collective-permute-start.14 = (bf16[768,256]{1,0:T(8,128)(2,1)S(1)}, bf16[768,256]{1,0:T(8,128)(2,1)}, u32[]{:S(2)}, u32[]{:S(2)}) collective-permute-start(bf16[768,256]{1,0:T(8,128)(2,1)S(1)} %pad_maximum_fusion.5.own), channel_id=1, source_target_pairs={{0,8},{1,9},{2,10},{3,11},{4,12},{5,13},{6,14},{7,15},{8,16},{9,17... | collective-permute-start | bytes 1179656 | tf_op jit(solution)/shard_map/ppermute | solution.py:47
  105.8 20.9 %collective-permute-start.13 = (bf16[1536,256]{1,0:T(8,128)(2,1)}, bf16[1536,256]{1,0:T(8,128)(2,1)}, u32[]{:S(2)}, u32[]{:S(2)}) collective-permute-start(bf16[1536,256]{1,0:T(8,128)(2,1)} %get-tuple-element.75), channel_id=1, source_target_pairs={{0,8},{1,9},{2,10},{3,11},{4,12},{5,13},{6,14},{7,15},{24,16},{25,... | collective-permute-start | bytes 2359304 | tf_op jit(solution)/shard_map/ppermute | solution.py:47
  107.2 12.8 %collective-permute-start.17 = (bf16[768,256]{1,0:T(8,128)(2,1)}, bf16[768,256]{1,0:T(8,128)(2,1)}, u32[]{:S(2)}, u32[]{:S(2)}) collective-permute-start(bf16[768,256]{1,0:T(8,128)(2,1)} %collective-permute-done.16.down), channel_id=1, source_target_pairs={{8,0},{9,1},{10,2},{11,3},{12,4},{13,5},{14,6},{15,7},{16,8},{17,9... | collective-permute-start | bytes 1179656 | tf_op jit(solution)/shard_map/ppermute | solution.py:47
  112.1 9.2 %collective-permute-start.15 = (bf16[768,256]{1,0:T(8,128)(2,1)}, bf16[768,256]{1,0:T(8,128)(2,1)}, u32[]{:S(2)}, u32[]{:S(2)}) collective-permute-start(bf16[768,256]{1,0:T(8,128)(2,1)} %collective-permute-done.14.up), channel_id=1, source_target_pairs={{8,16},{9,17},{10,18},{11,19},{12,20},{13,21},{14,22},{15,23},{16,... | collective-permute-start | bytes 1179656 | tf_op jit(solution)/shard_map/ppermute | solution.py:47
  122.3 11.3 %collective-permute-start.19 = (bf16[768,256]{1,0:T(8,128)(2,1)S(1)}, bf16[768,256]{1,0:T(8,128)(2,1)S(1)}, u32[]{:S(2)}, u32[]{:S(2)}) collective-permute-start(bf16[768,256]{1,0:T(8,128)(2,1)S(1)} %broadcast_select_fusion.1), channel_id=1, source_target_pairs={{8,0},{9,1},{10,2},{11,3},{12,4},{13,5},{14,6},{15,7},{16,24},{17,... | collective-permute-start | bytes 1179656 | tf_op jit(solution)/shard_map/ppermute | solution.py:47
  128.3 20.9 %collective-permute-start.20 = (bf16[1536,256]{1,0:T(8,128)(2,1)S(1)}, bf16[1536,256]{1,0:T(8,128)(2,1)S(1)}, u32[]{:S(2)}, u32[]{:S(2)}) collective-permute-start(bf16[1536,256]{1,0:T(8,128)(2,1)S(1)} %add_convert_fusion.4), channel_id=1, source_target_pairs={{16,8},{17,9},{18,10},{19,11},{20,12},{21,13},{22,14},{23,15},{24,... | collective-permute-start | bytes 2359304 | tf_op jit(solution)/shard_map/ppermute | solution.py:47
  129.6 19.6 %collective-permute-start.18 = (bf16[1536,256]{1,0:T(8,128)(2,1)S(1)}, bf16[1536,256]{1,0:T(8,128)(2,1)S(1)}, u32[]{:S(2)}, u32[]{:S(2)}) collective-permute-start(bf16[1536,256]{1,0:T(8,128)(2,1)S(1)} %add_convert_fusion.4), channel_id=1, source_target_pairs={{0,8},{1,9},{2,10},{3,11},{4,12},{5,13},{6,14},{7,15},{8,16},{9,17... | collective-permute-start | bytes 2359304 | tf_op jit(solution)/shard_map/ppermute | solution.py:47
  157.6 20.6 %collective-permute-start.25 = (bf16[1536,256]{1,0:T(8,128)(2,1)S(1)}, bf16[1536,256]{1,0:T(8,128)(2,1)S(1)}, u32[]{:S(2)}, u32[]{:S(2)}) collective-permute-start(bf16[1536,256]{1,0:T(8,128)(2,1)S(1)} %add_convert_fusion.3), channel_id=1, source_target_pairs={{0,8},{1,9},{2,10},{3,11},{4,12},{5,13},{6,14},{7,15},{8,16},{9,17... | collective-permute-start | bytes 2359304 | tf_op jit(solution)/shard_map/ppermute | solution.py:47
  161.0 20.3 %collective-permute-start.26 = (bf16[1536,256]{1,0:T(8,128)(2,1)S(1)}, bf16[1536,256]{1,0:T(8,128)(2,1)S(1)}, u32[]{:S(2)}, u32[]{:S(2)}) collective-permute-start(bf16[1536,256]{1,0:T(8,128)(2,1)S(1)} %add_convert_fusion.2), channel_id=1, source_target_pairs={{8,0},{9,1},{10,2},{11,3},{12,4},{13,5},{14,6},{15,7},{16,8},{17,9... | collective-permute-start | bytes 2359304 | tf_op jit(solution)/shard_map/ppermute | solution.py:47
  163.1 31.7 %collective-permute-start.22 = (bf16[2,72,4096]{2,1,0:T(8,128)(2,1)S(1)}, bf16[2,72,4096]{2,1,0:T(8,128)(2,1)S(1)}, u32[]{:S(2)}, u32[]{:S(2)}) collective-permute-start(bf16[2,72,4096]{2,1,0:T(8,128)(2,1)S(1)} %slice_bitcast_fusion), channel_id=1, source_target_pairs={{0,4},{1,5},{2,6},{3,7},{4,0},{5,1},{6,2},{7,3},{8,12},{9,13},{10,... | collective-permute-start | bytes 3538952 | tf_op jit(solution)/shard_map/ppermute | solution.py:47
  164.9 21.8 %collective-permute-start.24 = (bf16[768,256]{1,0:T(8,128)(2,1)S(1)}, bf16[768,256]{1,0:T(8,128)(2,1)S(1)}, u32[]{:S(2)}, u32[]{:S(2)}) collective-permute-start(bf16[768,256]{1,0:T(8,128)(2,1)S(1)} %get-tuple-element.98), channel_id=1, source_target_pairs={{0,8},{1,9},{2,10},{3,11},{4,12},{5,13},{6,14},{7,15},{24,16},{25,... | collective-permute-start | bytes 1179656 | tf_op jit(solution)/shard_map/ppermute | solution.py:47
  186.8 13.9 %collective-permute-start.28 = (bf16[768,256]{1,0:T(8,128)(2,1)S(1)}, bf16[768,256]{1,0:T(8,128)(2,1)S(1)}, u32[]{:S(2)}, u32[]{:S(2)}) collective-permute-start(bf16[768,256]{1,0:T(8,128)(2,1)S(1)} %add_convert_fusion.8), channel_id=1, source_target_pairs={{16,8},{17,9},{18,10},{19,11},{20,12},{21,13},{22,14},{23,15},{24,... | collective-permute-start | bytes 1179656 | tf_op jit(solution)/shard_map/ppermute | solution.py:47
  188.1 15.4 %collective-permute-start.27 = (bf16[768,256]{1,0:T(8,128)(2,1)S(1)}, bf16[768,256]{1,0:T(8,128)(2,1)S(1)}, u32[]{:S(2)}, u32[]{:S(2)}) collective-permute-start(bf16[768,256]{1,0:T(8,128)(2,1)S(1)} %add_convert_fusion.8), channel_id=1, source_target_pairs={{0,8},{1,9},{2,10},{3,11},{4,12},{5,13},{6,14},{7,15},{8,16},{9,17... | collective-permute-start | bytes 1179656 | tf_op jit(solution)/shard_map/ppermute | solution.py:47
  196.0 26.9 %collective-permute-start.23 = (bf16[2,72,4096]{2,1,0:T(8,128)(2,1)}, bf16[2,72,4096]{2,1,0:T(8,128)(2,1)}, u32[]{:S(2)}, u32[]{:S(2)}) collective-permute-start(bf16[2,72,4096]{2,1,0:T(8,128)(2,1)} %get-tuple-element.121), channel_id=1, source_target_pairs={{0,2},{1,3},{2,0},{3,1},{4,6},{5,7},{6,4},{7,5},{8,10},{9,11},{10,... | collective-permute-start | bytes 3538952 | tf_op jit(solution)/shard_map/ppermute | solution.py:47
  201.6 12.6 %collective-permute-start.31 = (bf16[768,256]{1,0:T(8,128)(2,1)}, bf16[768,256]{1,0:T(8,128)(2,1)S(1)}, u32[]{:S(2)}, u32[]{:S(2)}) collective-permute-start(bf16[768,256]{1,0:T(8,128)(2,1)} %add_convert_fusion.6), channel_id=1, source_target_pairs={{8,0},{9,1},{10,2},{11,3},{12,4},{13,5},{14,6},{15,7},{16,8},{17,9... | collective-permute-start | bytes 1179656 | tf_op jit(solution)/shard_map/ppermute | solution.py:47
  204.3 10.6 %collective-permute-start.30 = (bf16[768,256]{1,0:T(8,128)(2,1)}, bf16[768,256]{1,0:T(8,128)(2,1)}, u32[]{:S(2)}, u32[]{:S(2)}) collective-permute-start(bf16[768,256]{1,0:T(8,128)(2,1)} %add_convert_fusion.7), channel_id=1, source_target_pairs={{0,8},{1,9},{2,10},{3,11},{4,12},{5,13},{6,14},{7,15},{8,16},{9,17... | collective-permute-start | bytes 1179656 | tf_op jit(solution)/shard_map/ppermute | solution.py:47
  207.8 15.1 %collective-permute-start.32 = (bf16[768,256]{1,0:T(8,128)(2,1)S(1)}, bf16[768,256]{1,0:T(8,128)(2,1)S(1)}, u32[]{:S(2)}, u32[]{:S(2)}) collective-permute-start(bf16[768,256]{1,0:T(8,128)(2,1)S(1)} %get-tuple-element.126), channel_id=1, source_target_pairs={{0,4},{1,0},{2,6},{3,2},{4,5},{5,1},{6,7},{7,3},{8,12},{9,8},{10,1... | collective-permute-start | bytes 1179656 | tf_op jit(solution)/shard_map/ppermute | solution.py:47
  210.5 12.4 %collective-permute-start.29 = (bf16[768,256]{1,0:T(8,128)(2,1)S(1)}, bf16[768,256]{1,0:T(8,128)(2,1)S(1)}, u32[]{:S(2)}, u32[]{:S(2)}) collective-permute-start(bf16[768,256]{1,0:T(8,128)(2,1)S(1)} %get-tuple-element.127), channel_id=1, source_target_pairs={{0,0},{1,4},{2,2},{3,6},{4,1},{5,5},{6,3},{7,7},{8,8},{9,12},{10,1... | collective-permute-start | bytes 1179656 | tf_op jit(solution)/shard_map/ppermute | solution.py:47
  216.2 12.6 %collective-permute-start.34 = (bf16[384,256]{1,0:T(8,128)(2,1)S(1)}, bf16[384,256]{1,0:T(8,128)(2,1)S(1)}, u32[]{:S(2)}, u32[]{:S(2)}) collective-permute-start(bf16[384,256]{1,0:T(8,128)(2,1)S(1)} %get-tuple-element.130), channel_id=1, source_target_pairs={{0,4},{1,0},{2,6},{3,2},{4,5},{5,1},{6,7},{7,3},{8,12},{9,8},{10,1... | collective-permute-start | bytes 589832 | tf_op jit(solution)/shard_map/ppermute | solution.py:47
  219.3 9.5 %collective-permute-start.33 = (bf16[384,256]{1,0:T(8,128)(2,1)S(1)}, bf16[384,256]{1,0:T(8,128)(2,1)S(1)}, u32[]{:S(2)}, u32[]{:S(2)}) collective-permute-start(bf16[384,256]{1,0:T(8,128)(2,1)S(1)} %get-tuple-element.131), channel_id=1, source_target_pairs={{0,0},{1,4},{2,2},{3,6},{4,1},{5,5},{6,3},{7,7},{8,8},{9,12},{10,1... | collective-permute-start | bytes 589832 | tf_op jit(solution)/shard_map/ppermute | solution.py:47
  (30 other events, 297.6 us)

commit v16 on v15

--- a/solution.py
+++ b/solution.py
@@ -495,12 +495,11 @@
         sum_up, sum_down = added(terms[1], sum_up), added(terms[3], sum_down)
         give, outer2 = tie(give, sum_up, sum_down), tie(outer2, sum_up, sum_down)
         sums = added(keep, g.send(give, other_core)).reshape(g.qs, 2, cap, 2 * width)
-        sum_up, sum_down, sums = together((sum_up, sum_down, sums))
         sum_up, sum_down = g.hop(sum_up, ups), g.hop(sum_down, downs)
         begun2 = g.hop(outer2, outward)
         far_rows = g.send(sums[:, 1], lambda z, x, q, c: (z, 1 - x, q, c))
+        sum_up, sum_down, far_rows = together((sum_up, sum_down, far_rows))
         grad = added(terms[0], sum_up, sum_down)
-        begun2, grad = together((begun2, grad))
         middle2 = added(terms2[2], begun2)
         sum_up2, sum_down2 = g.hop(middle2, inward_up), g.hop(middle2, inward_down)
         near = jnp.stack([sums[:, 0], far_rows], axis=1)

time: 234 us -> 239 us (1.021)
  waiting for transfers between devices: 89.3 us -> 96.9 us
  starting transfers between devices: 82.6 us -> 79.2 us
    ppermute x35, waiting for transfers between devices: 89.3 us -> 96.9 us  [send(): return lax.ppermute(value, BOTH, pairs)]
    ppermute x35, starting transfers between devices: 82.6 us -> 79.2 us  [send(): return lax.ppermute(value, BOTH, pairs)]
    unnamed x54 -> x55, local copies, waits for them, and re-layouts: 6.34 us -> 6.49 us
where the time goes in v16:
time: 239 us; the launch traced here: 235 us
  waiting for transfers between devices  96.9 us (41%)
  starting transfers between devices  79.2 us (33%)
  Pallas kernels  28.3 us (12%)
  other arithmetic  16.4 us (7%)
  local copies, waits for them, and re-layouts  7.53 us (3%)
  matrix products  4.87 us (2%)
    ppermute x35, waiting for transfers between devices, send(): return lax.ppermute(value, BOTH, pairs)  96.9 us
    ppermute x35, starting transfers between devices, send(): return lax.ppermute(value, BOTH, pairs)  79.2 us
    pallas_call x2, Pallas kernels, expert(): pl.pallas_call(expert_kernel, out_shape=for_rows + [jax.ShapeDtypeStruct(...  17.8 us
    unnamed x55, local copies, waits for them, and re-layouts  6.49 us
    convert_element_type x9, other arithmetic, added(): return sum((t.astype(F32) for t in terms)).astype(BF)  6.26 us
    pallas_call x1, Pallas kernels, token_rows(): pl.pallas_call(functools.partial(rows_kernel, len(chunks)), grid=(2 * til...  5.14 us
    dot_general x7, matrix products, dot(): return lax.dot_general(a, b, (dims, ((), ())), preferred_element_type=F32)  4.87 us
  transfers between devices with their start and end apart: 35, of which 16 were waited for; matrix products, arithmetic and copies ran while one was open for 8% of the time, Pallas kernels for 10%

profile of v16, /device:TPU:9, one launch (start us, length us, event | category | flops | bytes accessed | tf_op | source)
XLA Modules:
  0.0 234.7 jit_solution(6835496148793949893)
XLA Ops:
  2.3 3.4 %shard_map.118 = (bf16[768,256]{1,0:T(8,128)(2,1)}, bf16[768,256]{1,0:T(8,128)(2,1)}, bf16[384,256]{1,0:T(8,128)(2,1)}, bf16[384,256]{1,0:T(8,128)(2,1)}) custom-call(s32[1]{0:T(128)} %bitcast.1.x_ref, bf16[256,768]{1,0:T(8,128)(2,1)} %bitcast.35, bf16[256,768]{1,0:T(8,128)(2,1)} %bitcast.36, bf16[96,2048]{1,0:T(8,128)(2,1)} %bitcast.37, ...), custom_call_target="tpu_custom_call" | custom-call | tf_op jit(solution)/shard_map/pallas_call | solution.py:294
  5.6 3.7 %collective-permute-start = (bf16[768,256]{1,0:T(8,128)(2,1)}, bf16[768,256]{1,0:T(8,128)(2,1)S(1)}, u32[]{:S(2)}, u32[]{:S(2)}) collective-permute-start(bf16[768,256]{1,0:T(8,128)(2,1)} %get-tuple-element.60), channel_id=1, source_target_pairs={{0,0},{1,4},{2,2},{3,6},{4,1},{5,5},{6,3},{7,7},{8,8},{9,12},{10,1... | collective-permute-start | bytes 1179656 | tf_op jit(solution)/shard_map/ppermute | solution.py:47
  11.9 3.1 %collective-permute-done = bf16[768,256]{1,0:T(8,128)(2,1)S(1)} collective-permute-done((bf16[768,256]{1,0:T(8,128)(2,1)}, bf16[768,256]{1,0:T(8,128)(2,1)S(1)}, u32[]{:S(2)}, u32[]{:S(2)}) %collective-permute-start) | collective-permute-done | bytes 393248 | tf_op jit(solution)/shard_map/ppermute | solution.py:47
  15.0 3.6 %collective-permute-done.1 = bf16[768,256]{1,0:T(8,128)(2,1)S(1)} collective-permute-done((bf16[768,256]{1,0:T(8,128)(2,1)}, bf16[768,256]{1,0:T(8,128)(2,1)S(1)}, u32[]{:S(2)}, u32[]{:S(2)}) %collective-permute-start.1) | collective-permute-done | bytes 393248 | tf_op jit(solution)/shard_map/ppermute | solution.py:47
  19.5 2.5 %collective-permute-start.7 = (bf16[384,256]{1,0:T(8,128)(2,1)S(1)}, bf16[384,256]{1,0:T(8,128)(2,1)S(1)}, u32[]{:S(2)}, u32[]{:S(2)}) collective-permute-start(bf16[384,256]{1,0:T(8,128)(2,1)S(1)} %copy-done.26), channel_id=1, source_target_pairs={{0,0},{1,4},{2,2},{3,6},{4,1},{5,5},{6,3},{7,7},{8,8},{9,12},{10,1... | collective-permute-start | bytes 589832 | tf_op jit(solution)/shard_map/ppermute | solution.py:47
  22.3 3.2 %collective-permute-start.2 = (bf16[1536,256]{1,0:T(8,128)(2,1)}, bf16[1536,256]{1,0:T(8,128)(2,1)}, u32[]{:S(2)}, u32[]{:S(2)}) collective-permute-start(bf16[1536,256]{1,0:T(8,128)(2,1)} %pad_maximum_fusion.4.own), channel_id=1, source_target_pairs={{0,8},{1,9},{2,10},{3,11},{4,12},{5,13},{6,14},{7,15},{8,16},{9,17... | collective-permute-start | bytes 2359304 | tf_op jit(solution)/shard_map/ppermute | solution.py:47
  25.5 3.0 %collective-permute-start.3 = (bf16[1536,256]{1,0:T(8,128)(2,1)}, bf16[1536,256]{1,0:T(8,128)(2,1)}, u32[]{:S(2)}, u32[]{:S(2)}) collective-permute-start(bf16[1536,256]{1,0:T(8,128)(2,1)} %pad_maximum_fusion.4.own), channel_id=1, source_target_pairs={{8,0},{9,1},{10,2},{11,3},{12,4},{13,5},{14,6},{15,7},{16,8},{17,9... | collective-permute-start | bytes 2359304 | tf_op jit(solution)/shard_map/ppermute | solution.py:47
  32.3 10.8 %collective-permute-done.2.up = bf16[1536,256]{1,0:T(8,128)(2,1)} collective-permute-done((bf16[1536,256]{1,0:T(8,128)(2,1)}, bf16[1536,256]{1,0:T(8,128)(2,1)}, u32[]{:S(2)}, u32[]{:S(2)}) %collective-permute-start.2) | collective-permute-done | bytes 786464 | tf_op jit(solution)/shard_map/ppermute | solution.py:47
  43.2 2.9 %collective-permute-done.3.down = bf16[1536,256]{1,0:T(8,128)(2,1)} collective-permute-done((bf16[1536,256]{1,0:T(8,128)(2,1)}, bf16[1536,256]{1,0:T(8,128)(2,1)}, u32[]{:S(2)}, u32[]{:S(2)}) %collective-permute-start.3) | collective-permute-done | bytes 786464 | tf_op jit(solution)/shard_map/ppermute | solution.py:47
  46.1 3.2 %collective-permute-start.4 = (bf16[1536,256]{1,0:T(8,128)(2,1)}, bf16[1536,256]{1,0:T(8,128)(2,1)S(1)}, u32[]{:S(2)}, u32[]{:S(2)}) collective-permute-start(bf16[1536,256]{1,0:T(8,128)(2,1)} %collective-permute-done.2.up), channel_id=1, source_target_pairs={{8,16},{9,17},{10,18},{11,19},{12,20},{13,21},{14,22},{15,23},{16,... | collective-permute-start | bytes 2359304 | tf_op jit(solution)/shard_map/ppermute | solution.py:47
  51.9 4.2 %collective-permute-done.10 = bf16[72,4096]{1,0:T(8,128)(2,1)S(1)} collective-permute-done((bf16[72,4096]{1,0:T(8,128)(2,1)S(1)}, bf16[72,4096]{1,0:T(8,128)(2,1)S(1)}, u32[]{:S(2)}, u32[]{:S(2)}) %collective-permute-start.10) | collective-permute-done | bytes 589856 | tf_op jit(solution)/shard_map/ppermute | solution.py:47
  58.3 23.2 %collective-permute-done.6.last = bf16[1536,256]{1,0:T(8,128)(2,1)S(1)} collective-permute-done((bf16[1536,256]{1,0:T(8,128)(2,1)S(1)}, bf16[1536,256]{1,0:T(8,128)(2,1)S(1)}, u32[]{:S(2)}, u32[]{:S(2)}) %collective-permute-start.6) | collective-permute-done | bytes 786464 | tf_op jit(solution)/shard_map/ppermute | solution.py:47
  81.5 4.6 %collective-permute-done.5.down_2 = bf16[1536,256]{1,0:T(8,128)(2,1)S(1)} collective-permute-done((bf16[1536,256]{1,0:T(8,128)(2,1)}, bf16[1536,256]{1,0:T(8,128)(2,1)S(1)}, u32[]{:S(2)}, u32[]{:S(2)}) %collective-permute-start.5) | collective-permute-done | bytes 786464 | tf_op jit(solution)/shard_map/ppermute | solution.py:47
  87.5 3.0 %collective-permute-start.14 = (bf16[768,256]{1,0:T(8,128)(2,1)S(1)}, bf16[768,256]{1,0:T(8,128)(2,1)}, u32[]{:S(2)}, u32[]{:S(2)}) collective-permute-start(bf16[768,256]{1,0:T(8,128)(2,1)S(1)} %pad_maximum_fusion.5.own), channel_id=1, source_target_pairs={{8,0},{9,1},{10,2},{11,3},{12,4},{13,5},{14,6},{15,7},{16,8},{17,9... | collective-permute-start | bytes 1179656 | tf_op jit(solution)/shard_map/ppermute | solution.py:47
  90.6 2.2 collective-permute-start.13
  94.3 9.9 %shard_map.119 = (bf16[2048,512]{1,0:T(8,128)(2,1)}, bf16[256,2048]{1,0:T(8,128)(2,1)}, bf16[576,256]{1,0:T(8,128)(2,1)S(1)}, bf16[576,512]{1,0:T(8,128)(2,1)S(1...) custom-call(s32[1]{0:T(128)} %bitcast.z_ref, ...), custom_call_target="tpu_custom_call" | custom-call | flops 3623878656 | bytes 4194304 | tf_op jit(solution)/shard_map/pallas_call | solution.py:320
  107.2 4.9 %collective-permute-start.16 = (bf16[768,256]{1,0:T(8,128)(2,1)}, bf16[768,256]{1,0:T(8,128)(2,1)}, u32[]{:S(2)}, u32[]{:S(2)}) collective-permute-start(bf16[768,256]{1,0:T(8,128)(2,1)} %collective-permute-done.14.down), channel_id=1, source_target_pairs={{8,0},{9,1},{10,2},{11,3},{12,4},{13,5},{14,6},{15,7},{16,8},{17,9... | collective-permute-start | bytes 1179656 | tf_op jit(solution)/shard_map/ppermute | solution.py:47
  114.1 5.8 %collective-permute-done.16.down_2 = bf16[768,256]{1,0:T(8,128)(2,1)} collective-permute-done((bf16[768,256]{1,0:T(8,128)(2,1)}, bf16[768,256]{1,0:T(8,128)(2,1)}, u32[]{:S(2)}, u32[]{:S(2)}) %collective-permute-start.16) | collective-permute-done | bytes 393248 | tf_op jit(solution)/shard_map/ppermute | solution.py:47
  122.3 2.8 %collective-permute-start.17 = (bf16[768,256]{1,0:T(8,128)(2,1)S(1)}, bf16[768,256]{1,0:T(8,128)(2,1)S(1)}, u32[]{:S(2)}, u32[]{:S(2)}) collective-permute-start(bf16[768,256]{1,0:T(8,128)(2,1)S(1)} %broadcast_select_fusion.1), channel_id=1, source_target_pairs={{8,0},{9,1},{10,2},{11,3},{12,4},{13,5},{14,6},{15,7},{16,24},{17,... | collective-permute-start | bytes 1179656 | tf_op jit(solution)/shard_map/ppermute | solution.py:47
  129.6 4.0 %collective-permute-start.19 = (bf16[1536,256]{1,0:T(8,128)(2,1)S(1)}, bf16[1536,256]{1,0:T(8,128)(2,1)S(1)}, u32[]{:S(2)}, u32[]{:S(2)}) collective-permute-start(bf16[1536,256]{1,0:T(8,128)(2,1)S(1)} %add_convert_fusion.4), channel_id=1, source_target_pairs={{0,8},{1,9},{2,10},{3,11},{4,12},{5,13},{6,14},{7,15},{8,16},{9,17... | collective-permute-start | bytes 2359304 | tf_op jit(solution)/shard_map/ppermute | solution.py:47
  135.3 7.9 %shard_map.120 = (bf16[2048,256]{1,0:T(8,128)(2,1)S(1)}, bf16[128,2048]{1,0:T(8,128)(2,1)S(1)}, bf16[576,128]{1,0:T(8,128)(2,1)S(1)}, bf16[576,256]{1,0:T(8,128)...) custom-call(s32[1]{0:T(128)} %bitcast.z_ref, ...), custom_call_target="tpu_custom_call" | custom-call | flops 1811939328 | bytes 4194304 | tf_op jit(solution)/shard_map/pallas_call | solution.py:320
  143.9 5.1 %shard_map.121 = (bf16[288,4096]{1,0:T(8,128)(2,1)S(1)}, bf16[288,4096]{1,0:T(8,128)(2,1)S(1)}) custom-call(bf16[2048,512]{1,0:T(8,128)(2,1)S(1)} %copy-done.8, bf16[256,2048]{1,0:T(8,128)(2,1)S(1)} %copy-done.9, bf16[576,256]{1,0:T(8,128)(2,1)S(1)} %copy-done.13, bf16[576,512]{1,0:T(8,128)(2,1)S(1)} %copy-done.11, ...), custom_call_target="tpu_custom_call" | custom-call | flops 2717908992 | bytes 2097152 | tf_op jit(solution)/shard_map/pallas_call | solution.py:360
  152.5 4.2 %collective-permute-done.21 = bf16[288,4096]{1,0:T(8,128)(2,1)S(1)} collective-permute-done((bf16[288,4096]{1,0:T(8,128)(2,1)S(1)}, bf16[288,4096]{1,0:T(8,128)(2,1)S(1)}, u32[]{:S(2)}, u32[]{:S(2)}) %collective-permute-start.21) | collective-permute-done | bytes 2359328 | tf_op jit(solution)/shard_map/ppermute | solution.py:47
  159.6 3.0 %collective-permute-start.23 = (bf16[1536,256]{1,0:T(8,128)(2,1)S(1)}, bf16[1536,256]{1,0:T(8,128)(2,1)S(1)}, u32[]{:S(2)}, u32[]{:S(2)}) collective-permute-start(bf16[1536,256]{1,0:T(8,128)(2,1)S(1)} %add_convert_fusion.2), channel_id=1, source_target_pairs={{8,0},{9,1},{10,2},{11,3},{12,4},{13,5},{14,6},{15,7},{16,8},{17,9... | collective-permute-start | bytes 2359304 | tf_op jit(solution)/shard_map/ppermute | solution.py:47
  162.6 2.4 %collective-permute-start.22 = (bf16[1536,256]{1,0:T(8,128)(2,1)S(1)}, bf16[1536,256]{1,0:T(8,128)(2,1)S(1)}, u32[]{:S(2)}, u32[]{:S(2)}) collective-permute-start(bf16[1536,256]{1,0:T(8,128)(2,1)S(1)} %add_convert_fusion.3), channel_id=1, source_target_pairs={{0,8},{1,9},{2,10},{3,11},{4,12},{5,13},{6,14},{7,15},{8,16},{9,17... | collective-permute-start | bytes 2359304 | tf_op jit(solution)/shard_map/ppermute | solution.py:47
  166.2 24.8 %collective-permute-done.26 = bf16[768,256]{1,0:T(8,128)(2,1)S(1)} collective-permute-done((bf16[768,256]{1,0:T(8,128)(2,1)S(1)}, bf16[768,256]{1,0:T(8,128)(2,1)S(1)}, u32[]{:S(2)}, u32[]{:S(2)}) %collective-permute-start.26) | collective-permute-done | bytes 393248 | tf_op jit(solution)/shard_map/ppermute | solution.py:47
  192.4 4.0 %collective-permute-start.27 = (bf16[768,256]{1,0:T(8,128)(2,1)S(1)}, bf16[768,256]{1,0:T(8,128)(2,1)S(1)}, u32[]{:S(2)}, u32[]{:S(2)}) collective-permute-start(bf16[768,256]{1,0:T(8,128)(2,1)S(1)} %add_convert_fusion.8), channel_id=1, source_target_pairs={{0,8},{1,9},{2,10},{3,11},{4,12},{5,13},{6,14},{7,15},{8,16},{9,17... | collective-permute-start | bytes 1179656 | tf_op jit(solution)/shard_map/ppermute | solution.py:47
  198.1 3.7 %collective-permute-done.28 = bf16[768,256]{1,0:T(8,128)(2,1)S(1)} collective-permute-done((bf16[768,256]{1,0:T(8,128)(2,1)S(1)}, bf16[768,256]{1,0:T(8,128)(2,1)S(1)}, u32[]{:S(2)}, u32[]{:S(2)}) %collective-permute-start.28) | collective-permute-done | bytes 393248 | tf_op jit(solution)/shard_map/ppermute | solution.py:47
  206.6 3.4 %collective-permute-start.30 = (bf16[768,256]{1,0:T(8,128)(2,1)}, bf16[768,256]{1,0:T(8,128)(2,1)}, u32[]{:S(2)}, u32[]{:S(2)}) collective-permute-start(bf16[768,256]{1,0:T(8,128)(2,1)} %add_convert_fusion.7), channel_id=1, source_target_pairs={{0,8},{1,9},{2,10},{3,11},{4,12},{5,13},{6,14},{7,15},{8,16},{9,17... | collective-permute-start | bytes 1179656 | tf_op jit(solution)/shard_map/ppermute | solution.py:47
  210.0 3.6 %collective-permute-start.32 = (bf16[768,256]{1,0:T(8,128)(2,1)S(1)}, bf16[768,256]{1,0:T(8,128)(2,1)S(1)}, u32[]{:S(2)}, u32[]{:S(2)}) collective-permute-start(bf16[768,256]{1,0:T(8,128)(2,1)S(1)} %get-tuple-element.124), channel_id=1, source_target_pairs={{0,4},{1,0},{2,6},{3,2},{4,5},{5,1},{6,7},{7,3},{8,12},{9,8},{10,1... | collective-permute-start | bytes 1179656 | tf_op jit(solution)/shard_map/ppermute | solution.py:47
  217.6 4.0 %collective-permute-start.34 = (bf16[384,256]{1,0:T(8,128)(2,1)S(1)}, bf16[384,256]{1,0:T(8,128)(2,1)S(1)}, u32[]{:S(2)}, u32[]{:S(2)}) collective-permute-start(bf16[384,256]{1,0:T(8,128)(2,1)S(1)} %get-tuple-element.128), channel_id=1, source_target_pairs={{0,4},{1,0},{2,6},{3,2},{4,5},{5,1},{6,7},{7,3},{8,12},{9,8},{10,1... | collective-permute-start | bytes 589832 | tf_op jit(solution)/shard_map/ppermute | solution.py:47
  221.5 2.5 %collective-permute-start.33 = (bf16[384,256]{1,0:T(8,128)(2,1)S(1)}, bf16[384,256]{1,0:T(8,128)(2,1)S(1)}, u32[]{:S(2)}, u32[]{:S(2)}) collective-permute-start(bf16[384,256]{1,0:T(8,128)(2,1)S(1)} %get-tuple-element.129), channel_id=1, source_target_pairs={{0,0},{1,4},{2,2},{3,6},{4,1},{5,5},{6,3},{7,7},{8,8},{9,12},{10,1... | collective-permute-start | bytes 589832 | tf_op jit(solution)/shard_map/ppermute | solution.py:47
  (139 shorter events, 60.8 us)
Async XLA Ops:
  5.6 9.3 %collective-permute-start = (bf16[768,256]{1,0:T(8,128)(2,1)}, bf16[768,256]{1,0:T(8,128)(2,1)S(1)}, u32[]{:S(2)}, u32[]{:S(2)}) collective-permute-start(bf16[768,256]{1,0:T(8,128)(2,1)} %get-tuple-element.60), channel_id=1, source_target_pairs={{0,0},{1,4},{2,2},{3,6},{4,1},{5,5},{6,3},{7,7},{8,8},{9,12},{10,1... | collective-permute-start | bytes 1179656 | tf_op jit(solution)/shard_map/ppermute | solution.py:47
  9.3 9.2 %collective-permute-start.1 = (bf16[768,256]{1,0:T(8,128)(2,1)}, bf16[768,256]{1,0:T(8,128)(2,1)S(1)}, u32[]{:S(2)}, u32[]{:S(2)}) collective-permute-start(bf16[768,256]{1,0:T(8,128)(2,1)} %get-tuple-element.61), channel_id=1, source_target_pairs={{0,1},{1,5},{2,3},{3,7},{4,0},{5,4},{6,2},{7,6},{8,9},{9,13},{10,1... | collective-permute-start | bytes 1179656 | tf_op jit(solution)/shard_map/ppermute | solution.py:47
  19.5 9.0 %collective-permute-start.7 = (bf16[384,256]{1,0:T(8,128)(2,1)S(1)}, bf16[384,256]{1,0:T(8,128)(2,1)S(1)}, u32[]{:S(2)}, u32[]{:S(2)}) collective-permute-start(bf16[384,256]{1,0:T(8,128)(2,1)S(1)} %copy-done.26), channel_id=1, source_target_pairs={{0,0},{1,4},{2,2},{3,6},{4,1},{5,5},{6,3},{7,7},{8,8},{9,12},{10,1... | collective-permute-start | bytes 589832 | tf_op jit(solution)/shard_map/ppermute | solution.py:47
  22.3 20.8 %collective-permute-start.2 = (bf16[1536,256]{1,0:T(8,128)(2,1)}, bf16[1536,256]{1,0:T(8,128)(2,1)}, u32[]{:S(2)}, u32[]{:S(2)}) collective-permute-start(bf16[1536,256]{1,0:T(8,128)(2,1)} %pad_maximum_fusion.4.own), channel_id=1, source_target_pairs={{0,8},{1,9},{2,10},{3,11},{4,12},{5,13},{6,14},{7,15},{8,16},{9,17... | collective-permute-start | bytes 2359304 | tf_op jit(solution)/shard_map/ppermute | solution.py:47
  25.5 20.5 %collective-permute-start.3 = (bf16[1536,256]{1,0:T(8,128)(2,1)}, bf16[1536,256]{1,0:T(8,128)(2,1)}, u32[]{:S(2)}, u32[]{:S(2)}) collective-permute-start(bf16[1536,256]{1,0:T(8,128)(2,1)} %pad_maximum_fusion.4.own), channel_id=1, source_target_pairs={{8,0},{9,1},{10,2},{11,3},{12,4},{13,5},{14,6},{15,7},{16,8},{17,9... | collective-permute-start | bytes 2359304 | tf_op jit(solution)/shard_map/ppermute | solution.py:47
  29.7 26.4 %collective-permute-start.10 = (bf16[72,4096]{1,0:T(8,128)(2,1)S(1)}, bf16[72,4096]{1,0:T(8,128)(2,1)S(1)}, u32[]{:S(2)}, u32[]{:S(2)}) collective-permute-start(bf16[72,4096]{1,0:T(8,128)(2,1)S(1)} %get-tuple-element.122), channel_id=1, source_target_pairs={{0,2},{1,3},{2,0},{3,1},{4,6},{5,7},{6,4},{7,5},{8,10},{9,11},{10,... | collective-permute-start | bytes 1769480 | tf_op jit(solution)/shard_map/ppermute | solution.py:47
  30.9 27.1 %collective-permute-start.11 = (bf16[72,4096]{1,0:T(8,128)(2,1)S(1)}, bf16[72,4096]{1,0:T(8,128)(2,1)S(1)}, u32[]{:S(2)}, u32[]{:S(2)}) collective-permute-start(bf16[72,4096]{1,0:T(8,128)(2,1)S(1)} %get-tuple-element.121), channel_id=1, source_target_pairs={{0,6},{1,7},{2,4},{3,5},{4,2},{5,3},{6,0},{7,1},{8,14},{9,15},{10,... | collective-permute-start | bytes 1769480 | tf_op jit(solution)/shard_map/ppermute | solution.py:47
  32.1 25.9 %collective-permute-start.9 = (bf16[72,4096]{1,0:T(8,128)(2,1)S(1)}, bf16[72,4096]{1,0:T(8,128)(2,1)S(1)}, u32[]{:S(2)}, u32[]{:S(2)}) collective-permute-start(bf16[72,4096]{1,0:T(8,128)(2,1)S(1)} %get-tuple-element.123), channel_id=1, source_target_pairs={{0,4},{1,5},{2,6},{3,7},{4,0},{5,1},{6,2},{7,3},{8,12},{9,13},{10,... | collective-permute-start | bytes 1769480 | tf_op jit(solution)/shard_map/ppermute | solution.py:47
  46.1 35.4 %collective-permute-start.4 = (bf16[1536,256]{1,0:T(8,128)(2,1)}, bf16[1536,256]{1,0:T(8,128)(2,1)S(1)}, u32[]{:S(2)}, u32[]{:S(2)}) collective-permute-start(bf16[1536,256]{1,0:T(8,128)(2,1)} %collective-permute-done.2.up), channel_id=1, source_target_pairs={{8,16},{9,17},{10,18},{11,19},{12,20},{13,21},{14,22},{15,23},{16,... | collective-permute-start | bytes 2359304 | tf_op jit(solution)/shard_map/ppermute | solution.py:47
  50.5 31.0 %collective-permute-start.6 = (bf16[1536,256]{1,0:T(8,128)(2,1)S(1)}, bf16[1536,256]{1,0:T(8,128)(2,1)S(1)}, u32[]{:S(2)}, u32[]{:S(2)}) collective-permute-start(bf16[1536,256]{1,0:T(8,128)(2,1)S(1)} %broadcast_select_fusion), channel_id=1, source_target_pairs={{8,24},{9,25},{10,26},{11,27},{12,28},{13,29},{14,30},{15,31},{16,... | collective-permute-start | bytes 2359304 | tf_op jit(solution)/shard_map/ppermute | solution.py:47
  56.1 30.0 %collective-permute-start.5 = (bf16[1536,256]{1,0:T(8,128)(2,1)}, bf16[1536,256]{1,0:T(8,128)(2,1)S(1)}, u32[]{:S(2)}, u32[]{:S(2)}) collective-permute-start(bf16[1536,256]{1,0:T(8,128)(2,1)} %collective-permute-done.3.down), channel_id=1, source_target_pairs={{8,0},{9,1},{10,2},{11,3},{12,4},{13,5},{14,6},{15,7},{16,8},{17,9... | collective-permute-start | bytes 2359304 | tf_op jit(solution)/shard_map/ppermute | solution.py:47
  87.5 19.6 %collective-permute-start.14 = (bf16[768,256]{1,0:T(8,128)(2,1)S(1)}, bf16[768,256]{1,0:T(8,128)(2,1)}, u32[]{:S(2)}, u32[]{:S(2)}) collective-permute-start(bf16[768,256]{1,0:T(8,128)(2,1)S(1)} %pad_maximum_fusion.5.own), channel_id=1, source_target_pairs={{8,0},{9,1},{10,2},{11,3},{12,4},{13,5},{14,6},{15,7},{16,8},{17,9... | collective-permute-start | bytes 1179656 | tf_op jit(solution)/shard_map/ppermute | solution.py:47
  90.6 21.5 %collective-permute-start.13 = (bf16[768,256]{1,0:T(8,128)(2,1)S(1)}, bf16[768,256]{1,0:T(8,128)(2,1)}, u32[]{:S(2)}, u32[]{:S(2)}) collective-permute-start(bf16[768,256]{1,0:T(8,128)(2,1)S(1)} %pad_maximum_fusion.5.own), channel_id=1, source_target_pairs={{0,8},{1,9},{2,10},{3,11},{4,12},{5,13},{6,14},{7,15},{8,16},{9,17... | collective-permute-start | bytes 1179656 | tf_op jit(solution)/shard_map/ppermute | solution.py:47
  105.7 20.9 %collective-permute-start.18 = (bf16[1536,256]{1,0:T(8,128)(2,1)}, bf16[1536,256]{1,0:T(8,128)(2,1)}, u32[]{:S(2)}, u32[]{:S(2)}) collective-permute-start(bf16[1536,256]{1,0:T(8,128)(2,1)} %get-tuple-element.77), channel_id=1, source_target_pairs={{0,8},{1,9},{2,10},{3,11},{4,12},{5,13},{6,14},{7,15},{24,16},{25,... | collective-permute-start | bytes 2359304 | tf_op jit(solution)/shard_map/ppermute | solution.py:47
  107.2 12.8 %collective-permute-start.16 = (bf16[768,256]{1,0:T(8,128)(2,1)}, bf16[768,256]{1,0:T(8,128)(2,1)}, u32[]{:S(2)}, u32[]{:S(2)}) collective-permute-start(bf16[768,256]{1,0:T(8,128)(2,1)} %collective-permute-done.14.down), channel_id=1, source_target_pairs={{8,0},{9,1},{10,2},{11,3},{12,4},{13,5},{14,6},{15,7},{16,8},{17,9... | collective-permute-start | bytes 1179656 | tf_op jit(solution)/shard_map/ppermute | solution.py:47
  112.1 9.2 %collective-permute-start.15 = (bf16[768,256]{1,0:T(8,128)(2,1)}, bf16[768,256]{1,0:T(8,128)(2,1)}, u32[]{:S(2)}, u32[]{:S(2)}) collective-permute-start(bf16[768,256]{1,0:T(8,128)(2,1)} %collective-permute-done.13.up), channel_id=1, source_target_pairs={{8,16},{9,17},{10,18},{11,19},{12,20},{13,21},{14,22},{15,23},{16,... | collective-permute-start | bytes 1179656 | tf_op jit(solution)/shard_map/ppermute | solution.py:47
  122.3 11.3 %collective-permute-start.17 = (bf16[768,256]{1,0:T(8,128)(2,1)S(1)}, bf16[768,256]{1,0:T(8,128)(2,1)S(1)}, u32[]{:S(2)}, u32[]{:S(2)}) collective-permute-start(bf16[768,256]{1,0:T(8,128)(2,1)S(1)} %broadcast_select_fusion.1), channel_id=1, source_target_pairs={{8,0},{9,1},{10,2},{11,3},{12,4},{13,5},{14,6},{15,7},{16,24},{17,... | collective-permute-start | bytes 1179656 | tf_op jit(solution)/shard_map/ppermute | solution.py:47
  128.3 20.8 %collective-permute-start.20 = (bf16[1536,256]{1,0:T(8,128)(2,1)S(1)}, bf16[1536,256]{1,0:T(8,128)(2,1)S(1)}, u32[]{:S(2)}, u32[]{:S(2)}) collective-permute-start(bf16[1536,256]{1,0:T(8,128)(2,1)S(1)} %add_convert_fusion.4), channel_id=1, source_target_pairs={{16,8},{17,9},{18,10},{19,11},{20,12},{21,13},{22,14},{23,15},{24,... | collective-permute-start | bytes 2359304 | tf_op jit(solution)/shard_map/ppermute | solution.py:47
  129.6 19.6 %collective-permute-start.19 = (bf16[1536,256]{1,0:T(8,128)(2,1)S(1)}, bf16[1536,256]{1,0:T(8,128)(2,1)S(1)}, u32[]{:S(2)}, u32[]{:S(2)}) collective-permute-start(bf16[1536,256]{1,0:T(8,128)(2,1)S(1)} %add_convert_fusion.4), channel_id=1, source_target_pairs={{0,8},{1,9},{2,10},{3,11},{4,12},{5,13},{6,14},{7,15},{8,16},{9,17... | collective-permute-start | bytes 2359304 | tf_op jit(solution)/shard_map/ppermute | solution.py:47
  157.7 38.7 %collective-permute-start.24 = (bf16[2,72,4096]{2,1,0:T(8,128)(2,1)S(1)}, bf16[2,72,4096]{2,1,0:T(8,128)(2,1)S(1)}, u32[]{:S(2)}, u32[]{:S(2)}) collective-permute-start(bf16[2,72,4096]{2,1,0:T(8,128)(2,1)S(1)} %get-tuple-element.119), channel_id=1, source_target_pairs={{0,4},{1,5},{2,6},{3,7},{4,0},{5,1},{6,2},{7,3},{8,12},{9,13},{10,... | collective-permute-start | bytes 3538952 | tf_op jit(solution)/shard_map/ppermute | solution.py:47
  159.6 36.8 %collective-permute-start.23 = (bf16[1536,256]{1,0:T(8,128)(2,1)S(1)}, bf16[1536,256]{1,0:T(8,128)(2,1)S(1)}, u32[]{:S(2)}, u32[]{:S(2)}) collective-permute-start(bf16[1536,256]{1,0:T(8,128)(2,1)S(1)} %add_convert_fusion.2), channel_id=1, source_target_pairs={{8,0},{9,1},{10,2},{11,3},{12,4},{13,5},{14,6},{15,7},{16,8},{17,9... | collective-permute-start | bytes 2359304 | tf_op jit(solution)/shard_map/ppermute | solution.py:47
  162.6 33.9 %collective-permute-start.22 = (bf16[1536,256]{1,0:T(8,128)(2,1)S(1)}, bf16[1536,256]{1,0:T(8,128)(2,1)S(1)}, u32[]{:S(2)}, u32[]{:S(2)}) collective-permute-start(bf16[1536,256]{1,0:T(8,128)(2,1)S(1)} %add_convert_fusion.3), channel_id=1, source_target_pairs={{0,8},{1,9},{2,10},{3,11},{4,12},{5,13},{6,14},{7,15},{8,16},{9,17... | collective-permute-start | bytes 2359304 | tf_op jit(solution)/shard_map/ppermute | solution.py:47
  164.9 26.1 %collective-permute-start.26 = (bf16[768,256]{1,0:T(8,128)(2,1)S(1)}, bf16[768,256]{1,0:T(8,128)(2,1)S(1)}, u32[]{:S(2)}, u32[]{:S(2)}) collective-permute-start(bf16[768,256]{1,0:T(8,128)(2,1)S(1)} %get-tuple-element.101), channel_id=1, source_target_pairs={{0,8},{1,9},{2,10},{3,11},{4,12},{5,13},{6,14},{7,15},{24,16},{25,... | collective-permute-start | bytes 1179656 | tf_op jit(solution)/shard_map/ppermute | solution.py:47
  191.1 10.7 %collective-permute-start.28 = (bf16[768,256]{1,0:T(8,128)(2,1)S(1)}, bf16[768,256]{1,0:T(8,128)(2,1)S(1)}, u32[]{:S(2)}, u32[]{:S(2)}) collective-permute-start(bf16[768,256]{1,0:T(8,128)(2,1)S(1)} %add_convert_fusion.8), channel_id=1, source_target_pairs={{16,8},{17,9},{18,10},{19,11},{20,12},{21,13},{22,14},{23,15},{24,... | collective-permute-start | bytes 1179656 | tf_op jit(solution)/shard_map/ppermute | solution.py:47
  192.4 13.4 %collective-permute-start.27 = (bf16[768,256]{1,0:T(8,128)(2,1)S(1)}, bf16[768,256]{1,0:T(8,128)(2,1)S(1)}, u32[]{:S(2)}, u32[]{:S(2)}) collective-permute-start(bf16[768,256]{1,0:T(8,128)(2,1)S(1)} %add_convert_fusion.8), channel_id=1, source_target_pairs={{0,8},{1,9},{2,10},{3,11},{4,12},{5,13},{6,14},{7,15},{8,16},{9,17... | collective-permute-start | bytes 1179656 | tf_op jit(solution)/shard_map/ppermute | solution.py:47
  201.7 25.0 %collective-permute-start.25 = (bf16[2,72,4096]{2,1,0:T(8,128)(2,1)}, bf16[2,72,4096]{2,1,0:T(8,128)(2,1)}, u32[]{:S(2)}, u32[]{:S(2)}) collective-permute-start(bf16[2,72,4096]{2,1,0:T(8,128)(2,1)} %get-tuple-element.117), channel_id=1, source_target_pairs={{0,2},{1,3},{2,0},{3,1},{4,6},{5,7},{6,4},{7,5},{8,10},{9,11},{10,... | collective-permute-start | bytes 3538952 | tf_op jit(solution)/shard_map/ppermute | solution.py:47
  203.8 12.0 %collective-permute-start.31 = (bf16[768,256]{1,0:T(8,128)(2,1)}, bf16[768,256]{1,0:T(8,128)(2,1)S(1)}, u32[]{:S(2)}, u32[]{:S(2)}) collective-permute-start(bf16[768,256]{1,0:T(8,128)(2,1)} %add_convert_fusion.6), channel_id=1, source_target_pairs={{8,0},{9,1},{10,2},{11,3},{12,4},{13,5},{14,6},{15,7},{16,8},{17,9... | collective-permute-start | bytes 1179656 | tf_op jit(solution)/shard_map/ppermute | solution.py:47
  206.6 9.8 %collective-permute-start.30 = (bf16[768,256]{1,0:T(8,128)(2,1)}, bf16[768,256]{1,0:T(8,128)(2,1)}, u32[]{:S(2)}, u32[]{:S(2)}) collective-permute-start(bf16[768,256]{1,0:T(8,128)(2,1)} %add_convert_fusion.7), channel_id=1, source_target_pairs={{0,8},{1,9},{2,10},{3,11},{4,12},{5,13},{6,14},{7,15},{8,16},{9,17... | collective-permute-start | bytes 1179656 | tf_op jit(solution)/shard_map/ppermute | solution.py:47
  210.0 14.0 %collective-permute-start.32 = (bf16[768,256]{1,0:T(8,128)(2,1)S(1)}, bf16[768,256]{1,0:T(8,128)(2,1)S(1)}, u32[]{:S(2)}, u32[]{:S(2)}) collective-permute-start(bf16[768,256]{1,0:T(8,128)(2,1)S(1)} %get-tuple-element.124), channel_id=1, source_target_pairs={{0,4},{1,0},{2,6},{3,2},{4,5},{5,1},{6,7},{7,3},{8,12},{9,8},{10,1... | collective-permute-start | bytes 1179656 | tf_op jit(solution)/shard_map/ppermute | solution.py:47
  213.7 11.6 %collective-permute-start.29 = (bf16[768,256]{1,0:T(8,128)(2,1)S(1)}, bf16[768,256]{1,0:T(8,128)(2,1)S(1)}, u32[]{:S(2)}, u32[]{:S(2)}) collective-permute-start(bf16[768,256]{1,0:T(8,128)(2,1)S(1)} %get-tuple-element.125), channel_id=1, source_target_pairs={{0,0},{1,4},{2,2},{3,6},{4,1},{5,5},{6,3},{7,7},{8,8},{9,12},{10,1... | collective-permute-start | bytes 1179656 | tf_op jit(solution)/shard_map/ppermute | solution.py:47
  217.6 15.1 %collective-permute-start.34 = (bf16[384,256]{1,0:T(8,128)(2,1)S(1)}, bf16[384,256]{1,0:T(8,128)(2,1)S(1)}, u32[]{:S(2)}, u32[]{:S(2)}) collective-permute-start(bf16[384,256]{1,0:T(8,128)(2,1)S(1)} %get-tuple-element.128), channel_id=1, source_target_pairs={{0,4},{1,0},{2,6},{3,2},{4,5},{5,1},{6,7},{7,3},{8,12},{9,8},{10,1... | collective-permute-start | bytes 589832 | tf_op jit(solution)/shard_map/ppermute | solution.py:47
  221.5 11.1 %collective-permute-start.33 = (bf16[384,256]{1,0:T(8,128)(2,1)S(1)}, bf16[384,256]{1,0:T(8,128)(2,1)S(1)}, u32[]{:S(2)}, u32[]{:S(2)}) collective-permute-start(bf16[384,256]{1,0:T(8,128)(2,1)S(1)} %get-tuple-element.129), channel_id=1, source_target_pairs={{0,0},{1,4},{2,2},{3,6},{4,1},{5,5},{6,3},{7,7},{8,8},{9,12},{10,1... | collective-permute-start | bytes 589832 | tf_op jit(solution)/shard_map/ppermute | solution.py:47
  (30 other events, 320.6 us)
